TPU v7x, 32 devices: a whole 2x2x4 slice. The times are simulated.
32 devices in a mesh: area: 16 (over z, x, core), snap: 2 (over y).
Axes of the slice: x: 2, y: 2, z: 4, core: 2. Of those that a mesh axis runs over, the one named last changes fastest.
Arguments:
- phasor_readings: float32 [64, 32768], P('snap', 'area')
- reading_error_spread: float32 [32768], P('area'), may hold values from 1 to 100
- starting_voltages: float32 [64, 32768], P('snap', 'area'), may hold values from -6 to 6
- derivative_pieces: bfloat16 [256, 4, 128, 128], P('area'), may hold values from -0.25 to 0.25
- derivative_tile_position: int32 [16, 16, 4], P('area'), may hold values from 0 to 23, as said below
- frontier_voltage_pieces: int32 [16, 2, 4], P('area'), may hold values from -1 to 15, as said below
- holder_line_order: int32 [16, 16, 256], P('area'), may hold values from -1 to 2047, as said below
- hub_line_order: int32 [16, 16, 256], P('area'), may hold values from -1 to 2047, as said below
- reciprocal_normal_operator: bfloat16 [32768, 2048], P(('area', 'snap'))
Outputs:
- state: float32 [64, 32768], P('snap', 'area')
Inputs may be any that keep to these rules, and one draw needn't show every extreme that they name: holder_line_order[d, c] lists the owner rows of area d that concentrator c handles, at most 256 of them, then -1; every owner row appears exactly once over all concentrators; some pair holds exactly 256. hub_line_order[c, d] lists the rows of concentrator c matching holder_line_order[d, c] entry by entry, with -1 at the same places; every concentrator row appears exactly once. `derivative_tile_position`: the 4 slots of one measurement block are distinct. frontier_voltage_pieces[a, 0] lists distinct blocks sent to area a - 1 and frontier_voltage_pieces[a, 1] those sent to area a + 1, 1 to 4 of them then -1; the list of area 0 toward lower and of the last area toward upper are all -1; some list holds 4.
All inputs are finite; a program needn't handle non-finite values.
Results may differ from a plain program's by a relative error of at most 0.0022.
Values may be sent and summed in bfloat16 or wider, within the bound.
No kernel may reach another device: no remote copies, remote signals or barrier semaphores. Data moves between devices by JAX's collectives and lax.ppermute only.
A program may use at most 64 MiB of HBM per device.

v0:
```python
import jax
import jax.numpy as jnp
from jax import lax
from jax.sharding import PartitionSpec as P

NS = 2048
BLK = 128
MEASURE_BLOCKS = 16
TOUCHED_BLOCKS = 4
TIES = 4
ITERS = 2
NB = 16
SLOT_COUNT = 24
READING_LINES = 2048


HIGHEST_PRECISION = lax.Precision.HIGHEST


def passed_along(block, axis, distance):
    devices = range(lax.axis_size(axis))
    route = [(i - distance, i) for i in devices if i - distance in devices]
    return lax.ppermute(block, axis, route)


def block_lookup(listing, total_blocks):
    return (listing[:, None] == jnp.arange(total_blocks, dtype=jnp.int32)[None, :]).astype(
        jnp.float32
    )


def pick_blocks(blocks, listing):
    onehot_table = block_lookup(listing, blocks.shape[1])
    return jnp.einsum("tb,sbc->stc", onehot_table, blocks, precision=HIGHEST_PRECISION)


def place_blocks(values, listing, total_blocks):
    onehot_table = block_lookup(listing, total_blocks)
    return jnp.einsum("stc,tb->sbc", values, onehot_table, precision=HIGHEST_PRECISION)


def pass_states(values, offset):
    return passed_along(values.astype(jnp.bfloat16), "area", offset).astype(values.dtype)


def return_grads(values, offset):
    return passed_along(values, "area", offset)


def snapshot_total(partial_sum):
    return lax.psum(partial_sum, "snap")


def on_device(
    phasor_readings,
    reading_error_spread,
    starting_voltages,
    derivative_pieces,
    derivative_tile_position,
    frontier_voltage_pieces,
    holder_line_order,
    hub_line_order,
    reciprocal_normal_operator,
):
    snap_dev = starting_voltages.shape[0]
    snaps_all = snap_dev * lax.axis_size("snap")
    slot_column_index = derivative_tile_position[0]
    ties_lower = frontier_voltage_pieces[0, 0]
    ties_upper = frontier_voltage_pieces[0, 1]
    own_flat = holder_line_order[0].reshape(-1)
    own_valid = own_flat >= 0
    own_gather = jnp.where(own_valid, own_flat, 0)
    own_place = jnp.where(own_valid, own_flat, READING_LINES)
    conc_flat = hub_line_order[0].reshape(-1)
    conc_valid = conc_flat >= 0
    hub_pickup = jnp.where(conc_valid, conc_flat, 0)
    slot_lookup = block_lookup(slot_column_index.reshape(-1), SLOT_COUNT)
    hub_readings = jnp.take(phasor_readings, hub_pickup, axis=1)
    collector_variance = jnp.take(reading_error_spread, hub_pickup)
    current = starting_voltages
    for step_index in range(ITERS):
        blocks = current.reshape(snap_dev, NB, BLK)
        from_below = pass_states(pick_blocks(blocks, ties_upper), 1)
        from_above = pass_states(pick_blocks(blocks, ties_lower), -1)
        augmented = jnp.concatenate([blocks, from_below, from_above], axis=1).astype(jnp.bfloat16)
        chosen = jnp.take(augmented, slot_column_index, axis=1)
        predicted = jnp.einsum(
            "jkrc,sjkc->sjr", derivative_pieces, chosen, preferred_element_type=jnp.float32
        ).reshape(snap_dev, READING_LINES)
        outgoing = jnp.where(own_valid[None, :], jnp.take(predicted, own_gather, axis=1), 0.0)
        incoming_blocks = lax.all_to_all(outgoing, "area", split_axis=1, concat_axis=1, tiled=True)
        residual_rows = hub_readings - incoming_blocks
        spread = snapshot_total(jnp.sum(residual_rows * residual_rows, axis=0)) / snaps_all
        scaled = jnp.where(
            conc_valid[None, :],
            residual_rows / (collector_variance[None, :] + spread[None, :]),
            0.0,
        ).astype(jnp.bfloat16)
        returned = lax.all_to_all(scaled, "area", split_axis=1, concat_axis=1, tiled=True)
        weighted = (
            jnp.zeros((snap_dev, READING_LINES), jnp.bfloat16)
            .at[:, own_place]
            .set(returned, mode="drop")
        )
        tile_grad = jnp.einsum(
            "jkrc,sjr->sjkc",
            derivative_pieces,
            weighted.reshape(snap_dev, MEASURE_BLOCKS, BLK),
            preferred_element_type=jnp.float32,
        )
        slot_grad = jnp.einsum(
            "sxc,xn->snc",
            tile_grad.reshape(snap_dev, MEASURE_BLOCKS * TOUCHED_BLOCKS, BLK),
            slot_lookup,
            precision=HIGHEST_PRECISION,
        )
        back_upper = return_grads(slot_grad[:, NB : NB + TIES], -1)
        back_lower = return_grads(slot_grad[:, NB + TIES :], 1)
        gradient = (
            slot_grad[:, :NB]
            + place_blocks(back_upper, ties_upper, NB)
            + place_blocks(back_lower, ties_lower, NB)
        )
        flat_grad = gradient.reshape(snap_dev, NS).astype(jnp.bfloat16)
        rows_all = jnp.einsum(
            "se,ie->si",
            lax.all_gather(flat_grad, "snap", axis=0, tiled=True),
            reciprocal_normal_operator,
            preferred_element_type=jnp.float32,
        )
        update = lax.all_to_all(rows_all, "snap", split_axis=0, concat_axis=1, tiled=True)
        current = current + update
    return current


def solution(mesh):
    placed = (
        P("snap", "area"),
        P("area"),
        P("snap", "area"),
        P("area", None, None, None),
        P("area", None, None),
        P("area", None, None),
        P("area", None, None),
        P("area", None, None),
        P(("area", "snap"), None),
    )
    return jax.shard_map(
        on_device, mesh=mesh, in_specs=placed, out_specs=P("snap", "area"), check_vma=False
    )
```

profile of v0, /device:TPU:16, one launch (start us, length us, event | category | flops | bytes accessed | tf_op | source)
XLA Modules:
  0.0 279.3 jit_solution(2333563131813938364)
XLA Ops:
  2.1 2.7 collective-permute-start.1
  5.1 1.9 collective-permute-start
  13.1 14.2 %gather_fusion.3 = f32[4096,32]{1,0:T(8,128)} fusion(f32[32,2048]{0,1:T(8,128)S(1)} %bitcast.194, s32[4096]{0:T(1024)S(1)} %fusion.28), kind=kCustom, calls=%fused_computation.2.clone | custom fusion | bytes 1064960 | tf_op jit(solution)/shard_map/jit(_take)/gather | solution.py:90
  27.3 6.0 %bitcast_select_fusion.1 = f32[32,4096]{0,1:T(8,128)} fusion(f32[4096,32]{1,0:T(8,128)} %gather_fusion.3, pred[4096]{0:T(1024)(128)(4,1)S(1)} %get-tuple-element.14, pred[4096]{0:T(1024)(128)(4,1)S(1)} %get-tuple-element.13), kind=kLoop, calls=%fused_computation.11 | loop fusion | flops 262144 | bytes 1056768 | tf_op jit(solution)/shard_map/jit(_where)/select_n | solution.py:90
  33.3 3.0 %copy.107 = f32[32,16,256]{2,0,1:T(8,128)} copy(f32[32,16,256]{0,2,1:T(8,128)} %bitcast.196) | data formatting | bytes 1048576 | tf_op jit(solution)/shard_map/all_to_all | solution.py:91
  36.3 6.4 %all-to-all-start = ((f32[32,16,256]{2,0,1:T(8,128)}), f32[32,16,256]{2,0,1:T(8,128)}, u32[]{:S(2)}, u32[]{:S(2)}) async-start(f32[32,16,256]{2,0,1:T(8,128)} %copy.107), calls=%async_computation | async-start | bytes 1048576 | tf_op jit(solution)/shard_map/all_to_all | solution.py:91
  43.4 23.0 %gather_fusion = f32[4096]{0:T(1024)S(1)} fusion(f32[2048]{0:T(1024)S(1)} %copy-done.1, s32[4096]{0:T(1024)S(1)} %broadcast_clamp_fusion), kind=kCustom, calls=%fused_computation.5 | custom fusion | bytes 49152 | tf_op jit(solution)/shard_map/jit(_take)/gather | solution.py:79
  66.4 14.2 %gather_fusion.1 = f32[4096,32]{1,0:T(8,128)} fusion(f32[32,2048]{0,1:T(8,128)S(1)} %copy.99, s32[4096]{0:T(1024)S(1)} %fusion.27), kind=kCustom, calls=%fused_computation.clone | custom fusion | bytes 1064960 | tf_op jit(solution)/shard_map/jit(_take)/gather | solution.py:78
  80.7 3.0 %copy.108 = f32[32,16,256]{0,2,1:T(8,128)} copy(f32[32,16,256]{2,0,1:T(8,128)} %all-to-all-done) | data formatting | bytes 1048576 | tf_op jit(solution)/shard_map/all_to_all | solution.py:91
  83.6 2.8 %multiply_reduce_fusion.1 = f32[4096]{0:T(1024)S(1)} fusion(f32[32,16,256]{0,2,1:T(8,128)} %copy.108, f32[4096,32]{1,0:T(8,128)} %gather_fusion.1, pred[4096]{0:T(1024)(128)(4,1)S(1)} %get-tuple-element.12), kind=kLoop, calls=%fused_computation.15 | loop fusion | flops 520192 | bytes 1069056 | tf_op jit(solution)/shard_map/reduce_sum | solution.py:93
  86.5 8.2 %psum.14 = f32[4096]{0:T(1024)S(1)} all-reduce(f32[4096]{0:T(1024)S(1)} %multiply_reduce_fusion.1), channel_id=1, replica_groups=mesh['area'=16,'snap'=2] {'snap'}, use_global_device_ids=true, to_apply=%region_1.4 | all-reduce | flops 4096 | bytes 32768 | tf_op jit(solution)/shard_map/psum | solution.py:51
  94.6 6.4 %select_convert_fusion.1 = bf16[32,4096]{0,1:T(8,128)(2,1)S(1)} fusion(f32[4096]{0:T(1024)S(1)} %multiply_add_fusion.1, pred[4096]{0:T(1024)(128)(4,1)S(1)} %get-tuple-element.11, f32[32,16,256]{0,2,1:T(8,128)} %copy.108, f32[4096,32]{1,0:T(8,128)} %gather_fusion.1, pred[4096]{0:T(1024)(128)(4,1)S(1)} %get-tuple-element.12), kind=kLoop, calls=%fused_computation.14 | loop fusion | flops 655360 | bytes 1335296 | tf_op jit(solution)/shard_map/convert_element_type | solution.py:98
  101.1 1.0 copy.109
  102.1 6.0 %all-to-all-start.1 = ((bf16[32,16,256]{2,0,1:T(8,128)(2,1)}), bf16[32,16,256]{2,0,1:T(8,128)(2,1)S(1)}, u32[]{:S(2)}, u32[]{:S(2)}) async-start(bf16[32,16,256]{2,0,1:T(8,128)(2,1)} %copy.109), calls=%async_computation.1 | async-start | bytes 524288 | tf_op jit(solution)/shard_map/all_to_all | solution.py:99
  108.2 8.2 %all-to-all-done.1 = bf16[32,16,256]{2,0,1:T(8,128)(2,1)S(1)} async-done(((bf16[32,16,256]{2,0,1:T(8,128)(2,1)}), bf16[32,16,256]{2,0,1:T(8,128)(2,1)S(1)}, u32[]{:S(2)}, u32[]{:S(2)}) %all-to-all-start.1) | async-done | bytes 262176 | tf_op jit(solution)/shard_map/all_to_all | solution.py:99
  116.4 1.3 copy.111
  117.8 11.2 %scatter_custom_fusion = bf16[32,2048]{0,1:T(8,128)(2,1)S(1)} fusion(s32[4096]{0:T(1024)S(1)} %bitcast.236, bf16[4096,32]{1,0:T(8,128)(2,1)} %copy.111, bf16[]{:T(256)} %constant.23.clone.1), kind=kCustom, calls=%fused_computation.52 | custom fusion | bytes 131584 | tf_op jit(solution)/shard_map/scatter | solution.py:103
  129.5 1.1 convolution_bitcast_fusion.1
  130.6 2.8 %collective-permute-start.2 = (f32[32,4,128]{2,1,0:T(4,128)S(1)}, f32[32,4,128]{2,1,0:T(4,128)S(1)}, u32[]{:S(2)}, u32[]{:S(2)}) collective-permute-start(f32[32,4,128]{2,1,0:T(4,128)S(1)} %get-tuple-element.10), channel_id=1, source_target_pairs={{2,0},{4,2},{6,4},{8,6},{10,8},{12,10},{14,12},{16,14},{18,16},{20... | collective-permute-start | bytes 196616 | tf_op jit(solution)/shard_map/ppermute | solution.py:23
  133.4 1.9 collective-permute-start.3
  135.8 4.1 %collective-permute-done.3 = f32[32,4,128]{2,1,0:T(4,128)S(1)} collective-permute-done((f32[32,4,128]{2,1,0:T(4,128)S(1)}, f32[32,4,128]{2,1,0:T(4,128)S(1)}, u32[]{:S(2)}, u32[]{:S(2)}) %collective-permute-start.3) | collective-permute-done | bytes 65568 | tf_op jit(solution)/shard_map/ppermute | solution.py:23
  140.3 5.6 %all_gather.6 = bf16[64,2048]{1,0:T(8,128)(2,1)S(1)} all-gather(bf16[32,2048]{1,0:T(8,128)(2,1)S(1)} %bitcast.221), channel_id=1, replica_groups=mesh['area'=16,'snap'=2] {'snap'}, dimensions={0}, use_global_device_ids=true | all-gather | bytes 393216 | tf_op jit(solution)/shard_map/all_gather | solution.py:127
  146.0 1.4 fusion.46
  147.4 7.6 %all_to_all.86 = f32[2,32,1024]{2,1,0:T(8,128)S(1)} all-to-all(f32[2,32,1024]{2,1,0:T(8,128)S(1)} %bitcast.213), channel_id=1, replica_groups=mesh['area'=16,'snap'=2] {'snap'}, dimensions={0} | all-to-all | bytes 524288 | tf_op jit(solution)/shard_map/all_to_all | solution.py:131
  155.6 1.9 collective-permute-start.5
  157.5 2.6 collective-permute-start.4
  160.2 3.5 %collective-permute-done.4 = bf16[32,4,128]{2,1,0:T(4,128)(2,1)S(1)} collective-permute-done((bf16[32,4,128]{2,1,0:T(4,128)(2,1)S(1)}, bf16[32,4,128]{2,1,0:T(4,128)(2,1)S(1)}, u32[]{:S(2)}, u32[]{:S(2)}) %collective-permute-start.4) | collective-permute-done | bytes 32800 | tf_op jit(solution)/shard_map/ppermute | solution.py:23
  164.4 1.5 convolution_bitcast_fusion.4
  165.9 1.3 copy.137
  167.2 14.2 %gather_fusion.5 = f32[4096,32]{1,0:T(8,128)} fusion(f32[32,2048]{0,1:T(8,128)S(1)} %bitcast.193, s32[4096]{0:T(1024)S(1)} %fusion.28), kind=kCustom, calls=%fused_computation.3.clone | custom fusion | bytes 1064960 | tf_op jit(solution)/shard_map/jit(_take)/gather | solution.py:90
  181.4 6.0 %bitcast_select_fusion = f32[32,4096]{0,1:T(8,128)} fusion(f32[4096,32]{1,0:T(8,128)} %gather_fusion.5, pred[4096]{0:T(1024)(128)(4,1)S(1)} %get-tuple-element.14, pred[4096]{0:T(1024)(128)(4,1)S(1)} %get-tuple-element.13), kind=kLoop, calls=%fused_computation.9 | loop fusion | flops 262144 | bytes 1056768 | tf_op jit(solution)/shard_map/jit(_where)/select_n | solution.py:90
  187.3 2.2 copy.122
  189.5 17.9 %all_to_all.87 = f32[32,16,256]{2,0,1:T(8,128)S(1)} all-to-all(f32[32,16,256]{2,0,1:T(8,128)S(1)} %copy.122), channel_id=1, replica_groups=mesh['area'=16,'snap'=2] {'area'}, dimensions={1} | all-to-all | bytes 1048576 | tf_op jit(solution)/shard_map/all_to_all | solution.py:91
  207.4 1.9 copy.123
  209.3 2.8 %multiply_reduce_fusion = f32[4096]{0:T(1024)S(1)} fusion(f32[32,16,256]{0,2,1:T(8,128)} %copy.123, f32[4096,32]{1,0:T(8,128)} %gather_fusion.1, pred[4096]{0:T(1024)(128)(4,1)S(1)} %get-tuple-element.12), kind=kLoop, calls=%fused_computation.13 | loop fusion | flops 520192 | bytes 1069056 | tf_op jit(solution)/shard_map/reduce_sum | solution.py:93
  212.2 6.7 %psum.15 = f32[4096]{0:T(1024)S(1)} all-reduce(f32[4096]{0:T(1024)S(1)} %multiply_reduce_fusion), channel_id=1, replica_groups=mesh['area'=16,'snap'=2] {'snap'}, use_global_device_ids=true, to_apply=%region_4.7 | all-reduce | flops 4096 | bytes 32768 | tf_op jit(solution)/shard_map/psum | solution.py:51
  218.9 6.4 %select_convert_fusion = bf16[32,4096]{0,1:T(8,128)(2,1)S(1)} fusion(f32[4096]{0:T(1024)S(1)} %multiply_add_fusion, pred[4096]{0:T(1024)(128)(4,1)S(1)} %get-tuple-element.11, f32[32,16,256]{0,2,1:T(8,128)} %copy.123, f32[4096,32]{1,0:T(8,128)} %gather_fusion.1, pred[4096]{0:T(1024)(128)(4,1)S(1)} %get-tuple-element.12), kind=kLoop, calls=%fused_computation.12 | loop fusion | flops 655360 | bytes 1335296 | tf_op jit(solution)/shard_map/convert_element_type | solution.py:98
  225.4 1.0 copy.124
  226.4 12.9 %all_to_all.88 = bf16[32,16,256]{2,0,1:T(8,128)(2,1)S(1)} all-to-all(bf16[32,16,256]{2,0,1:T(8,128)(2,1)} %copy.124), channel_id=1, replica_groups=mesh['area'=16,'snap'=2] {'area'}, dimensions={1} | all-to-all | bytes 524288 | tf_op jit(solution)/shard_map/all_to_all | solution.py:99
  239.3 1.3 copy.126
  240.7 11.2 %scatter_custom_fusion.1 = bf16[32,2048]{0,1:T(8,128)(2,1)S(1)} fusion(s32[4096]{0:T(1024)S(1)} %bitcast.237, bf16[4096,32]{1,0:T(8,128)(2,1)} %copy.126, bf16[]{:T(256)} %constant.23.clone.1), kind=kCustom, calls=%fused_computation.50 | custom fusion | bytes 131584 | tf_op jit(solution)/shard_map/scatter | solution.py:103
  252.4 1.1 convolution_bitcast_fusion
  253.5 2.8 %collective-permute-start.6 = (f32[32,4,128]{2,1,0:T(4,128)S(1)}, f32[32,4,128]{2,1,0:T(4,128)S(1)}, u32[]{:S(2)}, u32[]{:S(2)}) collective-permute-start(f32[32,4,128]{2,1,0:T(4,128)S(1)} %get-tuple-element.8), channel_id=1, source_target_pairs={{2,0},{4,2},{6,4},{8,6},{10,8},{12,10},{14,12},{16,14},{18,16},{20... | collective-permute-start | bytes 196616 | tf_op jit(solution)/shard_map/ppermute | solution.py:23
  256.3 1.9 collective-permute-start.7
  258.7 4.1 %collective-permute-done.7 = f32[32,4,128]{2,1,0:T(4,128)S(1)} collective-permute-done((f32[32,4,128]{2,1,0:T(4,128)S(1)}, f32[32,4,128]{2,1,0:T(4,128)S(1)}, u32[]{:S(2)}, u32[]{:S(2)}) %collective-permute-start.7) | collective-permute-done | bytes 65568 | tf_op jit(solution)/shard_map/ppermute | solution.py:23
  263.2 5.6 %all_gather.7 = bf16[64,2048]{1,0:T(8,128)(2,1)S(1)} all-gather(bf16[32,2048]{1,0:T(8,128)(2,1)S(1)} %bitcast.222), channel_id=1, replica_groups=mesh['area'=16,'snap'=2] {'snap'}, dimensions={0}, use_global_device_ids=true | all-gather | bytes 393216 | tf_op jit(solution)/shard_map/all_gather | solution.py:127
  268.9 1.4 fusion.48
  270.3 8.2 %all_to_all.89 = f32[2,32,1024]{2,1,0:T(8,128)S(1)} all-to-all(f32[2,32,1024]{2,1,0:T(8,128)S(1)} %bitcast.216), channel_id=1, replica_groups=mesh['area'=16,'snap'=2] {'snap'}, dimensions={0} | all-to-all | bytes 524288 | tf_op jit(solution)/shard_map/all_to_all | solution.py:131
  (81 shorter events, 13.9 us)
Async XLA Ops:
  0.0 11.9 %copy-start = (bf16[16,4,128,128]{3,2,1,0:T(8,128)(2,1)S(1)}, bf16[16,4,128,128]{3,2,1,0:T(8,128)(2,1)}, u32[]{:S(2)}) copy-start(bf16[16,4,128,128]{3,2,1,0:T(8,128)(2,1)} %param.16) | copy-start | bytes 6291460
  2.1 9.1 %collective-permute-start.1 = (bf16[32,4,128]{2,1,0:T(4,128)(2,1)S(1)}, bf16[32,4,128]{2,1,0:T(4,128)(2,1)S(1)}, u32[]{:S(2)}, u32[]{:S(2)}) collective-permute-start(bf16[32,4,128]{2,1,0:T(4,128)(2,1)S(1)} %fusion.7), channel_id=1, source_target_pairs={{2,0},{4,2},{6,4},{8,6},{10,8},{12,10},{14,12},{16,14},{18,16},{20... | collective-permute-start | bytes 98312 | tf_op jit(solution)/shard_map/ppermute | solution.py:23
  5.1 6.1 %collective-permute-start = (bf16[32,4,128]{2,1,0:T(4,128)(2,1)S(1)}, bf16[32,4,128]{2,1,0:T(4,128)(2,1)S(1)}, u32[]{:S(2)}, u32[]{:S(2)}) collective-permute-start(bf16[32,4,128]{2,1,0:T(4,128)(2,1)S(1)} %fusion.6), channel_id=1, source_target_pairs={{0,2},{2,4},{4,6},{6,8},{8,10},{10,12},{12,14},{14,16},{16,18},{18... | collective-permute-start | bytes 98312 | tf_op jit(solution)/shard_map/ppermute | solution.py:23
  33.3 9.5 %copy-start.8 = (s32[1,16,4]{1,2,0:T(4,128)S(1)}, s32[1,16,4]{1,2,0:T(4,128)}, u32[]{:S(2)}) copy-start(s32[1,16,4]{1,2,0:T(4,128)} %param.17) | copy-start | bytes 772
  33.3 9.7 %copy-start.6 = (s32[1,16,256]{2,1,0:T(8,128)S(1)}, s32[1,16,256]{2,1,0:T(8,128)}, u32[]{:S(2)}) copy-start(s32[1,16,256]{2,1,0:T(8,128)} %param.20) | copy-start | bytes 49156
  33.3 9.7 %copy-start.7 = (s32[1,16,256]{2,1,0:T(8,128)S(1)}, s32[1,16,256]{2,1,0:T(8,128)}, u32[]{:S(2)}) copy-start(s32[1,16,256]{2,1,0:T(8,128)} %param.19) | copy-start | bytes 49156
  33.3 9.7 %copy-start.5 = (f32[32,2048]{1,0:T(8,128)S(1)}, f32[32,2048]{1,0:T(8,128)}, u32[]{:S(2)}) copy-start(f32[32,2048]{1,0:T(8,128)} %param.13) | copy-start | bytes 786436
  33.3 10.1 %copy-start.1 = (f32[2048]{0:T(1024)S(1)}, f32[2048]{0:T(1024)}, u32[]{:S(2)}) copy-start(f32[2048]{0:T(1024)} %param.14) | copy-start | bytes 24580
  36.3 44.3 %all-to-all-start = ((f32[32,16,256]{2,0,1:T(8,128)}), f32[32,16,256]{2,0,1:T(8,128)}, u32[]{:S(2)}, u32[]{:S(2)}) async-start(f32[32,16,256]{2,0,1:T(8,128)} %copy.107), calls=%async_computation | async-start | bytes 1048576 | tf_op jit(solution)/shard_map/all_to_all | solution.py:91
  102.1 14.3 %all-to-all-start.1 = ((bf16[32,16,256]{2,0,1:T(8,128)(2,1)}), bf16[32,16,256]{2,0,1:T(8,128)(2,1)S(1)}, u32[]{:S(2)}, u32[]{:S(2)}) async-start(bf16[32,16,256]{2,0,1:T(8,128)(2,1)} %copy.109), calls=%async_computation.1 | async-start | bytes 524288 | tf_op jit(solution)/shard_map/all_to_all | solution.py:99
  129.0 17.0 %copy-start.2 = (bf16[1024,2048]{1,0:T(8,128)(2,1)S(1)}, bf16[1024,2048]{1,0:T(8,128)(2,1)}, u32[]{:S(2)}) copy-start(bf16[1024,2048]{1,0:T(8,128)(2,1)} %param.21) | copy-start | bytes 12582916
  130.6 4.7 %collective-permute-start.2 = (f32[32,4,128]{2,1,0:T(4,128)S(1)}, f32[32,4,128]{2,1,0:T(4,128)S(1)}, u32[]{:S(2)}, u32[]{:S(2)}) collective-permute-start(f32[32,4,128]{2,1,0:T(4,128)S(1)} %get-tuple-element.10), channel_id=1, source_target_pairs={{2,0},{4,2},{6,4},{8,6},{10,8},{12,10},{14,12},{16,14},{18,16},{20... | collective-permute-start | bytes 196616 | tf_op jit(solution)/shard_map/ppermute | solution.py:23
  133.4 6.5 %collective-permute-start.3 = (f32[32,4,128]{2,1,0:T(4,128)S(1)}, f32[32,4,128]{2,1,0:T(4,128)S(1)}, u32[]{:S(2)}, u32[]{:S(2)}) collective-permute-start(f32[32,4,128]{2,1,0:T(4,128)S(1)} %get-tuple-element.9), channel_id=1, source_target_pairs={{0,2},{2,4},{4,6},{6,8},{8,10},{10,12},{12,14},{14,16},{16,18},{18... | collective-permute-start | bytes 196616 | tf_op jit(solution)/shard_map/ppermute | solution.py:23
  146.0 9.0 %copy-start.4 = (f32[32,2048]{1,0:T(8,128)S(1)}, f32[32,2048]{1,0:T(8,128)}, u32[]{:S(2)}) copy-start(f32[32,2048]{1,0:T(8,128)} %param.15) | copy-start | bytes 786436
  155.6 4.6 %collective-permute-start.5 = (bf16[32,4,128]{2,1,0:T(4,128)(2,1)S(1)}, bf16[32,4,128]{2,1,0:T(4,128)(2,1)S(1)}, u32[]{:S(2)}, u32[]{:S(2)}) collective-permute-start(bf16[32,4,128]{2,1,0:T(4,128)(2,1)S(1)} %fusion.9), channel_id=1, source_target_pairs={{2,0},{4,2},{6,4},{8,6},{10,8},{12,10},{14,12},{16,14},{18,16},{20... | collective-permute-start | bytes 98312 | tf_op jit(solution)/shard_map/ppermute | solution.py:23
  157.5 6.1 %collective-permute-start.4 = (bf16[32,4,128]{2,1,0:T(4,128)(2,1)S(1)}, bf16[32,4,128]{2,1,0:T(4,128)(2,1)S(1)}, u32[]{:S(2)}, u32[]{:S(2)}) collective-permute-start(bf16[32,4,128]{2,1,0:T(4,128)(2,1)S(1)} %fusion.8), channel_id=1, source_target_pairs={{0,2},{2,4},{4,6},{6,8},{8,10},{10,12},{12,14},{14,16},{16,18},{18... | collective-permute-start | bytes 98312 | tf_op jit(solution)/shard_map/ppermute | solution.py:23
  251.9 17.0 %copy-start.3 = (bf16[1024,2048]{1,0:T(8,128)(2,1)S(1)}, bf16[1024,2048]{1,0:T(8,128)(2,1)}, u32[]{:S(2)}) copy-start(bf16[1024,2048]{1,0:T(8,128)(2,1)} %param.21) | copy-start | bytes 12582916
  253.5 4.7 %collective-permute-start.6 = (f32[32,4,128]{2,1,0:T(4,128)S(1)}, f32[32,4,128]{2,1,0:T(4,128)S(1)}, u32[]{:S(2)}, u32[]{:S(2)}) collective-permute-start(f32[32,4,128]{2,1,0:T(4,128)S(1)} %get-tuple-element.8), channel_id=1, source_target_pairs={{2,0},{4,2},{6,4},{8,6},{10,8},{12,10},{14,12},{16,14},{18,16},{20... | collective-permute-start | bytes 196616 | tf_op jit(solution)/shard_map/ppermute | solution.py:23
  256.3 6.5 %collective-permute-start.7 = (f32[32,4,128]{2,1,0:T(4,128)S(1)}, f32[32,4,128]{2,1,0:T(4,128)S(1)}, u32[]{:S(2)}, u32[]{:S(2)}) collective-permute-start(f32[32,4,128]{2,1,0:T(4,128)S(1)} %get-tuple-element.6), channel_id=1, source_target_pairs={{0,2},{2,4},{4,6},{6,8},{8,10},{10,12},{12,14},{14,16},{16,18},{18... | collective-permute-start | bytes 196616 | tf_op jit(solution)/shard_map/ppermute | solution.py:23
where the time goes:
time: 281 us; the launch traced here: 279 us
  local copies, waits for them, and re-layouts  111 us (40%)
  blocking collectives  72.8 us (26%)
  other arithmetic  32.8 us (12%)
  starting transfers between devices  31 us (11%)
  waiting for transfers between devices  20 us (7%)
  matrix products  10.9 us (4%)
    gather x2, local copies, waits for them, and re-layouts, on_device(): jnp.take(predicted, own_gather, axis=1)  28.4 us
    gather x1, local copies, waits for them, and re-layouts, on_device(): collector_variance = jnp.take(reading_error_spread, hub_pickup)  23 us
    scatter x2, local copies, waits for them, and re-layouts, on_device(): weighted = jnp.zeros((snap_dev, READING_LINES), jnp.bfloat16).at[:, own_p...  22.5 us
    ppermute x8, starting transfers between devices, passed_along(): return lax.ppermute(block, axis, route)  18.6 us
    all_to_all x1, blocking collectives, on_device(): lax.all_to_all(outgoing, 'area', split_axis=1, concat_axis=1, tiled=True)  17.9 us
    all_to_all x2, blocking collectives, on_device(): lax.all_to_all(rows_all, 'snap', split_axis=0, concat_axis=1, tiled=True)  15.8 us
    psum x2, blocking collectives, snapshot_total(): return lax.psum(partial_sum, 'snap')  14.9 us
    gather x1, local copies, waits for them, and re-layouts, on_device(): hub_readings = jnp.take(phasor_readings, hub_pickup, axis=1)  14.2 us
  transfers between devices with their start and end apart: 10, of which 4 were waited for; matrix products, arithmetic and copies ran while one was open for 15% of the time, Pallas kernels for 0%

commit v1 on v0

v1 whole, which is shorter than its diff:
```python
import functools

import jax
import jax.numpy as jnp
from jax import lax
from jax.experimental import pallas as pl
from jax.experimental.pallas import tpu as pltpu
from jax.sharding import PartitionSpec as P

BLK = 128
ITERS = 2
F32 = jnp.float32
BF16 = jnp.bfloat16
NT = (((1,), (1,)), ((), ()))
VMEM = pl.BlockSpec(memory_space=pltpu.VMEM)
SMEM = pl.BlockSpec(memory_space=pltpu.SMEM)


def call(kernel, outs, ins, args, scratch=(), flops=0, bytes_accessed=0, name=None):
    return pl.pallas_call(
        kernel,
        out_shape=outs,
        in_specs=ins,
        out_specs=jax.tree.map(lambda _: VMEM, outs),
        scratch_shapes=list(scratch),
        compiler_params=pltpu.CompilerParams(vmem_limit_bytes=40 * 1024 * 1024),
        cost_estimate=pl.CostEstimate(
            flops=flops, bytes_accessed=bytes_accessed, transcendentals=0
        ),
        name=name,
    )(*args)


def lane_gather(values, lanes):
    return jnp.take_along_axis(values, lanes, axis=1, mode="promise_in_bounds")


def rows_iota(shape):
    return lax.broadcasted_iota(jnp.int32, shape, 0)


def pack_kernel(z_ref, v_ref, hub_ref, out_ref, slot_ref):
    snaps, lines = z_ref.shape
    blocks = lines // BLK
    chunks, width = hub_ref.shape
    groups = width // BLK
    for d in range(chunks):
        for g in range(groups):
            slot_ref[d, g : g + 1] = hub_ref[d : d + 1, g * BLK : (g + 1) * BLK]

    def chunk(d, carry):
        tail = jnp.zeros((16, BLK), F32)
        for g in range(groups):
            slot = slot_ref[d, g : g + 1]
            high = jnp.right_shift(slot, 7)
            low = jnp.bitwise_and(slot, 127)
            lanes = jnp.broadcast_to(low, (snaps, BLK))
            block_of = jnp.broadcast_to(high, (snaps, BLK))
            picked = jnp.zeros((snaps, BLK), F32)
            for b in range(blocks):
                found = lane_gather(z_ref[:, b * BLK : (b + 1) * BLK], lanes)
                picked = jnp.where(block_of == b, found, picked)
            out_ref[d, g * snaps : (g + 1) * snaps, :] = picked.astype(BF16)
            found = lane_gather(v_ref[...], jnp.broadcast_to(low, (blocks, BLK)))
            mine = rows_iota((blocks, BLK)) == high
            variance = jnp.sum(jnp.where(mine, found, 0.0), axis=0, keepdims=True)
            upper = variance.astype(BF16).astype(F32)
            row = rows_iota((16, BLK))
            tail = jnp.where(row == 2 * g, upper, tail)
            tail = jnp.where(row == 2 * g + 1, variance - upper, tail)
        out_ref[d, groups * snaps :, :] = tail.astype(BF16)
        return carry

    lax.fori_loop(0, chunks, chunk, 0)


def inverse_kernel(own_ref, group_ref, lane_ref):
    chunks, width = own_ref.shape
    blocks = group_ref.shape[0]
    groups = width // BLK
    total = jnp.zeros((2 * blocks, BLK), F32)
    lane = lax.broadcasted_iota(jnp.int32, (2 * blocks, width), 1)
    row = rows_iota((2 * blocks, width))
    in_group = jnp.bitwise_and(lane, 127)
    group_in = jnp.right_shift(lane, 7)
    for d in range(chunks):
        owned = own_ref[d : d + 1, :]
        high = jnp.right_shift(owned, 7)
        low = jnp.bitwise_and(owned, 127)
        label = jnp.where(row < blocks, group_in + d * groups, in_group)
        hit = jnp.bitwise_and(row, blocks - 1) == high
        left = jnp.where(hit, label.astype(F32), 0.0).astype(BF16)
        right = jnp.where(rows_iota((BLK, width)) == low, 1.0, 0.0).astype(BF16)
        total += lax.dot_general(left, right, NT, preferred_element_type=F32)
    group_ref[...] = total[:blocks].astype(jnp.int32)
    lane_ref[...] = total[blocks:].astype(jnp.int32)


def unpack_kernel(message_ref, group_ref, lane_ref, z_ref, v_ref, wide_ref, upper_ref):
    chunks = message_ref.shape[0]
    snaps, lines = z_ref.shape
    blocks = lines // BLK
    groups = (message_ref.shape[1] - 16) // snaps
    for d in range(chunks):
        tail = message_ref[d, groups * snaps :, :].astype(F32)
        for g in range(groups):
            at = d * groups + g
            wide_ref[at] = message_ref[d, g * snaps : (g + 1) * snaps, :].astype(F32)
            upper_ref[at : at + 1, :] = tail[2 * g : 2 * g + 1] + tail[2 * g + 1 : 2 * g + 2]
    total = chunks * groups

    def block(b, carry):
        group = group_ref[pl.ds(b, 1), :]
        lane = lane_ref[pl.ds(b, 1), :]
        lanes = jnp.broadcast_to(lane, (snaps, BLK))
        group_of = jnp.broadcast_to(group, (snaps, BLK))
        picked = jnp.zeros((snaps, BLK), F32)
        for g in range(total):
            picked = jnp.where(group_of == g, lane_gather(wide_ref[g], lanes), picked)
        columns = pl.ds(pl.multiple_of(b * BLK, BLK), BLK)
        z_ref[:, columns] = picked.astype(BF16)
        found = lane_gather(upper_ref[...], jnp.broadcast_to(lane, (total, BLK)))
        mine = rows_iota((total, BLK)) == group
        v_ref[:, columns] = jnp.sum(jnp.where(mine, found, 0.0), axis=0, keepdims=True)
        return carry

    lax.fori_loop(0, blocks, block, 0)


def pick(source, listing_ref, side, out_ref):
    for t in range(out_ref.shape[0]):
        b = listing_ref[side, t]
        block = source(jnp.maximum(b, 0))
        out_ref[t] = jnp.where(b >= 0, block, jnp.zeros_like(block))


def first_states_kernel(own_ref, others_ref, ties_ref, aug_ref, lower_ref, upper_ref):
    snaps = own_ref.shape[0]
    for b in range(aug_ref.shape[0]):
        columns = slice(b * BLK, (b + 1) * BLK)
        aug_ref[b, :snaps] = own_ref[:, columns].astype(BF16)
        for i in range(others_ref.shape[0]):
            aug_ref[b, (i + 1) * snaps : (i + 2) * snaps] = others_ref[i, :, columns].astype(BF16)
    pick(lambda b: aug_ref[b], ties_ref, 0, lower_ref)
    pick(lambda b: aug_ref[b], ties_ref, 1, upper_ref)


def join_states_kernel(mine_ref, others_ref, ties_ref, aug_ref, lower_ref, upper_ref):
    held, everything = mine_ref.shape[:2]
    members = others_ref.shape[0] + 1
    snaps = everything // members
    me = lax.axis_index("snap")
    aug_ref[pl.ds(me * held, held)] = mine_ref[...]
    for i in range(1, members):
        at = lax.rem(me + members - i, members) * held
        for j in range(members):
            to = (j - i) % members
            aug_ref[pl.ds(at, held), to * snaps : (to + 1) * snaps] = others_ref[
                i - 1, :, j * snaps : (j + 1) * snaps
            ]
    pick(lambda b: aug_ref[b], ties_ref, 0, lower_ref)
    pick(lambda b: aug_ref[b], ties_ref, 1, upper_ref)


def slots_into(slots_ref, aug_ref, below_ref, above_ref):
    own = aug_ref.shape[0]
    ties = below_ref.shape[0]
    slots_ref[:own] = aug_ref[...]
    slots_ref[own : own + ties] = below_ref[...]
    slots_ref[own + ties :] = above_ref[...]


def predicted(j, slots_ref, tiles_ref, place_ref):
    touched = tiles_ref.shape[1]
    chosen = jnp.concatenate([slots_ref[place_ref[j, k]] for k in range(touched)], axis=1)
    weights = jnp.concatenate([tiles_ref[j, k] for k in range(touched)], axis=1)
    return lax.dot_general(chosen, weights, NT, preferred_element_type=F32)


def predict_kernel(aug_ref, below_ref, above_ref, tiles_ref, place_ref, out_ref, slots_ref):
    slots_into(slots_ref, aug_ref, below_ref, above_ref)
    for j in range(tiles_ref.shape[0]):
        out_ref[:, j * BLK : (j + 1) * BLK] = predicted(j, slots_ref, tiles_ref, place_ref)


def pull(j, guess, z_ref, others_ref, v_ref, tiles_ref, place_ref, total_ref):
    columns = slice(j * BLK, (j + 1) * BLK)
    readings = [z_ref[:, columns]] + [o[:, columns] for o in split(others_ref)]
    resid = jnp.concatenate(readings, axis=0).astype(F32) - guess
    spread = jnp.sum(resid * resid, axis=0, keepdims=True) / resid.shape[0]
    weighted = (resid / (v_ref[:, columns] + spread)).astype(BF16)
    touched = tiles_ref.shape[1]
    weights = jnp.concatenate([tiles_ref[j, k] for k in range(touched)], axis=1)
    part = jnp.dot(weighted, weights, preferred_element_type=F32)
    for k in range(touched):
        n = place_ref[j, k]
        total_ref[n] += part[:, k * BLK : (k + 1) * BLK]


def split(ref):
    return [ref.at[i] for i in range(ref.shape[0])]


def give(total_ref, own_ref, below_ref, above_ref):
    own = own_ref.shape[0]
    ties = below_ref.shape[0]
    own_ref[...] = total_ref[:own]
    below_ref[...] = total_ref[own : own + ties]
    above_ref[...] = total_ref[own + ties :]


def pull_kernel(
    guess_ref, z_ref, others_ref, v_ref, tiles_ref, place_ref, own_ref, below_ref, above_ref, total_ref
):
    total_ref[...] = jnp.zeros_like(total_ref)
    for j in range(tiles_ref.shape[0]):
        guess = guess_ref[:, j * BLK : (j + 1) * BLK]
        pull(j, guess, z_ref, others_ref, v_ref, tiles_ref, place_ref, total_ref)
    give(total_ref, own_ref, below_ref, above_ref)


def predict_pull_kernel(
    aug_ref, below_in_ref, above_in_ref, z_ref, others_ref, v_ref, tiles_ref, place_ref,
    own_ref, below_ref, above_ref, slots_ref, total_ref,
):
    slots_into(slots_ref, aug_ref, below_in_ref, above_in_ref)
    total_ref[...] = jnp.zeros_like(total_ref)
    for j in range(tiles_ref.shape[0]):
        guess = predicted(j, slots_ref, tiles_ref, place_ref)
        pull(j, guess, z_ref, others_ref, v_ref, tiles_ref, place_ref, total_ref)
    give(total_ref, own_ref, below_ref, above_ref)


def full_gradient(grad_ref, back_upper_ref, back_lower_ref, ties_ref, work_ref):
    work_ref[...] = grad_ref[...]
    for side, back_ref in ((1, back_upper_ref), (0, back_lower_ref)):
        for t in range(back_ref.shape[0]):
            b = ties_ref[side, t]

            @pl.when(b >= 0)
            def _(b=b, t=t, back_ref=back_ref):
                work_ref[b] += back_ref[t]

    return jnp.concatenate([work_ref[b].astype(BF16) for b in range(work_ref.shape[0])], axis=1)


def first_update_kernel(
    grad_ref, back_upper_ref, back_lower_ref, ties_ref, gain_ref, x_ref, x_others_ref,
    state_ref, message_ref, work_ref,
):
    gradient = full_gradient(grad_ref, back_upper_ref, back_lower_ref, ties_ref, work_ref)
    held = state_ref.shape[0]
    me = lax.axis_index("snap")
    for i in range(held):
        rows = gain_ref[i * BLK : (i + 1) * BLK, :]
        update = lax.dot_general(gradient, rows, NT, preferred_element_type=F32)
        columns = pl.ds(pl.multiple_of((me * held + i) * BLK, BLK), BLK)
        parts = [x_ref[:, columns]] + [o[:, columns] for o in split(x_others_ref)]
        state = jnp.concatenate(parts, axis=0) + update
        state_ref[i] = state
        message_ref[i] = state.astype(BF16)


def last_update_kernel(
    grad_ref, back_upper_ref, back_lower_ref, ties_ref, gain_ref, state_ref, mine_ref, send_ref, work_ref
):
    gradient = full_gradient(grad_ref, back_upper_ref, back_lower_ref, ties_ref, work_ref)
    snaps = mine_ref.shape[0]
    for i in range(state_ref.shape[0]):
        rows = gain_ref[i * BLK : (i + 1) * BLK, :]
        update = lax.dot_general(gradient, rows, NT, preferred_element_type=F32)
        state = state_ref[i] + update
        columns = slice(i * BLK, (i + 1) * BLK)
        mine_ref[:, columns] = state[:snaps]
        for j in range(send_ref.shape[0]):
            send_ref[j, :, columns] = state[(j + 1) * snaps : (j + 2) * snaps]


def finish_kernel(mine_ref, others_ref, out_ref):
    width = mine_ref.shape[1]
    members = others_ref.shape[0] + 1
    me = lax.axis_index("snap")
    out_ref[:, pl.ds(pl.multiple_of(me * width, BLK), width)] = mine_ref[...]
    for i in range(1, members):
        at = lax.rem(me + members - i, members) * width
        out_ref[:, pl.ds(pl.multiple_of(at, BLK), width)] = others_ref[i - 1]


def along_area(block, distance):
    areas = range(lax.axis_size("area"))
    route = [(i - distance, i) for i in areas if i - distance in areas]
    return lax.ppermute(block, "area", route)


def from_snap(block, distance):
    members = lax.axis_size("snap")
    return lax.ppermute(block, "snap", [(i, (i + distance) % members) for i in range(members)])


def from_all(block):
    return jnp.stack([from_snap(block, i) for i in range(1, lax.axis_size("snap"))])


def shape(dims, kind):
    return jax.ShapeDtypeStruct(dims, kind)


def on_device(
    phasor_readings,
    reading_error_spread,
    starting_voltages,
    derivative_pieces,
    derivative_tile_position,
    frontier_voltage_pieces,
    holder_line_order,
    hub_line_order,
    reciprocal_normal_operator,
):
    snaps, lines = phasor_readings.shape
    states = starting_voltages.shape[1]
    own = states // BLK
    measure = derivative_pieces.shape[0]
    ties_table = frontier_voltage_pieces[0]
    ties = ties_table.shape[1]
    slots = own + 2 * ties
    members = lax.axis_size("snap")
    areas = lax.axis_size("area")
    everything = snaps * members
    held = reciprocal_normal_operator.shape[0] // BLK
    place = derivative_tile_position[0]
    cap = hub_line_order.shape[2]
    width = max(cap, BLK)
    chunks = areas * cap // width
    hub = hub_line_order[0].reshape(chunks, width)
    holder = holder_line_order[0].reshape(chunks, width)
    depth = (width // BLK) * snaps + 16

    message = call(
        pack_kernel,
        shape((chunks, depth, BLK), BF16),
        [VMEM, VMEM, VMEM],
        (phasor_readings, reading_error_spread.reshape(lines // BLK, BLK), hub),
        scratch=[pltpu.VMEM((chunks, width // BLK, BLK), jnp.int32)],
        name="pack_readings",
    )
    if cap < BLK:
        each = BLK // cap
        message = message.reshape(chunks, depth, each, cap).transpose(0, 2, 1, 3)
        message = message.reshape(areas, depth, cap)
    message = lax.all_to_all(message, "area", split_axis=0, concat_axis=0, tiled=True)
    if cap < BLK:
        message = message.reshape(chunks, each, depth, cap).transpose(0, 2, 1, 3)
        message = message.reshape(chunks, depth, BLK)

    group, lane = call(
        inverse_kernel,
        (shape((lines // BLK, BLK), jnp.int32),) * 2,
        [VMEM],
        (holder,),
        flops=10**9,
        name="invert_order",
    )
    x_others = from_all(starting_voltages)
    aug, to_lower, to_upper = call(
        first_states_kernel,
        (
            shape((own, everything, BLK), BF16),
            shape((ties, everything, BLK), BF16),
            shape((ties, everything, BLK), BF16),
        ),
        [VMEM, VMEM, SMEM],
        (starting_voltages, x_others, ties_table),
        name="first_states",
    )
    below = along_area(to_upper, 1)
    above = along_area(to_lower, -1)
    guess = call(
        predict_kernel,
        shape((everything, lines), F32),
        [VMEM, VMEM, VMEM, VMEM, SMEM],
        (aug, below, above, derivative_pieces, place),
        scratch=[pltpu.VMEM((slots, everything, BLK), BF16)],
        flops=10**9,
        name="predict",
    )
    readings, variance = call(
        unpack_kernel,
        (shape((snaps, lines), BF16), shape((1, lines), F32)),
        [VMEM, VMEM, VMEM],
        (message, group, lane),
        scratch=[
            pltpu.VMEM((chunks * (width // BLK), snaps, BLK), F32),
            pltpu.VMEM((chunks * (width // BLK), BLK), F32),
        ],
        name="unpack_readings",
    )
    reading_others = from_all(readings)
    grads = (
        shape((own, everything, BLK), F32),
        shape((ties, everything, BLK), F32),
        shape((ties, everything, BLK), F32),
    )
    total = pltpu.VMEM((slots, everything, BLK), F32)
    work = pltpu.VMEM((own, everything, BLK), F32)
    grad, grad_below, grad_above = call(
        pull_kernel,
        grads,
        [VMEM, VMEM, VMEM, VMEM, VMEM, SMEM],
        (guess, readings, reading_others, variance, derivative_pieces, place),
        scratch=[total],
        name="pull",
    )
    back_upper = along_area(grad_below, -1)
    back_lower = along_area(grad_above, 1)
    state, mine = call(
        first_update_kernel,
        (shape((held, everything, BLK), F32), shape((held, everything, BLK), BF16)),
        [VMEM, VMEM, VMEM, SMEM, VMEM, VMEM, VMEM],
        (
            grad, back_upper, back_lower, ties_table, reciprocal_normal_operator,
            starting_voltages, x_others,
        ),
        scratch=[work],
        name="first_update",
    )
    others = from_all(mine)
    aug, to_lower, to_upper = call(
        join_states_kernel,
        (
            shape((own, everything, BLK), BF16),
            shape((ties, everything, BLK), BF16),
            shape((ties, everything, BLK), BF16),
        ),
        [VMEM, VMEM, SMEM],
        (mine, others, ties_table),
        name="join_states",
    )
    below = along_area(to_upper, 1)
    above = along_area(to_lower, -1)
    grad, grad_below, grad_above = call(
        predict_pull_kernel,
        grads,
        [VMEM, VMEM, VMEM, VMEM, VMEM, VMEM, VMEM, SMEM],
        (aug, below, above, readings, reading_others, variance, derivative_pieces, place),
        scratch=[pltpu.VMEM((slots, everything, BLK), BF16), total],
        name="predict_pull",
    )
    back_upper = along_area(grad_below, -1)
    back_lower = along_area(grad_above, 1)
    kept, sent = call(
        last_update_kernel,
        (shape((snaps, held * BLK), F32), shape((members - 1, snaps, held * BLK), F32)),
        [VMEM, VMEM, VMEM, SMEM, VMEM, VMEM],
        (grad, back_upper, back_lower, ties_table, reciprocal_normal_operator, state),
        scratch=[work],
        name="last_update",
    )
    arrived = jnp.stack([from_snap(sent[i - 1], i) for i in range(1, members)])
    return call(
        finish_kernel,
        shape((snaps, states), F32),
        [VMEM, VMEM],
        (kept, arrived),
        name="finish",
    )


def solution(mesh):
    placed = (
        P("snap", "area"),
        P("area"),
        P("snap", "area"),
        P("area", None, None, None),
        P("area", None, None),
        P("area", None, None),
        P("area", None, None),
        P("area", None, None),
        P(("area", "snap"), None),
    )
    return jax.shard_map(
        on_device, mesh=mesh, in_specs=placed, out_specs=P("snap", "area"), check_vma=False
    )
```

time: 281 us -> 90.3 us (0.32)
  local copies, waits for them, and re-layouts: 111 us -> 5.63 us
  blocking collectives: 72.8 us -> 0 us
  other arithmetic: 32.8 us -> 0 us
  Pallas kernels: 0 us -> 20.9 us
  matrix products: 10.9 us -> 0 us
  waiting for transfers between devices: 20 us -> 26.7 us
  starting transfers between devices: 31 us -> 36.2 us
    gather x6 -> x0, local copies, waits for them, and re-layouts: 66.9 us -> none  [the longest x2 28.4 us: on_device(): jnp.take(predicted, own_gather, axis=1)]
    all_to_all x4 -> x0, blocking collectives: 46.6 us -> none  [the longest x1 17.9 us: on_device(): lax.all_to_all(outgoing, 'area', split_axis=1, concat_axis=1, tiled=True)]
    scatter x2 -> x0, local copies, waits for them, and re-layouts: 22.5 us -> none  [on_device(): weighted = jnp.zeros((snap_dev, READING_LINES), jnp.bfloat16).at[:, own_p...]
    pallas_call x0 -> x11, Pallas kernels: none -> 20.9 us  [call(): pl.pallas_call(kernel, out_shape=outs, in_specs=ins, out_specs=jax.tree.m...]
    ppermute x8 -> x12, waiting for transfers between devices: 11.7 us -> 26.7 us  [the longest x4 14.8 us: from_snap(): lax.ppermute(block, 'snap', [(i, (i + distance) % members) for i in range...]
    psum x2 -> x0, blocking collectives: 14.9 us -> none  [snapshot_total(): return lax.psum(partial_sum, 'snap')]
    all_to_all x12 -> x0, local copies, waits for them, and re-layouts: 14.9 us -> none  [the longest x4 10.1 us: on_device(): lax.all_to_all(outgoing, 'area', split_axis=1, concat_axis=1, tiled=True)]
    convert_element_type x2 -> x0, other arithmetic: 12.9 us -> none  [on_device(): scaled = jnp.where(conc_valid[None, :], residual_rows / (collector_varian...]
  transfers between devices with their start and end apart: 10 -> 13, of which waited for: 4 -> 9; matrix products, arithmetic and copies ran while one was open for 15% -> 1% of each run, Pallas kernels for 0% -> 7%
where the time goes in v1:
time: 90.3 us; the launch traced here: 89.6 us
  starting transfers between devices  36.2 us (40%)
  waiting for transfers between devices  26.7 us (30%)
  Pallas kernels  20.9 us (23%)
  local copies, waits for them, and re-layouts  5.63 us (6%)
    ppermute x8, starting transfers between devices, along_area(): return lax.ppermute(block, 'area', route)  23.8 us
    pallas_call x11, Pallas kernels, call(): pl.pallas_call(kernel, out_shape=outs, in_specs=ins, out_specs=jax.tree.m...  20.9 us
    ppermute x4, waiting for transfers between devices, from_snap(): lax.ppermute(block, 'snap', [(i, (i + distance) % members) for i in range...  14.8 us
    ppermute x8, waiting for transfers between devices, along_area(): return lax.ppermute(block, 'area', route)  11.9 us
    ppermute x4, starting transfers between devices, from_snap(): lax.ppermute(block, 'snap', [(i, (i + distance) % members) for i in range...  6.27 us
    all_to_all x1, starting transfers between devices, on_device(): lax.all_to_all(message, 'area', split_axis=0, concat_axis=0, tiled=True)  6.16 us
    unnamed x20, local copies, waits for them, and re-layouts  4.87 us
  transfers between devices with their start and end apart: 13, of which 9 were waited for; matrix products, arithmetic and copies ran while one was open for 1% of the time, Pallas kernels for 7%

profile of v1, /device:TPU:16, one launch (start us, length us, event | category | flops | bytes accessed | tf_op | source)
XLA Modules:
  0.0 89.6 jit_solution(1534137520993118555)
XLA Ops:
  0.0 1.1 %copy-done.4 = f32[32,2048]{1,0:T(8,128)S(1)} copy-done((f32[32,2048]{1,0:T(8,128)S(1)}, f32[32,2048]{1,0:T(8,128)}, u32[]{:S(2)}) %copy-start.4) | copy-done | bytes 262168
  1.1 0.7 copy-done.5
  1.8 0.7 copy-done.8
  2.5 3.2 %pack_readings.1 = bf16[16,80,128]{2,1,0:T(8,128)(2,1)} custom-call(f32[32,2048]{1,0:T(8,128)S(1)} %copy-done.4, f32[16,128]{1,0:T(8,128)S(1)} %bitcast.21, s32[16,256]{1,0:T(8,128)S(1)} %bitcast.16), custom_call_target="tpu_custom_call" | custom-call | tf_op jit(solution)/shard_map/pack_readings/pallas_call | solution.py:20
  5.7 6.2 %all-to-all-start = ((bf16[16,80,128]{2,1,0:T(8,128)(2,1)}), bf16[16,80,128]{2,1,0:T(8,128)(2,1)S(1)}, u32[]{:S(2)}, u32[]{:S(2)}) async-start(bf16[16,80,128]{2,1,0:T(8,128)(2,1)} %pack_readings.1), calls=%async_computation | async-start | bytes 655360 | tf_op jit(solution)/shard_map/all_to_all | solution.py:350
  11.9 1.5 %collective-permute-start = (f32[32,2048]{1,0:T(8,128)}, f32[32,2048]{1,0:T(8,128)S(1)}, u32[]{:S(2)}, u32[]{:S(2)}) collective-permute-start(f32[32,2048]{1,0:T(8,128)} %x_ref.1), channel_id=1, source_target_pairs={{0,1},{1,0},{2,3},{3,2},{4,5},{5,4},{6,7},{7,6},{8,9},{9,8},{10,11... | collective-permute-start | bytes 786440 | tf_op jit(solution)/shard_map/ppermute | solution.py:297
  13.4 7.1 %collective-permute-done = f32[32,2048]{1,0:T(8,128)S(1)} collective-permute-done((f32[32,2048]{1,0:T(8,128)}, f32[32,2048]{1,0:T(8,128)S(1)}, u32[]{:S(2)}, u32[]{:S(2)}) %collective-permute-start) | collective-permute-done | bytes 262176 | tf_op jit(solution)/shard_map/ppermute | solution.py:297
  20.4 0.9 %copy-done.2 = f32[32,2048]{1,0:T(8,128)S(1)} copy-done((f32[32,2048]{1,0:T(8,128)S(1)}, f32[32,2048]{1,0:T(8,128)}, u32[]{:S(2)}) %copy-start.2) | copy-done | bytes 262168
  21.4 0.7 copy-done.6
  22.1 1.2 %first_states.1 = (bf16[16,64,128]{2,1,0:T(8,128)(2,1)S(1)}, bf16[4,64,128]{2,1,0:T(8,128)(2,1)S(1)}, bf16[4,64,128]{2,1,0:T(8,128)(2,1)}) custom-call(f32[32,2048]{1,0:T(8,128)S(1)} %copy-done.2, f32[1,32,2048]{2,1,0:T(8,128)S(1)} %bitcast.10, s32[2,4]{1,0:T(2,128)S(1)} %bitcast.17), custom_call_target="tpu_custom_call" | custom-call | tf_op jit(solution)/shard_map/first_states/pallas_call | solution.py:20
  23.3 1.9 %collective-permute-start.1 = (bf16[4,64,128]{2,1,0:T(8,128)(2,1)}, bf16[4,64,128]{2,1,0:T(8,128)(2,1)S(1)}, u32[]{:S(2)}, u32[]{:S(2)}) collective-permute-start(bf16[4,64,128]{2,1,0:T(8,128)(2,1)} %get-tuple-element.26), channel_id=1, source_target_pairs={{0,2},{2,4},{4,6},{6,8},{8,10},{10,12},{12,14},{14,16},{16,18},{18... | collective-permute-start | bytes 196616 | tf_op jit(solution)/shard_map/ppermute | solution.py:292
  25.2 4.5 %collective-permute-start.2 = (bf16[4,64,128]{2,1,0:T(8,128)(2,1)S(1)}, bf16[4,64,128]{2,1,0:T(8,128)(2,1)}, u32[]{:S(2)}, u32[]{:S(2)}) collective-permute-start(bf16[4,64,128]{2,1,0:T(8,128)(2,1)S(1)} %get-tuple-element.27), channel_id=1, source_target_pairs={{2,0},{4,2},{6,4},{8,6},{10,8},{12,10},{14,12},{16,14},{18,16},{20... | collective-permute-start | bytes 196616 | tf_op jit(solution)/shard_map/ppermute | solution.py:292
  29.8 0.0 copy-start.9
  29.8 0.7 copy-done.9
  30.5 0.4 invert_order.1
  30.9 0.0 copy-start.7
  30.9 0.0 all-to-all-done.message_ref
  31.0 2.4 %unpack_readings.1 = (bf16[32,2048]{1,0:T(8,128)(2,1)S(1)}, f32[1,2048]{1,0:T(1,128)S(1)}) custom-call(bf16[16,80,128]{2,1,0:T(8,128)(2,1)S(1)} %all-to-all-done.message_ref, s32[16,128]{1,0:T(8,128)S(1)} %get-tuple-element.28.group_ref, s32[16,128]{1,0:T(8,128)S(1)} %get-tuple-element.29.lane_ref), custom_call_target="tpu_custom_call" | custom-call | tf_op jit(solution)/shard_map/unpack_readings/pallas_call | solution.py:20
  33.3 1.6 %collective-permute-start.3 = (bf16[32,2048]{1,0:T(8,128)(2,1)S(1)}, bf16[32,2048]{1,0:T(8,128)(2,1)S(1)}, u32[]{:S(2)}, u32[]{:S(2)}) collective-permute-start(bf16[32,2048]{1,0:T(8,128)(2,1)S(1)} %get-tuple-element.30.z_ref), channel_id=1, source_target_pairs={{0,1},{1,0},{2,3},{3,2},{4,5},{5,4},{6,7},{7,6},{8,9},{9,8},{10,11... | collective-permute-start | bytes 393224 | tf_op jit(solution)/shard_map/ppermute | solution.py:297
  34.9 0.8 copy.10.place_ref
  35.7 0.0 collective-permute-done.1.below_ref
  35.7 0.0 collective-permute-done.2.above_ref
  35.7 1.8 %predict.1.guess_ref = f32[64,2048]{1,0:T(8,128)S(1)} custom-call(bf16[16,64,128]{2,1,0:T(8,128)(2,1)S(1)} %get-tuple-element.25.aug_ref, bf16[4,64,128]{2,1,0:T(8,128)(2,1)S(1)} %collective-permute-done.1.below_ref, bf16[4,64,128]{2,1,0:T(8,128)(2,1)} %collective-permute-done.2.above_ref, bf16[16,4,128,128]{3,2,1,0:T(8,128)(2,1)S(1)} %copy-done.1, ...), custom_call_target="tpu_custom_call" | custom-call | flops 1000000000 | tf_op jit(solution)/shard_map/predict/pallas_call | solution.py:20
  37.5 0.8 collective-permute-done.3
  38.4 1.4 %pull.1 = (f32[16,64,128]{2,1,0:T(8,128)S(1)}, f32[4,64,128]{2,1,0:T(8,128)S(1)}, f32[4,64,128]{2,1,0:T(8,128)S(1)}) custom-call(f32[64,2048]{1,0:T(8,128)S(1)} %predict.1.guess_ref, bf16[32,2048]{1,0:T(8,128)(2,1)S(1)} %get-tuple-element.30.z_ref, bf16[1,32,2048]{2,1,0:T(8,128)(2,1)S(1)} %bitcast.12, f32[1,2048]{1,0:T(1,128)S(1)} %get-tuple-element.31.v_ref, ...), custom_call_target="tpu_custom_call" | custom-call | tf_op jit(solution)/shard_map/pull/pallas_call | solution.py:20
  39.8 1.9 %collective-permute-start.4 = (f32[4,64,128]{2,1,0:T(8,128)S(1)}, f32[4,64,128]{2,1,0:T(8,128)S(1)}, u32[]{:S(2)}, u32[]{:S(2)}) collective-permute-start(f32[4,64,128]{2,1,0:T(8,128)S(1)} %get-tuple-element.33), channel_id=1, source_target_pairs={{2,0},{4,2},{6,4},{8,6},{10,8},{12,10},{14,12},{16,14},{18,16},{20... | collective-permute-start | bytes 393224 | tf_op jit(solution)/shard_map/ppermute | solution.py:292
  41.7 2.4 %collective-permute-start.5 = (f32[4,64,128]{2,1,0:T(8,128)S(1)}, f32[4,64,128]{2,1,0:T(8,128)S(1)}, u32[]{:S(2)}, u32[]{:S(2)}) collective-permute-start(f32[4,64,128]{2,1,0:T(8,128)S(1)} %get-tuple-element.34), channel_id=1, source_target_pairs={{0,2},{2,4},{4,6},{6,8},{8,10},{10,12},{12,14},{14,16},{16,18},{18... | collective-permute-start | bytes 393224 | tf_op jit(solution)/shard_map/ppermute | solution.py:292
  44.1 0.1 collective-permute-done.4.back_upper_ref
  44.2 4.7 %collective-permute-done.5.back_lower_ref = f32[4,64,128]{2,1,0:T(8,128)S(1)} collective-permute-done((f32[4,64,128]{2,1,0:T(8,128)S(1)}, f32[4,64,128]{2,1,0:T(8,128)S(1)}, u32[]{:S(2)}, u32[]{:S(2)}) %collective-permute-start.5) | collective-permute-done | bytes 131104 | tf_op jit(solution)/shard_map/ppermute | solution.py:292
  48.9 0.0 copy-done.3
  48.9 0.0 copy-done
  48.9 2.2 %first_update.1 = (f32[8,64,128]{2,1,0:T(8,128)S(1)}, bf16[8,64,128]{2,1,0:T(8,128)(2,1)S(1)}) custom-call(f32[16,64,128]{2,1,0:T(8,128)S(1)} %get-tuple-element.32.grad_ref, f32[4,64,128]{2,1,0:T(8,128)S(1)} %collective-permute-done.4.back_upper_ref, f32[4,64,128]{2,1,0:T(8,128)S(1)} %collective-permute-done.5.back_lower_ref, s32[2,4]{1,0:T(2,128)S(1)} %bitcast.18, ...), custom_call_target="tpu_custom_call" | custom-call | tf_op jit(solution)/shard_map/first_update/pallas_call | solution.py:20
  51.2 1.6 %collective-permute-start.6 = (bf16[8,64,128]{2,1,0:T(8,128)(2,1)S(1)}, bf16[8,64,128]{2,1,0:T(8,128)(2,1)S(1)}, u32[]{:S(2)}, u32[]{:S(2)}) collective-permute-start(bf16[8,64,128]{2,1,0:T(8,128)(2,1)S(1)} %get-tuple-element.35.mine_ref), channel_id=1, source_target_pairs={{0,1},{1,0},{2,3},{3,2},{4,5},{5,4},{6,7},{7,6},{8,9},{9,8},{10,11... | collective-permute-start | bytes 393224 | tf_op jit(solution)/shard_map/ppermute | solution.py:297
  52.7 3.4 %collective-permute-done.6 = bf16[8,64,128]{2,1,0:T(8,128)(2,1)S(1)} collective-permute-done((bf16[8,64,128]{2,1,0:T(8,128)(2,1)S(1)}, bf16[8,64,128]{2,1,0:T(8,128)(2,1)S(1)}, u32[]{:S(2)}, u32[]{:S(2)}) %collective-permute-start.6) | collective-permute-done | bytes 131104 | tf_op jit(solution)/shard_map/ppermute | solution.py:297
  56.2 0.6 join_states.1
  56.8 1.9 %collective-permute-start.7 = (bf16[4,64,128]{2,1,0:T(8,128)(2,1)S(1)}, bf16[4,64,128]{2,1,0:T(8,128)(2,1)S(1)}, u32[]{:S(2)}, u32[]{:S(2)}) collective-permute-start(bf16[4,64,128]{2,1,0:T(8,128)(2,1)S(1)} %get-tuple-element.37), channel_id=1, source_target_pairs={{0,2},{2,4},{4,6},{6,8},{8,10},{10,12},{12,14},{14,16},{16,18},{18... | collective-permute-start | bytes 196616 | tf_op jit(solution)/shard_map/ppermute | solution.py:292
  58.7 4.5 %collective-permute-start.8 = (bf16[4,64,128]{2,1,0:T(8,128)(2,1)S(1)}, bf16[4,64,128]{2,1,0:T(8,128)(2,1)S(1)}, u32[]{:S(2)}, u32[]{:S(2)}) collective-permute-start(bf16[4,64,128]{2,1,0:T(8,128)(2,1)S(1)} %get-tuple-element.38), channel_id=1, source_target_pairs={{2,0},{4,2},{6,4},{8,6},{10,8},{12,10},{14,12},{16,14},{18,16},{20... | collective-permute-start | bytes 196616 | tf_op jit(solution)/shard_map/ppermute | solution.py:292
  63.3 0.0 collective-permute-done.7.below_in_ref
  63.3 1.9 %collective-permute-done.8.above_in_ref = bf16[4,64,128]{2,1,0:T(8,128)(2,1)S(1)} collective-permute-done((bf16[4,64,128]{2,1,0:T(8,128)(2,1)S(1)}, bf16[4,64,128]{2,1,0:T(8,128)(2,1)S(1)}, u32[]{:S(2)}, u32[]{:S(2)}) %collective-permute-start.8) | collective-permute-done | bytes 65568 | tf_op jit(solution)/shard_map/ppermute | solution.py:292
  65.2 4.7 %predict_pull.1 = (f32[16,64,128]{2,1,0:T(8,128)S(1)}, f32[4,64,128]{2,1,0:T(8,128)S(1)}, f32[4,64,128]{2,1,0:T(8,128)S(1)}) custom-call(bf16[16,64,128]{2,1,0:T(8,128)(2,1)S(1)} %get-tuple-element.36.aug_ref, bf16[4,64,128]{2,1,0:T(8,128)(2,1)S(1)} %collective-permute-done.7.below_in_ref, bf16[4,64,128]{2,1,0:T(8,128)(2,1)S(1)} %collective-permute-done.8.above_in_ref, ...), custom_call_target="tpu_custom_call" | custom-call | tf_op jit(solution)/shard_map/predict_pull/pallas_call | solution.py:20
  69.8 4.6 %collective-permute-start.9 = (f32[4,64,128]{2,1,0:T(8,128)S(1)}, f32[4,64,128]{2,1,0:T(8,128)S(1)}, u32[]{:S(2)}, u32[]{:S(2)}) collective-permute-start(f32[4,64,128]{2,1,0:T(8,128)S(1)} %get-tuple-element.40), channel_id=1, source_target_pairs={{2,0},{4,2},{6,4},{8,6},{10,8},{12,10},{14,12},{16,14},{18,16},{20... | collective-permute-start | bytes 393224 | tf_op jit(solution)/shard_map/ppermute | solution.py:292
  74.4 1.9 %collective-permute-start.10 = (f32[4,64,128]{2,1,0:T(8,128)S(1)}, f32[4,64,128]{2,1,0:T(8,128)S(1)}, u32[]{:S(2)}, u32[]{:S(2)}) collective-permute-start(f32[4,64,128]{2,1,0:T(8,128)S(1)} %get-tuple-element.41), channel_id=1, source_target_pairs={{0,2},{2,4},{4,6},{6,8},{8,10},{10,12},{12,14},{14,16},{16,18},{18... | collective-permute-start | bytes 393224 | tf_op jit(solution)/shard_map/ppermute | solution.py:292
  76.4 0.6 collective-permute-done.9.back_upper_ref
  76.9 4.7 %collective-permute-done.10.back_lower_ref = f32[4,64,128]{2,1,0:T(8,128)S(1)} collective-permute-done((f32[4,64,128]{2,1,0:T(8,128)S(1)}, f32[4,64,128]{2,1,0:T(8,128)S(1)}, u32[]{:S(2)}, u32[]{:S(2)}) %collective-permute-start.10) | collective-permute-done | bytes 131104 | tf_op jit(solution)/shard_map/ppermute | solution.py:292
  81.6 2.2 %last_update.1 = (f32[32,1024]{1,0:T(8,128)S(1)}, f32[1,32,1024]{2,1,0:T(8,128)S(1)}) custom-call(f32[16,64,128]{2,1,0:T(8,128)S(1)} %get-tuple-element.39.grad_ref, f32[4,64,128]{2,1,0:T(8,128)S(1)} %collective-permute-done.9.back_upper_ref, f32[4,64,128]{2,1,0:T(8,128)S(1)} %collective-permute-done.10.back_lower_ref, s32[2,4]{1,0:T(2,128)S(1)} %bitcast.20, ...), custom_call_target="tpu_custom_call" | custom-call | tf_op jit(solution)/shard_map/last_update/pallas_call | solution.py:20
  83.9 1.6 %collective-permute-start.11 = (f32[32,1024]{1,0:T(8,128)S(1)}, f32[32,1024]{1,0:T(8,128)S(1)}, u32[]{:S(2)}, u32[]{:S(2)}) collective-permute-start(f32[32,1024]{1,0:T(8,128)S(1)} %bitcast.22), channel_id=1, source_target_pairs={{0,1},{1,0},{2,3},{3,2},{4,5},{5,4},{6,7},{7,6},{8,9},{9,8},{10,11... | collective-permute-start | bytes 393224 | tf_op jit(solution)/shard_map/ppermute | solution.py:297
  85.4 3.4 %collective-permute-done.11 = f32[32,1024]{1,0:T(8,128)S(1)} collective-permute-done((f32[32,1024]{1,0:T(8,128)S(1)}, f32[32,1024]{1,0:T(8,128)S(1)}, u32[]{:S(2)}, u32[]{:S(2)}) %collective-permute-start.11) | collective-permute-done | bytes 131104 | tf_op jit(solution)/shard_map/ppermute | solution.py:297
  88.9 0.7 finish.1
  (10 shorter events, 0.0 us)
Async XLA Ops:
  0.0 35.7 %copy-start.1 = (bf16[16,4,128,128]{3,2,1,0:T(8,128)(2,1)S(1)}, bf16[16,4,128,128]{3,2,1,0:T(8,128)(2,1)}, u32[]{:S(2)}) copy-start(bf16[16,4,128,128]{3,2,1,0:T(8,128)(2,1)} %tiles_ref.5) | copy-start | bytes 6291460
  0.0 1.1 %copy-start.4 = (f32[32,2048]{1,0:T(8,128)S(1)}, f32[32,2048]{1,0:T(8,128)}, u32[]{:S(2)}) copy-start(f32[32,2048]{1,0:T(8,128)} %z_ref.1) | copy-start | bytes 786436
  1.1 0.7 copy-start.5
  1.8 0.7 copy-start.8
  5.7 25.2 %all-to-all-start = ((bf16[16,80,128]{2,1,0:T(8,128)(2,1)}), bf16[16,80,128]{2,1,0:T(8,128)(2,1)S(1)}, u32[]{:S(2)}, u32[]{:S(2)}) async-start(bf16[16,80,128]{2,1,0:T(8,128)(2,1)} %pack_readings.1), calls=%async_computation | async-start | bytes 655360 | tf_op jit(solution)/shard_map/all_to_all | solution.py:350
  11.9 8.6 %collective-permute-start = (f32[32,2048]{1,0:T(8,128)}, f32[32,2048]{1,0:T(8,128)S(1)}, u32[]{:S(2)}, u32[]{:S(2)}) collective-permute-start(f32[32,2048]{1,0:T(8,128)} %x_ref.1), channel_id=1, source_target_pairs={{0,1},{1,0},{2,3},{3,2},{4,5},{5,4},{6,7},{7,6},{8,9},{9,8},{10,11... | collective-permute-start | bytes 786440 | tf_op jit(solution)/shard_map/ppermute | solution.py:297
  20.4 1.0 %copy-start.2 = (f32[32,2048]{1,0:T(8,128)S(1)}, f32[32,2048]{1,0:T(8,128)}, u32[]{:S(2)}) copy-start(f32[32,2048]{1,0:T(8,128)} %x_ref.1) | copy-start | bytes 786436
  21.4 0.7 copy-start.6
  23.3 12.4 %collective-permute-start.1 = (bf16[4,64,128]{2,1,0:T(8,128)(2,1)}, bf16[4,64,128]{2,1,0:T(8,128)(2,1)S(1)}, u32[]{:S(2)}, u32[]{:S(2)}) collective-permute-start(bf16[4,64,128]{2,1,0:T(8,128)(2,1)} %get-tuple-element.26), channel_id=1, source_target_pairs={{0,2},{2,4},{4,6},{6,8},{8,10},{10,12},{12,14},{14,16},{16,18},{18... | collective-permute-start | bytes 196616 | tf_op jit(solution)/shard_map/ppermute | solution.py:292
  25.2 10.5 %collective-permute-start.2 = (bf16[4,64,128]{2,1,0:T(8,128)(2,1)S(1)}, bf16[4,64,128]{2,1,0:T(8,128)(2,1)}, u32[]{:S(2)}, u32[]{:S(2)}) collective-permute-start(bf16[4,64,128]{2,1,0:T(8,128)(2,1)S(1)} %get-tuple-element.27), channel_id=1, source_target_pairs={{2,0},{4,2},{6,4},{8,6},{10,8},{12,10},{14,12},{16,14},{18,16},{20... | collective-permute-start | bytes 196616 | tf_op jit(solution)/shard_map/ppermute | solution.py:292
  29.8 0.7 copy-start.9
  30.9 18.0 %copy-start.3 = (f32[32,2048]{1,0:T(8,128)S(1)}, f32[32,2048]{1,0:T(8,128)}, u32[]{:S(2)}) copy-start(f32[32,2048]{1,0:T(8,128)} %x_ref.1) | copy-start | bytes 786436
  30.9 18.0 %copy-start.7 = (s32[1,2,4]{2,1,0:T(2,128)S(1)}, s32[1,2,4]{2,1,0:T(2,128)}, u32[]{:S(2)}) copy-start(s32[1,2,4]{2,1,0:T(2,128)} %param.14) | copy-start | bytes 100
  33.3 5.0 %collective-permute-start.3 = (bf16[32,2048]{1,0:T(8,128)(2,1)S(1)}, bf16[32,2048]{1,0:T(8,128)(2,1)S(1)}, u32[]{:S(2)}, u32[]{:S(2)}) collective-permute-start(bf16[32,2048]{1,0:T(8,128)(2,1)S(1)} %get-tuple-element.30.z_ref), channel_id=1, source_target_pairs={{0,1},{1,0},{2,3},{3,2},{4,5},{5,4},{6,7},{7,6},{8,9},{9,8},{10,11... | collective-permute-start | bytes 393224 | tf_op jit(solution)/shard_map/ppermute | solution.py:297
  35.7 13.2 %copy-start = (bf16[1024,2048]{1,0:T(8,128)(2,1)S(1)}, bf16[1024,2048]{1,0:T(8,128)(2,1)}, u32[]{:S(2)}) copy-start(bf16[1024,2048]{1,0:T(8,128)(2,1)} %gain_ref.3) | copy-start | bytes 12582916
  39.8 4.4 %collective-permute-start.4 = (f32[4,64,128]{2,1,0:T(8,128)S(1)}, f32[4,64,128]{2,1,0:T(8,128)S(1)}, u32[]{:S(2)}, u32[]{:S(2)}) collective-permute-start(f32[4,64,128]{2,1,0:T(8,128)S(1)} %get-tuple-element.33), channel_id=1, source_target_pairs={{2,0},{4,2},{6,4},{8,6},{10,8},{12,10},{14,12},{16,14},{18,16},{20... | collective-permute-start | bytes 393224 | tf_op jit(solution)/shard_map/ppermute | solution.py:292
  41.7 7.2 %collective-permute-start.5 = (f32[4,64,128]{2,1,0:T(8,128)S(1)}, f32[4,64,128]{2,1,0:T(8,128)S(1)}, u32[]{:S(2)}, u32[]{:S(2)}) collective-permute-start(f32[4,64,128]{2,1,0:T(8,128)S(1)} %get-tuple-element.34), channel_id=1, source_target_pairs={{0,2},{2,4},{4,6},{6,8},{8,10},{10,12},{12,14},{14,16},{16,18},{18... | collective-permute-start | bytes 393224 | tf_op jit(solution)/shard_map/ppermute | solution.py:292
  51.2 5.0 %collective-permute-start.6 = (bf16[8,64,128]{2,1,0:T(8,128)(2,1)S(1)}, bf16[8,64,128]{2,1,0:T(8,128)(2,1)S(1)}, u32[]{:S(2)}, u32[]{:S(2)}) collective-permute-start(bf16[8,64,128]{2,1,0:T(8,128)(2,1)S(1)} %get-tuple-element.35.mine_ref), channel_id=1, source_target_pairs={{0,1},{1,0},{2,3},{3,2},{4,5},{5,4},{6,7},{7,6},{8,9},{9,8},{10,11... | collective-permute-start | bytes 393224 | tf_op jit(solution)/shard_map/ppermute | solution.py:297
  56.8 6.5 %collective-permute-start.7 = (bf16[4,64,128]{2,1,0:T(8,128)(2,1)S(1)}, bf16[4,64,128]{2,1,0:T(8,128)(2,1)S(1)}, u32[]{:S(2)}, u32[]{:S(2)}) collective-permute-start(bf16[4,64,128]{2,1,0:T(8,128)(2,1)S(1)} %get-tuple-element.37), channel_id=1, source_target_pairs={{0,2},{2,4},{4,6},{6,8},{8,10},{10,12},{12,14},{14,16},{16,18},{18... | collective-permute-start | bytes 196616 | tf_op jit(solution)/shard_map/ppermute | solution.py:292
  58.7 6.4 %collective-permute-start.8 = (bf16[4,64,128]{2,1,0:T(8,128)(2,1)S(1)}, bf16[4,64,128]{2,1,0:T(8,128)(2,1)S(1)}, u32[]{:S(2)}, u32[]{:S(2)}) collective-permute-start(bf16[4,64,128]{2,1,0:T(8,128)(2,1)S(1)} %get-tuple-element.38), channel_id=1, source_target_pairs={{2,0},{4,2},{6,4},{8,6},{10,8},{12,10},{14,12},{16,14},{18,16},{20... | collective-permute-start | bytes 196616 | tf_op jit(solution)/shard_map/ppermute | solution.py:292
  69.8 7.1 %collective-permute-start.9 = (f32[4,64,128]{2,1,0:T(8,128)S(1)}, f32[4,64,128]{2,1,0:T(8,128)S(1)}, u32[]{:S(2)}, u32[]{:S(2)}) collective-permute-start(f32[4,64,128]{2,1,0:T(8,128)S(1)} %get-tuple-element.40), channel_id=1, source_target_pairs={{2,0},{4,2},{6,4},{8,6},{10,8},{12,10},{14,12},{16,14},{18,16},{20... | collective-permute-start | bytes 393224 | tf_op jit(solution)/shard_map/ppermute | solution.py:292
  74.4 7.2 %collective-permute-start.10 = (f32[4,64,128]{2,1,0:T(8,128)S(1)}, f32[4,64,128]{2,1,0:T(8,128)S(1)}, u32[]{:S(2)}, u32[]{:S(2)}) collective-permute-start(f32[4,64,128]{2,1,0:T(8,128)S(1)} %get-tuple-element.41), channel_id=1, source_target_pairs={{0,2},{2,4},{4,6},{6,8},{8,10},{10,12},{12,14},{14,16},{16,18},{18... | collective-permute-start | bytes 393224 | tf_op jit(solution)/shard_map/ppermute | solution.py:292
  83.9 5.0 %collective-permute-start.11 = (f32[32,1024]{1,0:T(8,128)S(1)}, f32[32,1024]{1,0:T(8,128)S(1)}, u32[]{:S(2)}, u32[]{:S(2)}) collective-permute-start(f32[32,1024]{1,0:T(8,128)S(1)} %bitcast.22), channel_id=1, source_target_pairs={{0,1},{1,0},{2,3},{3,2},{4,5},{5,4},{6,7},{7,6},{8,9},{9,8},{10,11... | collective-permute-start | bytes 393224 | tf_op jit(solution)/shard_map/ppermute | solution.py:297

commit v2 on v1

v2 whole, which is shorter than its diff:
```python
import functools

import jax
import jax.numpy as jnp
from jax import lax
from jax.experimental import pallas as pl
from jax.experimental.pallas import tpu as pltpu
from jax.sharding import PartitionSpec as P

BLK = 128
ITERS = 2
F32 = jnp.float32
BF16 = jnp.bfloat16
NT = (((1,), (1,)), ((), ()))
VMEM = pl.BlockSpec(memory_space=pltpu.VMEM)
SMEM = pl.BlockSpec(memory_space=pltpu.SMEM)


def call(kernel, outs, ins, args, scratch=(), flops=0, bytes_accessed=0, name=None):
    return pl.pallas_call(
        kernel,
        out_shape=outs,
        in_specs=ins,
        out_specs=jax.tree.map(lambda _: VMEM, outs),
        scratch_shapes=list(scratch),
        compiler_params=pltpu.CompilerParams(vmem_limit_bytes=40 * 1024 * 1024),
        cost_estimate=pl.CostEstimate(
            flops=flops, bytes_accessed=bytes_accessed, transcendentals=0
        ),
        name=name,
    )(*args)


def lane_gather(values, lanes):
    return jnp.take_along_axis(values, lanes, axis=1, mode="promise_in_bounds")


def rows_iota(shape):
    return lax.broadcasted_iota(jnp.int32, shape, 0)


def pack_kernel(z_ref, v_ref, hub_ref, out_ref, slot_ref):
    snaps, lines = z_ref.shape
    blocks = lines // BLK
    chunks, width = hub_ref.shape
    groups = width // BLK
    for d in range(chunks):
        for g in range(groups):
            slot_ref[d, g : g + 1] = hub_ref[d : d + 1, g * BLK : (g + 1) * BLK]

    def chunk(d, carry):
        tail = jnp.zeros((8, BLK), F32)
        for g in range(groups):
            slot = slot_ref[d, g : g + 1]
            high = jnp.right_shift(slot, 7)
            low = jnp.bitwise_and(slot, 127)
            lanes = jnp.broadcast_to(low, (snaps, BLK))
            block_of = jnp.broadcast_to(high, (snaps, BLK))
            picked = jnp.zeros((snaps, BLK), F32)
            for b in range(blocks):
                found = lane_gather(z_ref[:, b * BLK : (b + 1) * BLK], lanes)
                picked = jnp.where(block_of == b, found, picked)
            out_ref[d, g * snaps : (g + 1) * snaps, :] = picked
            found = lane_gather(v_ref[...], jnp.broadcast_to(low, (blocks, BLK)))
            mine = rows_iota((blocks, BLK)) == high
            variance = jnp.sum(jnp.where(mine, found, 0.0), axis=0, keepdims=True)
            tail = jnp.where(rows_iota((8, BLK)) == g, variance, tail)
        out_ref[d, groups * snaps :, :] = tail
        return carry

    lax.fori_loop(0, chunks, chunk, 0)


def inverse_kernel(own_ref, group_ref, lane_ref):
    chunks, width = own_ref.shape
    blocks = group_ref.shape[0]
    groups = width // BLK
    total = jnp.zeros((2 * blocks, BLK), F32)
    lane = lax.broadcasted_iota(jnp.int32, (2 * blocks, width), 1)
    row = rows_iota((2 * blocks, width))
    in_group = jnp.bitwise_and(lane, 127)
    group_in = jnp.right_shift(lane, 7)
    for d in range(chunks):
        owned = own_ref[d : d + 1, :]
        high = jnp.right_shift(owned, 7)
        low = jnp.bitwise_and(owned, 127)
        label = jnp.where(row < blocks, group_in + d * groups, in_group)
        hit = jnp.bitwise_and(row, blocks - 1) == high
        left = jnp.where(hit, label.astype(F32), 0.0).astype(BF16)
        right = jnp.where(rows_iota((BLK, width)) == low, 1.0, 0.0).astype(BF16)
        total += lax.dot_general(left, right, NT, preferred_element_type=F32)
    group_ref[...] = total[:blocks].astype(jnp.int32)
    lane_ref[...] = total[blocks:].astype(jnp.int32)


def unpack_kernel(message_ref, group_ref, lane_ref, z_ref, v_ref, variance_ref):
    chunks = message_ref.shape[0]
    snaps, lines = z_ref.shape
    blocks = lines // BLK
    groups = (message_ref.shape[1] - 8) // snaps
    for d in range(chunks):
        tail = message_ref[d, groups * snaps :, :]
        variance_ref[d * groups : (d + 1) * groups, :] = tail[:groups]
    total = chunks * groups

    def block(b, carry):
        group = group_ref[pl.ds(b, 1), :]
        lane = lane_ref[pl.ds(b, 1), :]
        lanes = jnp.broadcast_to(lane, (snaps, BLK))
        group_of = jnp.broadcast_to(group, (snaps, BLK))
        picked = jnp.zeros((snaps, BLK), F32)
        for g in range(total):
            rows = slice(g % groups * snaps, (g % groups + 1) * snaps)
            found = lane_gather(message_ref[g // groups, rows, :], lanes)
            picked = jnp.where(group_of == g, found, picked)
        columns = pl.ds(pl.multiple_of(b * BLK, BLK), BLK)
        z_ref[:, columns] = picked
        found = lane_gather(variance_ref[...], jnp.broadcast_to(lane, (total, BLK)))
        mine = rows_iota((total, BLK)) == group
        v_ref[:, columns] = jnp.sum(jnp.where(mine, found, 0.0), axis=0, keepdims=True)
        return carry

    lax.fori_loop(0, blocks, block, 0)


def split(ref):
    return [ref.at[i] for i in range(ref.shape[0])]


def parity():
    return lax.rem(lax.axis_index("area"), 2)


def pick(source, listing_ref, side, out_ref):
    for t in range(out_ref.shape[0]):
        b = listing_ref[side, t]
        block = source(jnp.maximum(b, 0))
        out_ref[t] = jnp.where(b >= 0, block, jnp.zeros_like(block))


def first_states_kernel(own_ref, others_ref, ties_ref, aug_ref, first_ref, second_ref):
    snaps = own_ref.shape[0]
    for b in range(aug_ref.shape[0]):
        columns = slice(b * BLK, (b + 1) * BLK)
        aug_ref[b, :snaps] = own_ref[:, columns].astype(BF16)
        for i in range(others_ref.shape[0]):
            aug_ref[b, (i + 1) * snaps : (i + 2) * snaps] = others_ref[i, :, columns].astype(BF16)
    pick(lambda b: aug_ref[b], ties_ref, 1 - parity(), first_ref)
    pick(lambda b: aug_ref[b], ties_ref, parity(), second_ref)


def join_states_kernel(mine_ref, others_ref, ties_ref, aug_ref, first_ref, second_ref):
    held, everything = mine_ref.shape[:2]
    members = others_ref.shape[0] + 1
    snaps = everything // members
    me = lax.axis_index("snap")
    aug_ref[pl.ds(me * held, held)] = mine_ref[...]
    for i in range(1, members):
        at = lax.rem(me + members - i, members) * held
        for j in range(members):
            to = (j - i) % members
            aug_ref[pl.ds(at, held), to * snaps : (to + 1) * snaps] = others_ref[
                i - 1, :, j * snaps : (j + 1) * snaps
            ]
    pick(lambda b: aug_ref[b], ties_ref, 1 - parity(), first_ref)
    pick(lambda b: aug_ref[b], ties_ref, parity(), second_ref)


def slots_into(slots_ref, aug_ref, first_ref, second_ref):
    own = aug_ref.shape[0]
    ties = first_ref.shape[0]
    slots_ref[:own] = aug_ref[...]
    slots_ref[pl.ds(own + ties * (1 - parity()), ties)] = first_ref[...]
    slots_ref[pl.ds(own + ties * parity(), ties)] = second_ref[...]


def predicted(j, slots_ref, tiles_ref, place_ref):
    touched = tiles_ref.shape[1]
    chosen = jnp.concatenate([slots_ref[place_ref[j, k]] for k in range(touched)], axis=1)
    weights = jnp.concatenate([tiles_ref[j, k] for k in range(touched)], axis=1)
    return lax.dot_general(chosen, weights, NT, preferred_element_type=F32)


def predict_kernel(aug_ref, first_ref, second_ref, tiles_ref, place_ref, out_ref, slots_ref):
    slots_into(slots_ref, aug_ref, first_ref, second_ref)
    for j in range(tiles_ref.shape[0]):
        out_ref[:, j * BLK : (j + 1) * BLK] = predicted(j, slots_ref, tiles_ref, place_ref)


def weigh(j, guess, z_ref, others_ref, v_ref):
    columns = slice(j * BLK, (j + 1) * BLK)
    readings = [z_ref[:, columns]] + [o[:, columns] for o in split(others_ref)]
    resid = jnp.concatenate(readings, axis=0) - guess
    spread = jnp.sum(resid * resid, axis=0, keepdims=True) / resid.shape[0]
    return (resid / (v_ref[:, columns] + spread)).astype(BF16)


def pull(weighted_ref, tiles_ref, place_ref, total_ref, own_ref, first_ref, second_ref):
    total_ref[...] = jnp.zeros_like(total_ref)
    touched = tiles_ref.shape[1]
    for j in range(tiles_ref.shape[0]):
        weighted = weighted_ref[:, j * BLK : (j + 1) * BLK]
        weights = jnp.concatenate([tiles_ref[j, k] for k in range(touched)], axis=1)
        part = jnp.dot(weighted, weights, preferred_element_type=F32)
        for k in range(touched):
            n = place_ref[j, k]
            total_ref[n] += part[:, k * BLK : (k + 1) * BLK]
    own = own_ref.shape[0]
    ties = first_ref.shape[0]
    own_ref[...] = total_ref[:own]
    first_ref[...] = total_ref[pl.ds(own + ties * (1 - parity()), ties)]
    second_ref[...] = total_ref[pl.ds(own + ties * parity(), ties)]


def pull_kernel(
    guess_ref, z_ref, others_ref, v_ref, tiles_ref, place_ref, own_ref, first_ref, second_ref,
    total_ref, weighted_ref,
):
    for j in range(tiles_ref.shape[0]):
        columns = slice(j * BLK, (j + 1) * BLK)
        weighted_ref[:, columns] = weigh(j, guess_ref[:, columns], z_ref, others_ref, v_ref)
    pull(weighted_ref, tiles_ref, place_ref, total_ref, own_ref, first_ref, second_ref)


def predict_pull_kernel(
    aug_ref, first_in_ref, second_in_ref, z_ref, others_ref, v_ref, tiles_ref, place_ref,
    own_ref, first_ref, second_ref, slots_ref, guess_ref, total_ref, weighted_ref,
):
    predict_kernel(aug_ref, first_in_ref, second_in_ref, tiles_ref, place_ref, guess_ref, slots_ref)
    pull_kernel(
        guess_ref, z_ref, others_ref, v_ref, tiles_ref, place_ref, own_ref, first_ref, second_ref,
        total_ref, weighted_ref,
    )


def full_gradient(grad_ref, back_first_ref, back_second_ref, ties_ref, work_ref):
    work_ref[...] = grad_ref[...]
    for side, back_ref in ((1 - parity(), back_first_ref), (parity(), back_second_ref)):
        for t in range(back_ref.shape[0]):
            b = ties_ref[side, t]

            @pl.when(b >= 0)
            def _(b=b, t=t, back_ref=back_ref):
                work_ref[b] += back_ref[t]

    return jnp.concatenate([work_ref[b].astype(BF16) for b in range(work_ref.shape[0])], axis=1)


def updates(gradient, gain_ref):
    step = min(2 * BLK, gain_ref.shape[0])
    for at in range(0, gain_ref.shape[0], step):
        rows = gain_ref[at : at + step, :]
        update = lax.dot_general(gradient, rows, NT, preferred_element_type=F32)
        for i in range(step // BLK):
            yield at // BLK + i, update[:, i * BLK : (i + 1) * BLK]


def first_update_kernel(
    grad_ref, back_first_ref, back_second_ref, ties_ref, gain_ref, x_ref, x_others_ref,
    state_ref, message_ref, work_ref,
):
    gradient = full_gradient(grad_ref, back_first_ref, back_second_ref, ties_ref, work_ref)
    held = state_ref.shape[0]
    me = lax.axis_index("snap")
    for i, update in updates(gradient, gain_ref):
        columns = pl.ds(pl.multiple_of((me * held + i) * BLK, BLK), BLK)
        parts = [x_ref[:, columns]] + [o[:, columns] for o in split(x_others_ref)]
        state = jnp.concatenate(parts, axis=0) + update
        state_ref[i] = state
        message_ref[i] = state.astype(BF16)


def last_update_kernel(
    grad_ref, back_first_ref, back_second_ref, ties_ref, gain_ref, state_ref, mine_ref, send_ref, work_ref
):
    gradient = full_gradient(grad_ref, back_first_ref, back_second_ref, ties_ref, work_ref)
    snaps = mine_ref.shape[0]
    for i, update in updates(gradient, gain_ref):
        state = state_ref[i] + update
        columns = slice(i * BLK, (i + 1) * BLK)
        mine_ref[:, columns] = state[:snaps]
        for j in range(send_ref.shape[0]):
            send_ref[j, :, columns] = state[(j + 1) * snaps : (j + 2) * snaps]


def finish_kernel(mine_ref, others_ref, out_ref):
    width = mine_ref.shape[1]
    members = others_ref.shape[0] + 1
    me = lax.axis_index("snap")
    out_ref[:, pl.ds(pl.multiple_of(me * width, BLK), width)] = mine_ref[...]
    for i in range(1, members):
        at = lax.rem(me + members - i, members) * width
        out_ref[:, pl.ds(pl.multiple_of(at, BLK), width)] = others_ref[i - 1]


def swap_pair(block, start):
    pairs = [(i, i + 1) for i in range(start, lax.axis_size("area") - 1, 2)]
    return lax.ppermute(block, "area", pairs + [(b, a) for a, b in pairs])


def with_neighbours(first, second):
    second = swap_pair(second, 1)
    return swap_pair(first, 0), second


def from_snap(block, distance):
    members = lax.axis_size("snap")
    return lax.ppermute(block, "snap", [(i, (i + distance) % members) for i in range(members)])


def from_all(block):
    return jnp.stack([from_snap(block, i) for i in range(1, lax.axis_size("snap"))])


def shape(dims, kind):
    return jax.ShapeDtypeStruct(dims, kind)


def on_device(
    phasor_readings,
    reading_error_spread,
    starting_voltages,
    derivative_pieces,
    derivative_tile_position,
    frontier_voltage_pieces,
    holder_line_order,
    hub_line_order,
    reciprocal_normal_operator,
):
    snaps, lines = phasor_readings.shape
    states = starting_voltages.shape[1]
    own = states // BLK
    measure = derivative_pieces.shape[0]
    ties_table = frontier_voltage_pieces[0]
    ties = ties_table.shape[1]
    slots = own + 2 * ties
    members = lax.axis_size("snap")
    areas = lax.axis_size("area")
    everything = snaps * members
    held = reciprocal_normal_operator.shape[0] // BLK
    place = derivative_tile_position[0]
    cap = hub_line_order.shape[2]
    width = max(cap, BLK)
    chunks = areas * cap // width
    hub = hub_line_order[0].reshape(chunks, width)
    holder = holder_line_order[0].reshape(chunks, width)
    depth = (width // BLK) * snaps + 8

    x_others = from_all(starting_voltages)
    message = call(
        pack_kernel,
        shape((chunks, depth, BLK), F32),
        [VMEM, VMEM, VMEM],
        (phasor_readings, reading_error_spread.reshape(lines // BLK, BLK), hub),
        scratch=[pltpu.VMEM((chunks, width // BLK, BLK), jnp.int32)],
        name="pack_readings",
    )
    if cap < BLK:
        each = BLK // cap
        message = message.reshape(chunks, depth, each, cap).transpose(0, 2, 1, 3)
        message = message.reshape(areas, depth, cap)
    message, x_others = lax.optimization_barrier((message, x_others))
    message = lax.all_to_all(message, "area", split_axis=0, concat_axis=0, tiled=True)
    if cap < BLK:
        message = message.reshape(chunks, each, depth, cap).transpose(0, 2, 1, 3)
        message = message.reshape(chunks, depth, BLK)

    group, lane = call(
        inverse_kernel,
        (shape((lines // BLK, BLK), jnp.int32),) * 2,
        [VMEM],
        (holder,),
        flops=10**9,
        name="invert_order",
    )
    aug, first, second = call(
        first_states_kernel,
        (
            shape((own, everything, BLK), BF16),
            shape((ties, everything, BLK), BF16),
            shape((ties, everything, BLK), BF16),
        ),
        [VMEM, VMEM, SMEM],
        (starting_voltages, x_others, ties_table),
        name="first_states",
    )
    first, second = with_neighbours(first, second)
    guess = call(
        predict_kernel,
        shape((everything, lines), F32),
        [VMEM, VMEM, VMEM, VMEM, SMEM],
        (aug, first, second, derivative_pieces, place),
        scratch=[pltpu.VMEM((slots, everything, BLK), BF16)],
        flops=10**9,
        name="predict",
    )
    message, guess = lax.optimization_barrier((message, guess))
    readings, variance = call(
        unpack_kernel,
        (shape((snaps, lines), F32), shape((1, lines), F32)),
        [VMEM, VMEM, VMEM],
        (message, group, lane),
        scratch=[pltpu.VMEM((chunks * (width // BLK), BLK), F32)],
        name="unpack_readings",
    )
    reading_others = from_all(readings)
    grads = (
        shape((own, everything, BLK), F32),
        shape((ties, everything, BLK), F32),
        shape((ties, everything, BLK), F32),
    )
    total = pltpu.VMEM((slots, everything, BLK), F32)
    work = pltpu.VMEM((own, everything, BLK), F32)
    grad, first, second = call(
        pull_kernel,
        grads,
        [VMEM, VMEM, VMEM, VMEM, VMEM, SMEM],
        (guess, readings, reading_others, variance, derivative_pieces, place),
        scratch=[total, pltpu.VMEM((everything, lines), BF16)],
        name="pull",
    )
    first, second = with_neighbours(first, second)
    state, mine = call(
        first_update_kernel,
        (shape((held, everything, BLK), F32), shape((held, everything, BLK), BF16)),
        [VMEM, VMEM, VMEM, SMEM, VMEM, VMEM, VMEM],
        (
            grad, first, second, ties_table, reciprocal_normal_operator,
            starting_voltages, x_others,
        ),
        scratch=[work],
        name="first_update",
    )
    others = from_all(mine)
    aug, first, second = call(
        join_states_kernel,
        (
            shape((own, everything, BLK), BF16),
            shape((ties, everything, BLK), BF16),
            shape((ties, everything, BLK), BF16),
        ),
        [VMEM, VMEM, SMEM],
        (mine, others, ties_table),
        name="join_states",
    )
    first, second = with_neighbours(first, second)
    grad, first, second = call(
        predict_pull_kernel,
        grads,
        [VMEM, VMEM, VMEM, VMEM, VMEM, VMEM, VMEM, SMEM],
        (aug, first, second, readings, reading_others, variance, derivative_pieces, place),
        scratch=[
            pltpu.VMEM((slots, everything, BLK), BF16),
            pltpu.VMEM((everything, lines), F32),
            total,
            pltpu.VMEM((everything, lines), BF16),
        ],
        name="predict_pull",
    )
    first, second = with_neighbours(first, second)
    kept, sent = call(
        last_update_kernel,
        (shape((snaps, held * BLK), F32), shape((members - 1, snaps, held * BLK), F32)),
        [VMEM, VMEM, VMEM, SMEM, VMEM, VMEM],
        (grad, first, second, ties_table, reciprocal_normal_operator, state),
        scratch=[work],
        name="last_update",
    )
    arrived = jnp.stack([from_snap(sent[i - 1], i) for i in range(1, members)])
    return call(
        finish_kernel,
        shape((snaps, states), F32),
        [VMEM, VMEM],
        (kept, arrived),
        name="finish",
    )


def solution(mesh):
    placed = (
        P("snap", "area"),
        P("area"),
        P("snap", "area"),
        P("area", None, None, None),
        P("area", None, None),
        P("area", None, None),
        P("area", None, None),
        P("area", None, None),
        P(("area", "snap"), None),
    )
    return jax.shard_map(
        on_device, mesh=mesh, in_specs=placed, out_specs=P("snap", "area"), check_vma=False
    )
```

time: 90.3 us -> 89.6 us (level)
  starting transfers between devices: 36.2 us -> 22.4 us
  waiting for transfers between devices: 26.7 us -> 37.7 us
  local copies, waits for them, and re-layouts: 5.63 us -> 9.51 us
  Pallas kernels: 20.9 us -> 19.2 us
    ppermute x8, starting transfers between devices: 23.8 us -> 9.94 us  [swap_pair(): return lax.ppermute(block, 'area', pairs + [(b, a) for a, b in pairs])]
    ppermute x8, waiting for transfers between devices: 11.9 us -> 23.4 us  [swap_pair(): return lax.ppermute(block, 'area', pairs + [(b, a) for a, b in pairs])]
    unnamed x20 -> x26, local copies, waits for them, and re-layouts: 4.87 us -> 8.75 us
    pallas_call x11, Pallas kernels: 20.9 us -> 19.2 us  [call(): pl.pallas_call(kernel, out_shape=outs, in_specs=ins, out_specs=jax.tree.m...]
  transfers between devices with their start and end apart: 13 -> 13, of which waited for: 9 -> 8; matrix products, arithmetic and copies ran while one was open for 1% -> 1% of each run, Pallas kernels for 7% -> 8%
where the time goes in v2:
time: 89.6 us; the launch traced here: 88.9 us
  waiting for transfers between devices  37.7 us (42%)
  starting transfers between devices  22.4 us (25%)
  Pallas kernels  19.2 us (21%)
  local copies, waits for them, and re-layouts  9.51 us (11%)
    ppermute x8, waiting for transfers between devices, swap_pair(): return lax.ppermute(block, 'area', pairs + [(b, a) for a, b in pairs])  23.4 us
    pallas_call x11, Pallas kernels, call(): pl.pallas_call(kernel, out_shape=outs, in_specs=ins, out_specs=jax.tree.m...  19.2 us
    ppermute x4, waiting for transfers between devices, from_snap(): lax.ppermute(block, 'snap', [(i, (i + distance) % members) for i in range...  14.3 us
    ppermute x8, starting transfers between devices, swap_pair(): return lax.ppermute(block, 'area', pairs + [(b, a) for a, b in pairs])  9.94 us
    unnamed x26, local copies, waits for them, and re-layouts  8.75 us
    ppermute x4, starting transfers between devices, from_snap(): lax.ppermute(block, 'snap', [(i, (i + distance) % members) for i in range...  6.27 us
    all_to_all x1, starting transfers between devices, on_device(): lax.all_to_all(message, 'area', split_axis=0, concat_axis=0, tiled=True)  6.16 us
  transfers between devices with their start and end apart: 13, of which 8 were waited for; matrix products, arithmetic and copies ran while one was open for 1% of the time, Pallas kernels for 8%

profile of v2, /device:TPU:16, one launch (start us, length us, event | category | flops | bytes accessed | tf_op | source)
XLA Modules:
  0.0 88.9 jit_solution(13952339083486384120)
XLA Ops:
  0.0 1.5 %collective-permute-start = (f32[32,2048]{1,0:T(8,128)}, f32[32,2048]{1,0:T(8,128)S(1)}, u32[]{:S(2)}, u32[]{:S(2)}) collective-permute-start(f32[32,2048]{1,0:T(8,128)} %x_ref.1), channel_id=1, source_target_pairs={{0,1},{1,0},{2,3},{3,2},{4,5},{5,4},{6,7},{7,6},{8,9},{9,8},{10,11... | collective-permute-start | bytes 786440 | tf_op jit(solution)/shard_map/ppermute | solution.py:308
  1.5 0.9 %copy-done.7 = f32[32,2048]{1,0:T(8,128)S(1)} copy-done((f32[32,2048]{1,0:T(8,128)S(1)}, f32[32,2048]{1,0:T(8,128)}, u32[]{:S(2)}) %copy-start.7) | copy-done | bytes 262168
  2.5 0.7 copy-done.8
  3.2 0.7 copy-done.11
  3.9 4.3 %pack_readings.1 = f32[16,72,128]{2,1,0:T(8,128)} custom-call(f32[32,2048]{1,0:T(8,128)S(1)} %copy-done.7, f32[16,128]{1,0:T(8,128)S(1)} %bitcast.21, s32[16,256]{1,0:T(8,128)S(1)} %bitcast.16), custom_call_target="tpu_custom_call" | custom-call | tf_op jit(solution)/shard_map/pack_readings/pallas_call | solution.py:20
  8.2 0.1 collective-permute-done
  8.3 6.2 %all-to-all-start = ((f32[16,72,128]{2,1,0:T(8,128)}), f32[16,72,128]{2,1,0:T(8,128)S(1)}, u32[]{:S(2)}, u32[]{:S(2)}) async-start(f32[16,72,128]{2,1,0:T(8,128)} %pack_readings.1), calls=%async_computation | async-start | bytes 1179648 | tf_op jit(solution)/shard_map/all_to_all | solution.py:363
  14.4 0.8 copy.10.place_ref
  15.2 0.9 %copy-done.3 = f32[32,2048]{1,0:T(8,128)S(1)} copy-done((f32[32,2048]{1,0:T(8,128)S(1)}, f32[32,2048]{1,0:T(8,128)}, u32[]{:S(2)}) %copy-start.3) | copy-done | bytes 262168
  16.1 0.7 copy-done.9
  16.8 0.6 first_states.1
  17.4 0.2 collective-permute-start.1
  17.6 3.3 %collective-permute-start.2 = (bf16[4,64,128]{2,1,0:T(8,128)(2,1)S(1)}, bf16[4,64,128]{2,1,0:T(8,128)(2,1)S(1)}, u32[]{:S(2)}, u32[]{:S(2)}) collective-permute-start(bf16[4,64,128]{2,1,0:T(8,128)(2,1)S(1)} %get-tuple-element.33), channel_id=1, source_target_pairs={{2,4},{6,8},{10,12},{14,16},{18,20},{22,24},{26,28},{4,2},{8,6},{1... | collective-permute-start | bytes 196616 | tf_op jit(solution)/shard_map/ppermute | solution.py:298
  21.0 0.0 copy-start.12
  21.0 0.7 copy-done.12
  21.7 0.4 invert_order.1
  22.1 0.0 copy-start.10
  22.1 0.0 collective-permute-done.1.first_ref
  22.2 8.3 %collective-permute-done.2.second_ref = bf16[4,64,128]{2,1,0:T(8,128)(2,1)S(1)} collective-permute-done((bf16[4,64,128]{2,1,0:T(8,128)(2,1)S(1)}, bf16[4,64,128]{2,1,0:T(8,128)(2,1)S(1)}, u32[]{:S(2)}, u32[]{:S(2)}) %collective-permute-start.2) | collective-permute-done | bytes 65568 | tf_op jit(solution)/shard_map/ppermute | solution.py:298
  30.4 1.5 %predict.1.guess_ref = f32[64,2048]{1,0:T(8,128)S(1)} custom-call(bf16[16,64,128]{2,1,0:T(8,128)(2,1)S(1)} %get-tuple-element.31.aug_ref, bf16[4,64,128]{2,1,0:T(8,128)(2,1)S(1)} %collective-permute-done.1.first_ref, bf16[4,64,128]{2,1,0:T(8,128)(2,1)S(1)} %collective-permute-done.2.second_ref, bf16[16,4,128,128]{3,2,1,0:T(8,128)(2,1)S(1)} %copy-done.2, ...), custom_call_target="tpu_custom_call" | custom-call | flops 1000000000 | tf_op jit(solution)/shard_map/predict/pallas_call | solution.py:20
  31.9 0.8 copy-done.5
  32.7 0.0 all-to-all-done.message_ref
  32.7 3.4 %unpack_readings.1 = (f32[32,2048]{1,0:T(8,128)S(1)}, f32[1,2048]{1,0:T(1,128)S(1)}) custom-call(f32[16,72,128]{2,1,0:T(8,128)S(1)} %all-to-all-done.message_ref, s32[16,128]{1,0:T(8,128)S(1)} %get-tuple-element.36.group_ref, s32[16,128]{1,0:T(8,128)S(1)} %get-tuple-element.37.lane_ref), custom_call_target="tpu_custom_call" | custom-call | tf_op jit(solution)/shard_map/unpack_readings/pallas_call | solution.py:20
  36.1 1.6 %collective-permute-start.3 = (f32[32,2048]{1,0:T(8,128)S(1)}, f32[32,2048]{1,0:T(8,128)S(1)}, u32[]{:S(2)}, u32[]{:S(2)}) collective-permute-start(f32[32,2048]{1,0:T(8,128)S(1)} %get-tuple-element.38.z_ref), channel_id=1, source_target_pairs={{0,1},{1,0},{2,3},{3,2},{4,5},{5,4},{6,7},{7,6},{8,9},{9,8},{10,11... | collective-permute-start | bytes 786440 | tf_op jit(solution)/shard_map/ppermute | solution.py:308
  37.7 4.9 %collective-permute-done.3 = f32[32,2048]{1,0:T(8,128)S(1)} collective-permute-done((f32[32,2048]{1,0:T(8,128)S(1)}, f32[32,2048]{1,0:T(8,128)S(1)}, u32[]{:S(2)}, u32[]{:S(2)}) %collective-permute-start.3) | collective-permute-done | bytes 262176 | tf_op jit(solution)/shard_map/ppermute | solution.py:308
  42.5 1.0 %copy-done.6 = f32[64,2048]{1,0:T(8,128)S(1)} copy-done((f32[64,2048]{1,0:T(8,128)S(1)}, f32[64,2048]{1,0:T(8,128)}, u32[]{:S(2)}) %copy-start.6) | copy-done | bytes 524312
  43.6 1.6 %pull.1 = (f32[16,64,128]{2,1,0:T(8,128)S(1)}, f32[4,64,128]{2,1,0:T(8,128)S(1)}, f32[4,64,128]{2,1,0:T(8,128)S(1)}) custom-call(f32[64,2048]{1,0:T(8,128)S(1)} %copy-done.6, f32[32,2048]{1,0:T(8,128)S(1)} %get-tuple-element.38.z_ref, f32[1,32,2048]{2,1,0:T(8,128)S(1)} %bitcast.10, f32[1,2048]{1,0:T(1,128)S(1)} %get-tuple-element.39.v_ref, ...), custom_call_target="tpu_custom_call" | custom-call | tf_op jit(solution)/shard_map/pull/pallas_call | solution.py:20
  45.1 0.1 collective-permute-start.4
  45.2 2.2 %collective-permute-start.5 = (f32[4,64,128]{2,1,0:T(8,128)S(1)}, f32[4,64,128]{2,1,0:T(8,128)S(1)}, u32[]{:S(2)}, u32[]{:S(2)}) collective-permute-start(f32[4,64,128]{2,1,0:T(8,128)S(1)} %get-tuple-element.42), channel_id=1, source_target_pairs={{2,4},{6,8},{10,12},{14,16},{18,20},{22,24},{26,28},{4,2},{8,6},{1... | collective-permute-start | bytes 393224 | tf_op jit(solution)/shard_map/ppermute | solution.py:298
  47.4 5.1 %collective-permute-done.5.back_second_ref = f32[4,64,128]{2,1,0:T(8,128)S(1)} collective-permute-done((f32[4,64,128]{2,1,0:T(8,128)S(1)}, f32[4,64,128]{2,1,0:T(8,128)S(1)}, u32[]{:S(2)}, u32[]{:S(2)}) %collective-permute-start.5) | collective-permute-done | bytes 131104 | tf_op jit(solution)/shard_map/ppermute | solution.py:298
  52.5 2.2 %copy-done = bf16[1024,2048]{1,0:T(8,128)(2,1)S(1)} copy-done((bf16[1024,2048]{1,0:T(8,128)(2,1)S(1)}, bf16[1024,2048]{1,0:T(8,128)(2,1)}, u32[]{:S(2)}) %copy-start) | copy-done | bytes 4194328
  54.7 2.0 %first_update.1 = (f32[8,64,128]{2,1,0:T(8,128)S(1)}, bf16[8,64,128]{2,1,0:T(8,128)(2,1)S(1)}) custom-call(f32[16,64,128]{2,1,0:T(8,128)S(1)} %get-tuple-element.40.grad_ref, f32[4,64,128]{2,1,0:T(8,128)S(1)} %collective-permute-done.4.back_first_ref, f32[4,64,128]{2,1,0:T(8,128)S(1)} %collective-permute-done.5.back_second_ref, s32[2,4]{1,0:T(2,128)S(1)} %bitcast.18, ...), custom_call_target="tpu_custom_call" | custom-call | tf_op jit(solution)/shard_map/first_update/pallas_call | solution.py:20
  56.8 1.6 %collective-permute-start.6 = (bf16[8,64,128]{2,1,0:T(8,128)(2,1)S(1)}, bf16[8,64,128]{2,1,0:T(8,128)(2,1)S(1)}, u32[]{:S(2)}, u32[]{:S(2)}) collective-permute-start(bf16[8,64,128]{2,1,0:T(8,128)(2,1)S(1)} %get-tuple-element.43.mine_ref), channel_id=1, source_target_pairs={{0,1},{1,0},{2,3},{3,2},{4,5},{5,4},{6,7},{7,6},{8,9},{9,8},{10,11... | collective-permute-start | bytes 393224 | tf_op jit(solution)/shard_map/ppermute | solution.py:308
  58.3 4.8 %collective-permute-done.6 = bf16[8,64,128]{2,1,0:T(8,128)(2,1)S(1)} collective-permute-done((bf16[8,64,128]{2,1,0:T(8,128)(2,1)S(1)}, bf16[8,64,128]{2,1,0:T(8,128)(2,1)S(1)}, u32[]{:S(2)}, u32[]{:S(2)}) %collective-permute-start.6) | collective-permute-done | bytes 131104 | tf_op jit(solution)/shard_map/ppermute | solution.py:308
  63.1 0.6 join_states.1
  63.7 0.1 collective-permute-start.7
  63.8 1.9 %collective-permute-start.8 = (bf16[4,64,128]{2,1,0:T(8,128)(2,1)S(1)}, bf16[4,64,128]{2,1,0:T(8,128)(2,1)S(1)}, u32[]{:S(2)}, u32[]{:S(2)}) collective-permute-start(bf16[4,64,128]{2,1,0:T(8,128)(2,1)S(1)} %get-tuple-element.46), channel_id=1, source_target_pairs={{2,4},{6,8},{10,12},{14,16},{18,20},{22,24},{26,28},{4,2},{8,6},{1... | collective-permute-start | bytes 196616 | tf_op jit(solution)/shard_map/ppermute | solution.py:298
  65.7 0.0 collective-permute-done.7.first_in_ref
  65.7 4.7 %collective-permute-done.8.second_in_ref = bf16[4,64,128]{2,1,0:T(8,128)(2,1)S(1)} collective-permute-done((bf16[4,64,128]{2,1,0:T(8,128)(2,1)S(1)}, bf16[4,64,128]{2,1,0:T(8,128)(2,1)S(1)}, u32[]{:S(2)}, u32[]{:S(2)}) %collective-permute-start.8) | collective-permute-done | bytes 65568 | tf_op jit(solution)/shard_map/ppermute | solution.py:298
  70.4 2.1 %predict_pull.1 = (f32[16,64,128]{2,1,0:T(8,128)S(1)}, f32[4,64,128]{2,1,0:T(8,128)S(1)}, f32[4,64,128]{2,1,0:T(8,128)S(1)}) custom-call(bf16[16,64,128]{2,1,0:T(8,128)(2,1)S(1)} %get-tuple-element.44.aug_ref, bf16[4,64,128]{2,1,0:T(8,128)(2,1)S(1)} %collective-permute-done.7.first_in_ref, bf16[4,64,128]{2,1,0:T(8,128)(2,1)S(1)} %collective-permute-done.8.second_in_ref, ...), custom_call_target="tpu_custom_call" | custom-call | tf_op jit(solution)/shard_map/predict_pull/pallas_call | solution.py:20
  72.4 0.2 collective-permute-start.9
  72.7 1.9 %collective-permute-start.10 = (f32[4,64,128]{2,1,0:T(8,128)S(1)}, f32[4,64,128]{2,1,0:T(8,128)S(1)}, u32[]{:S(2)}, u32[]{:S(2)}) collective-permute-start(f32[4,64,128]{2,1,0:T(8,128)S(1)} %get-tuple-element.49), channel_id=1, source_target_pairs={{2,4},{6,8},{10,12},{14,16},{18,20},{22,24},{26,28},{4,2},{8,6},{1... | collective-permute-start | bytes 393224 | tf_op jit(solution)/shard_map/ppermute | solution.py:298
  74.6 0.0 collective-permute-done.9.back_first_ref
  74.6 5.4 %collective-permute-done.10.back_second_ref = f32[4,64,128]{2,1,0:T(8,128)S(1)} collective-permute-done((f32[4,64,128]{2,1,0:T(8,128)S(1)}, f32[4,64,128]{2,1,0:T(8,128)S(1)}, u32[]{:S(2)}, u32[]{:S(2)}) %collective-permute-start.10) | collective-permute-done | bytes 131104 | tf_op jit(solution)/shard_map/ppermute | solution.py:298
  80.0 2.0 %last_update.1 = (f32[32,1024]{1,0:T(8,128)S(1)}, f32[1,32,1024]{2,1,0:T(8,128)S(1)}) custom-call(f32[16,64,128]{2,1,0:T(8,128)S(1)} %get-tuple-element.47.grad_ref, f32[4,64,128]{2,1,0:T(8,128)S(1)} %collective-permute-done.9.back_first_ref, f32[4,64,128]{2,1,0:T(8,128)S(1)} %collective-permute-done.10.back_second_ref, s32[2,4]{1,0:T(2,128)S(1)} %bitcast.20, ...), custom_call_target="tpu_custom_call" | custom-call | tf_op jit(solution)/shard_map/last_update/pallas_call | solution.py:20
  82.0 1.6 %collective-permute-start.11 = (f32[32,1024]{1,0:T(8,128)S(1)}, f32[32,1024]{1,0:T(8,128)S(1)}, u32[]{:S(2)}, u32[]{:S(2)}) collective-permute-start(f32[32,1024]{1,0:T(8,128)S(1)} %bitcast.22), channel_id=1, source_target_pairs={{0,1},{1,0},{2,3},{3,2},{4,5},{5,4},{6,7},{7,6},{8,9},{9,8},{10,11... | collective-permute-start | bytes 393224 | tf_op jit(solution)/shard_map/ppermute | solution.py:308
  83.6 4.6 %collective-permute-done.11 = f32[32,1024]{1,0:T(8,128)S(1)} collective-permute-done((f32[32,1024]{1,0:T(8,128)S(1)}, f32[32,1024]{1,0:T(8,128)S(1)}, u32[]{:S(2)}, u32[]{:S(2)}) %collective-permute-start.11) | collective-permute-done | bytes 131104 | tf_op jit(solution)/shard_map/ppermute | solution.py:308
  88.2 0.7 finish.1
  (16 shorter events, 0.0 us)
Async XLA Ops:
  0.0 30.4 %copy-start.2 = (bf16[16,4,128,128]{3,2,1,0:T(8,128)(2,1)S(1)}, bf16[16,4,128,128]{3,2,1,0:T(8,128)(2,1)}, u32[]{:S(2)}) copy-start(bf16[16,4,128,128]{3,2,1,0:T(8,128)(2,1)} %tiles_ref.5) | copy-start | bytes 6291460
  0.0 8.3 %collective-permute-start = (f32[32,2048]{1,0:T(8,128)}, f32[32,2048]{1,0:T(8,128)S(1)}, u32[]{:S(2)}, u32[]{:S(2)}) collective-permute-start(f32[32,2048]{1,0:T(8,128)} %x_ref.1), channel_id=1, source_target_pairs={{0,1},{1,0},{2,3},{3,2},{4,5},{5,4},{6,7},{7,6},{8,9},{9,8},{10,11... | collective-permute-start | bytes 786440 | tf_op jit(solution)/shard_map/ppermute | solution.py:308
  1.5 0.9 %copy-start.7 = (f32[32,2048]{1,0:T(8,128)S(1)}, f32[32,2048]{1,0:T(8,128)}, u32[]{:S(2)}) copy-start(f32[32,2048]{1,0:T(8,128)} %z_ref.1) | copy-start | bytes 786436
  2.5 0.7 copy-start.8
  3.2 0.7 copy-start.11
  8.3 24.5 %all-to-all-start = ((f32[16,72,128]{2,1,0:T(8,128)}), f32[16,72,128]{2,1,0:T(8,128)S(1)}, u32[]{:S(2)}, u32[]{:S(2)}) async-start(f32[16,72,128]{2,1,0:T(8,128)} %pack_readings.1), calls=%async_computation | async-start | bytes 1179648 | tf_op jit(solution)/shard_map/all_to_all | solution.py:363
  15.2 0.9 %copy-start.3 = (f32[32,2048]{1,0:T(8,128)S(1)}, f32[32,2048]{1,0:T(8,128)}, u32[]{:S(2)}) copy-start(f32[32,2048]{1,0:T(8,128)} %x_ref.1) | copy-start | bytes 786436
  16.1 0.7 copy-start.9
  17.4 4.7 %collective-permute-start.1 = (bf16[4,64,128]{2,1,0:T(8,128)(2,1)S(1)}, bf16[4,64,128]{2,1,0:T(8,128)(2,1)S(1)}, u32[]{:S(2)}, u32[]{:S(2)}) collective-permute-start(bf16[4,64,128]{2,1,0:T(8,128)(2,1)S(1)} %get-tuple-element.32), channel_id=1, source_target_pairs={{0,2},{4,6},{8,10},{12,14},{16,18},{20,22},{24,26},{28,30},{2,0},{... | collective-permute-start | bytes 196616 | tf_op jit(solution)/shard_map/ppermute | solution.py:298
  17.6 12.8 %collective-permute-start.2 = (bf16[4,64,128]{2,1,0:T(8,128)(2,1)S(1)}, bf16[4,64,128]{2,1,0:T(8,128)(2,1)S(1)}, u32[]{:S(2)}, u32[]{:S(2)}) collective-permute-start(bf16[4,64,128]{2,1,0:T(8,128)(2,1)S(1)} %get-tuple-element.33), channel_id=1, source_target_pairs={{2,4},{6,8},{10,12},{14,16},{18,20},{22,24},{26,28},{4,2},{8,6},{1... | collective-permute-start | bytes 196616 | tf_op jit(solution)/shard_map/ppermute | solution.py:298
  21.0 0.7 copy-start.12
  22.1 30.4 %copy-start.4 = (f32[32,2048]{1,0:T(8,128)S(1)}, f32[32,2048]{1,0:T(8,128)}, u32[]{:S(2)}) copy-start(f32[32,2048]{1,0:T(8,128)} %x_ref.1) | copy-start | bytes 786436
  22.1 30.4 %copy-start.10 = (s32[1,2,4]{2,1,0:T(2,128)S(1)}, s32[1,2,4]{2,1,0:T(2,128)}, u32[]{:S(2)}) copy-start(s32[1,2,4]{2,1,0:T(2,128)} %param.14) | copy-start | bytes 100
  31.9 0.8 copy-start.5
  36.1 6.4 %collective-permute-start.3 = (f32[32,2048]{1,0:T(8,128)S(1)}, f32[32,2048]{1,0:T(8,128)S(1)}, u32[]{:S(2)}, u32[]{:S(2)}) collective-permute-start(f32[32,2048]{1,0:T(8,128)S(1)} %get-tuple-element.38.z_ref), channel_id=1, source_target_pairs={{0,1},{1,0},{2,3},{3,2},{4,5},{5,4},{6,7},{7,6},{8,9},{9,8},{10,11... | collective-permute-start | bytes 786440 | tf_op jit(solution)/shard_map/ppermute | solution.py:308
  42.5 1.0 %copy-start.6 = (f32[64,2048]{1,0:T(8,128)S(1)}, f32[64,2048]{1,0:T(8,128)}, u32[]{:S(2)}) copy-start(f32[64,2048]{1,0:T(8,128)} %copy-done.5) | copy-start | bytes 1572868
  45.1 2.3 %collective-permute-start.4 = (f32[4,64,128]{2,1,0:T(8,128)S(1)}, f32[4,64,128]{2,1,0:T(8,128)S(1)}, u32[]{:S(2)}, u32[]{:S(2)}) collective-permute-start(f32[4,64,128]{2,1,0:T(8,128)S(1)} %get-tuple-element.41), channel_id=1, source_target_pairs={{0,2},{4,6},{8,10},{12,14},{16,18},{20,22},{24,26},{28,30},{2,0},{... | collective-permute-start | bytes 393224 | tf_op jit(solution)/shard_map/ppermute | solution.py:298
  45.2 7.3 %collective-permute-start.5 = (f32[4,64,128]{2,1,0:T(8,128)S(1)}, f32[4,64,128]{2,1,0:T(8,128)S(1)}, u32[]{:S(2)}, u32[]{:S(2)}) collective-permute-start(f32[4,64,128]{2,1,0:T(8,128)S(1)} %get-tuple-element.42), channel_id=1, source_target_pairs={{2,4},{6,8},{10,12},{14,16},{18,20},{22,24},{26,28},{4,2},{8,6},{1... | collective-permute-start | bytes 393224 | tf_op jit(solution)/shard_map/ppermute | solution.py:298
  52.5 2.2 %copy-start = (bf16[1024,2048]{1,0:T(8,128)(2,1)S(1)}, bf16[1024,2048]{1,0:T(8,128)(2,1)}, u32[]{:S(2)}) copy-start(bf16[1024,2048]{1,0:T(8,128)(2,1)} %gain_ref.3) | copy-start | bytes 12582916
  54.7 25.3 %copy-start.1 = (bf16[1024,2048]{1,0:T(8,128)(2,1)S(1)}, bf16[1024,2048]{1,0:T(8,128)(2,1)}, u32[]{:S(2)}) copy-start(bf16[1024,2048]{1,0:T(8,128)(2,1)} %gain_ref.3) | copy-start | bytes 12582916
  56.8 6.3 %collective-permute-start.6 = (bf16[8,64,128]{2,1,0:T(8,128)(2,1)S(1)}, bf16[8,64,128]{2,1,0:T(8,128)(2,1)S(1)}, u32[]{:S(2)}, u32[]{:S(2)}) collective-permute-start(bf16[8,64,128]{2,1,0:T(8,128)(2,1)S(1)} %get-tuple-element.43.mine_ref), channel_id=1, source_target_pairs={{0,1},{1,0},{2,3},{3,2},{4,5},{5,4},{6,7},{7,6},{8,9},{9,8},{10,11... | collective-permute-start | bytes 393224 | tf_op jit(solution)/shard_map/ppermute | solution.py:308
  63.7 2.0 %collective-permute-start.7 = (bf16[4,64,128]{2,1,0:T(8,128)(2,1)S(1)}, bf16[4,64,128]{2,1,0:T(8,128)(2,1)S(1)}, u32[]{:S(2)}, u32[]{:S(2)}) collective-permute-start(bf16[4,64,128]{2,1,0:T(8,128)(2,1)S(1)} %get-tuple-element.45), channel_id=1, source_target_pairs={{0,2},{4,6},{8,10},{12,14},{16,18},{20,22},{24,26},{28,30},{2,0},{... | collective-permute-start | bytes 196616 | tf_op jit(solution)/shard_map/ppermute | solution.py:298
  63.8 6.6 %collective-permute-start.8 = (bf16[4,64,128]{2,1,0:T(8,128)(2,1)S(1)}, bf16[4,64,128]{2,1,0:T(8,128)(2,1)S(1)}, u32[]{:S(2)}, u32[]{:S(2)}) collective-permute-start(bf16[4,64,128]{2,1,0:T(8,128)(2,1)S(1)} %get-tuple-element.46), channel_id=1, source_target_pairs={{2,4},{6,8},{10,12},{14,16},{18,20},{22,24},{26,28},{4,2},{8,6},{1... | collective-permute-start | bytes 196616 | tf_op jit(solution)/shard_map/ppermute | solution.py:298
  72.4 2.2 %collective-permute-start.9 = (f32[4,64,128]{2,1,0:T(8,128)S(1)}, f32[4,64,128]{2,1,0:T(8,128)S(1)}, u32[]{:S(2)}, u32[]{:S(2)}) collective-permute-start(f32[4,64,128]{2,1,0:T(8,128)S(1)} %get-tuple-element.48), channel_id=1, source_target_pairs={{0,2},{4,6},{8,10},{12,14},{16,18},{20,22},{24,26},{28,30},{2,0},{... | collective-permute-start | bytes 393224 | tf_op jit(solution)/shard_map/ppermute | solution.py:298
  72.7 7.3 %collective-permute-start.10 = (f32[4,64,128]{2,1,0:T(8,128)S(1)}, f32[4,64,128]{2,1,0:T(8,128)S(1)}, u32[]{:S(2)}, u32[]{:S(2)}) collective-permute-start(f32[4,64,128]{2,1,0:T(8,128)S(1)} %get-tuple-element.49), channel_id=1, source_target_pairs={{2,4},{6,8},{10,12},{14,16},{18,20},{22,24},{26,28},{4,2},{8,6},{1... | collective-permute-start | bytes 393224 | tf_op jit(solution)/shard_map/ppermute | solution.py:298
  82.0 6.2 %collective-permute-start.11 = (f32[32,1024]{1,0:T(8,128)S(1)}, f32[32,1024]{1,0:T(8,128)S(1)}, u32[]{:S(2)}, u32[]{:S(2)}) collective-permute-start(f32[32,1024]{1,0:T(8,128)S(1)} %bitcast.22), channel_id=1, source_target_pairs={{0,1},{1,0},{2,3},{3,2},{4,5},{5,4},{6,7},{7,6},{8,9},{9,8},{10,11... | collective-permute-start | bytes 393224 | tf_op jit(solution)/shard_map/ppermute | solution.py:308

commit v3 on v2

--- a/solution.py
+++ b/solution.py
@@ -13,6 +13,7 @@
 BF16 = jnp.bfloat16
 NT = (((1,), (1,)), ((), ()))
 VMEM = pl.BlockSpec(memory_space=pltpu.VMEM)
+ANY = pl.BlockSpec(memory_space=pl.ANY)
 SMEM = pl.BlockSpec(memory_space=pltpu.SMEM)
 
 
@@ -23,7 +24,7 @@
         in_specs=ins,
         out_specs=jax.tree.map(lambda _: VMEM, outs),
         scratch_shapes=list(scratch),
-        compiler_params=pltpu.CompilerParams(vmem_limit_bytes=40 * 1024 * 1024),
+        compiler_params=pltpu.CompilerParams(vmem_limit_bytes=12 * 1024 * 1024),
         cost_estimate=pl.CostEstimate(
             flops=flops, bytes_accessed=bytes_accessed, transcendentals=0
         ),
@@ -39,7 +40,24 @@
     return lax.broadcasted_iota(jnp.int32, shape, 0)
 
 
-def pack_kernel(z_ref, v_ref, hub_ref, out_ref, slot_ref):
+def pieces(refs):
+    return [refs[0].at[i] for i in range(refs[0].shape[0])] if refs[0].ndim == 3 else list(refs)
+
+
+def swapper(by_swaps):
+    return lax.axis_index("area") if by_swaps else 0
+
+
+def pack_kernel(by_swaps, z_in, v_in, hub_in, *refs):
+    out_refs, (z_ref, v_ref, hub_ref, slot_ref, sems) = refs[:-5], refs[-5:]
+    copies = [
+        pltpu.make_async_copy(source, target, sems.at[i])
+        for i, (source, target) in enumerate(((hub_in, hub_ref), (z_in, z_ref), (v_in, v_ref)))
+    ]
+    for copy in copies:
+        copy.start()
+    for copy in copies:
+        copy.wait()
     snaps, lines = z_ref.shape
     blocks = lines // BLK
     chunks, width = hub_ref.shape
@@ -47,11 +65,11 @@
     for d in range(chunks):
         for g in range(groups):
             slot_ref[d, g : g + 1] = hub_ref[d : d + 1, g * BLK : (g + 1) * BLK]
-
-    def chunk(d, carry):
+    me = swapper(by_swaps)
+    for m, out_ref in reversed(list(enumerate(pieces(out_refs)))):
         tail = jnp.zeros((8, BLK), F32)
         for g in range(groups):
-            slot = slot_ref[d, g : g + 1]
+            slot = slot_ref[jnp.bitwise_xor(me, m), g : g + 1]
             high = jnp.right_shift(slot, 7)
             low = jnp.bitwise_and(slot, 127)
             lanes = jnp.broadcast_to(low, (snaps, BLK))
@@ -60,15 +78,12 @@
             for b in range(blocks):
                 found = lane_gather(z_ref[:, b * BLK : (b + 1) * BLK], lanes)
                 picked = jnp.where(block_of == b, found, picked)
-            out_ref[d, g * snaps : (g + 1) * snaps, :] = picked
+            out_ref[g * snaps : (g + 1) * snaps, :] = picked
             found = lane_gather(v_ref[...], jnp.broadcast_to(low, (blocks, BLK)))
             mine = rows_iota((blocks, BLK)) == high
             variance = jnp.sum(jnp.where(mine, found, 0.0), axis=0, keepdims=True)
             tail = jnp.where(rows_iota((8, BLK)) == g, variance, tail)
-        out_ref[d, groups * snaps :, :] = tail
-        return carry
-
-    lax.fori_loop(0, chunks, chunk, 0)
+        out_ref[groups * snaps :, :] = tail
 
 
 def inverse_kernel(own_ref, group_ref, lane_ref):
@@ -93,34 +108,29 @@
     lane_ref[...] = total[blocks:].astype(jnp.int32)
 
 
-def unpack_kernel(message_ref, group_ref, lane_ref, z_ref, v_ref, variance_ref):
-    chunks = message_ref.shape[0]
+def unpack_kernel(by_swaps, start, group_ref, lane_ref, *refs):
+    message_refs, (z_ref, v_ref, variance_ref) = pieces(refs[:-3][::-1]), refs[-3:]
     snaps, lines = z_ref.shape
-    blocks = lines // BLK
-    groups = (message_ref.shape[1] - 8) // snaps
-    for d in range(chunks):
-        tail = message_ref[d, groups * snaps :, :]
-        variance_ref[d * groups : (d + 1) * groups, :] = tail[:groups]
-    total = chunks * groups
-
-    def block(b, carry):
-        group = group_ref[pl.ds(b, 1), :]
-        lane = lane_ref[pl.ds(b, 1), :]
+    groups = (message_refs[0].shape[0] - 8) // snaps
+    total = len(message_refs) * groups
+    for m, message_ref in enumerate(message_refs):
+        variance_ref[m * groups : (m + 1) * groups, :] = message_ref[groups * snaps :, :][:groups]
+    me = swapper(by_swaps) * groups
+    for b in range(lines // BLK):
+        group = jnp.bitwise_xor(group_ref[start + b : start + b + 1, :], me)
+        lane = lane_ref[start + b : start + b + 1, :]
         lanes = jnp.broadcast_to(lane, (snaps, BLK))
         group_of = jnp.broadcast_to(group, (snaps, BLK))
         picked = jnp.zeros((snaps, BLK), F32)
         for g in range(total):
             rows = slice(g % groups * snaps, (g % groups + 1) * snaps)
-            found = lane_gather(message_ref[g // groups, rows, :], lanes)
+            found = lane_gather(message_refs[g // groups][rows, :], lanes)
             picked = jnp.where(group_of == g, found, picked)
-        columns = pl.ds(pl.multiple_of(b * BLK, BLK), BLK)
+        columns = slice(b * BLK, (b + 1) * BLK)
         z_ref[:, columns] = picked
         found = lane_gather(variance_ref[...], jnp.broadcast_to(lane, (total, BLK)))
         mine = rows_iota((total, BLK)) == group
         v_ref[:, columns] = jnp.sum(jnp.where(mine, found, 0.0), axis=0, keepdims=True)
-        return carry
-
-    lax.fori_loop(0, blocks, block, 0)
 
 
 def split(ref):
@@ -128,7 +138,7 @@
 
 
 def parity():
-    return lax.rem(lax.axis_index("area"), 2)
+    return 1 - lax.rem(lax.axis_index("area"), 2)
 
 
 def pick(source, listing_ref, side, out_ref):
@@ -176,7 +186,7 @@
 
 def predicted(j, slots_ref, tiles_ref, place_ref):
     touched = tiles_ref.shape[1]
-    chosen = jnp.concatenate([slots_ref[place_ref[j, k]] for k in range(touched)], axis=1)
+    chosen = jnp.concatenate([slots_ref[place_ref[k, j]] for k in range(touched)], axis=1)
     weights = jnp.concatenate([tiles_ref[j, k] for k in range(touched)], axis=1)
     return lax.dot_general(chosen, weights, NT, preferred_element_type=F32)
 
@@ -187,8 +197,10 @@
         out_ref[:, j * BLK : (j + 1) * BLK] = predicted(j, slots_ref, tiles_ref, place_ref)
 
 
-def weigh(j, guess, z_ref, others_ref, v_ref):
-    columns = slice(j * BLK, (j + 1) * BLK)
+def weigh(j, guess, z_refs, others_refs, v_refs):
+    each = z_refs[0].shape[1] // BLK
+    z_ref, others_ref, v_ref = z_refs[j // each], others_refs[j // each], v_refs[j // each]
+    columns = slice(j % each * BLK, (j % each + 1) * BLK)
     readings = [z_ref[:, columns]] + [o[:, columns] for o in split(others_ref)]
     resid = jnp.concatenate(readings, axis=0) - guess
     spread = jnp.sum(resid * resid, axis=0, keepdims=True) / resid.shape[0]
@@ -203,7 +215,7 @@
         weights = jnp.concatenate([tiles_ref[j, k] for k in range(touched)], axis=1)
         part = jnp.dot(weighted, weights, preferred_element_type=F32)
         for k in range(touched):
-            n = place_ref[j, k]
+            n = place_ref[k, j]
             total_ref[n] += part[:, k * BLK : (k + 1) * BLK]
     own = own_ref.shape[0]
     ties = first_ref.shape[0]
@@ -213,22 +225,22 @@
 
 
 def pull_kernel(
-    guess_ref, z_ref, others_ref, v_ref, tiles_ref, place_ref, own_ref, first_ref, second_ref,
+    guess_ref, z_refs, others_refs, v_refs, tiles_ref, place_ref, own_ref, first_ref, second_ref,
     total_ref, weighted_ref,
 ):
     for j in range(tiles_ref.shape[0]):
         columns = slice(j * BLK, (j + 1) * BLK)
-        weighted_ref[:, columns] = weigh(j, guess_ref[:, columns], z_ref, others_ref, v_ref)
+        weighted_ref[:, columns] = weigh(j, guess_ref[:, columns], z_refs, others_refs, v_refs)
     pull(weighted_ref, tiles_ref, place_ref, total_ref, own_ref, first_ref, second_ref)
 
 
 def predict_pull_kernel(
-    aug_ref, first_in_ref, second_in_ref, z_ref, others_ref, v_ref, tiles_ref, place_ref,
+    aug_ref, first_in_ref, second_in_ref, z_refs, others_refs, v_refs, tiles_ref, place_ref,
     own_ref, first_ref, second_ref, slots_ref, guess_ref, total_ref, weighted_ref,
 ):
     predict_kernel(aug_ref, first_in_ref, second_in_ref, tiles_ref, place_ref, guess_ref, slots_ref)
     pull_kernel(
-        guess_ref, z_ref, others_ref, v_ref, tiles_ref, place_ref, own_ref, first_ref, second_ref,
+        guess_ref, z_refs, others_refs, v_refs, tiles_ref, place_ref, own_ref, first_ref, second_ref,
         total_ref, weighted_ref,
     )
 
@@ -299,8 +311,7 @@
 
 
 def with_neighbours(first, second):
-    second = swap_pair(second, 1)
-    return swap_pair(first, 0), second
+    return swap_pair(first, 1), swap_pair(second, 0)
 
 
 def from_snap(block, distance):
@@ -338,7 +349,7 @@
     areas = lax.axis_size("area")
     everything = snaps * members
     held = reciprocal_normal_operator.shape[0] // BLK
-    place = derivative_tile_position[0]
+    place = derivative_tile_position[0].T
     cap = hub_line_order.shape[2]
     width = max(cap, BLK)
     chunks = areas * cap // width
@@ -347,23 +358,42 @@
     depth = (width // BLK) * snaps + 8
 
     x_others = from_all(starting_voltages)
+    by_swaps = areas <= 16 and areas & (areas - 1) == 0 and cap >= BLK
+    if by_swaps:
+        packed = (shape((depth, BLK), F32),) * areas
+    else:
+        packed = (shape((chunks, depth, BLK), F32),)
     message = call(
-        pack_kernel,
-        shape((chunks, depth, BLK), F32),
-        [VMEM, VMEM, VMEM],
+        functools.partial(pack_kernel, by_swaps),
+        packed,
+        [ANY, ANY, ANY],
         (phasor_readings, reading_error_spread.reshape(lines // BLK, BLK), hub),
-        scratch=[pltpu.VMEM((chunks, width // BLK, BLK), jnp.int32)],
+        scratch=[
+            pltpu.VMEM((snaps, lines), F32),
+            pltpu.VMEM((lines // BLK, BLK), F32),
+            pltpu.VMEM((chunks, width), jnp.int32),
+            pltpu.VMEM((chunks, width // BLK, BLK), jnp.int32),
+            pltpu.SemaphoreType.DMA((3,)),
+        ],
         name="pack_readings",
     )
-    if cap < BLK:
-        each = BLK // cap
-        message = message.reshape(chunks, depth, each, cap).transpose(0, 2, 1, 3)
-        message = message.reshape(areas, depth, cap)
     message, x_others = lax.optimization_barrier((message, x_others))
-    message = lax.all_to_all(message, "area", split_axis=0, concat_axis=0, tiled=True)
-    if cap < BLK:
-        message = message.reshape(chunks, each, depth, cap).transpose(0, 2, 1, 3)
-        message = message.reshape(chunks, depth, BLK)
+    if by_swaps:
+        routes = [[(i, i ^ m) for i in range(areas)] for m in range(areas)]
+        message = [
+            lax.ppermute(message[m], "area", routes[m]) for m in reversed(range(1, areas))
+        ] + [message[0]]
+    else:
+        message = message[0]
+        each = width // cap
+        if each > 1:
+            message = message.reshape(chunks, depth, each, cap).transpose(0, 2, 1, 3)
+            message = message.reshape(areas, depth, cap)
+        message = lax.all_to_all(message, "area", split_axis=0, concat_axis=0, tiled=True)
+        if each > 1:
+            message = message.reshape(chunks, each, depth, cap).transpose(0, 2, 1, 3)
+            message = message.reshape(chunks, depth, BLK)
+        message = [message]
 
     group, lane = call(
         inverse_kernel,
@@ -395,15 +425,22 @@
         name="predict",
     )
     message, guess = lax.optimization_barrier((message, guess))
-    readings, variance = call(
-        unpack_kernel,
-        (shape((snaps, lines), F32), shape((1, lines), F32)),
-        [VMEM, VMEM, VMEM],
-        (message, group, lane),
-        scratch=[pltpu.VMEM((chunks * (width // BLK), BLK), F32)],
-        name="unpack_readings",
-    )
-    reading_others = from_all(readings)
+    halves = []
+    for part in range(2):
+        halves.append(
+            call(
+                functools.partial(unpack_kernel, by_swaps, part * (lines // BLK // 2)),
+                (shape((snaps, lines // 2), F32), shape((1, lines // 2), F32)),
+                [VMEM, VMEM] + [VMEM] * len(message),
+                (group, lane, *message),
+                scratch=[pltpu.VMEM((chunks * (width // BLK), BLK), F32)],
+                flops=2 * 10**9,
+                name="unpack_readings",
+            )
+        )
+    readings = [half[0] for half in halves]
+    variance = [half[1] for half in halves]
+    reading_others = [from_all(half) for half in readings]
     grads = (
         shape((own, everything, BLK), F32),
         shape((ties, everything, BLK), F32),
@@ -414,7 +451,7 @@
     grad, first, second = call(
         pull_kernel,
         grads,
-        [VMEM, VMEM, VMEM, VMEM, VMEM, SMEM],
+        [VMEM, [VMEM] * 2, [VMEM] * 2, [VMEM] * 2, VMEM, SMEM],
         (guess, readings, reading_others, variance, derivative_pieces, place),
         scratch=[total, pltpu.VMEM((everything, lines), BF16)],
         name="pull",
@@ -447,7 +484,7 @@
     grad, first, second = call(
         predict_pull_kernel,
         grads,
-        [VMEM, VMEM, VMEM, VMEM, VMEM, VMEM, VMEM, SMEM],
+        [VMEM, VMEM, VMEM, [VMEM] * 2, [VMEM] * 2, [VMEM] * 2, VMEM, SMEM],
         (aug, first, second, readings, reading_others, variance, derivative_pieces, place),
         scratch=[
             pltpu.VMEM((slots, everything, BLK), BF16),

time: 89.6 us -> 90.3 us (level)
  starting transfers between devices: 22.4 us -> 40 us
  waiting for transfers between devices: 37.7 us -> 27.9 us
  local copies, waits for them, and re-layouts: 9.51 us -> 4.73 us
  Pallas kernels: 19.2 us -> 16.3 us
    ppermute x0 -> x15, starting transfers between devices: none -> 20.9 us  [on_device(): lax.ppermute(message[m], 'area', routes[m])]
    ppermute x8, waiting for transfers between devices: 23.4 us -> 11.4 us  [swap_pair(): return lax.ppermute(block, 'area', pairs + [(b, a) for a, b in pairs])]
    all_to_all x1 -> x0, starting transfers between devices: 6.16 us -> none  [on_device(): lax.all_to_all(message, 'area', split_axis=0, concat_axis=0, tiled=True)]
    unnamed x26 -> x22, local copies, waits for them, and re-layouts: 8.75 us -> 4.73 us
    pallas_call x11 -> x12, Pallas kernels: 19.2 us -> 16.3 us  [call(): pl.pallas_call(kernel, out_shape=outs, in_specs=ins, out_specs=jax.tree.m...]
    ppermute x8, starting transfers between devices: 9.94 us -> 12.4 us  [swap_pair(): return lax.ppermute(block, 'area', pairs + [(b, a) for a, b in pairs])]
    ppermute x0 -> x15, waiting for transfers between devices: none -> 1.21 us  [on_device(): lax.ppermute(message[m], 'area', routes[m])]
    ppermute x4 -> x5, waiting for transfers between devices: 14.3 us -> 15.2 us  [from_snap(): lax.ppermute(block, 'snap', [(i, (i + distance) % members) for i in range...]
  transfers between devices with their start and end apart: 13 -> 28, of which waited for: 8 -> 10; matrix products, arithmetic and copies ran while one was open for 1% -> 0% of each run, Pallas kernels for 8% -> 6%
where the time goes in v3:
time: 90.3 us; the launch traced here: 89.2 us
  starting transfers between devices  40 us (44%)
  waiting for transfers between devices  27.9 us (31%)
  Pallas kernels  16.3 us (18%)
  local copies, waits for them, and re-layouts  4.73 us (5%)
    ppermute x15, starting transfers between devices, on_device(): lax.ppermute(message[m], 'area', routes[m])  20.9 us
    pallas_call x12, Pallas kernels, call(): pl.pallas_call(kernel, out_shape=outs, in_specs=ins, out_specs=jax.tree.m...  16.3 us
    ppermute x5, waiting for transfers between devices, from_snap(): lax.ppermute(block, 'snap', [(i, (i + distance) % members) for i in range...  15.2 us
    ppermute x8, starting transfers between devices, swap_pair(): return lax.ppermute(block, 'area', pairs + [(b, a) for a, b in pairs])  12.4 us
    ppermute x8, waiting for transfers between devices, swap_pair(): return lax.ppermute(block, 'area', pairs + [(b, a) for a, b in pairs])  11.4 us
    ppermute x5, starting transfers between devices, from_snap(): lax.ppermute(block, 'snap', [(i, (i + distance) % members) for i in range...  6.77 us
    unnamed x22, local copies, waits for them, and re-layouts  4.73 us
  transfers between devices with their start and end apart: 28, of which 10 were waited for; matrix products, arithmetic and copies ran while one was open for 0% of the time, Pallas kernels for 6%

profile of v3, /device:TPU:16, one launch (start us, length us, event | category | flops | bytes accessed | tf_op | source)
XLA Modules:
  0.0 89.2 jit_solution(13967019804429999632)
XLA Ops:
  0.0 1.5 %collective-permute-start = (f32[32,2048]{1,0:T(8,128)}, f32[32,2048]{1,0:T(8,128)S(1)}, u32[]{:S(2)}, u32[]{:S(2)}) collective-permute-start(f32[32,2048]{1,0:T(8,128)} %x_ref.1), channel_id=1, source_target_pairs={{0,1},{1,0},{2,3},{3,2},{4,5},{5,4},{6,7},{7,6},{8,9},{9,8},{10,11... | collective-permute-start | bytes 786440 | tf_op jit(solution)/shard_map/ppermute | solution.py:319
  1.5 0.9 %copy-done.4 = f32[32,2048]{1,0:T(8,128)S(1)} copy-done((f32[32,2048]{1,0:T(8,128)S(1)}, f32[32,2048]{1,0:T(8,128)}, u32[]{:S(2)}) %copy-start.4) | copy-done | bytes 262168
  2.5 0.7 copy-done.5
  3.2 0.7 copy-done.8
  3.9 2.5 %pack_readings.1 = (f32[72,128]{1,0:T(8,128)S(1)}, f32[72,128]{1,0:T(8,128)S(1)}, f32[72,128]{1,0:T(8,128)S(1)}, f32[72,128]{1,0:T(8,128)S(1)}, f32[72,128]{1,0:...) custom-call(f32[32,2048]{1,0:T(8,128)S(1)} %copy-done.4, ...), custom_call_target="tpu_custom_call" | custom-call | tf_op jit(solution)/shard_map/pack_readings/pallas_call | solution.py:21
  6.4 1.9 %collective-permute-done = f32[32,2048]{1,0:T(8,128)S(1)} collective-permute-done((f32[32,2048]{1,0:T(8,128)}, f32[32,2048]{1,0:T(8,128)S(1)}, u32[]{:S(2)}, u32[]{:S(2)}) %collective-permute-start) | collective-permute-done | bytes 262176 | tf_op jit(solution)/shard_map/ppermute | solution.py:319
  8.3 1.5 %collective-permute-start.2 = (f32[72,128]{1,0:T(8,128)S(1)}, f32[72,128]{1,0:T(8,128)S(1)}, u32[]{:S(2)}, u32[]{:S(2)}) collective-permute-start(f32[72,128]{1,0:T(8,128)S(1)} %get-tuple-element.94), channel_id=1, source_target_pairs={{0,28},{2,30},{4,24},{6,26},{8,20},{10,22},{12,16},{14,18},{16,12}... | collective-permute-start | bytes 110600 | tf_op jit(solution)/shard_map/ppermute | solution.py:384
  9.8 1.3 %collective-permute-start.3 = (f32[72,128]{1,0:T(8,128)S(1)}, f32[72,128]{1,0:T(8,128)S(1)}, u32[]{:S(2)}, u32[]{:S(2)}) collective-permute-start(f32[72,128]{1,0:T(8,128)S(1)} %get-tuple-element.95), channel_id=1, source_target_pairs={{0,26},{2,24},{4,30},{6,28},{8,18},{10,16},{12,22},{14,20},{16,10}... | collective-permute-start | bytes 110600 | tf_op jit(solution)/shard_map/ppermute | solution.py:384
  11.1 1.6 %collective-permute-start.4 = (f32[72,128]{1,0:T(8,128)S(1)}, f32[72,128]{1,0:T(8,128)S(1)}, u32[]{:S(2)}, u32[]{:S(2)}) collective-permute-start(f32[72,128]{1,0:T(8,128)S(1)} %get-tuple-element.96), channel_id=1, source_target_pairs={{0,24},{2,26},{4,28},{6,30},{8,16},{10,18},{12,20},{14,22},{16,8},... | collective-permute-start | bytes 110600 | tf_op jit(solution)/shard_map/ppermute | solution.py:384
  12.7 4.4 %collective-permute-start.5 = (f32[72,128]{1,0:T(8,128)S(1)}, f32[72,128]{1,0:T(8,128)S(1)}, u32[]{:S(2)}, u32[]{:S(2)}) collective-permute-start(f32[72,128]{1,0:T(8,128)S(1)} %get-tuple-element.97), channel_id=1, source_target_pairs={{0,22},{2,20},{4,18},{6,16},{8,30},{10,28},{12,26},{14,24},{16,6},... | collective-permute-start | bytes 110600 | tf_op jit(solution)/shard_map/ppermute | solution.py:384
  17.5 2.4 %collective-permute-start.7 = (f32[72,128]{1,0:T(8,128)S(1)}, f32[72,128]{1,0:T(8,128)S(1)}, u32[]{:S(2)}, u32[]{:S(2)}) collective-permute-start(f32[72,128]{1,0:T(8,128)S(1)} %get-tuple-element.99), channel_id=1, source_target_pairs={{0,18},{2,16},{4,22},{6,20},{8,26},{10,24},{12,30},{14,28},{16,2},... | collective-permute-start | bytes 110600 | tf_op jit(solution)/shard_map/ppermute | solution.py:384
  19.9 0.9 %copy-done.2 = f32[32,2048]{1,0:T(8,128)S(1)} copy-done((f32[32,2048]{1,0:T(8,128)S(1)}, f32[32,2048]{1,0:T(8,128)}, u32[]{:S(2)}) %copy-start.2) | copy-done | bytes 262168
  20.9 0.7 copy-done.6
  21.6 0.6 first_states.1
  22.6 3.2 %collective-permute-start.9 = (f32[72,128]{1,0:T(8,128)S(1)}, f32[72,128]{1,0:T(8,128)S(1)}, u32[]{:S(2)}, u32[]{:S(2)}) collective-permute-start(f32[72,128]{1,0:T(8,128)S(1)} %get-tuple-element.101), channel_id=1, source_target_pairs={{0,14},{2,12},{4,10},{6,8},{8,6},{10,4},{12,2},{14,0},{16,30},{18,... | collective-permute-start | bytes 110600 | tf_op jit(solution)/shard_map/ppermute | solution.py:384
  25.9 1.5 %collective-permute-start.10 = (f32[72,128]{1,0:T(8,128)S(1)}, f32[72,128]{1,0:T(8,128)S(1)}, u32[]{:S(2)}, u32[]{:S(2)}) collective-permute-start(f32[72,128]{1,0:T(8,128)S(1)} %get-tuple-element.102), channel_id=1, source_target_pairs={{0,12},{2,14},{4,8},{6,10},{8,4},{10,6},{12,0},{14,2},{16,28},{18,... | collective-permute-start | bytes 110600 | tf_op jit(solution)/shard_map/ppermute | solution.py:384
  27.4 2.8 %collective-permute-start.16 = (bf16[4,64,128]{2,1,0:T(8,128)(2,1)S(1)}, bf16[4,64,128]{2,1,0:T(8,128)(2,1)S(1)}, u32[]{:S(2)}, u32[]{:S(2)}) collective-permute-start(bf16[4,64,128]{2,1,0:T(8,128)(2,1)S(1)} %get-tuple-element.111), channel_id=1, source_target_pairs={{2,4},{6,8},{10,12},{14,16},{18,20},{22,24},{26,28},{4,2},{8,6},{1... | collective-permute-start | bytes 196616 | tf_op jit(solution)/shard_map/ppermute | solution.py:310
  30.3 0.7 copy-done.10
  31.5 0.9 %collective-permute-start.11 = (f32[72,128]{1,0:T(8,128)S(1)}, f32[72,128]{1,0:T(8,128)S(1)}, u32[]{:S(2)}, u32[]{:S(2)}) collective-permute-start(f32[72,128]{1,0:T(8,128)S(1)} %get-tuple-element.103), channel_id=1, source_target_pairs={{0,10},{2,8},{4,14},{6,12},{8,2},{10,0},{12,6},{14,4},{16,26},{18,... | collective-permute-start | bytes 110600 | tf_op jit(solution)/shard_map/ppermute | solution.py:384
  32.4 1.3 %collective-permute-start.12 = (f32[72,128]{1,0:T(8,128)S(1)}, f32[72,128]{1,0:T(8,128)S(1)}, u32[]{:S(2)}, u32[]{:S(2)}) collective-permute-start(f32[72,128]{1,0:T(8,128)S(1)} %get-tuple-element.104), channel_id=1, source_target_pairs={{0,8},{2,10},{4,12},{6,14},{8,0},{10,2},{12,4},{14,6},{16,24},{18,... | collective-permute-start | bytes 110600 | tf_op jit(solution)/shard_map/ppermute | solution.py:384
  34.1 0.9 collective-permute-start.14
  35.5 1.4 %predict.1.guess_ref = f32[64,2048]{1,0:T(8,128)S(1)} custom-call(bf16[16,64,128]{2,1,0:T(8,128)(2,1)S(1)} %get-tuple-element.110.aug_ref, bf16[4,64,128]{2,1,0:T(8,128)(2,1)S(1)} %collective-permute-done.16.first_ref, bf16[4,64,128]{2,1,0:T(8,128)(2,1)S(1)} %collective-permute-done.17.second_ref, bf16[16,4,128,128]{3,2,1,0:T(8,128)(2,1)S(1)} %copy-done.1, ...), custom_call_target="tpu_custom_call" | custom-call | flops 1000000000 | tf_op jit(solution)/shard_map/predict/pallas_call | solution.py:21
  37.4 0.8 collective-permute-done.14.refs_13_
  38.1 1.2 %unpack_readings.3 = (f32[32,1024]{1,0:T(8,128)S(1)}, f32[1,1024]{1,0:T(1,128)S(1)}) custom-call(s32[16,128]{1,0:T(8,128)S(1)} %get-tuple-element.114.group_ref, s32[16,128]{1,0:T(8,128)S(1)} %get-tuple-element.115.lane_ref, f32[72,128]{1,0:T(8,128)S(1)} %collective-permute-done.1.refs_0_, f32[72,128]{1,0:T(8,128)S(1)} %collective-permute-done.2.refs_1_, ...), custom_call_target="tpu_custom_call" | custom-call | flops 2000000000 | tf_op jit(solution)/shard_map/unpack_readings/pallas_call | solution.py:21
  39.4 1.2 %unpack_readings.2 = (f32[32,1024]{1,0:T(8,128)S(1)}, f32[1,1024]{1,0:T(1,128)S(1)}) custom-call(s32[16,128]{1,0:T(8,128)S(1)} %get-tuple-element.114.group_ref, s32[16,128]{1,0:T(8,128)S(1)} %get-tuple-element.115.lane_ref, f32[72,128]{1,0:T(8,128)S(1)} %collective-permute-done.1.refs_0_, f32[72,128]{1,0:T(8,128)S(1)} %collective-permute-done.2.refs_1_, ...), custom_call_target="tpu_custom_call" | custom-call | flops 2000000000 | tf_op jit(solution)/shard_map/unpack_readings/pallas_call | solution.py:21
  40.7 1.6 %collective-permute-start.19 = (f32[32,1024]{1,0:T(8,128)S(1)}, f32[32,1024]{1,0:T(8,128)S(1)}, u32[]{:S(2)}, u32[]{:S(2)}) collective-permute-start(f32[32,1024]{1,0:T(8,128)S(1)} %get-tuple-element.133.z_refs_1_), channel_id=1, source_target_pairs={{0,1},{1,0},{2,3},{3,2},{4,5},{5,4},{6,7},{7,6},{8,9},{9,8},{10,11... | collective-permute-start | bytes 393224 | tf_op jit(solution)/shard_map/ppermute | solution.py:319
  42.3 0.5 collective-permute-start.18
  42.8 4.4 %collective-permute-done.19 = f32[32,1024]{1,0:T(8,128)S(1)} collective-permute-done((f32[32,1024]{1,0:T(8,128)S(1)}, f32[32,1024]{1,0:T(8,128)S(1)}, u32[]{:S(2)}, u32[]{:S(2)}) %collective-permute-start.19) | collective-permute-done | bytes 131104 | tf_op jit(solution)/shard_map/ppermute | solution.py:319
  47.1 1.6 %collective-permute-done.18 = f32[32,1024]{1,0:T(8,128)S(1)} collective-permute-done((f32[32,1024]{1,0:T(8,128)S(1)}, f32[32,1024]{1,0:T(8,128)S(1)}, u32[]{:S(2)}, u32[]{:S(2)}) %collective-permute-start.18) | collective-permute-done | bytes 131104 | tf_op jit(solution)/shard_map/ppermute | solution.py:319
  48.7 1.5 %pull.1 = (f32[16,64,128]{2,1,0:T(8,128)S(1)}, f32[4,64,128]{2,1,0:T(8,128)S(1)}, f32[4,64,128]{2,1,0:T(8,128)S(1)}) custom-call(f32[64,2048]{1,0:T(8,128)S(1)} %predict.1.guess_ref, f32[32,1024]{1,0:T(8,128)S(1)} %get-tuple-element.132.z_refs_0_, f32[32,1024]{1,0:T(8,128)S(1)} %get-tuple-element.133.z_refs_1_, f32[1,32,1024]{2,1,0:T(8,128)S(1)} %bitcast.17, ...), custom_call_target="tpu_custom_call" | custom-call | tf_op jit(solution)/shard_map/pull/pallas_call | solution.py:21
  50.2 2.2 %collective-permute-start.20 = (f32[4,64,128]{2,1,0:T(8,128)S(1)}, f32[4,64,128]{2,1,0:T(8,128)S(1)}, u32[]{:S(2)}, u32[]{:S(2)}) collective-permute-start(f32[4,64,128]{2,1,0:T(8,128)S(1)} %get-tuple-element.137), channel_id=1, source_target_pairs={{2,4},{6,8},{10,12},{14,16},{18,20},{22,24},{26,28},{4,2},{8,6},{1... | collective-permute-start | bytes 393224 | tf_op jit(solution)/shard_map/ppermute | solution.py:310
  52.4 1.1 %collective-permute-start.21 = (f32[4,64,128]{2,1,0:T(8,128)S(1)}, f32[4,64,128]{2,1,0:T(8,128)S(1)}, u32[]{:S(2)}, u32[]{:S(2)}) collective-permute-start(f32[4,64,128]{2,1,0:T(8,128)S(1)} %get-tuple-element.138), channel_id=1, source_target_pairs={{0,2},{4,6},{8,10},{12,14},{16,18},{20,22},{24,26},{28,30},{2,0},{... | collective-permute-start | bytes 393224 | tf_op jit(solution)/shard_map/ppermute | solution.py:310
  53.5 4.0 %collective-permute-done.20.back_first_ref = f32[4,64,128]{2,1,0:T(8,128)S(1)} collective-permute-done((f32[4,64,128]{2,1,0:T(8,128)S(1)}, f32[4,64,128]{2,1,0:T(8,128)S(1)}, u32[]{:S(2)}, u32[]{:S(2)}) %collective-permute-start.20) | collective-permute-done | bytes 131104 | tf_op jit(solution)/shard_map/ppermute | solution.py:310
  57.5 2.1 %first_update.1 = (f32[8,64,128]{2,1,0:T(8,128)S(1)}, bf16[8,64,128]{2,1,0:T(8,128)(2,1)S(1)}) custom-call(f32[16,64,128]{2,1,0:T(8,128)S(1)} %get-tuple-element.136.grad_ref, f32[4,64,128]{2,1,0:T(8,128)S(1)} %collective-permute-done.20.back_first_ref, f32[4,64,128]{2,1,0:T(8,128)S(1)} %collective-permute-done.21.back_second_ref, s32[2,4]{1,0:T(2,128)S(1)} %bitcast.23, ...), custom_call_target="tpu_custom_call" | custom-call | tf_op jit(solution)/shard_map/first_update/pallas_call | solution.py:21
  59.5 1.6 %collective-permute-start.22 = (bf16[8,64,128]{2,1,0:T(8,128)(2,1)S(1)}, bf16[8,64,128]{2,1,0:T(8,128)(2,1)S(1)}, u32[]{:S(2)}, u32[]{:S(2)}) collective-permute-start(bf16[8,64,128]{2,1,0:T(8,128)(2,1)S(1)} %get-tuple-element.139.mine_ref), channel_id=1, source_target_pairs={{0,1},{1,0},{2,3},{3,2},{4,5},{5,4},{6,7},{7,6},{8,9},{9,8},{10,11... | collective-permute-start | bytes 393224 | tf_op jit(solution)/shard_map/ppermute | solution.py:319
  61.1 3.9 %collective-permute-done.22 = bf16[8,64,128]{2,1,0:T(8,128)(2,1)S(1)} collective-permute-done((bf16[8,64,128]{2,1,0:T(8,128)(2,1)S(1)}, bf16[8,64,128]{2,1,0:T(8,128)(2,1)S(1)}, u32[]{:S(2)}, u32[]{:S(2)}) %collective-permute-start.22) | collective-permute-done | bytes 131104 | tf_op jit(solution)/shard_map/ppermute | solution.py:319
  65.1 0.6 join_states.1
  65.7 1.9 %collective-permute-start.23 = (bf16[4,64,128]{2,1,0:T(8,128)(2,1)S(1)}, bf16[4,64,128]{2,1,0:T(8,128)(2,1)S(1)}, u32[]{:S(2)}, u32[]{:S(2)}) collective-permute-start(bf16[4,64,128]{2,1,0:T(8,128)(2,1)S(1)} %get-tuple-element.141), channel_id=1, source_target_pairs={{2,4},{6,8},{10,12},{14,16},{18,20},{22,24},{26,28},{4,2},{8,6},{1... | collective-permute-start | bytes 196616 | tf_op jit(solution)/shard_map/ppermute | solution.py:310
  67.6 1.3 %collective-permute-start.24 = (bf16[4,64,128]{2,1,0:T(8,128)(2,1)S(1)}, bf16[4,64,128]{2,1,0:T(8,128)(2,1)S(1)}, u32[]{:S(2)}, u32[]{:S(2)}) collective-permute-start(bf16[4,64,128]{2,1,0:T(8,128)(2,1)S(1)} %get-tuple-element.142), channel_id=1, source_target_pairs={{0,2},{4,6},{8,10},{12,14},{16,18},{20,22},{24,26},{28,30},{2,0},{... | collective-permute-start | bytes 196616 | tf_op jit(solution)/shard_map/ppermute | solution.py:310
  68.9 3.3 %collective-permute-done.23.first_in_ref = bf16[4,64,128]{2,1,0:T(8,128)(2,1)S(1)} collective-permute-done((bf16[4,64,128]{2,1,0:T(8,128)(2,1)S(1)}, bf16[4,64,128]{2,1,0:T(8,128)(2,1)S(1)}, u32[]{:S(2)}, u32[]{:S(2)}) %collective-permute-start.23) | collective-permute-done | bytes 65568 | tf_op jit(solution)/shard_map/ppermute | solution.py:310
  72.2 2.0 %predict_pull.1 = (f32[16,64,128]{2,1,0:T(8,128)S(1)}, f32[4,64,128]{2,1,0:T(8,128)S(1)}, f32[4,64,128]{2,1,0:T(8,128)S(1)}) custom-call(bf16[16,64,128]{2,1,0:T(8,128)(2,1)S(1)} %get-tuple-element.140.aug_ref, bf16[4,64,128]{2,1,0:T(8,128)(2,1)S(1)} %collective-permute-done.23.first_in_ref, bf16[4,64,128]{2,1,0:T(8,128)(2,1)S(1)} %collective-permute-done.24.second_in_ref, ...), custom_call_target="tpu_custom_call" | custom-call | tf_op jit(solution)/shard_map/predict_pull/pallas_call | solution.py:21
  74.2 2.0 %collective-permute-start.25 = (f32[4,64,128]{2,1,0:T(8,128)S(1)}, f32[4,64,128]{2,1,0:T(8,128)S(1)}, u32[]{:S(2)}, u32[]{:S(2)}) collective-permute-start(f32[4,64,128]{2,1,0:T(8,128)S(1)} %get-tuple-element.144), channel_id=1, source_target_pairs={{2,4},{6,8},{10,12},{14,16},{18,20},{22,24},{26,28},{4,2},{8,6},{1... | collective-permute-start | bytes 393224 | tf_op jit(solution)/shard_map/ppermute | solution.py:310
  76.1 1.0 %collective-permute-start.26 = (f32[4,64,128]{2,1,0:T(8,128)S(1)}, f32[4,64,128]{2,1,0:T(8,128)S(1)}, u32[]{:S(2)}, u32[]{:S(2)}) collective-permute-start(f32[4,64,128]{2,1,0:T(8,128)S(1)} %get-tuple-element.145), channel_id=1, source_target_pairs={{0,2},{4,6},{8,10},{12,14},{16,18},{20,22},{24,26},{28,30},{2,0},{... | collective-permute-start | bytes 393224 | tf_op jit(solution)/shard_map/ppermute | solution.py:310
  77.2 4.2 %collective-permute-done.25.back_first_ref = f32[4,64,128]{2,1,0:T(8,128)S(1)} collective-permute-done((f32[4,64,128]{2,1,0:T(8,128)S(1)}, f32[4,64,128]{2,1,0:T(8,128)S(1)}, u32[]{:S(2)}, u32[]{:S(2)}) %collective-permute-start.25) | collective-permute-done | bytes 131104 | tf_op jit(solution)/shard_map/ppermute | solution.py:310
  81.3 2.0 %last_update.1 = (f32[32,1024]{1,0:T(8,128)S(1)}, f32[1,32,1024]{2,1,0:T(8,128)S(1)}) custom-call(f32[16,64,128]{2,1,0:T(8,128)S(1)} %get-tuple-element.143.grad_ref, f32[4,64,128]{2,1,0:T(8,128)S(1)} %collective-permute-done.25.back_first_ref, f32[4,64,128]{2,1,0:T(8,128)S(1)} %collective-permute-done.26.back_second_ref, s32[2,4]{1,0:T(2,128)S(1)} %bitcast.25, ...), custom_call_target="tpu_custom_call" | custom-call | tf_op jit(solution)/shard_map/last_update/pallas_call | solution.py:21
  83.4 1.6 %collective-permute-start.27 = (f32[32,1024]{1,0:T(8,128)S(1)}, f32[32,1024]{1,0:T(8,128)S(1)}, u32[]{:S(2)}, u32[]{:S(2)}) collective-permute-start(f32[32,1024]{1,0:T(8,128)S(1)} %bitcast.30), channel_id=1, source_target_pairs={{0,1},{1,0},{2,3},{3,2},{4,5},{5,4},{6,7},{7,6},{8,9},{9,8},{10,11... | collective-permute-start | bytes 393224 | tf_op jit(solution)/shard_map/ppermute | solution.py:319
  85.0 3.4 %collective-permute-done.27 = f32[32,1024]{1,0:T(8,128)S(1)} collective-permute-done((f32[32,1024]{1,0:T(8,128)S(1)}, f32[32,1024]{1,0:T(8,128)S(1)}, u32[]{:S(2)}, u32[]{:S(2)}) %collective-permute-start.27) | collective-permute-done | bytes 131104 | tf_op jit(solution)/shard_map/ppermute | solution.py:319
  88.4 0.7 finish.1
  (42 shorter events, 2.9 us)
Async XLA Ops:
  0.0 35.5 %copy-start.1 = (bf16[16,4,128,128]{3,2,1,0:T(8,128)(2,1)S(1)}, bf16[16,4,128,128]{3,2,1,0:T(8,128)(2,1)}, u32[]{:S(2)}) copy-start(bf16[16,4,128,128]{3,2,1,0:T(8,128)(2,1)} %tiles_ref.5) | copy-start | bytes 6291460
  0.0 8.3 %collective-permute-start = (f32[32,2048]{1,0:T(8,128)}, f32[32,2048]{1,0:T(8,128)S(1)}, u32[]{:S(2)}, u32[]{:S(2)}) collective-permute-start(f32[32,2048]{1,0:T(8,128)} %x_ref.1), channel_id=1, source_target_pairs={{0,1},{1,0},{2,3},{3,2},{4,5},{5,4},{6,7},{7,6},{8,9},{9,8},{10,11... | collective-permute-start | bytes 786440 | tf_op jit(solution)/shard_map/ppermute | solution.py:319
  1.5 0.9 %copy-start.4 = (f32[32,2048]{1,0:T(8,128)S(1)}, f32[32,2048]{1,0:T(8,128)}, u32[]{:S(2)}) copy-start(f32[32,2048]{1,0:T(8,128)} %z_in.1) | copy-start | bytes 786436
  2.5 0.7 copy-start.5
  3.2 0.7 copy-start.8
  8.3 8.8 %collective-permute-start.1 = (f32[72,128]{1,0:T(8,128)S(1)}, f32[72,128]{1,0:T(8,128)S(1)}, u32[]{:S(2)}, u32[]{:S(2)}) collective-permute-start(f32[72,128]{1,0:T(8,128)S(1)} %get-tuple-element.93), channel_id=1, source_target_pairs={{0,30},{2,28},{4,26},{6,24},{8,22},{10,20},{12,18},{14,16},{16,14}... | collective-permute-start | bytes 110600 | tf_op jit(solution)/shard_map/ppermute | solution.py:384
  8.3 9.3 %collective-permute-start.2 = (f32[72,128]{1,0:T(8,128)S(1)}, f32[72,128]{1,0:T(8,128)S(1)}, u32[]{:S(2)}, u32[]{:S(2)}) collective-permute-start(f32[72,128]{1,0:T(8,128)S(1)} %get-tuple-element.94), channel_id=1, source_target_pairs={{0,28},{2,30},{4,24},{6,26},{8,20},{10,22},{12,16},{14,18},{16,12}... | collective-permute-start | bytes 110600 | tf_op jit(solution)/shard_map/ppermute | solution.py:384
  9.8 12.5 %collective-permute-start.3 = (f32[72,128]{1,0:T(8,128)S(1)}, f32[72,128]{1,0:T(8,128)S(1)}, u32[]{:S(2)}, u32[]{:S(2)}) collective-permute-start(f32[72,128]{1,0:T(8,128)S(1)} %get-tuple-element.95), channel_id=1, source_target_pairs={{0,26},{2,24},{4,30},{6,28},{8,18},{10,16},{12,22},{14,20},{16,10}... | collective-permute-start | bytes 110600 | tf_op jit(solution)/shard_map/ppermute | solution.py:384
  11.1 11.5 %collective-permute-start.4 = (f32[72,128]{1,0:T(8,128)S(1)}, f32[72,128]{1,0:T(8,128)S(1)}, u32[]{:S(2)}, u32[]{:S(2)}) collective-permute-start(f32[72,128]{1,0:T(8,128)S(1)} %get-tuple-element.96), channel_id=1, source_target_pairs={{0,24},{2,26},{4,28},{6,30},{8,16},{10,18},{12,20},{14,22},{16,8},... | collective-permute-start | bytes 110600 | tf_op jit(solution)/shard_map/ppermute | solution.py:384
  12.7 13.2 %collective-permute-start.5 = (f32[72,128]{1,0:T(8,128)S(1)}, f32[72,128]{1,0:T(8,128)S(1)}, u32[]{:S(2)}, u32[]{:S(2)}) collective-permute-start(f32[72,128]{1,0:T(8,128)S(1)} %get-tuple-element.97), channel_id=1, source_target_pairs={{0,22},{2,20},{4,18},{6,16},{8,30},{10,28},{12,26},{14,24},{16,6},... | collective-permute-start | bytes 110600 | tf_op jit(solution)/shard_map/ppermute | solution.py:384
  17.0 10.3 %collective-permute-start.6 = (f32[72,128]{1,0:T(8,128)S(1)}, f32[72,128]{1,0:T(8,128)S(1)}, u32[]{:S(2)}, u32[]{:S(2)}) collective-permute-start(f32[72,128]{1,0:T(8,128)S(1)} %get-tuple-element.98), channel_id=1, source_target_pairs={{0,20},{2,22},{4,16},{6,18},{8,28},{10,30},{12,24},{14,26},{16,4},... | collective-permute-start | bytes 110600 | tf_op jit(solution)/shard_map/ppermute | solution.py:384
  17.5 12.6 %collective-permute-start.7 = (f32[72,128]{1,0:T(8,128)S(1)}, f32[72,128]{1,0:T(8,128)S(1)}, u32[]{:S(2)}, u32[]{:S(2)}) collective-permute-start(f32[72,128]{1,0:T(8,128)S(1)} %get-tuple-element.99), channel_id=1, source_target_pairs={{0,18},{2,16},{4,22},{6,20},{8,26},{10,24},{12,30},{14,28},{16,2},... | collective-permute-start | bytes 110600 | tf_op jit(solution)/shard_map/ppermute | solution.py:384
  19.9 0.9 %copy-start.2 = (f32[32,2048]{1,0:T(8,128)S(1)}, f32[32,2048]{1,0:T(8,128)}, u32[]{:S(2)}) copy-start(f32[32,2048]{1,0:T(8,128)} %x_ref.1) | copy-start | bytes 786436
  20.9 0.7 copy-start.6
  21.6 14.0 %copy-start.9 = (s32[1,16,4]{1,2,0:T(4,128)S(1)}, s32[1,16,4]{1,2,0:T(4,128)}, u32[]{:S(2)}) copy-start(s32[1,16,4]{1,2,0:T(4,128)} %param.13) | copy-start | bytes 772
  22.2 9.2 %collective-permute-start.8 = (f32[72,128]{1,0:T(8,128)S(1)}, f32[72,128]{1,0:T(8,128)S(1)}, u32[]{:S(2)}, u32[]{:S(2)}) collective-permute-start(f32[72,128]{1,0:T(8,128)S(1)} %get-tuple-element.100), channel_id=1, source_target_pairs={{0,16},{2,18},{4,20},{6,22},{8,24},{10,26},{12,28},{14,30},{16,0},... | collective-permute-start | bytes 110600 | tf_op jit(solution)/shard_map/ppermute | solution.py:384
  22.6 9.8 %collective-permute-start.9 = (f32[72,128]{1,0:T(8,128)S(1)}, f32[72,128]{1,0:T(8,128)S(1)}, u32[]{:S(2)}, u32[]{:S(2)}) collective-permute-start(f32[72,128]{1,0:T(8,128)S(1)} %get-tuple-element.101), channel_id=1, source_target_pairs={{0,14},{2,12},{4,10},{6,8},{8,6},{10,4},{12,2},{14,0},{16,30},{18,... | collective-permute-start | bytes 110600 | tf_op jit(solution)/shard_map/ppermute | solution.py:384
  25.9 7.8 %collective-permute-start.10 = (f32[72,128]{1,0:T(8,128)S(1)}, f32[72,128]{1,0:T(8,128)S(1)}, u32[]{:S(2)}, u32[]{:S(2)}) collective-permute-start(f32[72,128]{1,0:T(8,128)S(1)} %get-tuple-element.102), channel_id=1, source_target_pairs={{0,12},{2,14},{4,8},{6,10},{8,4},{10,6},{12,0},{14,2},{16,28},{18,... | collective-permute-start | bytes 110600 | tf_op jit(solution)/shard_map/ppermute | solution.py:384
  27.4 6.8 %collective-permute-start.16 = (bf16[4,64,128]{2,1,0:T(8,128)(2,1)S(1)}, bf16[4,64,128]{2,1,0:T(8,128)(2,1)S(1)}, u32[]{:S(2)}, u32[]{:S(2)}) collective-permute-start(bf16[4,64,128]{2,1,0:T(8,128)(2,1)S(1)} %get-tuple-element.111), channel_id=1, source_target_pairs={{2,4},{6,8},{10,12},{14,16},{18,20},{22,24},{26,28},{4,2},{8,6},{1... | collective-permute-start | bytes 196616 | tf_op jit(solution)/shard_map/ppermute | solution.py:310
  30.2 4.8 %collective-permute-start.17 = (bf16[4,64,128]{2,1,0:T(8,128)(2,1)S(1)}, bf16[4,64,128]{2,1,0:T(8,128)(2,1)S(1)}, u32[]{:S(2)}, u32[]{:S(2)}) collective-permute-start(bf16[4,64,128]{2,1,0:T(8,128)(2,1)S(1)} %get-tuple-element.112), channel_id=1, source_target_pairs={{0,2},{4,6},{8,10},{12,14},{16,18},{20,22},{24,26},{28,30},{2,0},{... | collective-permute-start | bytes 196616 | tf_op jit(solution)/shard_map/ppermute | solution.py:310
  30.3 0.7 copy-start.10
  31.5 5.5 %collective-permute-start.11 = (f32[72,128]{1,0:T(8,128)S(1)}, f32[72,128]{1,0:T(8,128)S(1)}, u32[]{:S(2)}, u32[]{:S(2)}) collective-permute-start(f32[72,128]{1,0:T(8,128)S(1)} %get-tuple-element.103), channel_id=1, source_target_pairs={{0,10},{2,8},{4,14},{6,12},{8,2},{10,0},{12,6},{14,4},{16,26},{18,... | collective-permute-start | bytes 110600 | tf_op jit(solution)/shard_map/ppermute | solution.py:384
  32.4 4.6 %collective-permute-start.12 = (f32[72,128]{1,0:T(8,128)S(1)}, f32[72,128]{1,0:T(8,128)S(1)}, u32[]{:S(2)}, u32[]{:S(2)}) collective-permute-start(f32[72,128]{1,0:T(8,128)S(1)} %get-tuple-element.104), channel_id=1, source_target_pairs={{0,8},{2,10},{4,12},{6,14},{8,0},{10,2},{12,4},{14,6},{16,24},{18,... | collective-permute-start | bytes 110600 | tf_op jit(solution)/shard_map/ppermute | solution.py:384
  33.7 3.7 %collective-permute-start.13 = (f32[72,128]{1,0:T(8,128)S(1)}, f32[72,128]{1,0:T(8,128)S(1)}, u32[]{:S(2)}, u32[]{:S(2)}) collective-permute-start(f32[72,128]{1,0:T(8,128)S(1)} %get-tuple-element.105), channel_id=1, source_target_pairs={{0,6},{2,4},{4,2},{6,0},{8,14},{10,12},{12,10},{14,8},{16,22},{18,... | collective-permute-start | bytes 110600 | tf_op jit(solution)/shard_map/ppermute | solution.py:384
  34.1 4.0 %collective-permute-start.14 = (f32[72,128]{1,0:T(8,128)S(1)}, f32[72,128]{1,0:T(8,128)S(1)}, u32[]{:S(2)}, u32[]{:S(2)}) collective-permute-start(f32[72,128]{1,0:T(8,128)S(1)} %get-tuple-element.106), channel_id=1, source_target_pairs={{0,4},{2,6},{4,0},{6,2},{8,12},{10,14},{12,8},{14,10},{16,20},{18,... | collective-permute-start | bytes 110600 | tf_op jit(solution)/shard_map/ppermute | solution.py:384
  35.0 3.1 %collective-permute-start.15 = (f32[72,128]{1,0:T(8,128)S(1)}, f32[72,128]{1,0:T(8,128)S(1)}, u32[]{:S(2)}, u32[]{:S(2)}) collective-permute-start(f32[72,128]{1,0:T(8,128)S(1)} %get-tuple-element.107), channel_id=1, source_target_pairs={{0,2},{2,0},{4,6},{6,4},{8,10},{10,8},{12,14},{14,12},{16,18},{18,... | collective-permute-start | bytes 110600 | tf_op jit(solution)/shard_map/ppermute | solution.py:384
  39.4 18.1 %copy-start = (bf16[1024,2048]{1,0:T(8,128)(2,1)S(1)}, bf16[1024,2048]{1,0:T(8,128)(2,1)}, u32[]{:S(2)}) copy-start(bf16[1024,2048]{1,0:T(8,128)(2,1)} %gain_ref.3) | copy-start | bytes 12582916
  39.4 18.1 %copy-start.3 = (f32[32,2048]{1,0:T(8,128)S(1)}, f32[32,2048]{1,0:T(8,128)}, u32[]{:S(2)}) copy-start(f32[32,2048]{1,0:T(8,128)} %x_ref.1) | copy-start | bytes 786436
  39.4 18.1 %copy-start.7 = (s32[1,2,4]{2,1,0:T(2,128)S(1)}, s32[1,2,4]{2,1,0:T(2,128)}, u32[]{:S(2)}) copy-start(s32[1,2,4]{2,1,0:T(2,128)} %param.14) | copy-start | bytes 100
  40.7 6.5 %collective-permute-start.19 = (f32[32,1024]{1,0:T(8,128)S(1)}, f32[32,1024]{1,0:T(8,128)S(1)}, u32[]{:S(2)}, u32[]{:S(2)}) collective-permute-start(f32[32,1024]{1,0:T(8,128)S(1)} %get-tuple-element.133.z_refs_1_), channel_id=1, source_target_pairs={{0,1},{1,0},{2,3},{3,2},{4,5},{5,4},{6,7},{7,6},{8,9},{9,8},{10,11... | collective-permute-start | bytes 393224 | tf_op jit(solution)/shard_map/ppermute | solution.py:319
  42.3 6.5 %collective-permute-start.18 = (f32[32,1024]{1,0:T(8,128)S(1)}, f32[32,1024]{1,0:T(8,128)S(1)}, u32[]{:S(2)}, u32[]{:S(2)}) collective-permute-start(f32[32,1024]{1,0:T(8,128)S(1)} %get-tuple-element.132.z_refs_0_), channel_id=1, source_target_pairs={{0,1},{1,0},{2,3},{3,2},{4,5},{5,4},{6,7},{7,6},{8,9},{9,8},{10,11... | collective-permute-start | bytes 393224 | tf_op jit(solution)/shard_map/ppermute | solution.py:319
  50.2 7.3 %collective-permute-start.20 = (f32[4,64,128]{2,1,0:T(8,128)S(1)}, f32[4,64,128]{2,1,0:T(8,128)S(1)}, u32[]{:S(2)}, u32[]{:S(2)}) collective-permute-start(f32[4,64,128]{2,1,0:T(8,128)S(1)} %get-tuple-element.137), channel_id=1, source_target_pairs={{2,4},{6,8},{10,12},{14,16},{18,20},{22,24},{26,28},{4,2},{8,6},{1... | collective-permute-start | bytes 393224 | tf_op jit(solution)/shard_map/ppermute | solution.py:310
  52.4 5.1 %collective-permute-start.21 = (f32[4,64,128]{2,1,0:T(8,128)S(1)}, f32[4,64,128]{2,1,0:T(8,128)S(1)}, u32[]{:S(2)}, u32[]{:S(2)}) collective-permute-start(f32[4,64,128]{2,1,0:T(8,128)S(1)} %get-tuple-element.138), channel_id=1, source_target_pairs={{0,2},{4,6},{8,10},{12,14},{16,18},{20,22},{24,26},{28,30},{2,0},{... | collective-permute-start | bytes 393224 | tf_op jit(solution)/shard_map/ppermute | solution.py:310
  59.5 5.5 %collective-permute-start.22 = (bf16[8,64,128]{2,1,0:T(8,128)(2,1)S(1)}, bf16[8,64,128]{2,1,0:T(8,128)(2,1)S(1)}, u32[]{:S(2)}, u32[]{:S(2)}) collective-permute-start(bf16[8,64,128]{2,1,0:T(8,128)(2,1)S(1)} %get-tuple-element.139.mine_ref), channel_id=1, source_target_pairs={{0,1},{1,0},{2,3},{3,2},{4,5},{5,4},{6,7},{7,6},{8,9},{9,8},{10,11... | collective-permute-start | bytes 393224 | tf_op jit(solution)/shard_map/ppermute | solution.py:319
  65.7 6.5 %collective-permute-start.23 = (bf16[4,64,128]{2,1,0:T(8,128)(2,1)S(1)}, bf16[4,64,128]{2,1,0:T(8,128)(2,1)S(1)}, u32[]{:S(2)}, u32[]{:S(2)}) collective-permute-start(bf16[4,64,128]{2,1,0:T(8,128)(2,1)S(1)} %get-tuple-element.141), channel_id=1, source_target_pairs={{2,4},{6,8},{10,12},{14,16},{18,20},{22,24},{26,28},{4,2},{8,6},{1... | collective-permute-start | bytes 196616 | tf_op jit(solution)/shard_map/ppermute | solution.py:310
  67.6 4.6 %collective-permute-start.24 = (bf16[4,64,128]{2,1,0:T(8,128)(2,1)S(1)}, bf16[4,64,128]{2,1,0:T(8,128)(2,1)S(1)}, u32[]{:S(2)}, u32[]{:S(2)}) collective-permute-start(bf16[4,64,128]{2,1,0:T(8,128)(2,1)S(1)} %get-tuple-element.142), channel_id=1, source_target_pairs={{0,2},{4,6},{8,10},{12,14},{16,18},{20,22},{24,26},{28,30},{2,0},{... | collective-permute-start | bytes 196616 | tf_op jit(solution)/shard_map/ppermute | solution.py:310
  74.2 7.2 %collective-permute-start.25 = (f32[4,64,128]{2,1,0:T(8,128)S(1)}, f32[4,64,128]{2,1,0:T(8,128)S(1)}, u32[]{:S(2)}, u32[]{:S(2)}) collective-permute-start(f32[4,64,128]{2,1,0:T(8,128)S(1)} %get-tuple-element.144), channel_id=1, source_target_pairs={{2,4},{6,8},{10,12},{14,16},{18,20},{22,24},{26,28},{4,2},{8,6},{1... | collective-permute-start | bytes 393224 | tf_op jit(solution)/shard_map/ppermute | solution.py:310
  76.1 5.2 %collective-permute-start.26 = (f32[4,64,128]{2,1,0:T(8,128)S(1)}, f32[4,64,128]{2,1,0:T(8,128)S(1)}, u32[]{:S(2)}, u32[]{:S(2)}) collective-permute-start(f32[4,64,128]{2,1,0:T(8,128)S(1)} %get-tuple-element.145), channel_id=1, source_target_pairs={{0,2},{4,6},{8,10},{12,14},{16,18},{20,22},{24,26},{28,30},{2,0},{... | collective-permute-start | bytes 393224 | tf_op jit(solution)/shard_map/ppermute | solution.py:310
  83.4 5.0 %collective-permute-start.27 = (f32[32,1024]{1,0:T(8,128)S(1)}, f32[32,1024]{1,0:T(8,128)S(1)}, u32[]{:S(2)}, u32[]{:S(2)}) collective-permute-start(f32[32,1024]{1,0:T(8,128)S(1)} %bitcast.30), channel_id=1, source_target_pairs={{0,1},{1,0},{2,3},{3,2},{4,5},{5,4},{6,7},{7,6},{8,9},{9,8},{10,11... | collective-permute-start | bytes 393224 | tf_op jit(solution)/shard_map/ppermute | solution.py:319

commit v4 on v3

--- a/solution.py
+++ b/solution.py
@@ -13,7 +13,7 @@
 BF16 = jnp.bfloat16
 NT = (((1,), (1,)), ((), ()))
 VMEM = pl.BlockSpec(memory_space=pltpu.VMEM)
-ANY = pl.BlockSpec(memory_space=pl.ANY)
+HBM = pl.BlockSpec(memory_space=pltpu.HBM)
 SMEM = pl.BlockSpec(memory_space=pltpu.SMEM)
 
 
@@ -40,16 +40,7 @@
     return lax.broadcasted_iota(jnp.int32, shape, 0)
 
 
-def pieces(refs):
-    return [refs[0].at[i] for i in range(refs[0].shape[0])] if refs[0].ndim == 3 else list(refs)
-
-
-def swapper(by_swaps):
-    return lax.axis_index("area") if by_swaps else 0
-
-
-def pack_kernel(by_swaps, z_in, v_in, hub_in, *refs):
-    out_refs, (z_ref, v_ref, hub_ref, slot_ref, sems) = refs[:-5], refs[-5:]
+def pack_kernel(z_in, v_in, hub_in, out_ref, z_ref, v_ref, hub_ref, sems):
     copies = [
         pltpu.make_async_copy(source, target, sems.at[i])
         for i, (source, target) in enumerate(((hub_in, hub_ref), (z_in, z_ref), (v_in, v_ref)))
@@ -63,13 +54,9 @@
     chunks, width = hub_ref.shape
     groups = width // BLK
     for d in range(chunks):
-        for g in range(groups):
-            slot_ref[d, g : g + 1] = hub_ref[d : d + 1, g * BLK : (g + 1) * BLK]
-    me = swapper(by_swaps)
-    for m, out_ref in reversed(list(enumerate(pieces(out_refs)))):
         tail = jnp.zeros((8, BLK), F32)
         for g in range(groups):
-            slot = slot_ref[jnp.bitwise_xor(me, m), g : g + 1]
+            slot = hub_ref[d : d + 1, g * BLK : (g + 1) * BLK]
             high = jnp.right_shift(slot, 7)
             low = jnp.bitwise_and(slot, 127)
             lanes = jnp.broadcast_to(low, (snaps, BLK))
@@ -78,12 +65,12 @@
             for b in range(blocks):
                 found = lane_gather(z_ref[:, b * BLK : (b + 1) * BLK], lanes)
                 picked = jnp.where(block_of == b, found, picked)
-            out_ref[g * snaps : (g + 1) * snaps, :] = picked
+            out_ref[d, g * snaps : (g + 1) * snaps, :] = picked
             found = lane_gather(v_ref[...], jnp.broadcast_to(low, (blocks, BLK)))
             mine = rows_iota((blocks, BLK)) == high
             variance = jnp.sum(jnp.where(mine, found, 0.0), axis=0, keepdims=True)
             tail = jnp.where(rows_iota((8, BLK)) == g, variance, tail)
-        out_ref[groups * snaps :, :] = tail
+        out_ref[d, groups * snaps :, :] = tail
 
 
 def inverse_kernel(own_ref, group_ref, lane_ref):
@@ -108,23 +95,22 @@
     lane_ref[...] = total[blocks:].astype(jnp.int32)
 
 
-def unpack_kernel(by_swaps, start, group_ref, lane_ref, *refs):
-    message_refs, (z_ref, v_ref, variance_ref) = pieces(refs[:-3][::-1]), refs[-3:]
+def unpack_kernel(start, group_ref, lane_ref, message_ref, z_ref, v_ref, variance_ref):
     snaps, lines = z_ref.shape
-    groups = (message_refs[0].shape[0] - 8) // snaps
-    total = len(message_refs) * groups
-    for m, message_ref in enumerate(message_refs):
-        variance_ref[m * groups : (m + 1) * groups, :] = message_ref[groups * snaps :, :][:groups]
-    me = swapper(by_swaps) * groups
+    chunks = message_ref.shape[0]
+    groups = (message_ref.shape[1] - 8) // snaps
+    total = chunks * groups
+    for d in range(chunks):
+        variance_ref[d * groups : (d + 1) * groups, :] = message_ref[d, groups * snaps :, :][:groups]
     for b in range(lines // BLK):
-        group = jnp.bitwise_xor(group_ref[start + b : start + b + 1, :], me)
+        group = group_ref[start + b : start + b + 1, :]
         lane = lane_ref[start + b : start + b + 1, :]
         lanes = jnp.broadcast_to(lane, (snaps, BLK))
         group_of = jnp.broadcast_to(group, (snaps, BLK))
         picked = jnp.zeros((snaps, BLK), F32)
         for g in range(total):
             rows = slice(g % groups * snaps, (g % groups + 1) * snaps)
-            found = lane_gather(message_refs[g // groups][rows, :], lanes)
+            found = lane_gather(message_ref[g // groups, rows, :], lanes)
             picked = jnp.where(group_of == g, found, picked)
         columns = slice(b * BLK, (b + 1) * BLK)
         z_ref[:, columns] = picked
@@ -148,15 +134,22 @@
         out_ref[t] = jnp.where(b >= 0, block, jnp.zeros_like(block))
 
 
-def first_states_kernel(own_ref, others_ref, ties_ref, aug_ref, first_ref, second_ref):
+def first_states_kernel(
+    x_ref, own_ref, others_ref, ties_ref, aug_ref, first_ref, second_ref, sent_refs
+):
     snaps = own_ref.shape[0]
     for b in range(aug_ref.shape[0]):
         columns = slice(b * BLK, (b + 1) * BLK)
-        aug_ref[b, :snaps] = own_ref[:, columns].astype(BF16)
+        aug_ref[b, :snaps] = own_ref[:, columns]
         for i in range(others_ref.shape[0]):
-            aug_ref[b, (i + 1) * snaps : (i + 2) * snaps] = others_ref[i, :, columns].astype(BF16)
+            aug_ref[b, (i + 1) * snaps : (i + 2) * snaps] = others_ref[i, :, columns]
     pick(lambda b: aug_ref[b], ties_ref, 1 - parity(), first_ref)
     pick(lambda b: aug_ref[b], ties_ref, parity(), second_ref)
+    members = len(sent_refs) + 1
+    width = x_ref.shape[1] // members
+    for i, sent_ref in enumerate(sent_refs, 1):
+        at = lax.rem(lax.axis_index("snap") + i, members) * width
+        sent_ref[...] = x_ref[:, pl.ds(pl.multiple_of(at, BLK), width)]
 
 
 def join_states_kernel(mine_ref, others_ref, ties_ref, aug_ref, first_ref, second_ref):
@@ -268,7 +261,7 @@
 
 
 def first_update_kernel(
-    grad_ref, back_first_ref, back_second_ref, ties_ref, gain_ref, x_ref, x_others_ref,
+    grad_ref, back_first_ref, back_second_ref, ties_ref, gain_ref, x_ref, x_others_refs,
     state_ref, message_ref, work_ref,
 ):
     gradient = full_gradient(grad_ref, back_first_ref, back_second_ref, ties_ref, work_ref)
@@ -276,7 +269,7 @@
     me = lax.axis_index("snap")
     for i, update in updates(gradient, gain_ref):
         columns = pl.ds(pl.multiple_of((me * held + i) * BLK, BLK), BLK)
-        parts = [x_ref[:, columns]] + [o[:, columns] for o in split(x_others_ref)]
+        parts = [x_ref[:, columns]] + [o[:, i * BLK : (i + 1) * BLK] for o in x_others_refs]
         state = jnp.concatenate(parts, axis=0) + update
         state_ref[i] = state
         message_ref[i] = state.astype(BF16)
@@ -357,43 +350,30 @@
     holder = holder_line_order[0].reshape(chunks, width)
     depth = (width // BLK) * snaps + 8
 
-    x_others = from_all(starting_voltages)
-    by_swaps = areas <= 16 and areas & (areas - 1) == 0 and cap >= BLK
-    if by_swaps:
-        packed = (shape((depth, BLK), F32),) * areas
-    else:
-        packed = (shape((chunks, depth, BLK), F32),)
+    rounded = starting_voltages.astype(BF16)
+    rounded_others = from_all(rounded)
     message = call(
-        functools.partial(pack_kernel, by_swaps),
-        packed,
-        [ANY, ANY, ANY],
+        pack_kernel,
+        shape((chunks, depth, BLK), F32),
+        [HBM, HBM, HBM],
         (phasor_readings, reading_error_spread.reshape(lines // BLK, BLK), hub),
         scratch=[
             pltpu.VMEM((snaps, lines), F32),
             pltpu.VMEM((lines // BLK, BLK), F32),
             pltpu.VMEM((chunks, width), jnp.int32),
-            pltpu.VMEM((chunks, width // BLK, BLK), jnp.int32),
             pltpu.SemaphoreType.DMA((3,)),
         ],
         name="pack_readings",
     )
-    message, x_others = lax.optimization_barrier((message, x_others))
-    if by_swaps:
-        routes = [[(i, i ^ m) for i in range(areas)] for m in range(areas)]
-        message = [
-            lax.ppermute(message[m], "area", routes[m]) for m in reversed(range(1, areas))
-        ] + [message[0]]
-    else:
-        message = message[0]
-        each = width // cap
-        if each > 1:
-            message = message.reshape(chunks, depth, each, cap).transpose(0, 2, 1, 3)
-            message = message.reshape(areas, depth, cap)
-        message = lax.all_to_all(message, "area", split_axis=0, concat_axis=0, tiled=True)
-        if each > 1:
-            message = message.reshape(chunks, each, depth, cap).transpose(0, 2, 1, 3)
-            message = message.reshape(chunks, depth, BLK)
-        message = [message]
+    message, rounded_others = lax.optimization_barrier((message, rounded_others))
+    each = width // cap
+    if each > 1:
+        message = message.reshape(chunks, depth, each, cap).transpose(0, 2, 1, 3)
+        message = message.reshape(areas, depth, cap)
+    message = lax.all_to_all(message, "area", split_axis=0, concat_axis=0, tiled=True)
+    if each > 1:
+        message = message.reshape(chunks, each, depth, cap).transpose(0, 2, 1, 3)
+        message = message.reshape(chunks, depth, BLK)
 
     group, lane = call(
         inverse_kernel,
@@ -403,17 +383,19 @@
         flops=10**9,
         name="invert_order",
     )
-    aug, first, second = call(
+    aug, first, second, x_sent = call(
         first_states_kernel,
         (
             shape((own, everything, BLK), BF16),
             shape((ties, everything, BLK), BF16),
             shape((ties, everything, BLK), BF16),
+            [shape((snaps, held * BLK), F32)] * (members - 1),
         ),
-        [VMEM, VMEM, SMEM],
-        (starting_voltages, x_others, ties_table),
+        [VMEM, VMEM, VMEM, SMEM],
+        (starting_voltages, rounded, rounded_others, ties_table),
         name="first_states",
     )
+    x_others = [from_snap(sent, i) for i, sent in enumerate(x_sent, 1)]
     first, second = with_neighbours(first, second)
     guess = call(
         predict_kernel,
@@ -424,15 +406,15 @@
         flops=10**9,
         name="predict",
     )
-    message, guess = lax.optimization_barrier((message, guess))
+    message, guess, x_others = lax.optimization_barrier((message, guess, x_others))
     halves = []
     for part in range(2):
         halves.append(
             call(
-                functools.partial(unpack_kernel, by_swaps, part * (lines // BLK // 2)),
+                functools.partial(unpack_kernel, part * (lines // BLK // 2)),
                 (shape((snaps, lines // 2), F32), shape((1, lines // 2), F32)),
-                [VMEM, VMEM] + [VMEM] * len(message),
-                (group, lane, *message),
+                [VMEM, VMEM, VMEM],
+                (group, lane, message),
                 scratch=[pltpu.VMEM((chunks * (width // BLK), BLK), F32)],
                 flops=2 * 10**9,
                 name="unpack_readings",
@@ -460,7 +442,7 @@
     state, mine = call(
         first_update_kernel,
         (shape((held, everything, BLK), F32), shape((held, everything, BLK), BF16)),
-        [VMEM, VMEM, VMEM, SMEM, VMEM, VMEM, VMEM],
+        [VMEM, VMEM, VMEM, SMEM, VMEM, VMEM, [VMEM] * (members - 1)],
         (
             grad, first, second, ties_table, reciprocal_normal_operator,
             starting_voltages, x_others,

time: 90.3 us -> 82.1 us (0.909)
  starting transfers between devices: 40 us -> 24.3 us
  waiting for transfers between devices: 27.9 us -> 33.3 us
  other arithmetic: 0 us -> 1.11 us
    ppermute x15 -> x0, starting transfers between devices: 20.9 us -> none  [on_device(): lax.ppermute(message[m], 'area', routes[m])]
    ppermute x8, waiting for transfers between devices: 11.4 us -> 20.2 us  [swap_pair(): return lax.ppermute(block, 'area', pairs + [(b, a) for a, b in pairs])]
    all_to_all x0 -> x1, starting transfers between devices: none -> 6.17 us  [on_device(): lax.all_to_all(message, 'area', split_axis=0, concat_axis=0, tiled=True)]
    ppermute x5 -> x6, waiting for transfers between devices: 15.2 us -> 13 us  [from_snap(): lax.ppermute(block, 'snap', [(i, (i + distance) % members) for i in range...]
    ppermute x15 -> x0, waiting for transfers between devices: 1.21 us -> none  [on_device(): lax.ppermute(message[m], 'area', routes[m])]
    ppermute x5 -> x6, starting transfers between devices: 6.77 us -> 5.56 us  [from_snap(): lax.ppermute(block, 'snap', [(i, (i + distance) % members) for i in range...]
    convert_element_type x0 -> x1, other arithmetic: none -> 1.11 us  [on_device(): rounded = starting_voltages.astype(BF16)]
  transfers between devices with their start and end apart: 28 -> 15, of which waited for: 10 -> 8; matrix products, arithmetic and copies ran while one was open for 0% -> 0% of each run, Pallas kernels for 6% -> 7%
where the time goes in v4:
time: 82.1 us; the launch traced here: 80.6 us
  waiting for transfers between devices  33.3 us (41%)
  starting transfers between devices  24.3 us (30%)
  Pallas kernels  17 us (21%)
  local copies, waits for them, and re-layouts  4.73 us (6%)
  other arithmetic  1.11 us (1%)
    ppermute x8, waiting for transfers between devices, swap_pair(): return lax.ppermute(block, 'area', pairs + [(b, a) for a, b in pairs])  20.2 us
    pallas_call x12, Pallas kernels, call(): pl.pallas_call(kernel, out_shape=outs, in_specs=ins, out_specs=jax.tree.m...  17 us
    ppermute x6, waiting for transfers between devices, from_snap(): lax.ppermute(block, 'snap', [(i, (i + distance) % members) for i in range...  13 us
    ppermute x8, starting transfers between devices, swap_pair(): return lax.ppermute(block, 'area', pairs + [(b, a) for a, b in pairs])  12.6 us
    all_to_all x1, starting transfers between devices, on_device(): lax.all_to_all(message, 'area', split_axis=0, concat_axis=0, tiled=True)  6.17 us
    ppermute x6, starting transfers between devices, from_snap(): lax.ppermute(block, 'snap', [(i, (i + distance) % members) for i in range...  5.56 us
    unnamed x22, local copies, waits for them, and re-layouts  4.73 us
  transfers between devices with their start and end apart: 15, of which 8 were waited for; matrix products, arithmetic and copies ran while one was open for 0% of the time, Pallas kernels for 7%

profile of v4, /device:TPU:16, one launch (start us, length us, event | category | flops | bytes accessed | tf_op | source)
XLA Modules:
  0.0 80.6 jit_solution(12973928961496449376)
XLA Ops:
  0.0 1.1 %convert_element_type.3.own_ref = bf16[32,2048]{1,0:T(8,128)(2,1)S(1)} convert(f32[32,2048]{1,0:T(8,128)} %x_ref.3) | non-fusion elementwise | flops 65536 | bytes 393216 | tf_op jit(solution)/shard_map/convert_element_type | solution.py:353
  1.1 1.6 %collective-permute-start = (bf16[32,2048]{1,0:T(8,128)(2,1)S(1)}, bf16[32,2048]{1,0:T(8,128)(2,1)S(1)}, u32[]{:S(2)}, u32[]{:S(2)}) collective-permute-start(bf16[32,2048]{1,0:T(8,128)(2,1)S(1)} %convert_element_type.3.own_ref), channel_id=1, source_target_pairs={{0,1},{1,0},{2,3},{3,2},{4,5},{5,4},{6,7},{7,6},{8,9},{9,8},{10,11... | collective-permute-start | bytes 393224 | tf_op jit(solution)/shard_map/ppermute | solution.py:312
  2.7 0.9 %copy-done.4 = f32[32,2048]{1,0:T(8,128)S(1)} copy-done((f32[32,2048]{1,0:T(8,128)S(1)}, f32[32,2048]{1,0:T(8,128)}, u32[]{:S(2)}) %copy-start.4) | copy-done | bytes 262168
  3.7 0.7 copy-done.5
  4.4 0.7 copy-done.8
  5.1 3.3 %pack_readings.1 = f32[16,72,128]{2,1,0:T(8,128)} custom-call(f32[32,2048]{1,0:T(8,128)S(1)} %copy-done.4, f32[16,128]{1,0:T(8,128)S(1)} %bitcast.25, s32[16,256]{1,0:T(8,128)S(1)} %bitcast.20), custom_call_target="tpu_custom_call" | custom-call | tf_op jit(solution)/shard_map/pack_readings/pallas_call | solution.py:21
  8.3 0.0 collective-permute-done
  8.4 6.2 %all-to-all-start = ((f32[16,72,128]{2,1,0:T(8,128)}), f32[16,72,128]{2,1,0:T(8,128)S(1)}, u32[]{:S(2)}, u32[]{:S(2)}) async-start(f32[16,72,128]{2,1,0:T(8,128)} %pack_readings.1), calls=%async_computation | async-start | bytes 1179648 | tf_op jit(solution)/shard_map/all_to_all | solution.py:373
  14.5 0.9 %copy-done.2 = f32[32,2048]{1,0:T(8,128)S(1)} copy-done((f32[32,2048]{1,0:T(8,128)S(1)}, f32[32,2048]{1,0:T(8,128)}, u32[]{:S(2)}) %copy-start.2) | copy-done | bytes 262168
  15.5 0.7 copy-done.6
  16.2 0.7 first_states.1
  16.8 3.1 %collective-permute-start.1 = (bf16[4,64,128]{2,1,0:T(8,128)(2,1)S(1)}, bf16[4,64,128]{2,1,0:T(8,128)(2,1)S(1)}, u32[]{:S(2)}, u32[]{:S(2)}) collective-permute-start(bf16[4,64,128]{2,1,0:T(8,128)(2,1)S(1)} %get-tuple-element.36), channel_id=1, source_target_pairs={{2,4},{6,8},{10,12},{14,16},{18,20},{22,24},{26,28},{4,2},{8,6},{1... | collective-permute-start | bytes 196616 | tf_op jit(solution)/shard_map/ppermute | solution.py:303
  19.9 0.4 collective-permute-start.2
  20.4 0.5 collective-permute-start.3
  20.9 0.7 copy-done.10
  21.6 0.4 invert_order.1
  22.0 8.5 %collective-permute-done.1.first_ref = bf16[4,64,128]{2,1,0:T(8,128)(2,1)S(1)} collective-permute-done((bf16[4,64,128]{2,1,0:T(8,128)(2,1)S(1)}, bf16[4,64,128]{2,1,0:T(8,128)(2,1)S(1)}, u32[]{:S(2)}, u32[]{:S(2)}) %collective-permute-start.1) | collective-permute-done | bytes 65568 | tf_op jit(solution)/shard_map/ppermute | solution.py:303
  30.5 0.0 collective-permute-done.2.second_ref
  30.5 1.4 %predict.1.guess_ref = f32[64,2048]{1,0:T(8,128)S(1)} custom-call(bf16[16,64,128]{2,1,0:T(8,128)(2,1)S(1)} %get-tuple-element.35.aug_ref, bf16[4,64,128]{2,1,0:T(8,128)(2,1)S(1)} %collective-permute-done.1.first_ref, bf16[4,64,128]{2,1,0:T(8,128)(2,1)S(1)} %collective-permute-done.2.second_ref, bf16[16,4,128,128]{3,2,1,0:T(8,128)(2,1)S(1)} %copy-done.1, ...), custom_call_target="tpu_custom_call" | custom-call | flops 1000000000 | tf_op jit(solution)/shard_map/predict/pallas_call | solution.py:21
  31.9 0.0 collective-permute-done.3.x_others_refs_0_
  32.0 1.2 %unpack_readings.3 = (f32[32,1024]{1,0:T(8,128)S(1)}, f32[1,1024]{1,0:T(1,128)S(1)}) custom-call(s32[16,128]{1,0:T(8,128)S(1)} %get-tuple-element.40.group_ref, s32[16,128]{1,0:T(8,128)S(1)} %get-tuple-element.41.lane_ref, f32[16,72,128]{2,1,0:T(8,128)S(1)} %all-to-all-done.message_ref), custom_call_target="tpu_custom_call" | custom-call | flops 2000000000 | tf_op jit(solution)/shard_map/unpack_readings/pallas_call | solution.py:21
  33.2 0.0 copy-start
  33.2 0.0 copy-start.3
  33.2 0.0 copy-start.7
  33.2 1.2 %unpack_readings.2 = (f32[32,1024]{1,0:T(8,128)S(1)}, f32[1,1024]{1,0:T(1,128)S(1)}) custom-call(s32[16,128]{1,0:T(8,128)S(1)} %get-tuple-element.40.group_ref, s32[16,128]{1,0:T(8,128)S(1)} %get-tuple-element.41.lane_ref, f32[16,72,128]{2,1,0:T(8,128)S(1)} %all-to-all-done.message_ref), custom_call_target="tpu_custom_call" | custom-call | flops 2000000000 | tf_op jit(solution)/shard_map/unpack_readings/pallas_call | solution.py:21
  34.4 0.6 collective-permute-start.5
  35.0 1.5 %collective-permute-start.4 = (f32[32,1024]{1,0:T(8,128)S(1)}, f32[32,1024]{1,0:T(8,128)S(1)}, u32[]{:S(2)}, u32[]{:S(2)}) collective-permute-start(f32[32,1024]{1,0:T(8,128)S(1)} %get-tuple-element.43.z_refs_0_), channel_id=1, source_target_pairs={{0,1},{1,0},{2,3},{3,2},{4,5},{5,4},{6,7},{7,6},{8,9},{9,8},{10,11... | collective-permute-start | bytes 393224 | tf_op jit(solution)/shard_map/ppermute | solution.py:312
  36.5 2.9 %collective-permute-done.5 = f32[32,1024]{1,0:T(8,128)S(1)} collective-permute-done((f32[32,1024]{1,0:T(8,128)S(1)}, f32[32,1024]{1,0:T(8,128)S(1)}, u32[]{:S(2)}, u32[]{:S(2)}) %collective-permute-start.5) | collective-permute-done | bytes 131104 | tf_op jit(solution)/shard_map/ppermute | solution.py:312
  39.4 1.4 %collective-permute-done.4 = f32[32,1024]{1,0:T(8,128)S(1)} collective-permute-done((f32[32,1024]{1,0:T(8,128)S(1)}, f32[32,1024]{1,0:T(8,128)S(1)}, u32[]{:S(2)}, u32[]{:S(2)}) %collective-permute-start.4) | collective-permute-done | bytes 131104 | tf_op jit(solution)/shard_map/ppermute | solution.py:312
  40.8 1.5 %pull.1 = (f32[16,64,128]{2,1,0:T(8,128)S(1)}, f32[4,64,128]{2,1,0:T(8,128)S(1)}, f32[4,64,128]{2,1,0:T(8,128)S(1)}) custom-call(f32[64,2048]{1,0:T(8,128)S(1)} %predict.1.guess_ref, f32[32,1024]{1,0:T(8,128)S(1)} %get-tuple-element.43.z_refs_0_, f32[32,1024]{1,0:T(8,128)S(1)} %get-tuple-element.44.z_refs_1_, f32[1,32,1024]{2,1,0:T(8,128)S(1)} %bitcast.15, ...), custom_call_target="tpu_custom_call" | custom-call | tf_op jit(solution)/shard_map/pull/pallas_call | solution.py:21
  42.3 3.0 %collective-permute-start.6 = (f32[4,64,128]{2,1,0:T(8,128)S(1)}, f32[4,64,128]{2,1,0:T(8,128)S(1)}, u32[]{:S(2)}, u32[]{:S(2)}) collective-permute-start(f32[4,64,128]{2,1,0:T(8,128)S(1)} %get-tuple-element.48), channel_id=1, source_target_pairs={{2,4},{6,8},{10,12},{14,16},{18,20},{22,24},{26,28},{4,2},{8,6},{1... | collective-permute-start | bytes 393224 | tf_op jit(solution)/shard_map/ppermute | solution.py:303
  45.3 0.1 collective-permute-start.7
  45.4 4.1 %collective-permute-done.6.back_first_ref = f32[4,64,128]{2,1,0:T(8,128)S(1)} collective-permute-done((f32[4,64,128]{2,1,0:T(8,128)S(1)}, f32[4,64,128]{2,1,0:T(8,128)S(1)}, u32[]{:S(2)}, u32[]{:S(2)}) %collective-permute-start.6) | collective-permute-done | bytes 131104 | tf_op jit(solution)/shard_map/ppermute | solution.py:303
  49.5 2.0 %first_update.1 = (f32[8,64,128]{2,1,0:T(8,128)S(1)}, bf16[8,64,128]{2,1,0:T(8,128)(2,1)S(1)}) custom-call(f32[16,64,128]{2,1,0:T(8,128)S(1)} %get-tuple-element.47.grad_ref, f32[4,64,128]{2,1,0:T(8,128)S(1)} %collective-permute-done.6.back_first_ref, f32[4,64,128]{2,1,0:T(8,128)S(1)} %collective-permute-done.7.back_second_ref, s32[2,4]{1,0:T(2,128)S(1)} %bitcast.22, ...), custom_call_target="tpu_custom_call" | custom-call | tf_op jit(solution)/shard_map/first_update/pallas_call | solution.py:21
  51.6 0.7 collective-permute-start.8
  52.2 4.3 %collective-permute-done.8 = bf16[8,64,128]{2,1,0:T(8,128)(2,1)S(1)} collective-permute-done((bf16[8,64,128]{2,1,0:T(8,128)(2,1)S(1)}, bf16[8,64,128]{2,1,0:T(8,128)(2,1)S(1)}, u32[]{:S(2)}, u32[]{:S(2)}) %collective-permute-start.8) | collective-permute-done | bytes 131104 | tf_op jit(solution)/shard_map/ppermute | solution.py:312
  56.6 0.6 join_states.1
  57.2 2.9 %collective-permute-start.9 = (bf16[4,64,128]{2,1,0:T(8,128)(2,1)S(1)}, bf16[4,64,128]{2,1,0:T(8,128)(2,1)S(1)}, u32[]{:S(2)}, u32[]{:S(2)}) collective-permute-start(bf16[4,64,128]{2,1,0:T(8,128)(2,1)S(1)} %get-tuple-element.53), channel_id=1, source_target_pairs={{2,4},{6,8},{10,12},{14,16},{18,20},{22,24},{26,28},{4,2},{8,6},{1... | collective-permute-start | bytes 196616 | tf_op jit(solution)/shard_map/ppermute | solution.py:303
  60.1 0.1 collective-permute-start.10
  60.2 3.5 %collective-permute-done.9.first_in_ref = bf16[4,64,128]{2,1,0:T(8,128)(2,1)S(1)} collective-permute-done((bf16[4,64,128]{2,1,0:T(8,128)(2,1)S(1)}, bf16[4,64,128]{2,1,0:T(8,128)(2,1)S(1)}, u32[]{:S(2)}, u32[]{:S(2)}) %collective-permute-start.9) | collective-permute-done | bytes 65568 | tf_op jit(solution)/shard_map/ppermute | solution.py:303
  63.7 2.0 %predict_pull.1 = (f32[16,64,128]{2,1,0:T(8,128)S(1)}, f32[4,64,128]{2,1,0:T(8,128)S(1)}, f32[4,64,128]{2,1,0:T(8,128)S(1)}) custom-call(bf16[16,64,128]{2,1,0:T(8,128)(2,1)S(1)} %get-tuple-element.52.aug_ref, bf16[4,64,128]{2,1,0:T(8,128)(2,1)S(1)} %collective-permute-done.9.first_in_ref, bf16[4,64,128]{2,1,0:T(8,128)(2,1)S(1)} %collective-permute-done.10.second_in_ref, ...), custom_call_target="tpu_custom_call" | custom-call | tf_op jit(solution)/shard_map/predict_pull/pallas_call | solution.py:21
  65.7 2.9 %collective-permute-start.11 = (f32[4,64,128]{2,1,0:T(8,128)S(1)}, f32[4,64,128]{2,1,0:T(8,128)S(1)}, u32[]{:S(2)}, u32[]{:S(2)}) collective-permute-start(f32[4,64,128]{2,1,0:T(8,128)S(1)} %get-tuple-element.56), channel_id=1, source_target_pairs={{2,4},{6,8},{10,12},{14,16},{18,20},{22,24},{26,28},{4,2},{8,6},{1... | collective-permute-start | bytes 393224 | tf_op jit(solution)/shard_map/ppermute | solution.py:303
  68.6 0.1 collective-permute-start.12
  68.6 4.2 %collective-permute-done.11.back_first_ref = f32[4,64,128]{2,1,0:T(8,128)S(1)} collective-permute-done((f32[4,64,128]{2,1,0:T(8,128)S(1)}, f32[4,64,128]{2,1,0:T(8,128)S(1)}, u32[]{:S(2)}, u32[]{:S(2)}) %collective-permute-start.11) | collective-permute-done | bytes 131104 | tf_op jit(solution)/shard_map/ppermute | solution.py:303
  72.8 2.0 %last_update.1 = (f32[32,1024]{1,0:T(8,128)S(1)}, f32[1,32,1024]{2,1,0:T(8,128)S(1)}) custom-call(f32[16,64,128]{2,1,0:T(8,128)S(1)} %get-tuple-element.55.grad_ref, f32[4,64,128]{2,1,0:T(8,128)S(1)} %collective-permute-done.11.back_first_ref, f32[4,64,128]{2,1,0:T(8,128)S(1)} %collective-permute-done.12.back_second_ref, s32[2,4]{1,0:T(2,128)S(1)} %bitcast.24, ...), custom_call_target="tpu_custom_call" | custom-call | tf_op jit(solution)/shard_map/last_update/pallas_call | solution.py:21
  74.9 0.7 collective-permute-start.13
  75.6 4.3 %collective-permute-done.13 = f32[32,1024]{1,0:T(8,128)S(1)} collective-permute-done((f32[32,1024]{1,0:T(8,128)S(1)}, f32[32,1024]{1,0:T(8,128)S(1)}, u32[]{:S(2)}, u32[]{:S(2)}) %collective-permute-start.13) | collective-permute-done | bytes 131104 | tf_op jit(solution)/shard_map/ppermute | solution.py:312
  79.9 0.7 finish.1
  (17 shorter events, 0.0 us)
Async XLA Ops:
  0.0 30.5 %copy-start.1 = (bf16[16,4,128,128]{3,2,1,0:T(8,128)(2,1)S(1)}, bf16[16,4,128,128]{3,2,1,0:T(8,128)(2,1)}, u32[]{:S(2)}) copy-start(bf16[16,4,128,128]{3,2,1,0:T(8,128)(2,1)} %tiles_ref.5) | copy-start | bytes 6291460
  1.1 7.2 %collective-permute-start = (bf16[32,2048]{1,0:T(8,128)(2,1)S(1)}, bf16[32,2048]{1,0:T(8,128)(2,1)S(1)}, u32[]{:S(2)}, u32[]{:S(2)}) collective-permute-start(bf16[32,2048]{1,0:T(8,128)(2,1)S(1)} %convert_element_type.3.own_ref), channel_id=1, source_target_pairs={{0,1},{1,0},{2,3},{3,2},{4,5},{5,4},{6,7},{7,6},{8,9},{9,8},{10,11... | collective-permute-start | bytes 393224 | tf_op jit(solution)/shard_map/ppermute | solution.py:312
  2.7 0.9 %copy-start.4 = (f32[32,2048]{1,0:T(8,128)S(1)}, f32[32,2048]{1,0:T(8,128)}, u32[]{:S(2)}) copy-start(f32[32,2048]{1,0:T(8,128)} %z_in.1) | copy-start | bytes 786436
  3.7 0.7 copy-start.5
  4.4 0.7 copy-start.8
  5.1 25.5 %copy-start.9 = (s32[1,16,4]{1,2,0:T(4,128)S(1)}, s32[1,16,4]{1,2,0:T(4,128)}, u32[]{:S(2)}) copy-start(s32[1,16,4]{1,2,0:T(4,128)} %param.13) | copy-start | bytes 772
  8.4 23.6 %all-to-all-start = ((f32[16,72,128]{2,1,0:T(8,128)}), f32[16,72,128]{2,1,0:T(8,128)S(1)}, u32[]{:S(2)}, u32[]{:S(2)}) async-start(f32[16,72,128]{2,1,0:T(8,128)} %pack_readings.1), calls=%async_computation | async-start | bytes 1179648 | tf_op jit(solution)/shard_map/all_to_all | solution.py:373
  14.5 0.9 %copy-start.2 = (f32[32,2048]{1,0:T(8,128)S(1)}, f32[32,2048]{1,0:T(8,128)}, u32[]{:S(2)}) copy-start(f32[32,2048]{1,0:T(8,128)} %x_ref.3) | copy-start | bytes 786436
  15.5 0.7 copy-start.6
  16.8 13.7 %collective-permute-start.1 = (bf16[4,64,128]{2,1,0:T(8,128)(2,1)S(1)}, bf16[4,64,128]{2,1,0:T(8,128)(2,1)S(1)}, u32[]{:S(2)}, u32[]{:S(2)}) collective-permute-start(bf16[4,64,128]{2,1,0:T(8,128)(2,1)S(1)} %get-tuple-element.36), channel_id=1, source_target_pairs={{2,4},{6,8},{10,12},{14,16},{18,20},{22,24},{26,28},{4,2},{8,6},{1... | collective-permute-start | bytes 196616 | tf_op jit(solution)/shard_map/ppermute | solution.py:303
  19.9 10.6 %collective-permute-start.2 = (bf16[4,64,128]{2,1,0:T(8,128)(2,1)S(1)}, bf16[4,64,128]{2,1,0:T(8,128)(2,1)S(1)}, u32[]{:S(2)}, u32[]{:S(2)}) collective-permute-start(bf16[4,64,128]{2,1,0:T(8,128)(2,1)S(1)} %get-tuple-element.37), channel_id=1, source_target_pairs={{0,2},{4,6},{8,10},{12,14},{16,18},{20,22},{24,26},{28,30},{2,0},{... | collective-permute-start | bytes 196616 | tf_op jit(solution)/shard_map/ppermute | solution.py:303
  20.4 11.6 %collective-permute-start.3 = (f32[32,1024]{1,0:T(8,128)S(1)}, f32[32,1024]{1,0:T(8,128)S(1)}, u32[]{:S(2)}, u32[]{:S(2)}) collective-permute-start(f32[32,1024]{1,0:T(8,128)S(1)} %get-tuple-element.38), channel_id=1, source_target_pairs={{0,1},{1,0},{2,3},{3,2},{4,5},{5,4},{6,7},{7,6},{8,9},{9,8},{10,11... | collective-permute-start | bytes 393224 | tf_op jit(solution)/shard_map/ppermute | solution.py:312
  20.9 0.7 copy-start.10
  33.2 16.3 %copy-start = (bf16[1024,2048]{1,0:T(8,128)(2,1)S(1)}, bf16[1024,2048]{1,0:T(8,128)(2,1)}, u32[]{:S(2)}) copy-start(bf16[1024,2048]{1,0:T(8,128)(2,1)} %gain_ref.3) | copy-start | bytes 12582916
  33.2 16.3 %copy-start.3 = (f32[32,2048]{1,0:T(8,128)S(1)}, f32[32,2048]{1,0:T(8,128)}, u32[]{:S(2)}) copy-start(f32[32,2048]{1,0:T(8,128)} %x_ref.3) | copy-start | bytes 786436
  33.2 16.3 %copy-start.7 = (s32[1,2,4]{2,1,0:T(2,128)S(1)}, s32[1,2,4]{2,1,0:T(2,128)}, u32[]{:S(2)}) copy-start(s32[1,2,4]{2,1,0:T(2,128)} %param.14) | copy-start | bytes 100
  34.4 5.0 %collective-permute-start.5 = (f32[32,1024]{1,0:T(8,128)S(1)}, f32[32,1024]{1,0:T(8,128)S(1)}, u32[]{:S(2)}, u32[]{:S(2)}) collective-permute-start(f32[32,1024]{1,0:T(8,128)S(1)} %get-tuple-element.44.z_refs_1_), channel_id=1, source_target_pairs={{0,1},{1,0},{2,3},{3,2},{4,5},{5,4},{6,7},{7,6},{8,9},{9,8},{10,11... | collective-permute-start | bytes 393224 | tf_op jit(solution)/shard_map/ppermute | solution.py:312
  35.0 5.9 %collective-permute-start.4 = (f32[32,1024]{1,0:T(8,128)S(1)}, f32[32,1024]{1,0:T(8,128)S(1)}, u32[]{:S(2)}, u32[]{:S(2)}) collective-permute-start(f32[32,1024]{1,0:T(8,128)S(1)} %get-tuple-element.43.z_refs_0_), channel_id=1, source_target_pairs={{0,1},{1,0},{2,3},{3,2},{4,5},{5,4},{6,7},{7,6},{8,9},{9,8},{10,11... | collective-permute-start | bytes 393224 | tf_op jit(solution)/shard_map/ppermute | solution.py:312
  42.3 7.2 %collective-permute-start.6 = (f32[4,64,128]{2,1,0:T(8,128)S(1)}, f32[4,64,128]{2,1,0:T(8,128)S(1)}, u32[]{:S(2)}, u32[]{:S(2)}) collective-permute-start(f32[4,64,128]{2,1,0:T(8,128)S(1)} %get-tuple-element.48), channel_id=1, source_target_pairs={{2,4},{6,8},{10,12},{14,16},{18,20},{22,24},{26,28},{4,2},{8,6},{1... | collective-permute-start | bytes 393224 | tf_op jit(solution)/shard_map/ppermute | solution.py:303
  45.3 4.1 %collective-permute-start.7 = (f32[4,64,128]{2,1,0:T(8,128)S(1)}, f32[4,64,128]{2,1,0:T(8,128)S(1)}, u32[]{:S(2)}, u32[]{:S(2)}) collective-permute-start(f32[4,64,128]{2,1,0:T(8,128)S(1)} %get-tuple-element.49), channel_id=1, source_target_pairs={{0,2},{4,6},{8,10},{12,14},{16,18},{20,22},{24,26},{28,30},{2,0},{... | collective-permute-start | bytes 393224 | tf_op jit(solution)/shard_map/ppermute | solution.py:303
  51.6 5.0 %collective-permute-start.8 = (bf16[8,64,128]{2,1,0:T(8,128)(2,1)S(1)}, bf16[8,64,128]{2,1,0:T(8,128)(2,1)S(1)}, u32[]{:S(2)}, u32[]{:S(2)}) collective-permute-start(bf16[8,64,128]{2,1,0:T(8,128)(2,1)S(1)} %get-tuple-element.51.mine_ref), channel_id=1, source_target_pairs={{0,1},{1,0},{2,3},{3,2},{4,5},{5,4},{6,7},{7,6},{8,9},{9,8},{10,11... | collective-permute-start | bytes 393224 | tf_op jit(solution)/shard_map/ppermute | solution.py:312
  57.2 6.5 %collective-permute-start.9 = (bf16[4,64,128]{2,1,0:T(8,128)(2,1)S(1)}, bf16[4,64,128]{2,1,0:T(8,128)(2,1)S(1)}, u32[]{:S(2)}, u32[]{:S(2)}) collective-permute-start(bf16[4,64,128]{2,1,0:T(8,128)(2,1)S(1)} %get-tuple-element.53), channel_id=1, source_target_pairs={{2,4},{6,8},{10,12},{14,16},{18,20},{22,24},{26,28},{4,2},{8,6},{1... | collective-permute-start | bytes 196616 | tf_op jit(solution)/shard_map/ppermute | solution.py:303
  60.1 3.6 %collective-permute-start.10 = (bf16[4,64,128]{2,1,0:T(8,128)(2,1)S(1)}, bf16[4,64,128]{2,1,0:T(8,128)(2,1)S(1)}, u32[]{:S(2)}, u32[]{:S(2)}) collective-permute-start(bf16[4,64,128]{2,1,0:T(8,128)(2,1)S(1)} %get-tuple-element.54), channel_id=1, source_target_pairs={{0,2},{4,6},{8,10},{12,14},{16,18},{20,22},{24,26},{28,30},{2,0},{... | collective-permute-start | bytes 196616 | tf_op jit(solution)/shard_map/ppermute | solution.py:303
  65.7 7.2 %collective-permute-start.11 = (f32[4,64,128]{2,1,0:T(8,128)S(1)}, f32[4,64,128]{2,1,0:T(8,128)S(1)}, u32[]{:S(2)}, u32[]{:S(2)}) collective-permute-start(f32[4,64,128]{2,1,0:T(8,128)S(1)} %get-tuple-element.56), channel_id=1, source_target_pairs={{2,4},{6,8},{10,12},{14,16},{18,20},{22,24},{26,28},{4,2},{8,6},{1... | collective-permute-start | bytes 393224 | tf_op jit(solution)/shard_map/ppermute | solution.py:303
  68.6 4.3 %collective-permute-start.12 = (f32[4,64,128]{2,1,0:T(8,128)S(1)}, f32[4,64,128]{2,1,0:T(8,128)S(1)}, u32[]{:S(2)}, u32[]{:S(2)}) collective-permute-start(f32[4,64,128]{2,1,0:T(8,128)S(1)} %get-tuple-element.57), channel_id=1, source_target_pairs={{0,2},{4,6},{8,10},{12,14},{16,18},{20,22},{24,26},{28,30},{2,0},{... | collective-permute-start | bytes 393224 | tf_op jit(solution)/shard_map/ppermute | solution.py:303
  74.9 5.0 %collective-permute-start.13 = (f32[32,1024]{1,0:T(8,128)S(1)}, f32[32,1024]{1,0:T(8,128)S(1)}, u32[]{:S(2)}, u32[]{:S(2)}) collective-permute-start(f32[32,1024]{1,0:T(8,128)S(1)} %bitcast.29), channel_id=1, source_target_pairs={{0,1},{1,0},{2,3},{3,2},{4,5},{5,4},{6,7},{7,6},{8,9},{9,8},{10,11... | collective-permute-start | bytes 393224 | tf_op jit(solution)/shard_map/ppermute | solution.py:312

commit v5 on v4

--- a/solution.py
+++ b/solution.py
@@ -17,16 +17,16 @@
 SMEM = pl.BlockSpec(memory_space=pltpu.SMEM)
 
 
-def call(kernel, outs, ins, args, scratch=(), flops=0, bytes_accessed=0, name=None):
+def call(kernel, outs, ins, args, scratch=(), flops=0, mib=12, name=None):
     return pl.pallas_call(
         kernel,
         out_shape=outs,
         in_specs=ins,
         out_specs=jax.tree.map(lambda _: VMEM, outs),
         scratch_shapes=list(scratch),
-        compiler_params=pltpu.CompilerParams(vmem_limit_bytes=12 * 1024 * 1024),
+        compiler_params=pltpu.CompilerParams(vmem_limit_bytes=mib * 1024 * 1024),
         cost_estimate=pl.CostEstimate(
-            flops=flops, bytes_accessed=bytes_accessed, transcendentals=0
+            flops=flops, bytes_accessed=0, transcendentals=0
         ),
         name=name,
     )(*args)
@@ -127,11 +127,14 @@
     return 1 - lax.rem(lax.axis_index("area"), 2)
 
 
-def pick(source, listing_ref, side, out_ref):
+def pick(blocks_ref, listing_ref, side, out_ref, start=0):
+    held = blocks_ref.shape[0]
     for t in range(out_ref.shape[0]):
         b = listing_ref[side, t]
-        block = source(jnp.maximum(b, 0))
-        out_ref[t] = jnp.where(b >= 0, block, jnp.zeros_like(block))
+        at = b - start
+        block = blocks_ref[jnp.clip(at, 0, held - 1)]
+        here = (b >= 0) & (at >= 0) & (at < held)
+        out_ref[t] = jnp.where(here, block, jnp.zeros_like(block))
 
 
 def first_states_kernel(
@@ -143,30 +146,13 @@
         aug_ref[b, :snaps] = own_ref[:, columns]
         for i in range(others_ref.shape[0]):
             aug_ref[b, (i + 1) * snaps : (i + 2) * snaps] = others_ref[i, :, columns]
-    pick(lambda b: aug_ref[b], ties_ref, 1 - parity(), first_ref)
-    pick(lambda b: aug_ref[b], ties_ref, parity(), second_ref)
+    pick(aug_ref, ties_ref, 1 - parity(), first_ref)
+    pick(aug_ref, ties_ref, parity(), second_ref)
     members = len(sent_refs) + 1
     width = x_ref.shape[1] // members
     for i, sent_ref in enumerate(sent_refs, 1):
         at = lax.rem(lax.axis_index("snap") + i, members) * width
         sent_ref[...] = x_ref[:, pl.ds(pl.multiple_of(at, BLK), width)]
-
-
-def join_states_kernel(mine_ref, others_ref, ties_ref, aug_ref, first_ref, second_ref):
-    held, everything = mine_ref.shape[:2]
-    members = others_ref.shape[0] + 1
-    snaps = everything // members
-    me = lax.axis_index("snap")
-    aug_ref[pl.ds(me * held, held)] = mine_ref[...]
-    for i in range(1, members):
-        at = lax.rem(me + members - i, members) * held
-        for j in range(members):
-            to = (j - i) % members
-            aug_ref[pl.ds(at, held), to * snaps : (to + 1) * snaps] = others_ref[
-                i - 1, :, j * snaps : (j + 1) * snaps
-            ]
-    pick(lambda b: aug_ref[b], ties_ref, 1 - parity(), first_ref)
-    pick(lambda b: aug_ref[b], ties_ref, parity(), second_ref)
 
 
 def slots_into(slots_ref, aug_ref, first_ref, second_ref):
@@ -177,6 +163,27 @@
     slots_ref[pl.ds(own + ties * parity(), ties)] = second_ref[...]
 
 
+def reordered(ref, distance, members):
+    snaps = ref.shape[1] // members
+    order = [(n + distance) % members for n in range(members)]
+    return jnp.concatenate([ref[:, j * snaps : (j + 1) * snaps] for j in order], axis=1)
+
+
+def join_states(slots_ref, mine_ref, others_refs, first_refs, second_refs):
+    members = len(first_refs)
+    held = mine_ref.shape[0]
+    own = held * members
+    ties = first_refs[0].shape[0]
+    me = lax.axis_index("snap")
+    slots_ref[pl.ds(me * held, held)] = mine_ref[...]
+    for i, ref in enumerate(others_refs, 1):
+        at = lax.rem(me + members - i, members) * held
+        slots_ref[pl.ds(at, held)] = reordered(ref, i, members)
+    for side, refs in ((1 - parity(), first_refs), (parity(), second_refs)):
+        parts = [reordered(ref, i, members) for i, ref in enumerate(refs)]
+        slots_ref[pl.ds(own + ties * side, ties)] = sum(parts[1:], parts[0])
+
+
 def predicted(j, slots_ref, tiles_ref, place_ref):
     touched = tiles_ref.shape[1]
     chosen = jnp.concatenate([slots_ref[place_ref[k, j]] for k in range(touched)], axis=1)
@@ -186,6 +193,10 @@
 
 def predict_kernel(aug_ref, first_ref, second_ref, tiles_ref, place_ref, out_ref, slots_ref):
     slots_into(slots_ref, aug_ref, first_ref, second_ref)
+    predict(tiles_ref, place_ref, out_ref, slots_ref)
+
+
+def predict(tiles_ref, place_ref, out_ref, slots_ref):
     for j in range(tiles_ref.shape[0]):
         out_ref[:, j * BLK : (j + 1) * BLK] = predicted(j, slots_ref, tiles_ref, place_ref)
 
@@ -228,10 +239,11 @@
 
 
 def predict_pull_kernel(
-    aug_ref, first_in_ref, second_in_ref, z_refs, others_refs, v_refs, tiles_ref, place_ref,
+    first_refs, others_in_refs, second_refs, mine_ref, z_refs, others_refs, v_refs, tiles_ref, place_ref,
     own_ref, first_ref, second_ref, slots_ref, guess_ref, total_ref, weighted_ref,
 ):
-    predict_kernel(aug_ref, first_in_ref, second_in_ref, tiles_ref, place_ref, guess_ref, slots_ref)
+    join_states(slots_ref, mine_ref, others_in_refs, first_refs, second_refs)
+    predict(tiles_ref, place_ref, guess_ref, slots_ref)
     pull_kernel(
         guess_ref, z_refs, others_refs, v_refs, tiles_ref, place_ref, own_ref, first_ref, second_ref,
         total_ref, weighted_ref,
@@ -262,7 +274,7 @@
 
 def first_update_kernel(
     grad_ref, back_first_ref, back_second_ref, ties_ref, gain_ref, x_ref, x_others_refs,
-    state_ref, message_ref, work_ref,
+    state_ref, message_ref, first_ref, second_ref, work_ref,
 ):
     gradient = full_gradient(grad_ref, back_first_ref, back_second_ref, ties_ref, work_ref)
     held = state_ref.shape[0]
@@ -273,6 +285,8 @@
         state = jnp.concatenate(parts, axis=0) + update
         state_ref[i] = state
         message_ref[i] = state.astype(BF16)
+    pick(message_ref, ties_ref, 1 - parity(), first_ref, me * held)
+    pick(message_ref, ties_ref, parity(), second_ref, me * held)
 
 
 def last_update_kernel(
@@ -298,9 +312,15 @@
         out_ref[:, pl.ds(pl.multiple_of(at, BLK), width)] = others_ref[i - 1]
 
 
-def swap_pair(block, start):
+def swap_pair(block, start, distance=0):
+    members = lax.axis_size("snap")
     pairs = [(i, i + 1) for i in range(start, lax.axis_size("area") - 1, 2)]
-    return lax.ppermute(block, "area", pairs + [(b, a) for a, b in pairs])
+    route = [
+        (a * members + s, b * members + (s + distance) % members)
+        for a, b in pairs + [(b, a) for a, b in pairs]
+        for s in range(members)
+    ]
+    return lax.ppermute(block, ("area", "snap"), route)
 
 
 def with_neighbours(first, second):
@@ -363,6 +383,7 @@
             pltpu.VMEM((chunks, width), jnp.int32),
             pltpu.SemaphoreType.DMA((3,)),
         ],
+        mib=60,
         name="pack_readings",
     )
     message, rounded_others = lax.optimization_barrier((message, rounded_others))
@@ -438,36 +459,33 @@
         scratch=[total, pltpu.VMEM((everything, lines), BF16)],
         name="pull",
     )
-    first, second = with_neighbours(first, second)
-    state, mine = call(
+    arrived = with_neighbours(first, second)
+    boundary = shape((ties, everything, BLK), BF16)
+    state, mine, first, second = call(
         first_update_kernel,
-        (shape((held, everything, BLK), F32), shape((held, everything, BLK), BF16)),
+        (
+            shape((held, everything, BLK), F32),
+            shape((held, everything, BLK), BF16),
+            boundary,
+            boundary,
+        ),
         [VMEM, VMEM, VMEM, SMEM, VMEM, VMEM, [VMEM] * (members - 1)],
         (
-            grad, first, second, ties_table, reciprocal_normal_operator,
+            grad, *arrived, ties_table, reciprocal_normal_operator,
             starting_voltages, x_others,
         ),
         scratch=[work],
         name="first_update",
     )
-    others = from_all(mine)
-    aug, first, second = call(
-        join_states_kernel,
-        (
-            shape((own, everything, BLK), BF16),
-            shape((ties, everything, BLK), BF16),
-            shape((ties, everything, BLK), BF16),
-        ),
-        [VMEM, VMEM, SMEM],
-        (mine, others, ties_table),
-        name="join_states",
-    )
-    first, second = with_neighbours(first, second)
+    firsts = [swap_pair(first, 1, i) for i in range(members)]
+    others = [from_snap(mine, i) for i in range(1, members)]
+    seconds = [swap_pair(second, 0, i) for i in range(members)]
     grad, first, second = call(
         predict_pull_kernel,
         grads,
-        [VMEM, VMEM, VMEM, [VMEM] * 2, [VMEM] * 2, [VMEM] * 2, VMEM, SMEM],
-        (aug, first, second, readings, reading_others, variance, derivative_pieces, place),
+        [[VMEM] * members, [VMEM] * (members - 1), [VMEM] * members, VMEM]
+        + [[VMEM] * 2, [VMEM] * 2, [VMEM] * 2, VMEM, SMEM],
+        (firsts, others, seconds, mine, readings, reading_others, variance, derivative_pieces, place),
         scratch=[
             pltpu.VMEM((slots, everything, BLK), BF16),
             pltpu.VMEM((everything, lines), F32),

time: 82.1 us -> 80.7 us (0.983)
  starting transfers between devices: 24.3 us -> 30.3 us
  waiting for transfers between devices: 33.3 us -> 28.5 us
  local copies, waits for them, and re-layouts: 4.73 us -> 2.37 us
    ppermute x8 -> x10, starting transfers between devices: 12.6 us -> 17.3 us  [swap_pair(): return lax.ppermute(block, ('area', 'snap'), route)]
    ppermute x6, waiting for transfers between devices: 13 us -> 8.89 us  [from_snap(): lax.ppermute(block, 'snap', [(i, (i + distance) % members) for i in range...]
    unnamed x22 -> x16, local copies, waits for them, and re-layouts: 4.73 us -> 2.37 us
    ppermute x6, starting transfers between devices: 5.56 us -> 6.83 us  [from_snap(): lax.ppermute(block, 'snap', [(i, (i + distance) % members) for i in range...]
    ppermute x8 -> x10, waiting for transfers between devices: 20.2 us -> 19.6 us  [swap_pair(): return lax.ppermute(block, ('area', 'snap'), route)]
    pallas_call x12 -> x11, Pallas kernels: 17 us -> 17.5 us  [call(): pl.pallas_call(kernel, out_shape=outs, in_specs=ins, out_specs=jax.tree.m...]
  transfers between devices with their start and end apart: 15 -> 17, of which waited for: 8 -> 8; matrix products, arithmetic and copies ran while one was open for 0% -> 0% of each run, Pallas kernels for 7% -> 8%
where the time goes in v5:
time: 80.7 us; the launch traced here: 80 us
  starting transfers between devices  30.3 us (38%)
  waiting for transfers between devices  28.5 us (35%)
  Pallas kernels  17.5 us (22%)
  local copies, waits for them, and re-layouts  2.37 us (3%)
  other arithmetic  1.11 us (1%)
    ppermute x10, waiting for transfers between devices, swap_pair(): return lax.ppermute(block, ('area', 'snap'), route)  19.6 us
    pallas_call x11, Pallas kernels, call(): pl.pallas_call(kernel, out_shape=outs, in_specs=ins, out_specs=jax.tree.m...  17.5 us
    ppermute x10, starting transfers between devices, swap_pair(): return lax.ppermute(block, ('area', 'snap'), route)  17.3 us
    ppermute x6, waiting for transfers between devices, from_snap(): lax.ppermute(block, 'snap', [(i, (i + distance) % members) for i in range...  8.89 us
    ppermute x6, starting transfers between devices, from_snap(): lax.ppermute(block, 'snap', [(i, (i + distance) % members) for i in range...  6.83 us
    all_to_all x1, starting transfers between devices, on_device(): lax.all_to_all(message, 'area', split_axis=0, concat_axis=0, tiled=True)  6.17 us
    unnamed x16, local copies, waits for them, and re-layouts  2.37 us
  transfers between devices with their start and end apart: 17, of which 8 were waited for; matrix products, arithmetic and copies ran while one was open for 0% of the time, Pallas kernels for 8%

profile of v5, /device:TPU:16, one launch (start us, length us, event | category | flops | bytes accessed | tf_op | source)
XLA Modules:
  0.0 80.0 jit_solution(11550723317680716051)
XLA Ops:
  0.0 1.1 %convert_element_type.3.own_ref = bf16[32,2048]{1,0:T(8,128)(2,1)S(1)} convert(f32[32,2048]{1,0:T(8,128)} %x_ref.3) | non-fusion elementwise | flops 65536 | bytes 393216 | tf_op jit(solution)/shard_map/convert_element_type | solution.py:373
  1.1 1.6 %collective-permute-start = (bf16[32,2048]{1,0:T(8,128)(2,1)S(1)}, bf16[32,2048]{1,0:T(8,128)(2,1)S(1)}, u32[]{:S(2)}, u32[]{:S(2)}) collective-permute-start(bf16[32,2048]{1,0:T(8,128)(2,1)S(1)} %convert_element_type.3.own_ref), channel_id=1, source_target_pairs={{0,1},{1,0},{2,3},{3,2},{4,5},{5,4},{6,7},{7,6},{8,9},{9,8},{10,11... | collective-permute-start | bytes 393224 | tf_op jit(solution)/shard_map/ppermute | solution.py:332
  2.7 4.2 %pack_readings.1 = f32[16,72,128]{2,1,0:T(8,128)} custom-call(f32[32,2048]{1,0:T(8,128)} %z_in.1, f32[16,128]{1,0:T(8,128)} %bitcast.27, s32[16,256]{1,0:T(8,128)} %bitcast.26), custom_call_target="tpu_custom_call" | custom-call | tf_op jit(solution)/shard_map/pack_readings/pallas_call | solution.py:21
  6.9 0.0 collective-permute-done
  6.9 6.2 %all-to-all-start = ((f32[16,72,128]{2,1,0:T(8,128)}), f32[16,72,128]{2,1,0:T(8,128)S(1)}, u32[]{:S(2)}, u32[]{:S(2)}) async-start(f32[16,72,128]{2,1,0:T(8,128)} %pack_readings.1), calls=%async_computation | async-start | bytes 1179648 | tf_op jit(solution)/shard_map/all_to_all | solution.py:394
  13.1 0.9 %copy-done.2 = f32[32,2048]{1,0:T(8,128)S(1)} copy-done((f32[32,2048]{1,0:T(8,128)S(1)}, f32[32,2048]{1,0:T(8,128)}, u32[]{:S(2)}) %copy-start.2) | copy-done | bytes 262168
  14.0 0.7 copy-done.4
  14.7 0.7 first_states.1
  15.4 3.1 %collective-permute-start.1 = (bf16[4,64,128]{2,1,0:T(8,128)(2,1)S(1)}, bf16[4,64,128]{2,1,0:T(8,128)(2,1)S(1)}, u32[]{:S(2)}, u32[]{:S(2)}) collective-permute-start(bf16[4,64,128]{2,1,0:T(8,128)(2,1)S(1)} %get-tuple-element.35), channel_id=1, source_target_pairs={{2,4},{3,5},{6,8},{7,9},{10,12},{11,13},{14,16},{15,17},{18,20},{1... | collective-permute-start | bytes 196616 | tf_op jit(solution)/shard_map/ppermute | solution.py:323
  18.5 0.4 collective-permute-start.2
  19.0 1.0 %collective-permute-start.3 = (f32[32,1024]{1,0:T(8,128)S(1)}, f32[32,1024]{1,0:T(8,128)S(1)}, u32[]{:S(2)}, u32[]{:S(2)}) collective-permute-start(f32[32,1024]{1,0:T(8,128)S(1)} %get-tuple-element.37), channel_id=1, source_target_pairs={{0,1},{1,0},{2,3},{3,2},{4,5},{5,4},{6,7},{7,6},{8,9},{9,8},{10,11... | collective-permute-start | bytes 393224 | tf_op jit(solution)/shard_map/ppermute | solution.py:332
  20.0 0.7 copy-done.7
  20.7 0.4 invert_order.1
  21.1 8.0 %collective-permute-done.1.first_ref = bf16[4,64,128]{2,1,0:T(8,128)(2,1)S(1)} collective-permute-done((bf16[4,64,128]{2,1,0:T(8,128)(2,1)S(1)}, bf16[4,64,128]{2,1,0:T(8,128)(2,1)S(1)}, u32[]{:S(2)}, u32[]{:S(2)}) %collective-permute-start.1) | collective-permute-done | bytes 65568 | tf_op jit(solution)/shard_map/ppermute | solution.py:323
  29.1 0.0 collective-permute-done.2.second_ref
  29.1 1.4 %predict.1.guess_ref = f32[64,2048]{1,0:T(8,128)S(1)} custom-call(bf16[16,64,128]{2,1,0:T(8,128)(2,1)S(1)} %get-tuple-element.34.aug_ref, bf16[4,64,128]{2,1,0:T(8,128)(2,1)S(1)} %collective-permute-done.1.first_ref, bf16[4,64,128]{2,1,0:T(8,128)(2,1)S(1)} %collective-permute-done.2.second_ref, bf16[16,4,128,128]{3,2,1,0:T(8,128)(2,1)S(1)} %copy-done.1, ...), custom_call_target="tpu_custom_call" | custom-call | flops 1000000000 | tf_op jit(solution)/shard_map/predict/pallas_call | solution.py:21
  30.5 0.0 collective-permute-done.3.x_others_refs_0_
  30.5 0.0 all-to-all-done.message_ref
  30.5 1.2 %unpack_readings.3 = (f32[32,1024]{1,0:T(8,128)S(1)}, f32[1,1024]{1,0:T(1,128)S(1)}) custom-call(s32[16,128]{1,0:T(8,128)S(1)} %get-tuple-element.39.group_ref, s32[16,128]{1,0:T(8,128)S(1)} %get-tuple-element.40.lane_ref, f32[16,72,128]{2,1,0:T(8,128)S(1)} %all-to-all-done.message_ref), custom_call_target="tpu_custom_call" | custom-call | flops 2000000000 | tf_op jit(solution)/shard_map/unpack_readings/pallas_call | solution.py:21
  31.8 0.0 copy-start
  31.8 0.0 copy-start.3
  31.8 0.0 copy-start.5
  31.8 1.2 %unpack_readings.2 = (f32[32,1024]{1,0:T(8,128)S(1)}, f32[1,1024]{1,0:T(1,128)S(1)}) custom-call(s32[16,128]{1,0:T(8,128)S(1)} %get-tuple-element.39.group_ref, s32[16,128]{1,0:T(8,128)S(1)} %get-tuple-element.40.lane_ref, f32[16,72,128]{2,1,0:T(8,128)S(1)} %all-to-all-done.message_ref), custom_call_target="tpu_custom_call" | custom-call | flops 2000000000 | tf_op jit(solution)/shard_map/unpack_readings/pallas_call | solution.py:21
  33.0 1.1 %collective-permute-start.5 = (f32[32,1024]{1,0:T(8,128)S(1)}, f32[32,1024]{1,0:T(8,128)S(1)}, u32[]{:S(2)}, u32[]{:S(2)}) collective-permute-start(f32[32,1024]{1,0:T(8,128)S(1)} %get-tuple-element.43.z_refs_1_), channel_id=1, source_target_pairs={{0,1},{1,0},{2,3},{3,2},{4,5},{5,4},{6,7},{7,6},{8,9},{9,8},{10,11... | collective-permute-start | bytes 393224 | tf_op jit(solution)/shard_map/ppermute | solution.py:332
  34.1 1.0 %collective-permute-start.4 = (f32[32,1024]{1,0:T(8,128)S(1)}, f32[32,1024]{1,0:T(8,128)S(1)}, u32[]{:S(2)}, u32[]{:S(2)}) collective-permute-start(f32[32,1024]{1,0:T(8,128)S(1)} %get-tuple-element.42.z_refs_0_), channel_id=1, source_target_pairs={{0,1},{1,0},{2,3},{3,2},{4,5},{5,4},{6,7},{7,6},{8,9},{9,8},{10,11... | collective-permute-start | bytes 393224 | tf_op jit(solution)/shard_map/ppermute | solution.py:332
  35.1 2.9 %collective-permute-done.5 = f32[32,1024]{1,0:T(8,128)S(1)} collective-permute-done((f32[32,1024]{1,0:T(8,128)S(1)}, f32[32,1024]{1,0:T(8,128)S(1)}, u32[]{:S(2)}, u32[]{:S(2)}) %collective-permute-start.5) | collective-permute-done | bytes 131104 | tf_op jit(solution)/shard_map/ppermute | solution.py:332
  38.1 1.4 %collective-permute-done.4 = f32[32,1024]{1,0:T(8,128)S(1)} collective-permute-done((f32[32,1024]{1,0:T(8,128)S(1)}, f32[32,1024]{1,0:T(8,128)S(1)}, u32[]{:S(2)}, u32[]{:S(2)}) %collective-permute-start.4) | collective-permute-done | bytes 131104 | tf_op jit(solution)/shard_map/ppermute | solution.py:332
  39.5 1.5 %pull.1 = (f32[16,64,128]{2,1,0:T(8,128)S(1)}, f32[4,64,128]{2,1,0:T(8,128)S(1)}, f32[4,64,128]{2,1,0:T(8,128)S(1)}) custom-call(f32[64,2048]{1,0:T(8,128)S(1)} %predict.1.guess_ref, f32[32,1024]{1,0:T(8,128)S(1)} %get-tuple-element.42.z_refs_0_, f32[32,1024]{1,0:T(8,128)S(1)} %get-tuple-element.43.z_refs_1_, f32[1,32,1024]{2,1,0:T(8,128)S(1)} %bitcast.14, ...), custom_call_target="tpu_custom_call" | custom-call | tf_op jit(solution)/shard_map/pull/pallas_call | solution.py:21
  40.9 3.0 %collective-permute-start.6 = (f32[4,64,128]{2,1,0:T(8,128)S(1)}, f32[4,64,128]{2,1,0:T(8,128)S(1)}, u32[]{:S(2)}, u32[]{:S(2)}) collective-permute-start(f32[4,64,128]{2,1,0:T(8,128)S(1)} %get-tuple-element.47), channel_id=1, source_target_pairs={{2,4},{3,5},{6,8},{7,9},{10,12},{11,13},{14,16},{15,17},{18,20},{1... | collective-permute-start | bytes 393224 | tf_op jit(solution)/shard_map/ppermute | solution.py:323
  44.0 0.1 collective-permute-start.7
  44.0 4.1 %collective-permute-done.6.back_first_ref = f32[4,64,128]{2,1,0:T(8,128)S(1)} collective-permute-done((f32[4,64,128]{2,1,0:T(8,128)S(1)}, f32[4,64,128]{2,1,0:T(8,128)S(1)}, u32[]{:S(2)}, u32[]{:S(2)}) %collective-permute-start.6) | collective-permute-done | bytes 131104 | tf_op jit(solution)/shard_map/ppermute | solution.py:323
  48.1 0.0 collective-permute-done.7.back_second_ref
  48.1 2.1 %first_update.1 = (f32[8,64,128]{2,1,0:T(8,128)S(1)}, bf16[8,64,128]{2,1,0:T(8,128)(2,1)S(1)}, bf16[4,64,128]{2,1,0:T(8,128)(2,1)S(1)}, bf16[4,64,128]{2,1,0:T(8,128)(2,1)S(1)}) custom-call(f32[16,64,128]{2,1,0:T(8,128)S(1)} %get-tuple-element.46.grad_ref, f32[4,64,128]{2,1,0:T(8,128)S(1)} %collective-permute-done.6.back_first_ref, ...), custom_call_target="tpu_custom_call" | custom-call | tf_op jit(solution)/shard_map/first_update/pallas_call | solution.py:21
  50.2 1.1 %collective-permute-start.10 = (bf16[8,64,128]{2,1,0:T(8,128)(2,1)S(1)}, bf16[8,64,128]{2,1,0:T(8,128)(2,1)S(1)}, u32[]{:S(2)}, u32[]{:S(2)}) collective-permute-start(bf16[8,64,128]{2,1,0:T(8,128)(2,1)S(1)} %get-tuple-element.51.mine_ref), channel_id=1, source_target_pairs={{0,1},{1,0},{2,3},{3,2},{4,5},{5,4},{6,7},{7,6},{8,9},{9,8},{10,11... | collective-permute-start | bytes 393224 | tf_op jit(solution)/shard_map/ppermute | solution.py:332
  51.3 3.2 %collective-permute-start.9 = (bf16[4,64,128]{2,1,0:T(8,128)(2,1)S(1)}, bf16[4,64,128]{2,1,0:T(8,128)(2,1)S(1)}, u32[]{:S(2)}, u32[]{:S(2)}) collective-permute-start(bf16[4,64,128]{2,1,0:T(8,128)(2,1)S(1)} %get-tuple-element.50), channel_id=1, source_target_pairs={{2,5},{3,4},{6,9},{7,8},{10,13},{11,12},{14,17},{15,16},{18,21},{1... | collective-permute-start | bytes 196616 | tf_op jit(solution)/shard_map/ppermute | solution.py:323
  54.5 3.7 %collective-permute-start.8 = (bf16[4,64,128]{2,1,0:T(8,128)(2,1)S(1)}, bf16[4,64,128]{2,1,0:T(8,128)(2,1)S(1)}, u32[]{:S(2)}, u32[]{:S(2)}) collective-permute-start(bf16[4,64,128]{2,1,0:T(8,128)(2,1)S(1)} %get-tuple-element.50), channel_id=1, source_target_pairs={{2,4},{3,5},{6,8},{7,9},{10,12},{11,13},{14,16},{15,17},{18,20},{1... | collective-permute-start | bytes 196616 | tf_op jit(solution)/shard_map/ppermute | solution.py:323
  58.2 0.1 collective-permute-start.12
  58.3 1.1 %collective-permute-start.11 = (bf16[4,64,128]{2,1,0:T(8,128)(2,1)S(1)}, bf16[4,64,128]{2,1,0:T(8,128)(2,1)S(1)}, u32[]{:S(2)}, u32[]{:S(2)}) collective-permute-start(bf16[4,64,128]{2,1,0:T(8,128)(2,1)S(1)} %get-tuple-element.52), channel_id=1, source_target_pairs={{0,2},{1,3},{4,6},{5,7},{8,10},{9,11},{12,14},{13,15},{16,18},{17,... | collective-permute-start | bytes 196616 | tf_op jit(solution)/shard_map/ppermute | solution.py:323
  59.4 1.6 %collective-permute-done.8.first_refs_0_ = bf16[4,64,128]{2,1,0:T(8,128)(2,1)S(1)} collective-permute-done((bf16[4,64,128]{2,1,0:T(8,128)(2,1)S(1)}, bf16[4,64,128]{2,1,0:T(8,128)(2,1)S(1)}, u32[]{:S(2)}, u32[]{:S(2)}) %collective-permute-start.8) | collective-permute-done | bytes 65568 | tf_op jit(solution)/shard_map/ppermute | solution.py:323
  61.0 1.2 %collective-permute-done.12.second_refs_1_ = bf16[4,64,128]{2,1,0:T(8,128)(2,1)S(1)} collective-permute-done((bf16[4,64,128]{2,1,0:T(8,128)(2,1)S(1)}, bf16[4,64,128]{2,1,0:T(8,128)(2,1)S(1)}, u32[]{:S(2)}, u32[]{:S(2)}) %collective-permute-start.12) | collective-permute-done | bytes 65568 | tf_op jit(solution)/shard_map/ppermute | solution.py:323
  62.2 2.0 %predict_pull.1 = (f32[16,64,128]{2,1,0:T(8,128)S(1)}, f32[4,64,128]{2,1,0:T(8,128)S(1)}, f32[4,64,128]{2,1,0:T(8,128)S(1)}) custom-call(bf16[4,64,128]{2,1,0:T(8,128)(2,1)S(1)} %collective-permute-done.8.first_refs_0_, bf16[4,64,128]{2,1,0:T(8,128)(2,1)S(1)} %collective-permute-done.9.first_refs_1_, ...), custom_call_target="tpu_custom_call" | custom-call | tf_op jit(solution)/shard_map/predict_pull/pallas_call | solution.py:21
  64.3 2.5 %collective-permute-start.13 = (f32[4,64,128]{2,1,0:T(8,128)S(1)}, f32[4,64,128]{2,1,0:T(8,128)S(1)}, u32[]{:S(2)}, u32[]{:S(2)}) collective-permute-start(f32[4,64,128]{2,1,0:T(8,128)S(1)} %get-tuple-element.54), channel_id=1, source_target_pairs={{2,4},{3,5},{6,8},{7,9},{10,12},{11,13},{14,16},{15,17},{18,20},{1... | collective-permute-start | bytes 393224 | tf_op jit(solution)/shard_map/ppermute | solution.py:323
  66.8 0.1 collective-permute-start.14
  66.8 4.7 %collective-permute-done.13.back_first_ref = f32[4,64,128]{2,1,0:T(8,128)S(1)} collective-permute-done((f32[4,64,128]{2,1,0:T(8,128)S(1)}, f32[4,64,128]{2,1,0:T(8,128)S(1)}, u32[]{:S(2)}, u32[]{:S(2)}) %collective-permute-start.13) | collective-permute-done | bytes 131104 | tf_op jit(solution)/shard_map/ppermute | solution.py:323
  71.6 2.0 %last_update.1 = (f32[32,1024]{1,0:T(8,128)S(1)}, f32[1,32,1024]{2,1,0:T(8,128)S(1)}) custom-call(f32[16,64,128]{2,1,0:T(8,128)S(1)} %get-tuple-element.53.grad_ref, f32[4,64,128]{2,1,0:T(8,128)S(1)} %collective-permute-done.13.back_first_ref, f32[4,64,128]{2,1,0:T(8,128)S(1)} %collective-permute-done.14.back_second_ref, s32[2,4]{1,0:T(2,128)S(1)} %bitcast.20, ...), custom_call_target="tpu_custom_call" | custom-call | tf_op jit(solution)/shard_map/last_update/pallas_call | solution.py:21
  73.6 1.1 %collective-permute-start.15 = (f32[32,1024]{1,0:T(8,128)S(1)}, f32[32,1024]{1,0:T(8,128)S(1)}, u32[]{:S(2)}, u32[]{:S(2)}) collective-permute-start(f32[32,1024]{1,0:T(8,128)S(1)} %bitcast.24), channel_id=1, source_target_pairs={{0,1},{1,0},{2,3},{3,2},{4,5},{5,4},{6,7},{7,6},{8,9},{9,8},{10,11... | collective-permute-start | bytes 393224 | tf_op jit(solution)/shard_map/ppermute | solution.py:332
  74.7 4.5 %collective-permute-done.15 = f32[32,1024]{1,0:T(8,128)S(1)} collective-permute-done((f32[32,1024]{1,0:T(8,128)S(1)}, f32[32,1024]{1,0:T(8,128)S(1)}, u32[]{:S(2)}, u32[]{:S(2)}) %collective-permute-start.15) | collective-permute-done | bytes 131104 | tf_op jit(solution)/shard_map/ppermute | solution.py:332
  79.2 0.7 finish.1
  (14 shorter events, 0.0 us)
Async XLA Ops:
  0.0 29.1 %copy-start.1 = (bf16[16,4,128,128]{3,2,1,0:T(8,128)(2,1)S(1)}, bf16[16,4,128,128]{3,2,1,0:T(8,128)(2,1)}, u32[]{:S(2)}) copy-start(bf16[16,4,128,128]{3,2,1,0:T(8,128)(2,1)} %tiles_ref.5) | copy-start | bytes 6291460
  0.0 29.1 %copy-start.6 = (s32[1,16,4]{1,2,0:T(4,128)S(1)}, s32[1,16,4]{1,2,0:T(4,128)}, u32[]{:S(2)}) copy-start(s32[1,16,4]{1,2,0:T(4,128)} %param.13) | copy-start | bytes 772
  1.1 5.8 %collective-permute-start = (bf16[32,2048]{1,0:T(8,128)(2,1)S(1)}, bf16[32,2048]{1,0:T(8,128)(2,1)S(1)}, u32[]{:S(2)}, u32[]{:S(2)}) collective-permute-start(bf16[32,2048]{1,0:T(8,128)(2,1)S(1)} %convert_element_type.3.own_ref), channel_id=1, source_target_pairs={{0,1},{1,0},{2,3},{3,2},{4,5},{5,4},{6,7},{7,6},{8,9},{9,8},{10,11... | collective-permute-start | bytes 393224 | tf_op jit(solution)/shard_map/ppermute | solution.py:332
  6.9 23.6 %all-to-all-start = ((f32[16,72,128]{2,1,0:T(8,128)}), f32[16,72,128]{2,1,0:T(8,128)S(1)}, u32[]{:S(2)}, u32[]{:S(2)}) async-start(f32[16,72,128]{2,1,0:T(8,128)} %pack_readings.1), calls=%async_computation | async-start | bytes 1179648 | tf_op jit(solution)/shard_map/all_to_all | solution.py:394
  13.1 0.9 %copy-start.2 = (f32[32,2048]{1,0:T(8,128)S(1)}, f32[32,2048]{1,0:T(8,128)}, u32[]{:S(2)}) copy-start(f32[32,2048]{1,0:T(8,128)} %x_ref.3) | copy-start | bytes 786436
  14.0 0.7 copy-start.4
  15.4 13.7 %collective-permute-start.1 = (bf16[4,64,128]{2,1,0:T(8,128)(2,1)S(1)}, bf16[4,64,128]{2,1,0:T(8,128)(2,1)S(1)}, u32[]{:S(2)}, u32[]{:S(2)}) collective-permute-start(bf16[4,64,128]{2,1,0:T(8,128)(2,1)S(1)} %get-tuple-element.35), channel_id=1, source_target_pairs={{2,4},{3,5},{6,8},{7,9},{10,12},{11,13},{14,16},{15,17},{18,20},{1... | collective-permute-start | bytes 196616 | tf_op jit(solution)/shard_map/ppermute | solution.py:323
  18.5 10.6 %collective-permute-start.2 = (bf16[4,64,128]{2,1,0:T(8,128)(2,1)S(1)}, bf16[4,64,128]{2,1,0:T(8,128)(2,1)S(1)}, u32[]{:S(2)}, u32[]{:S(2)}) collective-permute-start(bf16[4,64,128]{2,1,0:T(8,128)(2,1)S(1)} %get-tuple-element.36), channel_id=1, source_target_pairs={{0,2},{1,3},{4,6},{5,7},{8,10},{9,11},{12,14},{13,15},{16,18},{17,... | collective-permute-start | bytes 196616 | tf_op jit(solution)/shard_map/ppermute | solution.py:323
  19.0 11.6 %collective-permute-start.3 = (f32[32,1024]{1,0:T(8,128)S(1)}, f32[32,1024]{1,0:T(8,128)S(1)}, u32[]{:S(2)}, u32[]{:S(2)}) collective-permute-start(f32[32,1024]{1,0:T(8,128)S(1)} %get-tuple-element.37), channel_id=1, source_target_pairs={{0,1},{1,0},{2,3},{3,2},{4,5},{5,4},{6,7},{7,6},{8,9},{9,8},{10,11... | collective-permute-start | bytes 393224 | tf_op jit(solution)/shard_map/ppermute | solution.py:332
  20.0 0.7 copy-start.7
  31.8 16.4 %copy-start = (bf16[1024,2048]{1,0:T(8,128)(2,1)S(1)}, bf16[1024,2048]{1,0:T(8,128)(2,1)}, u32[]{:S(2)}) copy-start(bf16[1024,2048]{1,0:T(8,128)(2,1)} %gain_ref.3) | copy-start | bytes 12582916
  31.8 16.3 %copy-start.3 = (f32[32,2048]{1,0:T(8,128)S(1)}, f32[32,2048]{1,0:T(8,128)}, u32[]{:S(2)}) copy-start(f32[32,2048]{1,0:T(8,128)} %x_ref.3) | copy-start | bytes 786436
  31.8 16.3 %copy-start.5 = (s32[1,2,4]{2,1,0:T(2,128)S(1)}, s32[1,2,4]{2,1,0:T(2,128)}, u32[]{:S(2)}) copy-start(s32[1,2,4]{2,1,0:T(2,128)} %param.14) | copy-start | bytes 100
  33.0 5.0 %collective-permute-start.5 = (f32[32,1024]{1,0:T(8,128)S(1)}, f32[32,1024]{1,0:T(8,128)S(1)}, u32[]{:S(2)}, u32[]{:S(2)}) collective-permute-start(f32[32,1024]{1,0:T(8,128)S(1)} %get-tuple-element.43.z_refs_1_), channel_id=1, source_target_pairs={{0,1},{1,0},{2,3},{3,2},{4,5},{5,4},{6,7},{7,6},{8,9},{9,8},{10,11... | collective-permute-start | bytes 393224 | tf_op jit(solution)/shard_map/ppermute | solution.py:332
  34.1 5.4 %collective-permute-start.4 = (f32[32,1024]{1,0:T(8,128)S(1)}, f32[32,1024]{1,0:T(8,128)S(1)}, u32[]{:S(2)}, u32[]{:S(2)}) collective-permute-start(f32[32,1024]{1,0:T(8,128)S(1)} %get-tuple-element.42.z_refs_0_), channel_id=1, source_target_pairs={{0,1},{1,0},{2,3},{3,2},{4,5},{5,4},{6,7},{7,6},{8,9},{9,8},{10,11... | collective-permute-start | bytes 393224 | tf_op jit(solution)/shard_map/ppermute | solution.py:332
  40.9 7.2 %collective-permute-start.6 = (f32[4,64,128]{2,1,0:T(8,128)S(1)}, f32[4,64,128]{2,1,0:T(8,128)S(1)}, u32[]{:S(2)}, u32[]{:S(2)}) collective-permute-start(f32[4,64,128]{2,1,0:T(8,128)S(1)} %get-tuple-element.47), channel_id=1, source_target_pairs={{2,4},{3,5},{6,8},{7,9},{10,12},{11,13},{14,16},{15,17},{18,20},{1... | collective-permute-start | bytes 393224 | tf_op jit(solution)/shard_map/ppermute | solution.py:323
  44.0 4.1 %collective-permute-start.7 = (f32[4,64,128]{2,1,0:T(8,128)S(1)}, f32[4,64,128]{2,1,0:T(8,128)S(1)}, u32[]{:S(2)}, u32[]{:S(2)}) collective-permute-start(f32[4,64,128]{2,1,0:T(8,128)S(1)} %get-tuple-element.48), channel_id=1, source_target_pairs={{0,2},{1,3},{4,6},{5,7},{8,10},{9,11},{12,14},{13,15},{16,18},{17,... | collective-permute-start | bytes 393224 | tf_op jit(solution)/shard_map/ppermute | solution.py:323
  50.2 12.0 %collective-permute-start.10 = (bf16[8,64,128]{2,1,0:T(8,128)(2,1)S(1)}, bf16[8,64,128]{2,1,0:T(8,128)(2,1)S(1)}, u32[]{:S(2)}, u32[]{:S(2)}) collective-permute-start(bf16[8,64,128]{2,1,0:T(8,128)(2,1)S(1)} %get-tuple-element.51.mine_ref), channel_id=1, source_target_pairs={{0,1},{1,0},{2,3},{3,2},{4,5},{5,4},{6,7},{7,6},{8,9},{9,8},{10,11... | collective-permute-start | bytes 393224 | tf_op jit(solution)/shard_map/ppermute | solution.py:332
  51.3 8.1 %collective-permute-start.9 = (bf16[4,64,128]{2,1,0:T(8,128)(2,1)S(1)}, bf16[4,64,128]{2,1,0:T(8,128)(2,1)S(1)}, u32[]{:S(2)}, u32[]{:S(2)}) collective-permute-start(bf16[4,64,128]{2,1,0:T(8,128)(2,1)S(1)} %get-tuple-element.50), channel_id=1, source_target_pairs={{2,5},{3,4},{6,9},{7,8},{10,13},{11,12},{14,17},{15,16},{18,21},{1... | collective-permute-start | bytes 196616 | tf_op jit(solution)/shard_map/ppermute | solution.py:323
  54.5 6.5 %collective-permute-start.8 = (bf16[4,64,128]{2,1,0:T(8,128)(2,1)S(1)}, bf16[4,64,128]{2,1,0:T(8,128)(2,1)S(1)}, u32[]{:S(2)}, u32[]{:S(2)}) collective-permute-start(bf16[4,64,128]{2,1,0:T(8,128)(2,1)S(1)} %get-tuple-element.50), channel_id=1, source_target_pairs={{2,4},{3,5},{6,8},{7,9},{10,12},{11,13},{14,16},{15,17},{18,20},{1... | collective-permute-start | bytes 196616 | tf_op jit(solution)/shard_map/ppermute | solution.py:323
  58.2 4.0 %collective-permute-start.12 = (bf16[4,64,128]{2,1,0:T(8,128)(2,1)S(1)}, bf16[4,64,128]{2,1,0:T(8,128)(2,1)S(1)}, u32[]{:S(2)}, u32[]{:S(2)}) collective-permute-start(bf16[4,64,128]{2,1,0:T(8,128)(2,1)S(1)} %get-tuple-element.52), channel_id=1, source_target_pairs={{0,3},{1,2},{4,7},{5,6},{8,11},{9,10},{12,15},{13,14},{16,19},{17,... | collective-permute-start | bytes 196616 | tf_op jit(solution)/shard_map/ppermute | solution.py:323
  58.3 3.9 %collective-permute-start.11 = (bf16[4,64,128]{2,1,0:T(8,128)(2,1)S(1)}, bf16[4,64,128]{2,1,0:T(8,128)(2,1)S(1)}, u32[]{:S(2)}, u32[]{:S(2)}) collective-permute-start(bf16[4,64,128]{2,1,0:T(8,128)(2,1)S(1)} %get-tuple-element.52), channel_id=1, source_target_pairs={{0,2},{1,3},{4,6},{5,7},{8,10},{9,11},{12,14},{13,15},{16,18},{17,... | collective-permute-start | bytes 196616 | tf_op jit(solution)/shard_map/ppermute | solution.py:323
  64.3 7.3 %collective-permute-start.13 = (f32[4,64,128]{2,1,0:T(8,128)S(1)}, f32[4,64,128]{2,1,0:T(8,128)S(1)}, u32[]{:S(2)}, u32[]{:S(2)}) collective-permute-start(f32[4,64,128]{2,1,0:T(8,128)S(1)} %get-tuple-element.54), channel_id=1, source_target_pairs={{2,4},{3,5},{6,8},{7,9},{10,12},{11,13},{14,16},{15,17},{18,20},{1... | collective-permute-start | bytes 393224 | tf_op jit(solution)/shard_map/ppermute | solution.py:323
  66.8 4.8 %collective-permute-start.14 = (f32[4,64,128]{2,1,0:T(8,128)S(1)}, f32[4,64,128]{2,1,0:T(8,128)S(1)}, u32[]{:S(2)}, u32[]{:S(2)}) collective-permute-start(f32[4,64,128]{2,1,0:T(8,128)S(1)} %get-tuple-element.55), channel_id=1, source_target_pairs={{0,2},{1,3},{4,6},{5,7},{8,10},{9,11},{12,14},{13,15},{16,18},{17,... | collective-permute-start | bytes 393224 | tf_op jit(solution)/shard_map/ppermute | solution.py:323
  73.6 5.6 %collective-permute-start.15 = (f32[32,1024]{1,0:T(8,128)S(1)}, f32[32,1024]{1,0:T(8,128)S(1)}, u32[]{:S(2)}, u32[]{:S(2)}) collective-permute-start(f32[32,1024]{1,0:T(8,128)S(1)} %bitcast.24), channel_id=1, source_target_pairs={{0,1},{1,0},{2,3},{3,2},{4,5},{5,4},{6,7},{7,6},{8,9},{9,8},{10,11... | collective-permute-start | bytes 393224 | tf_op jit(solution)/shard_map/ppermute | solution.py:332

commit v6 on v5

--- a/solution.py
+++ b/solution.py
@@ -17,12 +17,12 @@
 SMEM = pl.BlockSpec(memory_space=pltpu.SMEM)
 
 
-def call(kernel, outs, ins, args, scratch=(), flops=0, mib=12, name=None):
+def call(kernel, outs, ins, args, scratch=(), flops=0, mib=12, out_spec=VMEM, name=None):
     return pl.pallas_call(
         kernel,
         out_shape=outs,
         in_specs=ins,
-        out_specs=jax.tree.map(lambda _: VMEM, outs),
+        out_specs=jax.tree.map(lambda _: out_spec, outs),
         scratch_shapes=list(scratch),
         compiler_params=pltpu.CompilerParams(vmem_limit_bytes=mib * 1024 * 1024),
         cost_estimate=pl.CostEstimate(
@@ -40,7 +40,7 @@
     return lax.broadcasted_iota(jnp.int32, shape, 0)
 
 
-def pack_kernel(z_in, v_in, hub_in, out_ref, z_ref, v_ref, hub_ref, sems):
+def pack_kernel(z_in, v_in, hub_in, out, z_ref, v_ref, hub_ref, out_ref, sems, out_sems):
     copies = [
         pltpu.make_async_copy(source, target, sems.at[i])
         for i, (source, target) in enumerate(((hub_in, hub_ref), (z_in, z_ref), (v_in, v_ref)))
@@ -71,6 +71,9 @@
             variance = jnp.sum(jnp.where(mine, found, 0.0), axis=0, keepdims=True)
             tail = jnp.where(rows_iota((8, BLK)) == g, variance, tail)
         out_ref[d, groups * snaps :, :] = tail
+        pltpu.make_async_copy(out_ref.at[d], out.at[d], out_sems.at[d]).start()
+    for d in range(chunks):
+        pltpu.make_async_copy(out_ref.at[d], out.at[d], out_sems.at[d]).wait()
 
 
 def inverse_kernel(own_ref, group_ref, lane_ref):
@@ -155,11 +158,11 @@
         sent_ref[...] = x_ref[:, pl.ds(pl.multiple_of(at, BLK), width)]
 
 
-def slots_into(slots_ref, aug_ref, first_ref, second_ref):
+def slots_into(slots_ref, aug_ref, first, second_ref):
     own = aug_ref.shape[0]
-    ties = first_ref.shape[0]
+    ties = second_ref.shape[0]
     slots_ref[:own] = aug_ref[...]
-    slots_ref[pl.ds(own + ties * (1 - parity()), ties)] = first_ref[...]
+    slots_ref[pl.ds(own + ties * (1 - parity()), ties)] = first
     slots_ref[pl.ds(own + ties * parity(), ties)] = second_ref[...]
 
 
@@ -169,19 +172,15 @@
     return jnp.concatenate([ref[:, j * snaps : (j + 1) * snaps] for j in order], axis=1)
 
 
-def join_states(slots_ref, mine_ref, others_refs, first_refs, second_refs):
-    members = len(first_refs)
+def join_states_kernel(mine_ref, others_refs, ties_ref, aug_ref, second_ref):
+    members = len(others_refs) + 1
     held = mine_ref.shape[0]
-    own = held * members
-    ties = first_refs[0].shape[0]
     me = lax.axis_index("snap")
-    slots_ref[pl.ds(me * held, held)] = mine_ref[...]
+    aug_ref[pl.ds(me * held, held)] = mine_ref[...]
     for i, ref in enumerate(others_refs, 1):
         at = lax.rem(me + members - i, members) * held
-        slots_ref[pl.ds(at, held)] = reordered(ref, i, members)
-    for side, refs in ((1 - parity(), first_refs), (parity(), second_refs)):
-        parts = [reordered(ref, i, members) for i, ref in enumerate(refs)]
-        slots_ref[pl.ds(own + ties * side, ties)] = sum(parts[1:], parts[0])
+        aug_ref[pl.ds(at, held)] = reordered(ref, i, members)
+    pick(aug_ref, ties_ref, parity(), second_ref)
 
 
 def predicted(j, slots_ref, tiles_ref, place_ref):
@@ -192,7 +191,7 @@
 
 
 def predict_kernel(aug_ref, first_ref, second_ref, tiles_ref, place_ref, out_ref, slots_ref):
-    slots_into(slots_ref, aug_ref, first_ref, second_ref)
+    slots_into(slots_ref, aug_ref, first_ref[...], second_ref)
     predict(tiles_ref, place_ref, out_ref, slots_ref)
 
 
@@ -224,8 +223,10 @@
     own = own_ref.shape[0]
     ties = first_ref.shape[0]
     own_ref[...] = total_ref[:own]
-    first_ref[...] = total_ref[pl.ds(own + ties * (1 - parity()), ties)]
-    second_ref[...] = total_ref[pl.ds(own + ties * parity(), ties)]
+    first = total_ref[pl.ds(own + ties * (1 - parity()), ties)]
+    second = total_ref[pl.ds(own + ties * parity(), ties)]
+    first_ref[...] = first.astype(first_ref.dtype)
+    second_ref[...] = second.astype(second_ref.dtype)
 
 
 def pull_kernel(
@@ -239,10 +240,11 @@
 
 
 def predict_pull_kernel(
-    first_refs, others_in_refs, second_refs, mine_ref, z_refs, others_refs, v_refs, tiles_ref, place_ref,
+    first_refs, aug_ref, second_in_ref, z_refs, others_refs, v_refs, tiles_ref, place_ref,
     own_ref, first_ref, second_ref, slots_ref, guess_ref, total_ref, weighted_ref,
 ):
-    join_states(slots_ref, mine_ref, others_in_refs, first_refs, second_refs)
+    parts = [reordered(ref, i, len(first_refs)) for i, ref in enumerate(first_refs)]
+    slots_into(slots_ref, aug_ref, sum(parts[1:], parts[0]), second_in_ref)
     predict(tiles_ref, place_ref, guess_ref, slots_ref)
     pull_kernel(
         guess_ref, z_refs, others_refs, v_refs, tiles_ref, place_ref, own_ref, first_ref, second_ref,
@@ -258,7 +260,7 @@
 
             @pl.when(b >= 0)
             def _(b=b, t=t, back_ref=back_ref):
-                work_ref[b] += back_ref[t]
+                work_ref[b] += back_ref[t].astype(F32)
 
     return jnp.concatenate([work_ref[b].astype(BF16) for b in range(work_ref.shape[0])], axis=1)
 
@@ -274,7 +276,7 @@
 
 def first_update_kernel(
     grad_ref, back_first_ref, back_second_ref, ties_ref, gain_ref, x_ref, x_others_refs,
-    state_ref, message_ref, first_ref, second_ref, work_ref,
+    state_ref, message_ref, first_ref, work_ref,
 ):
     gradient = full_gradient(grad_ref, back_first_ref, back_second_ref, ties_ref, work_ref)
     held = state_ref.shape[0]
@@ -286,7 +288,6 @@
         state_ref[i] = state
         message_ref[i] = state.astype(BF16)
     pick(message_ref, ties_ref, 1 - parity(), first_ref, me * held)
-    pick(message_ref, ties_ref, parity(), second_ref, me * held)
 
 
 def last_update_kernel(
@@ -312,15 +313,9 @@
         out_ref[:, pl.ds(pl.multiple_of(at, BLK), width)] = others_ref[i - 1]
 
 
-def swap_pair(block, start, distance=0):
-    members = lax.axis_size("snap")
+def swap_pair(block, start):
     pairs = [(i, i + 1) for i in range(start, lax.axis_size("area") - 1, 2)]
-    route = [
-        (a * members + s, b * members + (s + distance) % members)
-        for a, b in pairs + [(b, a) for a, b in pairs]
-        for s in range(members)
-    ]
-    return lax.ppermute(block, ("area", "snap"), route)
+    return lax.ppermute(block, "area", pairs + [(b, a) for a, b in pairs])
 
 
 def with_neighbours(first, second):
@@ -381,12 +376,14 @@
             pltpu.VMEM((snaps, lines), F32),
             pltpu.VMEM((lines // BLK, BLK), F32),
             pltpu.VMEM((chunks, width), jnp.int32),
+            pltpu.VMEM((chunks, depth, BLK), F32),
             pltpu.SemaphoreType.DMA((3,)),
+            pltpu.SemaphoreType.DMA((chunks,)),
         ],
+        out_spec=HBM,
         mib=60,
         name="pack_readings",
     )
-    message, rounded_others = lax.optimization_barrier((message, rounded_others))
     each = width // cap
     if each > 1:
         message = message.reshape(chunks, depth, each, cap).transpose(0, 2, 1, 3)
@@ -461,12 +458,11 @@
     )
     arrived = with_neighbours(first, second)
     boundary = shape((ties, everything, BLK), BF16)
-    state, mine, first, second = call(
+    state, mine, first = call(
         first_update_kernel,
         (
             shape((held, everything, BLK), F32),
             shape((held, everything, BLK), BF16),
-            boundary,
             boundary,
         ),
         [VMEM, VMEM, VMEM, SMEM, VMEM, VMEM, [VMEM] * (members - 1)],
@@ -477,15 +473,22 @@
         scratch=[work],
         name="first_update",
     )
-    firsts = [swap_pair(first, 1, i) for i in range(members)]
     others = [from_snap(mine, i) for i in range(1, members)]
-    seconds = [swap_pair(second, 0, i) for i in range(members)]
+    first = swap_pair(first, 1)
+    firsts = [first] + [from_snap(first, i) for i in range(1, members)]
+    aug, second = call(
+        join_states_kernel,
+        (shape((own, everything, BLK), BF16), boundary),
+        [VMEM, [VMEM] * (members - 1), SMEM],
+        (mine, others, ties_table),
+        name="join_states",
+    )
+    second = swap_pair(second, 0)
     grad, first, second = call(
         predict_pull_kernel,
-        grads,
-        [[VMEM] * members, [VMEM] * (members - 1), [VMEM] * members, VMEM]
-        + [[VMEM] * 2, [VMEM] * 2, [VMEM] * 2, VMEM, SMEM],
-        (firsts, others, seconds, mine, readings, reading_others, variance, derivative_pieces, place),
+        (grads[0], boundary, boundary),
+        [[VMEM] * members, VMEM, VMEM, [VMEM] * 2, [VMEM] * 2, [VMEM] * 2, VMEM, SMEM],
+        (firsts, aug, second, readings, reading_others, variance, derivative_pieces, place),
         scratch=[
             pltpu.VMEM((slots, everything, BLK), BF16),
             pltpu.VMEM((everything, lines), F32),

time: 80.7 us -> 79.1 us (0.980)
  starting transfers between devices: 30.3 us -> 26.3 us
  waiting for transfers between devices: 28.5 us -> 30.1 us
    ppermute x6 -> x7, waiting for transfers between devices: 8.89 us -> 17.5 us  [from_snap(): lax.ppermute(block, 'snap', [(i, (i + distance) % members) for i in range...]
    ppermute x10 -> x8, waiting for transfers between devices: 19.6 us -> 12.6 us  [swap_pair(): return lax.ppermute(block, 'area', pairs + [(b, a) for a, b in pairs])]
    ppermute x10 -> x8, starting transfers between devices: 17.3 us -> 12.3 us  [swap_pair(): return lax.ppermute(block, 'area', pairs + [(b, a) for a, b in pairs])]
    ppermute x6 -> x7, starting transfers between devices: 6.83 us -> 7.86 us  [from_snap(): lax.ppermute(block, 'snap', [(i, (i + distance) % members) for i in range...]
    pallas_call x11 -> x12, Pallas kernels: 17.5 us -> 18.1 us  [call(): pl.pallas_call(kernel, out_shape=outs, in_specs=ins, out_specs=jax.tree.m...]
  transfers between devices with their start and end apart: 17 -> 16, of which waited for: 8 -> 10; matrix products, arithmetic and copies ran while one was open for 0% -> 1% of each run, Pallas kernels for 8% -> 4%
where the time goes in v6:
time: 79.1 us; the launch traced here: 78 us
  waiting for transfers between devices  30.1 us (38%)
  starting transfers between devices  26.3 us (33%)
  Pallas kernels  18.1 us (23%)
  local copies, waits for them, and re-layouts  2.37 us (3%)
  other arithmetic  0.96 us (1%)
    pallas_call x12, Pallas kernels, call(): pl.pallas_call(kernel, out_shape=outs, in_specs=ins, out_specs=jax.tree.m...  18.1 us
    ppermute x7, waiting for transfers between devices, from_snap(): lax.ppermute(block, 'snap', [(i, (i + distance) % members) for i in range...  17.5 us
    ppermute x8, waiting for transfers between devices, swap_pair(): return lax.ppermute(block, 'area', pairs + [(b, a) for a, b in pairs])  12.6 us
    ppermute x8, starting transfers between devices, swap_pair(): return lax.ppermute(block, 'area', pairs + [(b, a) for a, b in pairs])  12.3 us
    ppermute x7, starting transfers between devices, from_snap(): lax.ppermute(block, 'snap', [(i, (i + distance) % members) for i in range...  7.86 us
    all_to_all x1, starting transfers between devices, on_device(): lax.all_to_all(message, 'area', split_axis=0, concat_axis=0, tiled=True)  6.17 us
    unnamed x16, local copies, waits for them, and re-layouts  2.37 us
  transfers between devices with their start and end apart: 16, of which 10 were waited for; matrix products, arithmetic and copies ran while one was open for 1% of the time, Pallas kernels for 4%

profile of v6, /device:TPU:16, one launch (start us, length us, event | category | flops | bytes accessed | tf_op | source)
XLA Modules:
  0.0 78.0 jit_solution(1575441501214527868)
XLA Ops:
  0.0 4.3 %pack_readings.1 = f32[16,72,128]{2,1,0:T(8,128)} custom-call(f32[32,2048]{1,0:T(8,128)} %z_in.1, f32[16,128]{1,0:T(8,128)} %bitcast.28, s32[16,256]{1,0:T(8,128)} %bitcast.27), custom_call_target="tpu_custom_call" | custom-call | tf_op jit(solution)/shard_map/pack_readings/pallas_call | solution.py:21
  4.3 6.2 %all-to-all-start = ((f32[16,72,128]{2,1,0:T(8,128)}), f32[16,72,128]{2,1,0:T(8,128)S(1)}, u32[]{:S(2)}, u32[]{:S(2)}) async-start(f32[16,72,128]{2,1,0:T(8,128)} %pack_readings.1), calls=%async_computation | async-start | bytes 1179648 | tf_op jit(solution)/shard_map/all_to_all | solution.py:391
  10.5 1.0 %convert_element_type.3.own_ref = bf16[32,2048]{1,0:T(8,128)(2,1)S(1)} convert(f32[32,2048]{1,0:T(8,128)} %x_ref.3) | non-fusion elementwise | flops 65536 | bytes 393216 | tf_op jit(solution)/shard_map/convert_element_type | solution.py:368
  11.4 1.6 %collective-permute-start = (bf16[32,2048]{1,0:T(8,128)(2,1)S(1)}, bf16[32,2048]{1,0:T(8,128)(2,1)S(1)}, u32[]{:S(2)}, u32[]{:S(2)}) collective-permute-start(bf16[32,2048]{1,0:T(8,128)(2,1)S(1)} %convert_element_type.3.own_ref), channel_id=1, source_target_pairs={{0,1},{1,0},{2,3},{3,2},{4,5},{5,4},{6,7},{7,6},{8,9},{9,8},{10,11... | collective-permute-start | bytes 393224 | tf_op jit(solution)/shard_map/ppermute | solution.py:327
  13.0 4.0 %collective-permute-done = bf16[32,2048]{1,0:T(8,128)(2,1)S(1)} collective-permute-done((bf16[32,2048]{1,0:T(8,128)(2,1)S(1)}, bf16[32,2048]{1,0:T(8,128)(2,1)S(1)}, u32[]{:S(2)}, u32[]{:S(2)}) %collective-permute-start) | collective-permute-done | bytes 131104 | tf_op jit(solution)/shard_map/ppermute | solution.py:327
  17.1 0.9 %copy-done.2 = f32[32,2048]{1,0:T(8,128)S(1)} copy-done((f32[32,2048]{1,0:T(8,128)S(1)}, f32[32,2048]{1,0:T(8,128)}, u32[]{:S(2)}) %copy-start.2) | copy-done | bytes 262168
  18.0 0.7 copy-done.4
  18.7 0.7 first_states.1
  19.3 2.3 %collective-permute-start.1 = (bf16[4,64,128]{2,1,0:T(8,128)(2,1)S(1)}, bf16[4,64,128]{2,1,0:T(8,128)(2,1)S(1)}, u32[]{:S(2)}, u32[]{:S(2)}) collective-permute-start(bf16[4,64,128]{2,1,0:T(8,128)(2,1)S(1)} %get-tuple-element.32), channel_id=1, source_target_pairs={{2,4},{6,8},{10,12},{14,16},{18,20},{22,24},{26,28},{4,2},{8,6},{1... | collective-permute-start | bytes 196616 | tf_op jit(solution)/shard_map/ppermute | solution.py:318
  21.6 1.3 %collective-permute-start.2 = (bf16[4,64,128]{2,1,0:T(8,128)(2,1)S(1)}, bf16[4,64,128]{2,1,0:T(8,128)(2,1)S(1)}, u32[]{:S(2)}, u32[]{:S(2)}) collective-permute-start(bf16[4,64,128]{2,1,0:T(8,128)(2,1)S(1)} %get-tuple-element.33), channel_id=1, source_target_pairs={{0,2},{4,6},{8,10},{12,14},{16,18},{20,22},{24,26},{28,30},{2,0},{... | collective-permute-start | bytes 196616 | tf_op jit(solution)/shard_map/ppermute | solution.py:318
  22.9 1.5 %collective-permute-start.3 = (f32[32,1024]{1,0:T(8,128)S(1)}, f32[32,1024]{1,0:T(8,128)S(1)}, u32[]{:S(2)}, u32[]{:S(2)}) collective-permute-start(f32[32,1024]{1,0:T(8,128)S(1)} %get-tuple-element.34), channel_id=1, source_target_pairs={{0,1},{1,0},{2,3},{3,2},{4,5},{5,4},{6,7},{7,6},{8,9},{9,8},{10,11... | collective-permute-start | bytes 393224 | tf_op jit(solution)/shard_map/ppermute | solution.py:327
  24.4 0.7 copy-done.7
  25.1 0.4 invert_order.1
  25.6 0.9 %collective-permute-done.1.first_ref = bf16[4,64,128]{2,1,0:T(8,128)(2,1)S(1)} collective-permute-done((bf16[4,64,128]{2,1,0:T(8,128)(2,1)S(1)}, bf16[4,64,128]{2,1,0:T(8,128)(2,1)S(1)}, u32[]{:S(2)}, u32[]{:S(2)}) %collective-permute-start.1) | collective-permute-done | bytes 65568 | tf_op jit(solution)/shard_map/ppermute | solution.py:318
  26.5 1.4 %predict.1.guess_ref = f32[64,2048]{1,0:T(8,128)S(1)} custom-call(bf16[16,64,128]{2,1,0:T(8,128)(2,1)S(1)} %get-tuple-element.31.aug_ref, bf16[4,64,128]{2,1,0:T(8,128)(2,1)S(1)} %collective-permute-done.1.first_ref, bf16[4,64,128]{2,1,0:T(8,128)(2,1)S(1)} %collective-permute-done.2.second_ref, bf16[16,4,128,128]{3,2,1,0:T(8,128)(2,1)S(1)} %copy-done.1, ...), custom_call_target="tpu_custom_call" | custom-call | flops 1000000000 | tf_op jit(solution)/shard_map/predict/pallas_call | solution.py:21
  27.9 0.5 collective-permute-done.3.x_others_refs_0_
  28.4 0.0 all-to-all-done.message_ref
  28.4 1.2 %unpack_readings.3 = (f32[32,1024]{1,0:T(8,128)S(1)}, f32[1,1024]{1,0:T(1,128)S(1)}) custom-call(s32[16,128]{1,0:T(8,128)S(1)} %get-tuple-element.36.group_ref, s32[16,128]{1,0:T(8,128)S(1)} %get-tuple-element.37.lane_ref, f32[16,72,128]{2,1,0:T(8,128)S(1)} %all-to-all-done.message_ref), custom_call_target="tpu_custom_call" | custom-call | flops 2000000000 | tf_op jit(solution)/shard_map/unpack_readings/pallas_call | solution.py:21
  29.6 0.0 copy-start
  29.6 0.0 copy-start.3
  29.6 0.0 copy-start.5
  29.7 1.2 %unpack_readings.2 = (f32[32,1024]{1,0:T(8,128)S(1)}, f32[1,1024]{1,0:T(1,128)S(1)}) custom-call(s32[16,128]{1,0:T(8,128)S(1)} %get-tuple-element.36.group_ref, s32[16,128]{1,0:T(8,128)S(1)} %get-tuple-element.37.lane_ref, f32[16,72,128]{2,1,0:T(8,128)S(1)} %all-to-all-done.message_ref), custom_call_target="tpu_custom_call" | custom-call | flops 2000000000 | tf_op jit(solution)/shard_map/unpack_readings/pallas_call | solution.py:21
  30.9 1.6 %collective-permute-start.5 = (f32[32,1024]{1,0:T(8,128)S(1)}, f32[32,1024]{1,0:T(8,128)S(1)}, u32[]{:S(2)}, u32[]{:S(2)}) collective-permute-start(f32[32,1024]{1,0:T(8,128)S(1)} %get-tuple-element.40.z_refs_1_), channel_id=1, source_target_pairs={{0,1},{1,0},{2,3},{3,2},{4,5},{5,4},{6,7},{7,6},{8,9},{9,8},{10,11... | collective-permute-start | bytes 393224 | tf_op jit(solution)/shard_map/ppermute | solution.py:327
  32.5 0.5 collective-permute-start.4
  33.0 4.0 %collective-permute-done.5 = f32[32,1024]{1,0:T(8,128)S(1)} collective-permute-done((f32[32,1024]{1,0:T(8,128)S(1)}, f32[32,1024]{1,0:T(8,128)S(1)}, u32[]{:S(2)}, u32[]{:S(2)}) %collective-permute-start.5) | collective-permute-done | bytes 131104 | tf_op jit(solution)/shard_map/ppermute | solution.py:327
  37.0 1.4 %collective-permute-done.4 = f32[32,1024]{1,0:T(8,128)S(1)} collective-permute-done((f32[32,1024]{1,0:T(8,128)S(1)}, f32[32,1024]{1,0:T(8,128)S(1)}, u32[]{:S(2)}, u32[]{:S(2)}) %collective-permute-start.4) | collective-permute-done | bytes 131104 | tf_op jit(solution)/shard_map/ppermute | solution.py:327
  38.4 1.5 %pull.1 = (f32[16,64,128]{2,1,0:T(8,128)S(1)}, f32[4,64,128]{2,1,0:T(8,128)S(1)}, f32[4,64,128]{2,1,0:T(8,128)S(1)}) custom-call(f32[64,2048]{1,0:T(8,128)S(1)} %predict.1.guess_ref, f32[32,1024]{1,0:T(8,128)S(1)} %get-tuple-element.39.z_refs_0_, f32[32,1024]{1,0:T(8,128)S(1)} %get-tuple-element.40.z_refs_1_, f32[1,32,1024]{2,1,0:T(8,128)S(1)} %bitcast.14, ...), custom_call_target="tpu_custom_call" | custom-call | tf_op jit(solution)/shard_map/pull/pallas_call | solution.py:21
  39.9 1.9 %collective-permute-start.6 = (f32[4,64,128]{2,1,0:T(8,128)S(1)}, f32[4,64,128]{2,1,0:T(8,128)S(1)}, u32[]{:S(2)}, u32[]{:S(2)}) collective-permute-start(f32[4,64,128]{2,1,0:T(8,128)S(1)} %get-tuple-element.44), channel_id=1, source_target_pairs={{2,4},{6,8},{10,12},{14,16},{18,20},{22,24},{26,28},{4,2},{8,6},{1... | collective-permute-start | bytes 393224 | tf_op jit(solution)/shard_map/ppermute | solution.py:318
  41.8 1.6 %collective-permute-start.7 = (f32[4,64,128]{2,1,0:T(8,128)S(1)}, f32[4,64,128]{2,1,0:T(8,128)S(1)}, u32[]{:S(2)}, u32[]{:S(2)}) collective-permute-start(f32[4,64,128]{2,1,0:T(8,128)S(1)} %get-tuple-element.45), channel_id=1, source_target_pairs={{0,2},{4,6},{8,10},{12,14},{16,18},{20,22},{24,26},{28,30},{2,0},{... | collective-permute-start | bytes 393224 | tf_op jit(solution)/shard_map/ppermute | solution.py:318
  43.4 3.7 %collective-permute-done.6.back_first_ref = f32[4,64,128]{2,1,0:T(8,128)S(1)} collective-permute-done((f32[4,64,128]{2,1,0:T(8,128)S(1)}, f32[4,64,128]{2,1,0:T(8,128)S(1)}, u32[]{:S(2)}, u32[]{:S(2)}) %collective-permute-start.6) | collective-permute-done | bytes 131104 | tf_op jit(solution)/shard_map/ppermute | solution.py:318
  47.1 0.0 collective-permute-done.7.back_second_ref
  47.2 2.1 %first_update.1 = (f32[8,64,128]{2,1,0:T(8,128)S(1)}, bf16[8,64,128]{2,1,0:T(8,128)(2,1)S(1)}, bf16[4,64,128]{2,1,0:T(8,128)(2,1)S(1)}) custom-call(f32[16,64,128]{2,1,0:T(8,128)S(1)} %get-tuple-element.43.grad_ref, f32[4,64,128]{2,1,0:T(8,128)S(1)} %collective-permute-done.6.back_first_ref, f32[4,64,128]{2,1,0:T(8,128)S(1)} %collective-permute-done.7.back_second_ref, ...), custom_call_target="tpu_custom_call" | custom-call | tf_op jit(solution)/shard_map/first_update/pallas_call | solution.py:21
  49.2 1.6 %collective-permute-start.10 = (bf16[8,64,128]{2,1,0:T(8,128)(2,1)S(1)}, bf16[8,64,128]{2,1,0:T(8,128)(2,1)S(1)}, u32[]{:S(2)}, u32[]{:S(2)}) collective-permute-start(bf16[8,64,128]{2,1,0:T(8,128)(2,1)S(1)} %get-tuple-element.48.mine_ref), channel_id=1, source_target_pairs={{0,1},{1,0},{2,3},{3,2},{4,5},{5,4},{6,7},{7,6},{8,9},{9,8},{10,11... | collective-permute-start | bytes 393224 | tf_op jit(solution)/shard_map/ppermute | solution.py:327
  50.8 1.9 %collective-permute-start.8 = (bf16[4,64,128]{2,1,0:T(8,128)(2,1)S(1)}, bf16[4,64,128]{2,1,0:T(8,128)(2,1)S(1)}, u32[]{:S(2)}, u32[]{:S(2)}) collective-permute-start(bf16[4,64,128]{2,1,0:T(8,128)(2,1)S(1)} %get-tuple-element.47), channel_id=1, source_target_pairs={{2,4},{6,8},{10,12},{14,16},{18,20},{22,24},{26,28},{4,2},{8,6},{1... | collective-permute-start | bytes 196616 | tf_op jit(solution)/shard_map/ppermute | solution.py:318
  52.7 4.7 %collective-permute-done.8.first_refs_0_ = bf16[4,64,128]{2,1,0:T(8,128)(2,1)S(1)} collective-permute-done((bf16[4,64,128]{2,1,0:T(8,128)(2,1)S(1)}, bf16[4,64,128]{2,1,0:T(8,128)(2,1)S(1)}, u32[]{:S(2)}, u32[]{:S(2)}) %collective-permute-start.8) | collective-permute-done | bytes 65568 | tf_op jit(solution)/shard_map/ppermute | solution.py:318
  57.4 0.5 collective-permute-start.9
  57.9 0.0 collective-permute-done.10.others_refs_0_
  57.9 0.6 join_states.1
  58.5 0.1 collective-permute-start.11
  58.6 3.1 %collective-permute-done.9.first_refs_1_ = bf16[4,64,128]{2,1,0:T(8,128)(2,1)S(1)} collective-permute-done((bf16[4,64,128]{2,1,0:T(8,128)(2,1)S(1)}, bf16[4,64,128]{2,1,0:T(8,128)(2,1)S(1)}, u32[]{:S(2)}, u32[]{:S(2)}) %collective-permute-start.9) | collective-permute-done | bytes 65568 | tf_op jit(solution)/shard_map/ppermute | solution.py:327
  61.7 2.0 %predict_pull.1 = (f32[16,64,128]{2,1,0:T(8,128)S(1)}, bf16[4,64,128]{2,1,0:T(8,128)(2,1)S(1)}, bf16[4,64,128]{2,1,0:T(8,128)(2,1)S(1)}) custom-call(bf16[4,64,128]{2,1,0:T(8,128)(2,1)S(1)} %collective-permute-done.8.first_refs_0_, bf16[4,64,128]{2,1,0:T(8,128)(2,1)S(1)} %collective-permute-done.9.first_refs_1_, ...), custom_call_target="tpu_custom_call" | custom-call | tf_op jit(solution)/shard_map/predict_pull/pallas_call | solution.py:21
  63.7 1.9 %collective-permute-start.12 = (bf16[4,64,128]{2,1,0:T(8,128)(2,1)S(1)}, bf16[4,64,128]{2,1,0:T(8,128)(2,1)S(1)}, u32[]{:S(2)}, u32[]{:S(2)}) collective-permute-start(bf16[4,64,128]{2,1,0:T(8,128)(2,1)S(1)} %get-tuple-element.52), channel_id=1, source_target_pairs={{2,4},{6,8},{10,12},{14,16},{18,20},{22,24},{26,28},{4,2},{8,6},{1... | collective-permute-start | bytes 196616 | tf_op jit(solution)/shard_map/ppermute | solution.py:318
  65.6 1.2 %collective-permute-start.13 = (bf16[4,64,128]{2,1,0:T(8,128)(2,1)S(1)}, bf16[4,64,128]{2,1,0:T(8,128)(2,1)S(1)}, u32[]{:S(2)}, u32[]{:S(2)}) collective-permute-start(bf16[4,64,128]{2,1,0:T(8,128)(2,1)S(1)} %get-tuple-element.53), channel_id=1, source_target_pairs={{0,2},{4,6},{8,10},{12,14},{16,18},{20,22},{24,26},{28,30},{2,0},{... | collective-permute-start | bytes 196616 | tf_op jit(solution)/shard_map/ppermute | solution.py:318
  66.8 3.3 %collective-permute-done.12.back_first_ref = bf16[4,64,128]{2,1,0:T(8,128)(2,1)S(1)} collective-permute-done((bf16[4,64,128]{2,1,0:T(8,128)(2,1)S(1)}, bf16[4,64,128]{2,1,0:T(8,128)(2,1)S(1)}, u32[]{:S(2)}, u32[]{:S(2)}) %collective-permute-start.12) | collective-permute-done | bytes 65568 | tf_op jit(solution)/shard_map/ppermute | solution.py:318
  70.1 2.0 %last_update.1 = (f32[32,1024]{1,0:T(8,128)S(1)}, f32[1,32,1024]{2,1,0:T(8,128)S(1)}) custom-call(f32[16,64,128]{2,1,0:T(8,128)S(1)} %get-tuple-element.51.grad_ref, bf16[4,64,128]{2,1,0:T(8,128)(2,1)S(1)} %collective-permute-done.12.back_first_ref, bf16[4,64,128]{2,1,0:T(8,128)(2,1)S(1)} %collective-permute-done.13.back_second_ref, s32[2,4]{1,0:T(2,128)S(1)} %bitcast.21, ...), custom_call_target="tpu_custom_call" | custom-call | tf_op jit(solution)/shard_map/last_update/pallas_call | solution.py:21
  72.2 0.6 collective-permute-start.14
  72.8 4.5 %collective-permute-done.14 = f32[32,1024]{1,0:T(8,128)S(1)} collective-permute-done((f32[32,1024]{1,0:T(8,128)S(1)}, f32[32,1024]{1,0:T(8,128)S(1)}, u32[]{:S(2)}, u32[]{:S(2)}) %collective-permute-start.14) | collective-permute-done | bytes 131104 | tf_op jit(solution)/shard_map/ppermute | solution.py:327
  77.2 0.7 finish.1
  (13 shorter events, 0.0 us)
Async XLA Ops:
  0.0 26.5 %copy-start.1 = (bf16[16,4,128,128]{3,2,1,0:T(8,128)(2,1)S(1)}, bf16[16,4,128,128]{3,2,1,0:T(8,128)(2,1)}, u32[]{:S(2)}) copy-start(bf16[16,4,128,128]{3,2,1,0:T(8,128)(2,1)} %tiles_ref.5) | copy-start | bytes 6291460
  0.0 26.5 %copy-start.6 = (s32[1,16,4]{1,2,0:T(4,128)S(1)}, s32[1,16,4]{1,2,0:T(4,128)}, u32[]{:S(2)}) copy-start(s32[1,16,4]{1,2,0:T(4,128)} %param.13) | copy-start | bytes 772
  4.3 24.1 %all-to-all-start = ((f32[16,72,128]{2,1,0:T(8,128)}), f32[16,72,128]{2,1,0:T(8,128)S(1)}, u32[]{:S(2)}, u32[]{:S(2)}) async-start(f32[16,72,128]{2,1,0:T(8,128)} %pack_readings.1), calls=%async_computation | async-start | bytes 1179648 | tf_op jit(solution)/shard_map/all_to_all | solution.py:391
  11.4 5.6 %collective-permute-start = (bf16[32,2048]{1,0:T(8,128)(2,1)S(1)}, bf16[32,2048]{1,0:T(8,128)(2,1)S(1)}, u32[]{:S(2)}, u32[]{:S(2)}) collective-permute-start(bf16[32,2048]{1,0:T(8,128)(2,1)S(1)} %convert_element_type.3.own_ref), channel_id=1, source_target_pairs={{0,1},{1,0},{2,3},{3,2},{4,5},{5,4},{6,7},{7,6},{8,9},{9,8},{10,11... | collective-permute-start | bytes 393224 | tf_op jit(solution)/shard_map/ppermute | solution.py:327
  17.1 1.0 %copy-start.2 = (f32[32,2048]{1,0:T(8,128)S(1)}, f32[32,2048]{1,0:T(8,128)}, u32[]{:S(2)}) copy-start(f32[32,2048]{1,0:T(8,128)} %x_ref.3) | copy-start | bytes 786436
  18.0 0.7 copy-start.4
  19.3 7.1 %collective-permute-start.1 = (bf16[4,64,128]{2,1,0:T(8,128)(2,1)S(1)}, bf16[4,64,128]{2,1,0:T(8,128)(2,1)S(1)}, u32[]{:S(2)}, u32[]{:S(2)}) collective-permute-start(bf16[4,64,128]{2,1,0:T(8,128)(2,1)S(1)} %get-tuple-element.32), channel_id=1, source_target_pairs={{2,4},{6,8},{10,12},{14,16},{18,20},{22,24},{26,28},{4,2},{8,6},{1... | collective-permute-start | bytes 196616 | tf_op jit(solution)/shard_map/ppermute | solution.py:318
  21.6 4.8 %collective-permute-start.2 = (bf16[4,64,128]{2,1,0:T(8,128)(2,1)S(1)}, bf16[4,64,128]{2,1,0:T(8,128)(2,1)S(1)}, u32[]{:S(2)}, u32[]{:S(2)}) collective-permute-start(bf16[4,64,128]{2,1,0:T(8,128)(2,1)S(1)} %get-tuple-element.33), channel_id=1, source_target_pairs={{0,2},{4,6},{8,10},{12,14},{16,18},{20,22},{24,26},{28,30},{2,0},{... | collective-permute-start | bytes 196616 | tf_op jit(solution)/shard_map/ppermute | solution.py:318
  22.9 5.5 %collective-permute-start.3 = (f32[32,1024]{1,0:T(8,128)S(1)}, f32[32,1024]{1,0:T(8,128)S(1)}, u32[]{:S(2)}, u32[]{:S(2)}) collective-permute-start(f32[32,1024]{1,0:T(8,128)S(1)} %get-tuple-element.34), channel_id=1, source_target_pairs={{0,1},{1,0},{2,3},{3,2},{4,5},{5,4},{6,7},{7,6},{8,9},{9,8},{10,11... | collective-permute-start | bytes 393224 | tf_op jit(solution)/shard_map/ppermute | solution.py:327
  24.4 0.7 copy-start.7
  29.6 17.5 %copy-start = (bf16[1024,2048]{1,0:T(8,128)(2,1)S(1)}, bf16[1024,2048]{1,0:T(8,128)(2,1)}, u32[]{:S(2)}) copy-start(bf16[1024,2048]{1,0:T(8,128)(2,1)} %gain_ref.3) | copy-start | bytes 12582916
  29.6 17.5 %copy-start.3 = (f32[32,2048]{1,0:T(8,128)S(1)}, f32[32,2048]{1,0:T(8,128)}, u32[]{:S(2)}) copy-start(f32[32,2048]{1,0:T(8,128)} %x_ref.3) | copy-start | bytes 786436
  29.6 17.5 %copy-start.5 = (s32[1,2,4]{2,1,0:T(2,128)S(1)}, s32[1,2,4]{2,1,0:T(2,128)}, u32[]{:S(2)}) copy-start(s32[1,2,4]{2,1,0:T(2,128)} %param.14) | copy-start | bytes 100
  30.9 6.1 %collective-permute-start.5 = (f32[32,1024]{1,0:T(8,128)S(1)}, f32[32,1024]{1,0:T(8,128)S(1)}, u32[]{:S(2)}, u32[]{:S(2)}) collective-permute-start(f32[32,1024]{1,0:T(8,128)S(1)} %get-tuple-element.40.z_refs_1_), channel_id=1, source_target_pairs={{0,1},{1,0},{2,3},{3,2},{4,5},{5,4},{6,7},{7,6},{8,9},{9,8},{10,11... | collective-permute-start | bytes 393224 | tf_op jit(solution)/shard_map/ppermute | solution.py:327
  32.5 5.9 %collective-permute-start.4 = (f32[32,1024]{1,0:T(8,128)S(1)}, f32[32,1024]{1,0:T(8,128)S(1)}, u32[]{:S(2)}, u32[]{:S(2)}) collective-permute-start(f32[32,1024]{1,0:T(8,128)S(1)} %get-tuple-element.39.z_refs_0_), channel_id=1, source_target_pairs={{0,1},{1,0},{2,3},{3,2},{4,5},{5,4},{6,7},{7,6},{8,9},{9,8},{10,11... | collective-permute-start | bytes 393224 | tf_op jit(solution)/shard_map/ppermute | solution.py:327
  39.9 7.3 %collective-permute-start.6 = (f32[4,64,128]{2,1,0:T(8,128)S(1)}, f32[4,64,128]{2,1,0:T(8,128)S(1)}, u32[]{:S(2)}, u32[]{:S(2)}) collective-permute-start(f32[4,64,128]{2,1,0:T(8,128)S(1)} %get-tuple-element.44), channel_id=1, source_target_pairs={{2,4},{6,8},{10,12},{14,16},{18,20},{22,24},{26,28},{4,2},{8,6},{1... | collective-permute-start | bytes 393224 | tf_op jit(solution)/shard_map/ppermute | solution.py:318
  41.8 5.4 %collective-permute-start.7 = (f32[4,64,128]{2,1,0:T(8,128)S(1)}, f32[4,64,128]{2,1,0:T(8,128)S(1)}, u32[]{:S(2)}, u32[]{:S(2)}) collective-permute-start(f32[4,64,128]{2,1,0:T(8,128)S(1)} %get-tuple-element.45), channel_id=1, source_target_pairs={{0,2},{4,6},{8,10},{12,14},{16,18},{20,22},{24,26},{28,30},{2,0},{... | collective-permute-start | bytes 393224 | tf_op jit(solution)/shard_map/ppermute | solution.py:318
  49.2 8.7 %collective-permute-start.10 = (bf16[8,64,128]{2,1,0:T(8,128)(2,1)S(1)}, bf16[8,64,128]{2,1,0:T(8,128)(2,1)S(1)}, u32[]{:S(2)}, u32[]{:S(2)}) collective-permute-start(bf16[8,64,128]{2,1,0:T(8,128)(2,1)S(1)} %get-tuple-element.48.mine_ref), channel_id=1, source_target_pairs={{0,1},{1,0},{2,3},{3,2},{4,5},{5,4},{6,7},{7,6},{8,9},{9,8},{10,11... | collective-permute-start | bytes 393224 | tf_op jit(solution)/shard_map/ppermute | solution.py:327
  50.8 6.6 %collective-permute-start.8 = (bf16[4,64,128]{2,1,0:T(8,128)(2,1)S(1)}, bf16[4,64,128]{2,1,0:T(8,128)(2,1)S(1)}, u32[]{:S(2)}, u32[]{:S(2)}) collective-permute-start(bf16[4,64,128]{2,1,0:T(8,128)(2,1)S(1)} %get-tuple-element.47), channel_id=1, source_target_pairs={{2,4},{6,8},{10,12},{14,16},{18,20},{22,24},{26,28},{4,2},{8,6},{1... | collective-permute-start | bytes 196616 | tf_op jit(solution)/shard_map/ppermute | solution.py:318
  57.4 4.3 %collective-permute-start.9 = (bf16[4,64,128]{2,1,0:T(8,128)(2,1)S(1)}, bf16[4,64,128]{2,1,0:T(8,128)(2,1)S(1)}, u32[]{:S(2)}, u32[]{:S(2)}) collective-permute-start(bf16[4,64,128]{2,1,0:T(8,128)(2,1)S(1)} %collective-permute-done.8.first_refs_0_), channel_id=1, source_target_pairs={{0,1},{1,0},{2,3},{3,2},{4,5},{5,4},{6,7},{7,6},{8,9},{9,8},{10,11... | collective-permute-start | bytes 196616 | tf_op jit(solution)/shard_map/ppermute | solution.py:327
  58.5 3.1 %collective-permute-start.11 = (bf16[4,64,128]{2,1,0:T(8,128)(2,1)S(1)}, bf16[4,64,128]{2,1,0:T(8,128)(2,1)S(1)}, u32[]{:S(2)}, u32[]{:S(2)}) collective-permute-start(bf16[4,64,128]{2,1,0:T(8,128)(2,1)S(1)} %get-tuple-element.50), channel_id=1, source_target_pairs={{0,2},{4,6},{8,10},{12,14},{16,18},{20,22},{24,26},{28,30},{2,0},{... | collective-permute-start | bytes 196616 | tf_op jit(solution)/shard_map/ppermute | solution.py:318
  63.7 6.5 %collective-permute-start.12 = (bf16[4,64,128]{2,1,0:T(8,128)(2,1)S(1)}, bf16[4,64,128]{2,1,0:T(8,128)(2,1)S(1)}, u32[]{:S(2)}, u32[]{:S(2)}) collective-permute-start(bf16[4,64,128]{2,1,0:T(8,128)(2,1)S(1)} %get-tuple-element.52), channel_id=1, source_target_pairs={{2,4},{6,8},{10,12},{14,16},{18,20},{22,24},{26,28},{4,2},{8,6},{1... | collective-permute-start | bytes 196616 | tf_op jit(solution)/shard_map/ppermute | solution.py:318
  65.6 4.6 %collective-permute-start.13 = (bf16[4,64,128]{2,1,0:T(8,128)(2,1)S(1)}, bf16[4,64,128]{2,1,0:T(8,128)(2,1)S(1)}, u32[]{:S(2)}, u32[]{:S(2)}) collective-permute-start(bf16[4,64,128]{2,1,0:T(8,128)(2,1)S(1)} %get-tuple-element.53), channel_id=1, source_target_pairs={{0,2},{4,6},{8,10},{12,14},{16,18},{20,22},{24,26},{28,30},{2,0},{... | collective-permute-start | bytes 196616 | tf_op jit(solution)/shard_map/ppermute | solution.py:318
  72.2 5.0 %collective-permute-start.14 = (f32[32,1024]{1,0:T(8,128)S(1)}, f32[32,1024]{1,0:T(8,128)S(1)}, u32[]{:S(2)}, u32[]{:S(2)}) collective-permute-start(f32[32,1024]{1,0:T(8,128)S(1)} %bitcast.25), channel_id=1, source_target_pairs={{0,1},{1,0},{2,3},{3,2},{4,5},{5,4},{6,7},{7,6},{8,9},{9,8},{10,11... | collective-permute-start | bytes 393224 | tf_op jit(solution)/shard_map/ppermute | solution.py:327

commit v7 on v6

--- a/solution.py
+++ b/solution.py
@@ -140,9 +140,7 @@
         out_ref[t] = jnp.where(here, block, jnp.zeros_like(block))
 
 
-def first_states_kernel(
-    x_ref, own_ref, others_ref, ties_ref, aug_ref, first_ref, second_ref, sent_refs
-):
+def first_states_kernel(own_ref, others_ref, ties_ref, aug_ref, first_ref, second_ref):
     snaps = own_ref.shape[0]
     for b in range(aug_ref.shape[0]):
         columns = slice(b * BLK, (b + 1) * BLK)
@@ -151,11 +149,6 @@
             aug_ref[b, (i + 1) * snaps : (i + 2) * snaps] = others_ref[i, :, columns]
     pick(aug_ref, ties_ref, 1 - parity(), first_ref)
     pick(aug_ref, ties_ref, parity(), second_ref)
-    members = len(sent_refs) + 1
-    width = x_ref.shape[1] // members
-    for i, sent_ref in enumerate(sent_refs, 1):
-        at = lax.rem(lax.axis_index("snap") + i, members) * width
-        sent_ref[...] = x_ref[:, pl.ds(pl.multiple_of(at, BLK), width)]
 
 
 def slots_into(slots_ref, aug_ref, first, second_ref):
@@ -276,41 +269,45 @@
 
 def first_update_kernel(
     grad_ref, back_first_ref, back_second_ref, ties_ref, gain_ref, x_ref, x_others_refs,
-    state_ref, message_ref, first_ref, work_ref,
+    kept_ref, given_refs, message_ref, first_ref, work_ref,
 ):
     gradient = full_gradient(grad_ref, back_first_ref, back_second_ref, ties_ref, work_ref)
-    held = state_ref.shape[0]
+    held, snaps = kept_ref.shape[:2]
     me = lax.axis_index("snap")
     for i, update in updates(gradient, gain_ref):
         columns = pl.ds(pl.multiple_of((me * held + i) * BLK, BLK), BLK)
         parts = [x_ref[:, columns]] + [o[:, i * BLK : (i + 1) * BLK] for o in x_others_refs]
         state = jnp.concatenate(parts, axis=0) + update
-        state_ref[i] = state
+        kept_ref[i] = state[:snaps]
+        for j, given_ref in enumerate(given_refs, 1):
+            given_ref[i] = state[j * snaps : (j + 1) * snaps]
         message_ref[i] = state.astype(BF16)
     pick(message_ref, ties_ref, 1 - parity(), first_ref, me * held)
 
 
 def last_update_kernel(
-    grad_ref, back_first_ref, back_second_ref, ties_ref, gain_ref, state_ref, mine_ref, send_ref, work_ref
+    grad_ref, back_first_ref, back_second_ref, ties_ref, gain_ref, kept_ref, mine_ref, sent_refs, work_ref
 ):
     gradient = full_gradient(grad_ref, back_first_ref, back_second_ref, ties_ref, work_ref)
     snaps = mine_ref.shape[0]
     for i, update in updates(gradient, gain_ref):
-        state = state_ref[i] + update
         columns = slice(i * BLK, (i + 1) * BLK)
-        mine_ref[:, columns] = state[:snaps]
-        for j in range(send_ref.shape[0]):
-            send_ref[j, :, columns] = state[(j + 1) * snaps : (j + 2) * snaps]
-
-
-def finish_kernel(mine_ref, others_ref, out_ref):
+        mine_ref[:, columns] = kept_ref[i] + update[:snaps]
+        for j, sent_ref in enumerate(sent_refs, 1):
+            sent_ref[:, columns] = update[j * snaps : (j + 1) * snaps].astype(BF16)
+
+
+def finish_kernel(mine_ref, states_refs, updates_refs, out_ref):
     width = mine_ref.shape[1]
-    members = others_ref.shape[0] + 1
+    members = len(states_refs) + 1
     me = lax.axis_index("snap")
     out_ref[:, pl.ds(pl.multiple_of(me * width, BLK), width)] = mine_ref[...]
-    for i in range(1, members):
+    for i, (state_ref, update_ref) in enumerate(zip(states_refs, updates_refs), 1):
         at = lax.rem(me + members - i, members) * width
-        out_ref[:, pl.ds(pl.multiple_of(at, BLK), width)] = others_ref[i - 1]
+        for b in range(width // BLK):
+            update = update_ref[:, b * BLK : (b + 1) * BLK].astype(F32)
+            columns = pl.ds(pl.multiple_of(at + b * BLK, BLK), BLK)
+            out_ref[:, columns] = state_ref[b] + update
 
 
 def swap_pair(block, start):
@@ -401,19 +398,18 @@
         flops=10**9,
         name="invert_order",
     )
-    aug, first, second, x_sent = call(
+    boundary = shape((ties, everything, BLK), BF16)
+    aug, first, second = call(
         first_states_kernel,
         (
             shape((own, everything, BLK), BF16),
-            shape((ties, everything, BLK), BF16),
-            shape((ties, everything, BLK), BF16),
-            [shape((snaps, held * BLK), F32)] * (members - 1),
+            boundary,
+            boundary,
         ),
-        [VMEM, VMEM, VMEM, SMEM],
-        (starting_voltages, rounded, rounded_others, ties_table),
+        [VMEM, VMEM, SMEM],
+        (rounded, rounded_others, ties_table),
         name="first_states",
     )
-    x_others = [from_snap(sent, i) for i, sent in enumerate(x_sent, 1)]
     first, second = with_neighbours(first, second)
     guess = call(
         predict_kernel,
@@ -424,7 +420,7 @@
         flops=10**9,
         name="predict",
     )
-    message, guess, x_others = lax.optimization_barrier((message, guess, x_others))
+    message, guess = lax.optimization_barrier((message, guess))
     halves = []
     for part in range(2):
         halves.append(
@@ -443,8 +439,8 @@
     reading_others = [from_all(half) for half in readings]
     grads = (
         shape((own, everything, BLK), F32),
-        shape((ties, everything, BLK), F32),
-        shape((ties, everything, BLK), F32),
+        boundary,
+        boundary,
     )
     total = pltpu.VMEM((slots, everything, BLK), F32)
     work = pltpu.VMEM((own, everything, BLK), F32)
@@ -456,12 +452,20 @@
         scratch=[total, pltpu.VMEM((everything, lines), BF16)],
         name="pull",
     )
+    x_late, first, second = lax.optimization_barrier((starting_voltages, first, second))
     arrived = with_neighbours(first, second)
-    boundary = shape((ties, everything, BLK), BF16)
-    state, mine, first = call(
+    me = lax.axis_index("snap")
+    x_others = [
+        from_snap(
+            lax.dynamic_slice_in_dim(x_late, (me + i) % members * held * BLK, held * BLK, 1), i
+        )
+        for i in range(1, members)
+    ]
+    kept, given, mine, first = call(
         first_update_kernel,
         (
-            shape((held, everything, BLK), F32),
+            shape((held, snaps, BLK), F32),
+            [shape((held, snaps, BLK), F32)] * (members - 1),
             shape((held, everything, BLK), BF16),
             boundary,
         ),
@@ -486,7 +490,7 @@
     second = swap_pair(second, 0)
     grad, first, second = call(
         predict_pull_kernel,
-        (grads[0], boundary, boundary),
+        grads,
         [[VMEM] * members, VMEM, VMEM, [VMEM] * 2, [VMEM] * 2, [VMEM] * 2, VMEM, SMEM],
         (firsts, aug, second, readings, reading_others, variance, derivative_pieces, place),
         scratch=[
@@ -497,21 +501,25 @@
         ],
         name="predict_pull",
     )
+    given, first, second = lax.optimization_barrier((given, first, second))
     first, second = with_neighbours(first, second)
-    kept, sent = call(
+    states_in = [from_snap(block, i) for i, block in enumerate(given, 1)]
+    mine, sent = call(
         last_update_kernel,
-        (shape((snaps, held * BLK), F32), shape((members - 1, snaps, held * BLK), F32)),
+        (
+            shape((snaps, held * BLK), F32),
+            [shape((snaps, held * BLK), BF16)] * (members - 1),
+        ),
         [VMEM, VMEM, VMEM, SMEM, VMEM, VMEM],
-        (grad, first, second, ties_table, reciprocal_normal_operator, state),
+        (grad, first, second, ties_table, reciprocal_normal_operator, kept),
         scratch=[work],
         name="last_update",
     )
-    arrived = jnp.stack([from_snap(sent[i - 1], i) for i in range(1, members)])
     return call(
         finish_kernel,
         shape((snaps, states), F32),
-        [VMEM, VMEM],
-        (kept, arrived),
+        [VMEM, [VMEM] * (members - 1), [VMEM] * (members - 1)],
+        (mine, states_in, [from_snap(block, i) for i, block in enumerate(sent, 1)]),
         name="finish",
     )
 

time: 79.1 us -> 80.4 us (1.016)
  waiting for transfers between devices: 30.1 us -> 27 us
  Pallas kernels: 18.1 us -> 20.2 us
  starting transfers between devices: 26.3 us -> 28 us
  local copies, waits for them, and re-layouts: 2.37 us -> 3.62 us
    ppermute x7 -> x8, waiting for transfers between devices: 17.5 us -> 13.7 us  [from_snap(): lax.ppermute(block, 'snap', [(i, (i + distance) % members) for i in range...]
    ppermute x7 -> x8, starting transfers between devices: 7.86 us -> 10.1 us  [from_snap(): lax.ppermute(block, 'snap', [(i, (i + distance) % members) for i in range...]
    pallas_call x12, Pallas kernels: 18.1 us -> 20.2 us  [call(): pl.pallas_call(kernel, out_shape=outs, in_specs=ins, out_specs=jax.tree.m...]
    unnamed x16, local copies, waits for them, and re-layouts: 2.37 us -> 3.6 us
  transfers between devices with their start and end apart: 16 -> 17, of which waited for: 10 -> 9; matrix products, arithmetic and copies ran while one was open for 1% -> 1% of each run, Pallas kernels for 4% -> 6%
where the time goes in v7:
time: 80.4 us; the launch traced here: 79.8 us
  starting transfers between devices  28 us (35%)
  waiting for transfers between devices  27 us (34%)
  Pallas kernels  20.2 us (25%)
  local copies, waits for them, and re-layouts  3.62 us (5%)
  other arithmetic  0.96 us (1%)
    pallas_call x12, Pallas kernels, call(): pl.pallas_call(kernel, out_shape=outs, in_specs=ins, out_specs=jax.tree.m...  20.2 us
    ppermute x8, waiting for transfers between devices, from_snap(): lax.ppermute(block, 'snap', [(i, (i + distance) % members) for i in range...  13.7 us
    ppermute x8, waiting for transfers between devices, swap_pair(): return lax.ppermute(block, 'area', pairs + [(b, a) for a, b in pairs])  13.2 us
    ppermute x8, starting transfers between devices, swap_pair(): return lax.ppermute(block, 'area', pairs + [(b, a) for a, b in pairs])  11.7 us
    ppermute x8, starting transfers between devices, from_snap(): lax.ppermute(block, 'snap', [(i, (i + distance) % members) for i in range...  10.1 us
    all_to_all x1, starting transfers between devices, on_device(): lax.all_to_all(message, 'area', split_axis=0, concat_axis=0, tiled=True)  6.17 us
    unnamed x16, local copies, waits for them, and re-layouts  3.6 us
  transfers between devices with their start and end apart: 17, of which 9 were waited for; matrix products, arithmetic and copies ran while one was open for 1% of the time, Pallas kernels for 6%

profile of v7, /device:TPU:16, one launch (start us, length us, event | category | flops | bytes accessed | tf_op | source)
XLA Modules:
  0.0 79.8 jit_solution(15466216874950881619)
XLA Ops:
  0.0 4.3 %pack_readings.1 = f32[16,72,128]{2,1,0:T(8,128)} custom-call(f32[32,2048]{1,0:T(8,128)} %z_in.1, f32[16,128]{1,0:T(8,128)} %bitcast.24, s32[16,256]{1,0:T(8,128)} %bitcast.23), custom_call_target="tpu_custom_call" | custom-call | tf_op jit(solution)/shard_map/pack_readings/pallas_call | solution.py:21
  4.3 6.2 %all-to-all-start = ((f32[16,72,128]{2,1,0:T(8,128)}), f32[16,72,128]{2,1,0:T(8,128)S(1)}, u32[]{:S(2)}, u32[]{:S(2)}) async-start(f32[16,72,128]{2,1,0:T(8,128)} %pack_readings.1), calls=%async_computation | async-start | bytes 1179648 | tf_op jit(solution)/shard_map/all_to_all | solution.py:388
  10.5 1.0 %convert_element_type.3.own_ref = bf16[32,2048]{1,0:T(8,128)(2,1)S(1)} convert(f32[32,2048]{1,0:T(8,128)} %x_ref.1) | non-fusion elementwise | flops 65536 | bytes 393216 | tf_op jit(solution)/shard_map/convert_element_type | solution.py:365
  11.4 1.6 %collective-permute-start = (bf16[32,2048]{1,0:T(8,128)(2,1)S(1)}, bf16[32,2048]{1,0:T(8,128)(2,1)S(1)}, u32[]{:S(2)}, u32[]{:S(2)}) collective-permute-start(bf16[32,2048]{1,0:T(8,128)(2,1)S(1)} %convert_element_type.3.own_ref), channel_id=1, source_target_pairs={{0,1},{1,0},{2,3},{3,2},{4,5},{5,4},{6,7},{7,6},{8,9},{9,8},{10,11... | collective-permute-start | bytes 393224 | tf_op jit(solution)/shard_map/ppermute | solution.py:324
  13.0 4.0 %collective-permute-done = bf16[32,2048]{1,0:T(8,128)(2,1)S(1)} collective-permute-done((bf16[32,2048]{1,0:T(8,128)(2,1)S(1)}, bf16[32,2048]{1,0:T(8,128)(2,1)S(1)}, u32[]{:S(2)}, u32[]{:S(2)}) %collective-permute-start) | collective-permute-done | bytes 131104 | tf_op jit(solution)/shard_map/ppermute | solution.py:324
  17.1 0.7 copy-done.4
  17.7 0.6 first_states.1
  18.4 2.3 %collective-permute-start.1 = (bf16[4,64,128]{2,1,0:T(8,128)(2,1)S(1)}, bf16[4,64,128]{2,1,0:T(8,128)(2,1)S(1)}, u32[]{:S(2)}, u32[]{:S(2)}) collective-permute-start(bf16[4,64,128]{2,1,0:T(8,128)(2,1)S(1)} %get-tuple-element.37), channel_id=1, source_target_pairs={{2,4},{6,8},{10,12},{14,16},{18,20},{22,24},{26,28},{4,2},{8,6},{1... | collective-permute-start | bytes 196616 | tf_op jit(solution)/shard_map/ppermute | solution.py:315
  20.7 1.3 %collective-permute-start.2 = (bf16[4,64,128]{2,1,0:T(8,128)(2,1)S(1)}, bf16[4,64,128]{2,1,0:T(8,128)(2,1)S(1)}, u32[]{:S(2)}, u32[]{:S(2)}) collective-permute-start(bf16[4,64,128]{2,1,0:T(8,128)(2,1)S(1)} %get-tuple-element.38), channel_id=1, source_target_pairs={{0,2},{4,6},{8,10},{12,14},{16,18},{20,22},{24,26},{28,30},{2,0},{... | collective-permute-start | bytes 196616 | tf_op jit(solution)/shard_map/ppermute | solution.py:315
  22.0 0.7 copy-done.7
  22.7 0.4 invert_order.1
  23.1 3.4 %collective-permute-done.1.first_ref = bf16[4,64,128]{2,1,0:T(8,128)(2,1)S(1)} collective-permute-done((bf16[4,64,128]{2,1,0:T(8,128)(2,1)S(1)}, bf16[4,64,128]{2,1,0:T(8,128)(2,1)S(1)}, u32[]{:S(2)}, u32[]{:S(2)}) %collective-permute-start.1) | collective-permute-done | bytes 65568 | tf_op jit(solution)/shard_map/ppermute | solution.py:315
  26.5 0.0 collective-permute-done.2.second_ref
  26.5 1.4 %predict.1.guess_ref = f32[64,2048]{1,0:T(8,128)S(1)} custom-call(bf16[16,64,128]{2,1,0:T(8,128)(2,1)S(1)} %get-tuple-element.36.aug_ref, bf16[4,64,128]{2,1,0:T(8,128)(2,1)S(1)} %collective-permute-done.1.first_ref, bf16[4,64,128]{2,1,0:T(8,128)(2,1)S(1)} %collective-permute-done.2.second_ref, bf16[16,4,128,128]{3,2,1,0:T(8,128)(2,1)S(1)} %copy-done.2, ...), custom_call_target="tpu_custom_call" | custom-call | flops 1000000000 | tf_op jit(solution)/shard_map/predict/pallas_call | solution.py:21
  27.9 0.0 all-to-all-done.message_ref
  27.9 1.9 %unpack_readings.3 = (f32[32,1024]{1,0:T(8,128)}, f32[1,1024]{1,0:T(1,128)S(1)}) custom-call(s32[16,128]{1,0:T(8,128)S(1)} %get-tuple-element.40.group_ref, s32[16,128]{1,0:T(8,128)S(1)} %get-tuple-element.41.lane_ref, f32[16,72,128]{2,1,0:T(8,128)S(1)} %all-to-all-done.message_ref), custom_call_target="tpu_custom_call" | custom-call | flops 2000000000 | tf_op jit(solution)/shard_map/unpack_readings/pallas_call | solution.py:21
  29.7 1.9 %unpack_readings.2 = (f32[32,1024]{1,0:T(8,128)}, f32[1,1024]{1,0:T(1,128)S(1)}) custom-call(s32[16,128]{1,0:T(8,128)S(1)} %get-tuple-element.40.group_ref, s32[16,128]{1,0:T(8,128)S(1)} %get-tuple-element.41.lane_ref, f32[16,72,128]{2,1,0:T(8,128)S(1)} %all-to-all-done.message_ref), custom_call_target="tpu_custom_call" | custom-call | flops 2000000000 | tf_op jit(solution)/shard_map/unpack_readings/pallas_call | solution.py:21
  31.6 1.5 %collective-permute-start.4 = (f32[32,1024]{1,0:T(8,128)}, f32[32,1024]{1,0:T(8,128)S(1)}, u32[]{:S(2)}, u32[]{:S(2)}) collective-permute-start(f32[32,1024]{1,0:T(8,128)} %get-tuple-element.44.z_refs_1_), channel_id=1, source_target_pairs={{0,1},{1,0},{2,3},{3,2},{4,5},{5,4},{6,7},{7,6},{8,9},{9,8},{10,11... | collective-permute-start | bytes 393224 | tf_op jit(solution)/shard_map/ppermute | solution.py:324
  33.1 0.5 collective-permute-start.3
  33.6 3.2 %collective-permute-done.4 = f32[32,1024]{1,0:T(8,128)S(1)} collective-permute-done((f32[32,1024]{1,0:T(8,128)}, f32[32,1024]{1,0:T(8,128)S(1)}, u32[]{:S(2)}, u32[]{:S(2)}) %collective-permute-start.4) | collective-permute-done | bytes 131104 | tf_op jit(solution)/shard_map/ppermute | solution.py:324
  36.8 1.5 %collective-permute-done.3 = f32[32,1024]{1,0:T(8,128)S(1)} collective-permute-done((f32[32,1024]{1,0:T(8,128)}, f32[32,1024]{1,0:T(8,128)S(1)}, u32[]{:S(2)}, u32[]{:S(2)}) %collective-permute-start.3) | collective-permute-done | bytes 131104 | tf_op jit(solution)/shard_map/ppermute | solution.py:324
  38.3 1.8 %pull.1 = (f32[16,64,128]{2,1,0:T(8,128)S(1)}, bf16[4,64,128]{2,1,0:T(8,128)(2,1)S(1)}, bf16[4,64,128]{2,1,0:T(8,128)(2,1)S(1)}) custom-call(f32[64,2048]{1,0:T(8,128)S(1)} %predict.1.guess_ref, f32[32,1024]{1,0:T(8,128)} %get-tuple-element.43.z_refs_0_, f32[32,1024]{1,0:T(8,128)} %get-tuple-element.44.z_refs_1_, f32[1,32,1024]{2,1,0:T(8,128)S(1)} %bitcast.12, ...), custom_call_target="tpu_custom_call" | custom-call | tf_op jit(solution)/shard_map/pull/pallas_call | solution.py:21
  40.2 1.5 %collective-permute-start.7 = (f32[32,1024]{1,0:T(8,128)S(1)}, f32[32,1024]{1,0:T(8,128)S(1)}, u32[]{:S(2)}, u32[]{:S(2)}) collective-permute-start(f32[32,1024]{1,0:T(8,128)S(1)} %constant_dynamic-slice_fusion), channel_id=1, source_target_pairs={{0,1},{1,0},{2,3},{3,2},{4,5},{5,4},{6,7},{7,6},{8,9},{9,8},{10,11... | collective-permute-start | bytes 393224 | tf_op jit(solution)/shard_map/ppermute | solution.py:324
  41.7 2.8 %collective-permute-start.5 = (bf16[4,64,128]{2,1,0:T(8,128)(2,1)S(1)}, bf16[4,64,128]{2,1,0:T(8,128)(2,1)S(1)}, u32[]{:S(2)}, u32[]{:S(2)}) collective-permute-start(bf16[4,64,128]{2,1,0:T(8,128)(2,1)S(1)} %get-tuple-element.50), channel_id=1, source_target_pairs={{2,4},{6,8},{10,12},{14,16},{18,20},{22,24},{26,28},{4,2},{8,6},{1... | collective-permute-start | bytes 196616 | tf_op jit(solution)/shard_map/ppermute | solution.py:315
  44.5 0.5 collective-permute-start.6
  44.9 3.2 %collective-permute-done.5.back_first_ref = bf16[4,64,128]{2,1,0:T(8,128)(2,1)S(1)} collective-permute-done((bf16[4,64,128]{2,1,0:T(8,128)(2,1)S(1)}, bf16[4,64,128]{2,1,0:T(8,128)(2,1)S(1)}, u32[]{:S(2)}, u32[]{:S(2)}) %collective-permute-start.5) | collective-permute-done | bytes 65568 | tf_op jit(solution)/shard_map/ppermute | solution.py:315
  48.1 0.0 collective-permute-done.6.back_second_ref
  48.1 0.0 copy-start
  48.2 2.2 %copy-done = bf16[1024,2048]{1,0:T(8,128)(2,1)S(1)} copy-done((bf16[1024,2048]{1,0:T(8,128)(2,1)S(1)}, bf16[1024,2048]{1,0:T(8,128)(2,1)}, u32[]{:S(2)}) %copy-start) | copy-done | bytes 4194328
  50.3 2.1 %first_update.1 = (f32[8,32,128]{2,1,0:T(8,128)S(1)}, f32[8,32,128]{2,1,0:T(8,128)S(1)}, bf16[8,64,128]{2,1,0:T(8,128)(2,1)S(1)}, bf16[4,64,128]{2,1,0:T(8,128)(2,1)S(1)}) custom-call(f32[16,64,128]{2,1,0:T(8,128)S(1)} %get-tuple-element.47.grad_ref, bf16[4,64,128]{2,1,0:T(8,128)(2,1)S(1)} %collective-permute-done.5.back_first_ref, ...), custom_call_target="tpu_custom_call" | custom-call | tf_op jit(solution)/shard_map/first_update/pallas_call | solution.py:21
  52.4 0.7 collective-permute-start.10
  53.1 2.4 %collective-permute-start.8 = (bf16[4,64,128]{2,1,0:T(8,128)(2,1)S(1)}, bf16[4,64,128]{2,1,0:T(8,128)(2,1)S(1)}, u32[]{:S(2)}, u32[]{:S(2)}) collective-permute-start(bf16[4,64,128]{2,1,0:T(8,128)(2,1)S(1)} %get-tuple-element.53), channel_id=1, source_target_pairs={{2,4},{6,8},{10,12},{14,16},{18,20},{22,24},{26,28},{4,2},{8,6},{1... | collective-permute-start | bytes 196616 | tf_op jit(solution)/shard_map/ppermute | solution.py:315
  55.5 4.0 %collective-permute-done.8.first_refs_0_ = bf16[4,64,128]{2,1,0:T(8,128)(2,1)S(1)} collective-permute-done((bf16[4,64,128]{2,1,0:T(8,128)(2,1)S(1)}, bf16[4,64,128]{2,1,0:T(8,128)(2,1)S(1)}, u32[]{:S(2)}, u32[]{:S(2)}) %collective-permute-start.8) | collective-permute-done | bytes 65568 | tf_op jit(solution)/shard_map/ppermute | solution.py:315
  59.6 1.4 %collective-permute-start.9 = (bf16[4,64,128]{2,1,0:T(8,128)(2,1)S(1)}, bf16[4,64,128]{2,1,0:T(8,128)(2,1)S(1)}, u32[]{:S(2)}, u32[]{:S(2)}) collective-permute-start(bf16[4,64,128]{2,1,0:T(8,128)(2,1)S(1)} %collective-permute-done.8.first_refs_0_), channel_id=1, source_target_pairs={{0,1},{1,0},{2,3},{3,2},{4,5},{5,4},{6,7},{7,6},{8,9},{9,8},{10,11... | collective-permute-start | bytes 196616 | tf_op jit(solution)/shard_map/ppermute | solution.py:324
  61.0 0.0 collective-permute-done.10.others_refs_0_
  61.0 0.6 join_states.1
  61.6 0.1 collective-permute-start.11
  61.7 2.2 %collective-permute-done.9.first_refs_1_ = bf16[4,64,128]{2,1,0:T(8,128)(2,1)S(1)} collective-permute-done((bf16[4,64,128]{2,1,0:T(8,128)(2,1)S(1)}, bf16[4,64,128]{2,1,0:T(8,128)(2,1)S(1)}, u32[]{:S(2)}, u32[]{:S(2)}) %collective-permute-start.9) | collective-permute-done | bytes 65568 | tf_op jit(solution)/shard_map/ppermute | solution.py:324
  63.8 0.0 collective-permute-done.11.second_in_ref
  63.8 2.4 %predict_pull.1 = (f32[16,64,128]{2,1,0:T(8,128)S(1)}, bf16[4,64,128]{2,1,0:T(8,128)(2,1)S(1)}, bf16[4,64,128]{2,1,0:T(8,128)(2,1)S(1)}) custom-call(bf16[4,64,128]{2,1,0:T(8,128)(2,1)S(1)} %collective-permute-done.8.first_refs_0_, bf16[4,64,128]{2,1,0:T(8,128)(2,1)S(1)} %collective-permute-done.9.first_refs_1_, ...), custom_call_target="tpu_custom_call" | custom-call | tf_op jit(solution)/shard_map/predict_pull/pallas_call | solution.py:21
  66.2 1.9 %collective-permute-start.12 = (bf16[4,64,128]{2,1,0:T(8,128)(2,1)S(1)}, bf16[4,64,128]{2,1,0:T(8,128)(2,1)S(1)}, u32[]{:S(2)}, u32[]{:S(2)}) collective-permute-start(bf16[4,64,128]{2,1,0:T(8,128)(2,1)S(1)} %get-tuple-element.61), channel_id=1, source_target_pairs={{2,4},{6,8},{10,12},{14,16},{18,20},{22,24},{26,28},{4,2},{8,6},{1... | collective-permute-start | bytes 196616 | tf_op jit(solution)/shard_map/ppermute | solution.py:315
  68.2 0.4 collective-permute-start.13
  68.6 1.5 %collective-permute-start.14 = (f32[8,32,128]{2,1,0:T(8,128)S(1)}, f32[8,32,128]{2,1,0:T(8,128)S(1)}, u32[]{:S(2)}, u32[]{:S(2)}) collective-permute-start(f32[8,32,128]{2,1,0:T(8,128)S(1)} %get-tuple-element.65), channel_id=1, source_target_pairs={{0,1},{1,0},{2,3},{3,2},{4,5},{5,4},{6,7},{7,6},{8,9},{9,8},{10,11... | collective-permute-start | bytes 393224 | tf_op jit(solution)/shard_map/ppermute | solution.py:324
  70.1 2.6 %collective-permute-done.12.back_first_ref = bf16[4,64,128]{2,1,0:T(8,128)(2,1)S(1)} collective-permute-done((bf16[4,64,128]{2,1,0:T(8,128)(2,1)S(1)}, bf16[4,64,128]{2,1,0:T(8,128)(2,1)S(1)}, u32[]{:S(2)}, u32[]{:S(2)}) %collective-permute-start.12) | collective-permute-done | bytes 65568 | tf_op jit(solution)/shard_map/ppermute | solution.py:315
  72.7 2.0 %last_update.1 = (f32[32,1024]{1,0:T(8,128)S(1)}, bf16[32,1024]{1,0:T(8,128)(2,1)S(1)}) custom-call(f32[16,64,128]{2,1,0:T(8,128)S(1)} %get-tuple-element.57.grad_ref, bf16[4,64,128]{2,1,0:T(8,128)(2,1)S(1)} %collective-permute-done.12.back_first_ref, bf16[4,64,128]{2,1,0:T(8,128)(2,1)S(1)} %collective-permute-done.13.back_second_ref, s32[2,4]{1,0:T(2,128)S(1)} %bitcast.18, ...), custom_call_target="tpu_custom_call" | custom-call | tf_op jit(solution)/shard_map/last_update/pallas_call | solution.py:21
  74.8 1.5 %collective-permute-start.15 = (bf16[32,1024]{1,0:T(8,128)(2,1)S(1)}, bf16[32,1024]{1,0:T(8,128)(2,1)S(1)}, u32[]{:S(2)}, u32[]{:S(2)}) collective-permute-start(bf16[32,1024]{1,0:T(8,128)(2,1)S(1)} %get-tuple-element.66), channel_id=1, source_target_pairs={{0,1},{1,0},{2,3},{3,2},{4,5},{5,4},{6,7},{7,6},{8,9},{9,8},{10,11... | collective-permute-start | bytes 196616 | tf_op jit(solution)/shard_map/ppermute | solution.py:324
  76.2 2.9 %collective-permute-done.15.updates_refs_0_ = bf16[32,1024]{1,0:T(8,128)(2,1)S(1)} collective-permute-done((bf16[32,1024]{1,0:T(8,128)(2,1)S(1)}, bf16[32,1024]{1,0:T(8,128)(2,1)S(1)}, u32[]{:S(2)}, u32[]{:S(2)}) %collective-permute-start.15) | collective-permute-done | bytes 65568 | tf_op jit(solution)/shard_map/ppermute | solution.py:324
  79.1 0.7 finish.1
  (16 shorter events, 0.0 us)
Async XLA Ops:
  0.0 26.5 %copy-start.2 = (bf16[16,4,128,128]{3,2,1,0:T(8,128)(2,1)S(1)}, bf16[16,4,128,128]{3,2,1,0:T(8,128)(2,1)}, u32[]{:S(2)}) copy-start(bf16[16,4,128,128]{3,2,1,0:T(8,128)(2,1)} %tiles_ref.5) | copy-start | bytes 6291460
  0.0 26.5 %copy-start.6 = (s32[1,16,4]{1,2,0:T(4,128)S(1)}, s32[1,16,4]{1,2,0:T(4,128)}, u32[]{:S(2)}) copy-start(s32[1,16,4]{1,2,0:T(4,128)} %param.13) | copy-start | bytes 772
  4.3 23.6 %all-to-all-start = ((f32[16,72,128]{2,1,0:T(8,128)}), f32[16,72,128]{2,1,0:T(8,128)S(1)}, u32[]{:S(2)}, u32[]{:S(2)}) async-start(f32[16,72,128]{2,1,0:T(8,128)} %pack_readings.1), calls=%async_computation | async-start | bytes 1179648 | tf_op jit(solution)/shard_map/all_to_all | solution.py:388
  11.4 5.6 %collective-permute-start = (bf16[32,2048]{1,0:T(8,128)(2,1)S(1)}, bf16[32,2048]{1,0:T(8,128)(2,1)S(1)}, u32[]{:S(2)}, u32[]{:S(2)}) collective-permute-start(bf16[32,2048]{1,0:T(8,128)(2,1)S(1)} %convert_element_type.3.own_ref), channel_id=1, source_target_pairs={{0,1},{1,0},{2,3},{3,2},{4,5},{5,4},{6,7},{7,6},{8,9},{9,8},{10,11... | collective-permute-start | bytes 393224 | tf_op jit(solution)/shard_map/ppermute | solution.py:324
  17.1 0.7 copy-start.4
  18.4 8.1 %collective-permute-start.1 = (bf16[4,64,128]{2,1,0:T(8,128)(2,1)S(1)}, bf16[4,64,128]{2,1,0:T(8,128)(2,1)S(1)}, u32[]{:S(2)}, u32[]{:S(2)}) collective-permute-start(bf16[4,64,128]{2,1,0:T(8,128)(2,1)S(1)} %get-tuple-element.37), channel_id=1, source_target_pairs={{2,4},{6,8},{10,12},{14,16},{18,20},{22,24},{26,28},{4,2},{8,6},{1... | collective-permute-start | bytes 196616 | tf_op jit(solution)/shard_map/ppermute | solution.py:315
  20.7 5.8 %collective-permute-start.2 = (bf16[4,64,128]{2,1,0:T(8,128)(2,1)S(1)}, bf16[4,64,128]{2,1,0:T(8,128)(2,1)S(1)}, u32[]{:S(2)}, u32[]{:S(2)}) collective-permute-start(bf16[4,64,128]{2,1,0:T(8,128)(2,1)S(1)} %get-tuple-element.38), channel_id=1, source_target_pairs={{0,2},{4,6},{8,10},{12,14},{16,18},{20,22},{24,26},{28,30},{2,0},{... | collective-permute-start | bytes 196616 | tf_op jit(solution)/shard_map/ppermute | solution.py:315
  21.9 0.7 copy-start.7
  29.7 10.4 %copy-start.3 = (f32[32,2048]{1,0:T(8,128)S(1)}, f32[32,2048]{1,0:T(8,128)}, u32[]{:S(2)}) copy-start(f32[32,2048]{1,0:T(8,128)} %x_ref.1) | copy-start | bytes 786436
  29.7 18.4 %copy-start.5 = (s32[1,2,4]{2,1,0:T(2,128)S(1)}, s32[1,2,4]{2,1,0:T(2,128)}, u32[]{:S(2)}) copy-start(s32[1,2,4]{2,1,0:T(2,128)} %param.14) | copy-start | bytes 100
  31.6 5.2 %collective-permute-start.4 = (f32[32,1024]{1,0:T(8,128)}, f32[32,1024]{1,0:T(8,128)S(1)}, u32[]{:S(2)}, u32[]{:S(2)}) collective-permute-start(f32[32,1024]{1,0:T(8,128)} %get-tuple-element.44.z_refs_1_), channel_id=1, source_target_pairs={{0,1},{1,0},{2,3},{3,2},{4,5},{5,4},{6,7},{7,6},{8,9},{9,8},{10,11... | collective-permute-start | bytes 393224 | tf_op jit(solution)/shard_map/ppermute | solution.py:324
  33.1 5.2 %collective-permute-start.3 = (f32[32,1024]{1,0:T(8,128)}, f32[32,1024]{1,0:T(8,128)S(1)}, u32[]{:S(2)}, u32[]{:S(2)}) collective-permute-start(f32[32,1024]{1,0:T(8,128)} %get-tuple-element.43.z_refs_0_), channel_id=1, source_target_pairs={{0,1},{1,0},{2,3},{3,2},{4,5},{5,4},{6,7},{7,6},{8,9},{9,8},{10,11... | collective-permute-start | bytes 393224 | tf_op jit(solution)/shard_map/ppermute | solution.py:324
  40.2 7.9 %collective-permute-start.7 = (f32[32,1024]{1,0:T(8,128)S(1)}, f32[32,1024]{1,0:T(8,128)S(1)}, u32[]{:S(2)}, u32[]{:S(2)}) collective-permute-start(f32[32,1024]{1,0:T(8,128)S(1)} %constant_dynamic-slice_fusion), channel_id=1, source_target_pairs={{0,1},{1,0},{2,3},{3,2},{4,5},{5,4},{6,7},{7,6},{8,9},{9,8},{10,11... | collective-permute-start | bytes 393224 | tf_op jit(solution)/shard_map/ppermute | solution.py:324
  41.7 6.5 %collective-permute-start.5 = (bf16[4,64,128]{2,1,0:T(8,128)(2,1)S(1)}, bf16[4,64,128]{2,1,0:T(8,128)(2,1)S(1)}, u32[]{:S(2)}, u32[]{:S(2)}) collective-permute-start(bf16[4,64,128]{2,1,0:T(8,128)(2,1)S(1)} %get-tuple-element.50), channel_id=1, source_target_pairs={{2,4},{6,8},{10,12},{14,16},{18,20},{22,24},{26,28},{4,2},{8,6},{1... | collective-permute-start | bytes 196616 | tf_op jit(solution)/shard_map/ppermute | solution.py:315
  44.5 3.6 %collective-permute-start.6 = (bf16[4,64,128]{2,1,0:T(8,128)(2,1)S(1)}, bf16[4,64,128]{2,1,0:T(8,128)(2,1)S(1)}, u32[]{:S(2)}, u32[]{:S(2)}) collective-permute-start(bf16[4,64,128]{2,1,0:T(8,128)(2,1)S(1)} %get-tuple-element.51), channel_id=1, source_target_pairs={{0,2},{4,6},{8,10},{12,14},{16,18},{20,22},{24,26},{28,30},{2,0},{... | collective-permute-start | bytes 196616 | tf_op jit(solution)/shard_map/ppermute | solution.py:315
  48.1 2.2 %copy-start = (bf16[1024,2048]{1,0:T(8,128)(2,1)S(1)}, bf16[1024,2048]{1,0:T(8,128)(2,1)}, u32[]{:S(2)}) copy-start(bf16[1024,2048]{1,0:T(8,128)(2,1)} %gain_ref.3) | copy-start | bytes 12582916
  50.3 22.4 %copy-start.1 = (bf16[1024,2048]{1,0:T(8,128)(2,1)S(1)}, bf16[1024,2048]{1,0:T(8,128)(2,1)}, u32[]{:S(2)}) copy-start(bf16[1024,2048]{1,0:T(8,128)(2,1)} %gain_ref.3) | copy-start | bytes 12582916
  52.4 8.6 %collective-permute-start.10 = (bf16[8,64,128]{2,1,0:T(8,128)(2,1)S(1)}, bf16[8,64,128]{2,1,0:T(8,128)(2,1)S(1)}, u32[]{:S(2)}, u32[]{:S(2)}) collective-permute-start(bf16[8,64,128]{2,1,0:T(8,128)(2,1)S(1)} %get-tuple-element.54.mine_ref), channel_id=1, source_target_pairs={{0,1},{1,0},{2,3},{3,2},{4,5},{5,4},{6,7},{7,6},{8,9},{9,8},{10,11... | collective-permute-start | bytes 393224 | tf_op jit(solution)/shard_map/ppermute | solution.py:324
  53.1 6.5 %collective-permute-start.8 = (bf16[4,64,128]{2,1,0:T(8,128)(2,1)S(1)}, bf16[4,64,128]{2,1,0:T(8,128)(2,1)S(1)}, u32[]{:S(2)}, u32[]{:S(2)}) collective-permute-start(bf16[4,64,128]{2,1,0:T(8,128)(2,1)S(1)} %get-tuple-element.53), channel_id=1, source_target_pairs={{2,4},{6,8},{10,12},{14,16},{18,20},{22,24},{26,28},{4,2},{8,6},{1... | collective-permute-start | bytes 196616 | tf_op jit(solution)/shard_map/ppermute | solution.py:315
  59.6 4.3 %collective-permute-start.9 = (bf16[4,64,128]{2,1,0:T(8,128)(2,1)S(1)}, bf16[4,64,128]{2,1,0:T(8,128)(2,1)S(1)}, u32[]{:S(2)}, u32[]{:S(2)}) collective-permute-start(bf16[4,64,128]{2,1,0:T(8,128)(2,1)S(1)} %collective-permute-done.8.first_refs_0_), channel_id=1, source_target_pairs={{0,1},{1,0},{2,3},{3,2},{4,5},{5,4},{6,7},{7,6},{8,9},{9,8},{10,11... | collective-permute-start | bytes 196616 | tf_op jit(solution)/shard_map/ppermute | solution.py:324
  61.6 2.3 %collective-permute-start.11 = (bf16[4,64,128]{2,1,0:T(8,128)(2,1)S(1)}, bf16[4,64,128]{2,1,0:T(8,128)(2,1)S(1)}, u32[]{:S(2)}, u32[]{:S(2)}) collective-permute-start(bf16[4,64,128]{2,1,0:T(8,128)(2,1)S(1)} %get-tuple-element.56), channel_id=1, source_target_pairs={{0,2},{4,6},{8,10},{12,14},{16,18},{20,22},{24,26},{28,30},{2,0},{... | collective-permute-start | bytes 196616 | tf_op jit(solution)/shard_map/ppermute | solution.py:315
  66.2 6.5 %collective-permute-start.12 = (bf16[4,64,128]{2,1,0:T(8,128)(2,1)S(1)}, bf16[4,64,128]{2,1,0:T(8,128)(2,1)S(1)}, u32[]{:S(2)}, u32[]{:S(2)}) collective-permute-start(bf16[4,64,128]{2,1,0:T(8,128)(2,1)S(1)} %get-tuple-element.61), channel_id=1, source_target_pairs={{2,4},{6,8},{10,12},{14,16},{18,20},{22,24},{26,28},{4,2},{8,6},{1... | collective-permute-start | bytes 196616 | tf_op jit(solution)/shard_map/ppermute | solution.py:315
  68.2 4.6 %collective-permute-start.13 = (bf16[4,64,128]{2,1,0:T(8,128)(2,1)S(1)}, bf16[4,64,128]{2,1,0:T(8,128)(2,1)S(1)}, u32[]{:S(2)}, u32[]{:S(2)}) collective-permute-start(bf16[4,64,128]{2,1,0:T(8,128)(2,1)S(1)} %get-tuple-element.62), channel_id=1, source_target_pairs={{0,2},{4,6},{8,10},{12,14},{16,18},{20,22},{24,26},{28,30},{2,0},{... | collective-permute-start | bytes 196616 | tf_op jit(solution)/shard_map/ppermute | solution.py:315
  68.6 10.5 %collective-permute-start.14 = (f32[8,32,128]{2,1,0:T(8,128)S(1)}, f32[8,32,128]{2,1,0:T(8,128)S(1)}, u32[]{:S(2)}, u32[]{:S(2)}) collective-permute-start(f32[8,32,128]{2,1,0:T(8,128)S(1)} %get-tuple-element.65), channel_id=1, source_target_pairs={{0,1},{1,0},{2,3},{3,2},{4,5},{5,4},{6,7},{7,6},{8,9},{9,8},{10,11... | collective-permute-start | bytes 393224 | tf_op jit(solution)/shard_map/ppermute | solution.py:324
  74.8 4.3 %collective-permute-start.15 = (bf16[32,1024]{1,0:T(8,128)(2,1)S(1)}, bf16[32,1024]{1,0:T(8,128)(2,1)S(1)}, u32[]{:S(2)}, u32[]{:S(2)}) collective-permute-start(bf16[32,1024]{1,0:T(8,128)(2,1)S(1)} %get-tuple-element.66), channel_id=1, source_target_pairs={{0,1},{1,0},{2,3},{3,2},{4,5},{5,4},{6,7},{7,6},{8,9},{9,8},{10,11... | collective-permute-start | bytes 196616 | tf_op jit(solution)/shard_map/ppermute | solution.py:324

commit v8 on v7

--- a/solution.py
+++ b/solution.py
@@ -17,12 +17,12 @@
 SMEM = pl.BlockSpec(memory_space=pltpu.SMEM)
 
 
-def call(kernel, outs, ins, args, scratch=(), flops=0, mib=12, out_spec=VMEM, name=None):
+def call(kernel, outs, ins, args, scratch=(), flops=0, mib=12, out_spec=None, name=None):
     return pl.pallas_call(
         kernel,
         out_shape=outs,
         in_specs=ins,
-        out_specs=jax.tree.map(lambda _: out_spec, outs),
+        out_specs=jax.tree.map(lambda _: VMEM, outs) if out_spec is None else out_spec,
         scratch_shapes=list(scratch),
         compiler_params=pltpu.CompilerParams(vmem_limit_bytes=mib * 1024 * 1024),
         cost_estimate=pl.CostEstimate(
@@ -40,15 +40,27 @@
     return lax.broadcasted_iota(jnp.int32, shape, 0)
 
 
-def pack_kernel(z_in, v_in, hub_in, out, z_ref, v_ref, hub_ref, out_ref, sems, out_sems):
+def pack_kernel(
+    z_in, v_in, hub_in, x_in, out, rounded_ref, sent_refs,
+    z_ref, v_ref, hub_ref, x_ref, out_ref, sems, out_sems, sent_sems,
+):
+    pairs = ((hub_in, hub_ref), (z_in, z_ref), (v_in, v_ref), (x_in, x_ref))
     copies = [
         pltpu.make_async_copy(source, target, sems.at[i])
-        for i, (source, target) in enumerate(((hub_in, hub_ref), (z_in, z_ref), (v_in, v_ref)))
+        for i, (source, target) in enumerate(pairs)
     ]
-    for copy in copies:
+    members = len(sent_refs) + 1
+    part = x_in.shape[1] // members
+    sends = []
+    for i, sent_ref in enumerate(sent_refs, 1):
+        at = lax.rem(lax.axis_index("snap") + i, members) * part
+        source = x_in.at[:, pl.ds(pl.multiple_of(at, BLK), part)]
+        sends.append(pltpu.make_async_copy(source, sent_ref, sent_sems.at[i - 1]))
+    for copy in copies + sends:
         copy.start()
     for copy in copies:
         copy.wait()
+    rounded_ref[...] = x_ref[...].astype(BF16)
     snaps, lines = z_ref.shape
     blocks = lines // BLK
     chunks, width = hub_ref.shape
@@ -74,6 +86,8 @@
         pltpu.make_async_copy(out_ref.at[d], out.at[d], out_sems.at[d]).start()
     for d in range(chunks):
         pltpu.make_async_copy(out_ref.at[d], out.at[d], out_sems.at[d]).wait()
+    for copy in sends:
+        copy.wait()
 
 
 def inverse_kernel(own_ref, group_ref, lane_ref):
@@ -362,25 +376,35 @@
     holder = holder_line_order[0].reshape(chunks, width)
     depth = (width // BLK) * snaps + 8
 
-    rounded = starting_voltages.astype(BF16)
-    rounded_others = from_all(rounded)
-    message = call(
+    message, rounded, x_sent = call(
         pack_kernel,
-        shape((chunks, depth, BLK), F32),
-        [HBM, HBM, HBM],
-        (phasor_readings, reading_error_spread.reshape(lines // BLK, BLK), hub),
+        (
+            shape((chunks, depth, BLK), F32),
+            shape((snaps, states), BF16),
+            [shape((snaps, held * BLK), F32)] * (members - 1),
+        ),
+        [HBM] * 4,
+        (
+            phasor_readings,
+            reading_error_spread.reshape(lines // BLK, BLK),
+            hub,
+            starting_voltages,
+        ),
         scratch=[
             pltpu.VMEM((snaps, lines), F32),
             pltpu.VMEM((lines // BLK, BLK), F32),
             pltpu.VMEM((chunks, width), jnp.int32),
+            pltpu.VMEM((snaps, states), F32),
             pltpu.VMEM((chunks, depth, BLK), F32),
-            pltpu.SemaphoreType.DMA((3,)),
+            pltpu.SemaphoreType.DMA((4,)),
             pltpu.SemaphoreType.DMA((chunks,)),
+            pltpu.SemaphoreType.DMA((members,)),
         ],
-        out_spec=HBM,
+        out_spec=(HBM, VMEM, [HBM] * (members - 1)),
         mib=60,
         name="pack_readings",
     )
+    rounded_others = from_all(rounded)
     each = width // cap
     if each > 1:
         message = message.reshape(chunks, depth, each, cap).transpose(0, 2, 1, 3)
@@ -410,7 +434,9 @@
         (rounded, rounded_others, ties_table),
         name="first_states",
     )
+    first, second, x_sent = lax.optimization_barrier((first, second, x_sent))
     first, second = with_neighbours(first, second)
+    x_others = [from_snap(block, i) for i, block in enumerate(x_sent, 1)]
     guess = call(
         predict_kernel,
         shape((everything, lines), F32),
@@ -420,7 +446,7 @@
         flops=10**9,
         name="predict",
     )
-    message, guess = lax.optimization_barrier((message, guess))
+    message, guess, x_others = lax.optimization_barrier((message, guess, x_others))
     halves = []
     for part in range(2):
         halves.append(
@@ -452,15 +478,7 @@
         scratch=[total, pltpu.VMEM((everything, lines), BF16)],
         name="pull",
     )
-    x_late, first, second = lax.optimization_barrier((starting_voltages, first, second))
     arrived = with_neighbours(first, second)
-    me = lax.axis_index("snap")
-    x_others = [
-        from_snap(
-            lax.dynamic_slice_in_dim(x_late, (me + i) % members * held * BLK, held * BLK, 1), i
-        )
-        for i in range(1, members)
-    ]
     kept, given, mine, first = call(
         first_update_kernel,
         (

time: 80.4 us -> 78.3 us (0.974)
  waiting for transfers between devices: 27 us -> 24.6 us
  starting transfers between devices: 28 us -> 29.8 us
  other arithmetic: 0.96 us -> 0 us
    ppermute x8, waiting for transfers between devices: 13.2 us -> 8.9 us  [swap_pair(): return lax.ppermute(block, 'area', pairs + [(b, a) for a, b in pairs])]
    ppermute x8, starting transfers between devices: 11.7 us -> 15.3 us  [swap_pair(): return lax.ppermute(block, 'area', pairs + [(b, a) for a, b in pairs])]
    ppermute x8, waiting for transfers between devices: 13.7 us -> 15.7 us  [from_snap(): lax.ppermute(block, 'snap', [(i, (i + distance) % members) for i in range...]
    ppermute x8, starting transfers between devices: 10.1 us -> 8.35 us  [from_snap(): lax.ppermute(block, 'snap', [(i, (i + distance) % members) for i in range...]
    convert_element_type x1 -> x0, other arithmetic: 0.96 us -> none  [on_device(): rounded = starting_voltages.astype(BF16)]
    unnamed x16 -> x18, local copies, waits for them, and re-layouts: 3.6 us -> 3.01 us
  transfers between devices with their start and end apart: 17 -> 17, of which waited for: 9 -> 9; matrix products, arithmetic and copies ran while one was open for 1% -> 0% of each run, Pallas kernels for 6% -> 7%
where the time goes in v8:
time: 78.3 us; the launch traced here: 77.3 us
  starting transfers between devices  29.8 us (38%)
  waiting for transfers between devices  24.6 us (31%)
  Pallas kernels  19.7 us (25%)
  local copies, waits for them, and re-layouts  3.01 us (4%)
    pallas_call x12, Pallas kernels, call(): pl.pallas_call(kernel, out_shape=outs, in_specs=ins, out_specs=jax.tree.m...  19.7 us
    ppermute x8, waiting for transfers between devices, from_snap(): lax.ppermute(block, 'snap', [(i, (i + distance) % members) for i in range...  15.7 us
    ppermute x8, starting transfers between devices, swap_pair(): return lax.ppermute(block, 'area', pairs + [(b, a) for a, b in pairs])  15.3 us
    ppermute x8, waiting for transfers between devices, swap_pair(): return lax.ppermute(block, 'area', pairs + [(b, a) for a, b in pairs])  8.9 us
    ppermute x8, starting transfers between devices, from_snap(): lax.ppermute(block, 'snap', [(i, (i + distance) % members) for i in range...  8.35 us
    all_to_all x1, starting transfers between devices, on_device(): lax.all_to_all(message, 'area', split_axis=0, concat_axis=0, tiled=True)  6.17 us
    unnamed x18, local copies, waits for them, and re-layouts  3.01 us
  transfers between devices with their start and end apart: 17, of which 9 were waited for; matrix products, arithmetic and copies ran while one was open for 0% of the time, Pallas kernels for 7%

profile of v8, /device:TPU:16, one launch (start us, length us, event | category | flops | bytes accessed | tf_op | source)
XLA Modules:
  0.0 77.3 jit_solution(2739383343032104639)
XLA Ops:
  0.0 5.9 %pack_readings.1 = (f32[16,72,128]{2,1,0:T(8,128)}, bf16[32,2048]{1,0:T(8,128)(2,1)}, f32[32,1024]{1,0:T(8,128)}) custom-call(f32[32,2048]{1,0:T(8,128)} %z_in.1, f32[16,128]{1,0:T(8,128)} %bitcast.24, s32[16,256]{1,0:T(8,128)} %bitcast.23, f32[32,2048]{1,0:T(8,128)} %x_ref.1), custom_call_target="tpu_custom_call" | custom-call | tf_op jit(solution)/shard_map/pack_readings/pallas_call | solution.py:21
  5.9 6.2 %all-to-all-start = ((f32[16,72,128]{2,1,0:T(8,128)}), f32[16,72,128]{2,1,0:T(8,128)S(1)}, u32[]{:S(2)}, u32[]{:S(2)}) async-start(f32[16,72,128]{2,1,0:T(8,128)} %get-tuple-element.40), calls=%async_computation | async-start | bytes 1179648 | tf_op jit(solution)/shard_map/all_to_all | solution.py:412
  12.1 1.5 %collective-permute-start = (bf16[32,2048]{1,0:T(8,128)(2,1)}, bf16[32,2048]{1,0:T(8,128)(2,1)S(1)}, u32[]{:S(2)}, u32[]{:S(2)}) collective-permute-start(bf16[32,2048]{1,0:T(8,128)(2,1)} %get-tuple-element.41.own_ref), channel_id=1, source_target_pairs={{0,1},{1,0},{2,3},{3,2},{4,5},{5,4},{6,7},{7,6},{8,9},{9,8},{10,11... | collective-permute-start | bytes 393224 | tf_op jit(solution)/shard_map/ppermute | solution.py:338
  13.6 4.2 %collective-permute-done = bf16[32,2048]{1,0:T(8,128)(2,1)S(1)} collective-permute-done((bf16[32,2048]{1,0:T(8,128)(2,1)}, bf16[32,2048]{1,0:T(8,128)(2,1)S(1)}, u32[]{:S(2)}, u32[]{:S(2)}) %collective-permute-start) | collective-permute-done | bytes 131104 | tf_op jit(solution)/shard_map/ppermute | solution.py:338
  17.9 0.9 %copy-done.3 = bf16[32,2048]{1,0:T(8,128)(2,1)S(1)} copy-done((bf16[32,2048]{1,0:T(8,128)(2,1)S(1)}, bf16[32,2048]{1,0:T(8,128)(2,1)}, u32[]{:S(2)}) %copy-start.3) | copy-done | bytes 131096
  18.8 0.7 copy-done.4
  19.4 0.6 first_states.1
  20.1 2.3 %collective-permute-start.1 = (bf16[4,64,128]{2,1,0:T(8,128)(2,1)S(1)}, bf16[4,64,128]{2,1,0:T(8,128)(2,1)S(1)}, u32[]{:S(2)}, u32[]{:S(2)}) collective-permute-start(bf16[4,64,128]{2,1,0:T(8,128)(2,1)S(1)} %get-tuple-element.46), channel_id=1, source_target_pairs={{2,4},{6,8},{10,12},{14,16},{18,20},{22,24},{26,28},{4,2},{8,6},{1... | collective-permute-start | bytes 196616 | tf_op jit(solution)/shard_map/ppermute | solution.py:329
  22.4 1.3 %collective-permute-start.2 = (bf16[4,64,128]{2,1,0:T(8,128)(2,1)S(1)}, bf16[4,64,128]{2,1,0:T(8,128)(2,1)S(1)}, u32[]{:S(2)}, u32[]{:S(2)}) collective-permute-start(bf16[4,64,128]{2,1,0:T(8,128)(2,1)S(1)} %get-tuple-element.47), channel_id=1, source_target_pairs={{0,2},{4,6},{8,10},{12,14},{16,18},{20,22},{24,26},{28,30},{2,0},{... | collective-permute-start | bytes 196616 | tf_op jit(solution)/shard_map/ppermute | solution.py:329
  23.7 1.5 %collective-permute-start.3 = (f32[32,1024]{1,0:T(8,128)}, f32[32,1024]{1,0:T(8,128)S(1)}, u32[]{:S(2)}, u32[]{:S(2)}) collective-permute-start(f32[32,1024]{1,0:T(8,128)} %get-tuple-element.48), channel_id=1, source_target_pairs={{0,1},{1,0},{2,3},{3,2},{4,5},{5,4},{6,7},{7,6},{8,9},{9,8},{10,11... | collective-permute-start | bytes 393224 | tf_op jit(solution)/shard_map/ppermute | solution.py:338
  25.2 0.7 copy-done.8
  25.9 0.4 invert_order.1
  26.3 1.8 %collective-permute-done.1.first_ref = bf16[4,64,128]{2,1,0:T(8,128)(2,1)S(1)} collective-permute-done((bf16[4,64,128]{2,1,0:T(8,128)(2,1)S(1)}, bf16[4,64,128]{2,1,0:T(8,128)(2,1)S(1)}, u32[]{:S(2)}, u32[]{:S(2)}) %collective-permute-start.1) | collective-permute-done | bytes 65568 | tf_op jit(solution)/shard_map/ppermute | solution.py:329
  28.1 0.0 collective-permute-done.2.second_ref
  28.1 0.7 copy-done.6
  28.8 1.4 %predict.1.guess_ref = f32[64,2048]{1,0:T(8,128)S(1)} custom-call(bf16[16,64,128]{2,1,0:T(8,128)(2,1)S(1)} %get-tuple-element.42.aug_ref, bf16[4,64,128]{2,1,0:T(8,128)(2,1)S(1)} %collective-permute-done.1.first_ref, bf16[4,64,128]{2,1,0:T(8,128)(2,1)S(1)} %collective-permute-done.2.second_ref, bf16[16,4,128,128]{3,2,1,0:T(8,128)(2,1)S(1)} %copy-done.1, ...), custom_call_target="tpu_custom_call" | custom-call | flops 1000000000 | tf_op jit(solution)/shard_map/predict/pallas_call | solution.py:21
  30.2 0.0 collective-permute-done.3.x_others_refs_0_
  30.2 1.2 %unpack_readings.3 = (f32[32,1024]{1,0:T(8,128)S(1)}, f32[1,1024]{1,0:T(1,128)S(1)}) custom-call(s32[16,128]{1,0:T(8,128)S(1)} %get-tuple-element.50.group_ref, s32[16,128]{1,0:T(8,128)S(1)} %get-tuple-element.51.lane_ref, f32[16,72,128]{2,1,0:T(8,128)S(1)} %all-to-all-done.message_ref), custom_call_target="tpu_custom_call" | custom-call | flops 2000000000 | tf_op jit(solution)/shard_map/unpack_readings/pallas_call | solution.py:21
  31.4 0.0 copy-start.7
  31.4 0.0 copy-start
  31.4 0.0 copy-start.2
  31.5 0.0 copy-start.5
  31.5 1.2 %unpack_readings.2 = (f32[32,1024]{1,0:T(8,128)S(1)}, f32[1,1024]{1,0:T(1,128)S(1)}) custom-call(s32[16,128]{1,0:T(8,128)S(1)} %get-tuple-element.50.group_ref, s32[16,128]{1,0:T(8,128)S(1)} %get-tuple-element.51.lane_ref, f32[16,72,128]{2,1,0:T(8,128)S(1)} %all-to-all-done.message_ref), custom_call_target="tpu_custom_call" | custom-call | flops 2000000000 | tf_op jit(solution)/shard_map/unpack_readings/pallas_call | solution.py:21
  32.7 1.6 %collective-permute-start.5 = (f32[32,1024]{1,0:T(8,128)S(1)}, f32[32,1024]{1,0:T(8,128)S(1)}, u32[]{:S(2)}, u32[]{:S(2)}) collective-permute-start(f32[32,1024]{1,0:T(8,128)S(1)} %get-tuple-element.54.z_refs_1_), channel_id=1, source_target_pairs={{0,1},{1,0},{2,3},{3,2},{4,5},{5,4},{6,7},{7,6},{8,9},{9,8},{10,11... | collective-permute-start | bytes 393224 | tf_op jit(solution)/shard_map/ppermute | solution.py:338
  34.3 0.5 collective-permute-start.4
  34.8 3.2 %collective-permute-done.5 = f32[32,1024]{1,0:T(8,128)S(1)} collective-permute-done((f32[32,1024]{1,0:T(8,128)S(1)}, f32[32,1024]{1,0:T(8,128)S(1)}, u32[]{:S(2)}, u32[]{:S(2)}) %collective-permute-start.5) | collective-permute-done | bytes 131104 | tf_op jit(solution)/shard_map/ppermute | solution.py:338
  37.9 1.4 %collective-permute-done.4 = f32[32,1024]{1,0:T(8,128)S(1)} collective-permute-done((f32[32,1024]{1,0:T(8,128)S(1)}, f32[32,1024]{1,0:T(8,128)S(1)}, u32[]{:S(2)}, u32[]{:S(2)}) %collective-permute-start.4) | collective-permute-done | bytes 131104 | tf_op jit(solution)/shard_map/ppermute | solution.py:338
  39.3 1.4 %pull.1 = (f32[16,64,128]{2,1,0:T(8,128)S(1)}, bf16[4,64,128]{2,1,0:T(8,128)(2,1)S(1)}, bf16[4,64,128]{2,1,0:T(8,128)(2,1)S(1)}) custom-call(f32[64,2048]{1,0:T(8,128)S(1)} %predict.1.guess_ref, f32[32,1024]{1,0:T(8,128)S(1)} %get-tuple-element.53.z_refs_0_, f32[32,1024]{1,0:T(8,128)S(1)} %get-tuple-element.54.z_refs_1_, f32[1,32,1024]{2,1,0:T(8,128)S(1)} %bitcast.12, ...), custom_call_target="tpu_custom_call" | custom-call | tf_op jit(solution)/shard_map/pull/pallas_call | solution.py:21
  40.8 4.3 %collective-permute-start.6 = (bf16[4,64,128]{2,1,0:T(8,128)(2,1)S(1)}, bf16[4,64,128]{2,1,0:T(8,128)(2,1)S(1)}, u32[]{:S(2)}, u32[]{:S(2)}) collective-permute-start(bf16[4,64,128]{2,1,0:T(8,128)(2,1)S(1)} %get-tuple-element.58), channel_id=1, source_target_pairs={{2,4},{6,8},{10,12},{14,16},{18,20},{22,24},{26,28},{4,2},{8,6},{1... | collective-permute-start | bytes 196616 | tf_op jit(solution)/shard_map/ppermute | solution.py:329
  45.1 0.1 collective-permute-start.7
  45.2 2.1 %collective-permute-done.6.back_first_ref = bf16[4,64,128]{2,1,0:T(8,128)(2,1)S(1)} collective-permute-done((bf16[4,64,128]{2,1,0:T(8,128)(2,1)S(1)}, bf16[4,64,128]{2,1,0:T(8,128)(2,1)S(1)}, u32[]{:S(2)}, u32[]{:S(2)}) %collective-permute-start.6) | collective-permute-done | bytes 65568 | tf_op jit(solution)/shard_map/ppermute | solution.py:329
  47.3 2.1 %first_update.1 = (f32[8,32,128]{2,1,0:T(8,128)S(1)}, f32[8,32,128]{2,1,0:T(8,128)S(1)}, bf16[8,64,128]{2,1,0:T(8,128)(2,1)S(1)}, bf16[4,64,128]{2,1,0:T(8,128)(2,1)S(1)}) custom-call(f32[16,64,128]{2,1,0:T(8,128)S(1)} %get-tuple-element.57.grad_ref, bf16[4,64,128]{2,1,0:T(8,128)(2,1)S(1)} %collective-permute-done.6.back_first_ref, ...), custom_call_target="tpu_custom_call" | custom-call | tf_op jit(solution)/shard_map/first_update/pallas_call | solution.py:21
  49.3 1.6 %collective-permute-start.10 = (bf16[8,64,128]{2,1,0:T(8,128)(2,1)S(1)}, bf16[8,64,128]{2,1,0:T(8,128)(2,1)S(1)}, u32[]{:S(2)}, u32[]{:S(2)}) collective-permute-start(bf16[8,64,128]{2,1,0:T(8,128)(2,1)S(1)} %get-tuple-element.62.mine_ref), channel_id=1, source_target_pairs={{0,1},{1,0},{2,3},{3,2},{4,5},{5,4},{6,7},{7,6},{8,9},{9,8},{10,11... | collective-permute-start | bytes 393224 | tf_op jit(solution)/shard_map/ppermute | solution.py:338
  50.9 4.0 %collective-permute-start.8 = (bf16[4,64,128]{2,1,0:T(8,128)(2,1)S(1)}, bf16[4,64,128]{2,1,0:T(8,128)(2,1)S(1)}, u32[]{:S(2)}, u32[]{:S(2)}) collective-permute-start(bf16[4,64,128]{2,1,0:T(8,128)(2,1)S(1)} %get-tuple-element.61), channel_id=1, source_target_pairs={{2,4},{6,8},{10,12},{14,16},{18,20},{22,24},{26,28},{4,2},{8,6},{1... | collective-permute-start | bytes 196616 | tf_op jit(solution)/shard_map/ppermute | solution.py:329
  55.0 2.4 %collective-permute-done.8.first_refs_0_ = bf16[4,64,128]{2,1,0:T(8,128)(2,1)S(1)} collective-permute-done((bf16[4,64,128]{2,1,0:T(8,128)(2,1)S(1)}, bf16[4,64,128]{2,1,0:T(8,128)(2,1)S(1)}, u32[]{:S(2)}, u32[]{:S(2)}) %collective-permute-start.8) | collective-permute-done | bytes 65568 | tf_op jit(solution)/shard_map/ppermute | solution.py:329
  57.4 0.5 collective-permute-start.9
  57.9 0.6 join_states.1
  58.5 0.1 collective-permute-start.11
  58.6 3.1 %collective-permute-done.9.first_refs_1_ = bf16[4,64,128]{2,1,0:T(8,128)(2,1)S(1)} collective-permute-done((bf16[4,64,128]{2,1,0:T(8,128)(2,1)S(1)}, bf16[4,64,128]{2,1,0:T(8,128)(2,1)S(1)}, u32[]{:S(2)}, u32[]{:S(2)}) %collective-permute-start.9) | collective-permute-done | bytes 65568 | tf_op jit(solution)/shard_map/ppermute | solution.py:338
  61.7 2.0 %predict_pull.1 = (f32[16,64,128]{2,1,0:T(8,128)S(1)}, bf16[4,64,128]{2,1,0:T(8,128)(2,1)S(1)}, bf16[4,64,128]{2,1,0:T(8,128)(2,1)S(1)}) custom-call(bf16[4,64,128]{2,1,0:T(8,128)(2,1)S(1)} %collective-permute-done.8.first_refs_0_, bf16[4,64,128]{2,1,0:T(8,128)(2,1)S(1)} %collective-permute-done.9.first_refs_1_, ...), custom_call_target="tpu_custom_call" | custom-call | tf_op jit(solution)/shard_map/predict_pull/pallas_call | solution.py:21
  63.7 3.2 %collective-permute-start.12 = (bf16[4,64,128]{2,1,0:T(8,128)(2,1)S(1)}, bf16[4,64,128]{2,1,0:T(8,128)(2,1)S(1)}, u32[]{:S(2)}, u32[]{:S(2)}) collective-permute-start(bf16[4,64,128]{2,1,0:T(8,128)(2,1)S(1)} %get-tuple-element.69), channel_id=1, source_target_pairs={{2,4},{6,8},{10,12},{14,16},{18,20},{22,24},{26,28},{4,2},{8,6},{1... | collective-permute-start | bytes 196616 | tf_op jit(solution)/shard_map/ppermute | solution.py:329
  66.8 0.1 collective-permute-start.13
  66.9 0.6 collective-permute-start.14
  67.5 2.6 %collective-permute-done.12.back_first_ref = bf16[4,64,128]{2,1,0:T(8,128)(2,1)S(1)} collective-permute-done((bf16[4,64,128]{2,1,0:T(8,128)(2,1)S(1)}, bf16[4,64,128]{2,1,0:T(8,128)(2,1)S(1)}, u32[]{:S(2)}, u32[]{:S(2)}) %collective-permute-start.12) | collective-permute-done | bytes 65568 | tf_op jit(solution)/shard_map/ppermute | solution.py:329
  70.1 2.0 %last_update.1 = (f32[32,1024]{1,0:T(8,128)S(1)}, bf16[32,1024]{1,0:T(8,128)(2,1)S(1)}) custom-call(f32[16,64,128]{2,1,0:T(8,128)S(1)} %get-tuple-element.65.grad_ref, bf16[4,64,128]{2,1,0:T(8,128)(2,1)S(1)} %collective-permute-done.12.back_first_ref, bf16[4,64,128]{2,1,0:T(8,128)(2,1)S(1)} %collective-permute-done.13.back_second_ref, s32[2,4]{1,0:T(2,128)S(1)} %bitcast.18, ...), custom_call_target="tpu_custom_call" | custom-call | tf_op jit(solution)/shard_map/last_update/pallas_call | solution.py:21
  72.2 0.6 collective-permute-start.15
  72.7 3.8 %collective-permute-done.15.updates_refs_0_ = bf16[32,1024]{1,0:T(8,128)(2,1)S(1)} collective-permute-done((bf16[32,1024]{1,0:T(8,128)(2,1)S(1)}, bf16[32,1024]{1,0:T(8,128)(2,1)S(1)}, u32[]{:S(2)}, u32[]{:S(2)}) %collective-permute-start.15) | collective-permute-done | bytes 65568 | tf_op jit(solution)/shard_map/ppermute | solution.py:338
  76.5 0.7 finish.1
  (16 shorter events, 0.0 us)
Async XLA Ops:
  0.0 28.1 %copy-start.1 = (bf16[16,4,128,128]{3,2,1,0:T(8,128)(2,1)S(1)}, bf16[16,4,128,128]{3,2,1,0:T(8,128)(2,1)}, u32[]{:S(2)}) copy-start(bf16[16,4,128,128]{3,2,1,0:T(8,128)(2,1)} %tiles_ref.5) | copy-start | bytes 6291460
  5.9 24.3 %all-to-all-start = ((f32[16,72,128]{2,1,0:T(8,128)}), f32[16,72,128]{2,1,0:T(8,128)S(1)}, u32[]{:S(2)}, u32[]{:S(2)}) async-start(f32[16,72,128]{2,1,0:T(8,128)} %get-tuple-element.40), calls=%async_computation | async-start | bytes 1179648 | tf_op jit(solution)/shard_map/all_to_all | solution.py:412
  12.1 5.8 %collective-permute-start = (bf16[32,2048]{1,0:T(8,128)(2,1)}, bf16[32,2048]{1,0:T(8,128)(2,1)S(1)}, u32[]{:S(2)}, u32[]{:S(2)}) collective-permute-start(bf16[32,2048]{1,0:T(8,128)(2,1)} %get-tuple-element.41.own_ref), channel_id=1, source_target_pairs={{0,1},{1,0},{2,3},{3,2},{4,5},{5,4},{6,7},{7,6},{8,9},{9,8},{10,11... | collective-permute-start | bytes 393224 | tf_op jit(solution)/shard_map/ppermute | solution.py:338
  17.9 0.9 %copy-start.3 = (bf16[32,2048]{1,0:T(8,128)(2,1)S(1)}, bf16[32,2048]{1,0:T(8,128)(2,1)}, u32[]{:S(2)}) copy-start(bf16[32,2048]{1,0:T(8,128)(2,1)} %get-tuple-element.41.own_ref) | copy-start | bytes 393220
  18.8 0.7 copy-start.4
  20.1 8.0 %collective-permute-start.1 = (bf16[4,64,128]{2,1,0:T(8,128)(2,1)S(1)}, bf16[4,64,128]{2,1,0:T(8,128)(2,1)S(1)}, u32[]{:S(2)}, u32[]{:S(2)}) collective-permute-start(bf16[4,64,128]{2,1,0:T(8,128)(2,1)S(1)} %get-tuple-element.46), channel_id=1, source_target_pairs={{2,4},{6,8},{10,12},{14,16},{18,20},{22,24},{26,28},{4,2},{8,6},{1... | collective-permute-start | bytes 196616 | tf_op jit(solution)/shard_map/ppermute | solution.py:329
  22.4 5.7 %collective-permute-start.2 = (bf16[4,64,128]{2,1,0:T(8,128)(2,1)S(1)}, bf16[4,64,128]{2,1,0:T(8,128)(2,1)S(1)}, u32[]{:S(2)}, u32[]{:S(2)}) collective-permute-start(bf16[4,64,128]{2,1,0:T(8,128)(2,1)S(1)} %get-tuple-element.47), channel_id=1, source_target_pairs={{0,2},{4,6},{8,10},{12,14},{16,18},{20,22},{24,26},{28,30},{2,0},{... | collective-permute-start | bytes 196616 | tf_op jit(solution)/shard_map/ppermute | solution.py:329
  23.7 6.5 %collective-permute-start.3 = (f32[32,1024]{1,0:T(8,128)}, f32[32,1024]{1,0:T(8,128)S(1)}, u32[]{:S(2)}, u32[]{:S(2)}) collective-permute-start(f32[32,1024]{1,0:T(8,128)} %get-tuple-element.48), channel_id=1, source_target_pairs={{0,1},{1,0},{2,3},{3,2},{4,5},{5,4},{6,7},{7,6},{8,9},{9,8},{10,11... | collective-permute-start | bytes 393224 | tf_op jit(solution)/shard_map/ppermute | solution.py:338
  25.2 0.7 copy-start.8
  28.1 0.7 copy-start.6
  31.4 7.9 %copy-start.7 = (s32[1,16,4]{1,2,0:T(4,128)S(1)}, s32[1,16,4]{1,2,0:T(4,128)}, u32[]{:S(2)}) copy-start(s32[1,16,4]{1,2,0:T(4,128)} %param.13) | copy-start | bytes 772
  31.4 15.8 %copy-start = (bf16[1024,2048]{1,0:T(8,128)(2,1)S(1)}, bf16[1024,2048]{1,0:T(8,128)(2,1)}, u32[]{:S(2)}) copy-start(bf16[1024,2048]{1,0:T(8,128)(2,1)} %gain_ref.3) | copy-start | bytes 12582916
  31.4 15.8 %copy-start.2 = (f32[32,2048]{1,0:T(8,128)S(1)}, f32[32,2048]{1,0:T(8,128)}, u32[]{:S(2)}) copy-start(f32[32,2048]{1,0:T(8,128)} %x_ref.1) | copy-start | bytes 786436
  31.5 15.8 %copy-start.5 = (s32[1,2,4]{2,1,0:T(2,128)S(1)}, s32[1,2,4]{2,1,0:T(2,128)}, u32[]{:S(2)}) copy-start(s32[1,2,4]{2,1,0:T(2,128)} %param.14) | copy-start | bytes 100
  32.7 5.3 %collective-permute-start.5 = (f32[32,1024]{1,0:T(8,128)S(1)}, f32[32,1024]{1,0:T(8,128)S(1)}, u32[]{:S(2)}, u32[]{:S(2)}) collective-permute-start(f32[32,1024]{1,0:T(8,128)S(1)} %get-tuple-element.54.z_refs_1_), channel_id=1, source_target_pairs={{0,1},{1,0},{2,3},{3,2},{4,5},{5,4},{6,7},{7,6},{8,9},{9,8},{10,11... | collective-permute-start | bytes 393224 | tf_op jit(solution)/shard_map/ppermute | solution.py:338
  34.3 5.1 %collective-permute-start.4 = (f32[32,1024]{1,0:T(8,128)S(1)}, f32[32,1024]{1,0:T(8,128)S(1)}, u32[]{:S(2)}, u32[]{:S(2)}) collective-permute-start(f32[32,1024]{1,0:T(8,128)S(1)} %get-tuple-element.53.z_refs_0_), channel_id=1, source_target_pairs={{0,1},{1,0},{2,3},{3,2},{4,5},{5,4},{6,7},{7,6},{8,9},{9,8},{10,11... | collective-permute-start | bytes 393224 | tf_op jit(solution)/shard_map/ppermute | solution.py:338
  40.8 6.5 %collective-permute-start.6 = (bf16[4,64,128]{2,1,0:T(8,128)(2,1)S(1)}, bf16[4,64,128]{2,1,0:T(8,128)(2,1)S(1)}, u32[]{:S(2)}, u32[]{:S(2)}) collective-permute-start(bf16[4,64,128]{2,1,0:T(8,128)(2,1)S(1)} %get-tuple-element.58), channel_id=1, source_target_pairs={{2,4},{6,8},{10,12},{14,16},{18,20},{22,24},{26,28},{4,2},{8,6},{1... | collective-permute-start | bytes 196616 | tf_op jit(solution)/shard_map/ppermute | solution.py:329
  45.1 2.1 %collective-permute-start.7 = (bf16[4,64,128]{2,1,0:T(8,128)(2,1)S(1)}, bf16[4,64,128]{2,1,0:T(8,128)(2,1)S(1)}, u32[]{:S(2)}, u32[]{:S(2)}) collective-permute-start(bf16[4,64,128]{2,1,0:T(8,128)(2,1)S(1)} %get-tuple-element.59), channel_id=1, source_target_pairs={{0,2},{4,6},{8,10},{12,14},{16,18},{20,22},{24,26},{28,30},{2,0},{... | collective-permute-start | bytes 196616 | tf_op jit(solution)/shard_map/ppermute | solution.py:329
  49.3 8.6 %collective-permute-start.10 = (bf16[8,64,128]{2,1,0:T(8,128)(2,1)S(1)}, bf16[8,64,128]{2,1,0:T(8,128)(2,1)S(1)}, u32[]{:S(2)}, u32[]{:S(2)}) collective-permute-start(bf16[8,64,128]{2,1,0:T(8,128)(2,1)S(1)} %get-tuple-element.62.mine_ref), channel_id=1, source_target_pairs={{0,1},{1,0},{2,3},{3,2},{4,5},{5,4},{6,7},{7,6},{8,9},{9,8},{10,11... | collective-permute-start | bytes 393224 | tf_op jit(solution)/shard_map/ppermute | solution.py:338
  50.9 6.5 %collective-permute-start.8 = (bf16[4,64,128]{2,1,0:T(8,128)(2,1)S(1)}, bf16[4,64,128]{2,1,0:T(8,128)(2,1)S(1)}, u32[]{:S(2)}, u32[]{:S(2)}) collective-permute-start(bf16[4,64,128]{2,1,0:T(8,128)(2,1)S(1)} %get-tuple-element.61), channel_id=1, source_target_pairs={{2,4},{6,8},{10,12},{14,16},{18,20},{22,24},{26,28},{4,2},{8,6},{1... | collective-permute-start | bytes 196616 | tf_op jit(solution)/shard_map/ppermute | solution.py:329
  57.4 4.3 %collective-permute-start.9 = (bf16[4,64,128]{2,1,0:T(8,128)(2,1)S(1)}, bf16[4,64,128]{2,1,0:T(8,128)(2,1)S(1)}, u32[]{:S(2)}, u32[]{:S(2)}) collective-permute-start(bf16[4,64,128]{2,1,0:T(8,128)(2,1)S(1)} %collective-permute-done.8.first_refs_0_), channel_id=1, source_target_pairs={{0,1},{1,0},{2,3},{3,2},{4,5},{5,4},{6,7},{7,6},{8,9},{9,8},{10,11... | collective-permute-start | bytes 196616 | tf_op jit(solution)/shard_map/ppermute | solution.py:338
  58.5 3.1 %collective-permute-start.11 = (bf16[4,64,128]{2,1,0:T(8,128)(2,1)S(1)}, bf16[4,64,128]{2,1,0:T(8,128)(2,1)S(1)}, u32[]{:S(2)}, u32[]{:S(2)}) collective-permute-start(bf16[4,64,128]{2,1,0:T(8,128)(2,1)S(1)} %get-tuple-element.64), channel_id=1, source_target_pairs={{0,2},{4,6},{8,10},{12,14},{16,18},{20,22},{24,26},{28,30},{2,0},{... | collective-permute-start | bytes 196616 | tf_op jit(solution)/shard_map/ppermute | solution.py:329
  63.7 6.5 %collective-permute-start.12 = (bf16[4,64,128]{2,1,0:T(8,128)(2,1)S(1)}, bf16[4,64,128]{2,1,0:T(8,128)(2,1)S(1)}, u32[]{:S(2)}, u32[]{:S(2)}) collective-permute-start(bf16[4,64,128]{2,1,0:T(8,128)(2,1)S(1)} %get-tuple-element.69), channel_id=1, source_target_pairs={{2,4},{6,8},{10,12},{14,16},{18,20},{22,24},{26,28},{4,2},{8,6},{1... | collective-permute-start | bytes 196616 | tf_op jit(solution)/shard_map/ppermute | solution.py:329
  66.8 3.3 %collective-permute-start.13 = (bf16[4,64,128]{2,1,0:T(8,128)(2,1)S(1)}, bf16[4,64,128]{2,1,0:T(8,128)(2,1)S(1)}, u32[]{:S(2)}, u32[]{:S(2)}) collective-permute-start(bf16[4,64,128]{2,1,0:T(8,128)(2,1)S(1)} %get-tuple-element.70), channel_id=1, source_target_pairs={{0,2},{4,6},{8,10},{12,14},{16,18},{20,22},{24,26},{28,30},{2,0},{... | collective-permute-start | bytes 196616 | tf_op jit(solution)/shard_map/ppermute | solution.py:329
  66.9 9.6 %collective-permute-start.14 = (f32[8,32,128]{2,1,0:T(8,128)S(1)}, f32[8,32,128]{2,1,0:T(8,128)S(1)}, u32[]{:S(2)}, u32[]{:S(2)}) collective-permute-start(f32[8,32,128]{2,1,0:T(8,128)S(1)} %get-tuple-element.73), channel_id=1, source_target_pairs={{0,1},{1,0},{2,3},{3,2},{4,5},{5,4},{6,7},{7,6},{8,9},{9,8},{10,11... | collective-permute-start | bytes 393224 | tf_op jit(solution)/shard_map/ppermute | solution.py:338
  72.2 4.3 %collective-permute-start.15 = (bf16[32,1024]{1,0:T(8,128)(2,1)S(1)}, bf16[32,1024]{1,0:T(8,128)(2,1)S(1)}, u32[]{:S(2)}, u32[]{:S(2)}) collective-permute-start(bf16[32,1024]{1,0:T(8,128)(2,1)S(1)} %get-tuple-element.74), channel_id=1, source_target_pairs={{0,1},{1,0},{2,3},{3,2},{4,5},{5,4},{6,7},{7,6},{8,9},{9,8},{10,11... | collective-permute-start | bytes 196616 | tf_op jit(solution)/shard_map/ppermute | solution.py:338

commit v9 on v8

--- a/solution.py
+++ b/solution.py
@@ -41,26 +41,37 @@
 
 
 def pack_kernel(
-    z_in, v_in, hub_in, x_in, out, rounded_ref, sent_refs,
-    z_ref, v_ref, hub_ref, x_ref, out_ref, sems, out_sems, sent_sems,
-):
-    pairs = ((hub_in, hub_ref), (z_in, z_ref), (v_in, v_ref), (x_in, x_ref))
+    z_in, v_in, hub_in, x_in, ties_in, out, rounded_out, first_out, second_out, sent_outs,
+    z_ref, v_ref, hub_ref, x_ref, ties_ref, out_ref, rounded_ref, first_ref, second_ref,
+    sems, out_sems, sent_sems,
+):
+    pairs = (
+        (x_in, x_ref), (ties_in, ties_ref), (hub_in, hub_ref), (z_in, z_ref), (v_in, v_ref)
+    )
     copies = [
         pltpu.make_async_copy(source, target, sems.at[i])
         for i, (source, target) in enumerate(pairs)
     ]
-    members = len(sent_refs) + 1
-    part = x_in.shape[1] // members
-    sends = []
-    for i, sent_ref in enumerate(sent_refs, 1):
-        at = lax.rem(lax.axis_index("snap") + i, members) * part
-        source = x_in.at[:, pl.ds(pl.multiple_of(at, BLK), part)]
-        sends.append(pltpu.make_async_copy(source, sent_ref, sent_sems.at[i - 1]))
-    for copy in copies + sends:
+    for copy in copies:
         copy.start()
     for copy in copies:
         copy.wait()
-    rounded_ref[...] = x_ref[...].astype(BF16)
+    for b in range(rounded_ref.shape[0]):
+        rounded_ref[b] = x_ref[:, b * BLK : (b + 1) * BLK].astype(BF16)
+    pick(rounded_ref, ties_ref, 1 - parity(), first_ref)
+    pick(rounded_ref, ties_ref, parity(), second_ref)
+    ready = [(first_ref, first_out), (second_ref, second_out), (rounded_ref, rounded_out)]
+    members = len(sent_outs) + 1
+    part = x_ref.shape[1] // members
+    for i, sent_out in enumerate(sent_outs, 1):
+        at = lax.rem(lax.axis_index("snap") + i, members) * part
+        ready.append((x_ref.at[:, pl.ds(pl.multiple_of(at, BLK), part)], sent_out))
+    sends = [
+        pltpu.make_async_copy(source, target, sent_sems.at[i])
+        for i, (source, target) in enumerate(ready)
+    ]
+    for copy in sends:
+        copy.start()
     snaps, lines = z_ref.shape
     blocks = lines // BLK
     chunks, width = hub_ref.shape
@@ -154,17 +165,6 @@
         out_ref[t] = jnp.where(here, block, jnp.zeros_like(block))
 
 
-def first_states_kernel(own_ref, others_ref, ties_ref, aug_ref, first_ref, second_ref):
-    snaps = own_ref.shape[0]
-    for b in range(aug_ref.shape[0]):
-        columns = slice(b * BLK, (b + 1) * BLK)
-        aug_ref[b, :snaps] = own_ref[:, columns]
-        for i in range(others_ref.shape[0]):
-            aug_ref[b, (i + 1) * snaps : (i + 2) * snaps] = others_ref[i, :, columns]
-    pick(aug_ref, ties_ref, 1 - parity(), first_ref)
-    pick(aug_ref, ties_ref, parity(), second_ref)
-
-
 def slots_into(slots_ref, aug_ref, first, second_ref):
     own = aug_ref.shape[0]
     ties = second_ref.shape[0]
@@ -175,7 +175,7 @@
 
 def reordered(ref, distance, members):
     snaps = ref.shape[1] // members
-    order = [(n + distance) % members for n in range(members)]
+    order = [(n - distance) % members for n in range(members)]
     return jnp.concatenate([ref[:, j * snaps : (j + 1) * snaps] for j in order], axis=1)
 
 
@@ -197,8 +197,16 @@
     return lax.dot_general(chosen, weights, NT, preferred_element_type=F32)
 
 
-def predict_kernel(aug_ref, first_ref, second_ref, tiles_ref, place_ref, out_ref, slots_ref):
-    slots_into(slots_ref, aug_ref, first_ref[...], second_ref)
+def predict_kernel(
+    first_refs, second_refs, own_refs, tiles_ref, place_ref, out_ref, slots_ref
+):
+    own, snaps = own_refs[0].shape[:2]
+    ties = first_refs[0].shape[0]
+    for i in range(len(own_refs)):
+        rows = slice(i * snaps, (i + 1) * snaps)
+        slots_ref[:own, rows] = own_refs[i][...]
+        slots_ref[pl.ds(own + ties * (1 - parity()), ties), rows] = first_refs[i][...]
+        slots_ref[pl.ds(own + ties * parity(), ties), rows] = second_refs[i][...]
     predict(tiles_ref, place_ref, out_ref, slots_ref)
 
 
@@ -317,7 +325,7 @@
     me = lax.axis_index("snap")
     out_ref[:, pl.ds(pl.multiple_of(me * width, BLK), width)] = mine_ref[...]
     for i, (state_ref, update_ref) in enumerate(zip(states_refs, updates_refs), 1):
-        at = lax.rem(me + members - i, members) * width
+        at = lax.rem(me + i, members) * width
         for b in range(width // BLK):
             update = update_ref[:, b * BLK : (b + 1) * BLK].astype(F32)
             columns = pl.ds(pl.multiple_of(at + b * BLK, BLK), BLK)
@@ -376,35 +384,42 @@
     holder = holder_line_order[0].reshape(chunks, width)
     depth = (width // BLK) * snaps + 8
 
-    message, rounded, x_sent = call(
+    few = shape((ties, snaps, BLK), BF16)
+    message, rounded, first, second, x_sent = call(
         pack_kernel,
         (
             shape((chunks, depth, BLK), F32),
-            shape((snaps, states), BF16),
+            shape((own, snaps, BLK), BF16),
+            few,
+            few,
             [shape((snaps, held * BLK), F32)] * (members - 1),
         ),
-        [HBM] * 4,
+        [HBM] * 5,
         (
             phasor_readings,
             reading_error_spread.reshape(lines // BLK, BLK),
             hub,
             starting_voltages,
+            ties_table,
         ),
         scratch=[
             pltpu.VMEM((snaps, lines), F32),
             pltpu.VMEM((lines // BLK, BLK), F32),
             pltpu.VMEM((chunks, width), jnp.int32),
             pltpu.VMEM((snaps, states), F32),
+            pltpu.SMEM(ties_table.shape, jnp.int32),
             pltpu.VMEM((chunks, depth, BLK), F32),
-            pltpu.SemaphoreType.DMA((4,)),
+            pltpu.VMEM((own, snaps, BLK), BF16),
+            pltpu.VMEM((ties, snaps, BLK), BF16),
+            pltpu.VMEM((ties, snaps, BLK), BF16),
+            pltpu.SemaphoreType.DMA((5,)),
             pltpu.SemaphoreType.DMA((chunks,)),
-            pltpu.SemaphoreType.DMA((members,)),
+            pltpu.SemaphoreType.DMA((members + 2,)),
         ],
-        out_spec=(HBM, VMEM, [HBM] * (members - 1)),
+        out_spec=(HBM, HBM, HBM, HBM, [HBM] * (members - 1)),
         mib=60,
         name="pack_readings",
     )
-    rounded_others = from_all(rounded)
     each = width // cap
     if each > 1:
         message = message.reshape(chunks, depth, each, cap).transpose(0, 2, 1, 3)
@@ -423,25 +438,17 @@
         name="invert_order",
     )
     boundary = shape((ties, everything, BLK), BF16)
-    aug, first, second = call(
-        first_states_kernel,
-        (
-            shape((own, everything, BLK), BF16),
-            boundary,
-            boundary,
-        ),
-        [VMEM, VMEM, SMEM],
-        (rounded, rounded_others, ties_table),
-        name="first_states",
-    )
+    owns = [rounded] + [from_snap(rounded, i) for i in range(1, members)]
+    first, second = with_neighbours(first, second)
     first, second, x_sent = lax.optimization_barrier((first, second, x_sent))
-    first, second = with_neighbours(first, second)
+    firsts = [first] + [from_snap(first, i) for i in range(1, members)]
+    seconds = [second] + [from_snap(second, i) for i in range(1, members)]
     x_others = [from_snap(block, i) for i, block in enumerate(x_sent, 1)]
     guess = call(
         predict_kernel,
         shape((everything, lines), F32),
-        [VMEM, VMEM, VMEM, VMEM, SMEM],
-        (aug, first, second, derivative_pieces, place),
+        [[VMEM] * members, [VMEM] * members, [VMEM] * members, VMEM, SMEM],
+        (firsts, seconds, owns, derivative_pieces, place),
         scratch=[pltpu.VMEM((slots, everything, BLK), BF16)],
         flops=10**9,
         name="predict",
@@ -521,7 +528,7 @@
     )
     given, first, second = lax.optimization_barrier((given, first, second))
     first, second = with_neighbours(first, second)
-    states_in = [from_snap(block, i) for i, block in enumerate(given, 1)]
+    states_in = [from_snap(block, -i) for i, block in enumerate(given, 1)]
     mine, sent = call(
         last_update_kernel,
         (
@@ -537,7 +544,7 @@
         finish_kernel,
         shape((snaps, states), F32),
         [VMEM, [VMEM] * (members - 1), [VMEM] * (members - 1)],
-        (mine, states_in, [from_snap(block, i) for i, block in enumerate(sent, 1)]),
+        (mine, states_in, [from_snap(block, -i) for i, block in enumerate(sent, 1)]),
         name="finish",
     )
 

time: 78.3 us -> 82.3 us (1.051)
  waiting for transfers between devices: 24.6 us -> 36.9 us
  starting transfers between devices: 29.8 us -> 26.4 us
  local copies, waits for them, and re-layouts: 3.01 us -> 0.75 us
  Pallas kernels: 19.7 us -> 17.7 us
    ppermute x8, waiting for transfers between devices: 8.9 us -> 23.3 us  [swap_pair(): return lax.ppermute(block, 'area', pairs + [(b, a) for a, b in pairs])]
    ppermute x8, starting transfers between devices: 15.3 us -> 9.5 us  [swap_pair(): return lax.ppermute(block, 'area', pairs + [(b, a) for a, b in pairs])]
    ppermute x8 -> x10, starting transfers between devices: 8.35 us -> 10.6 us  [from_snap(): lax.ppermute(block, 'snap', [(i, (i + distance) % members) for i in range...]
    unnamed x18 -> x14, local copies, waits for them, and re-layouts: 3.01 us -> 0.75 us
    ppermute x8 -> x10, waiting for transfers between devices: 15.7 us -> 13.5 us  [from_snap(): lax.ppermute(block, 'snap', [(i, (i + distance) % members) for i in range...]
    pallas_call x12 -> x11, Pallas kernels: 19.7 us -> 17.7 us  [call(): pl.pallas_call(kernel, out_shape=outs, in_specs=ins, out_specs=jax.tree.m...]
  transfers between devices with their start and end apart: 17 -> 19, of which waited for: 9 -> 10; matrix products, arithmetic and copies ran while one was open for 0% -> 0% of each run, Pallas kernels for 7% -> 5%
where the time goes in v9:
time: 82.3 us; the launch traced here: 81.9 us
  waiting for transfers between devices  36.9 us (45%)
  starting transfers between devices  26.4 us (32%)
  Pallas kernels  17.7 us (22%)
    ppermute x8, waiting for transfers between devices, swap_pair(): return lax.ppermute(block, 'area', pairs + [(b, a) for a, b in pairs])  23.3 us
    pallas_call x11, Pallas kernels, call(): pl.pallas_call(kernel, out_shape=outs, in_specs=ins, out_specs=jax.tree.m...  17.7 us
    ppermute x10, waiting for transfers between devices, from_snap(): lax.ppermute(block, 'snap', [(i, (i + distance) % members) for i in range...  13.5 us
    ppermute x10, starting transfers between devices, from_snap(): lax.ppermute(block, 'snap', [(i, (i + distance) % members) for i in range...  10.6 us
    ppermute x8, starting transfers between devices, swap_pair(): return lax.ppermute(block, 'area', pairs + [(b, a) for a, b in pairs])  9.5 us
    all_to_all x1, starting transfers between devices, on_device(): lax.all_to_all(message, 'area', split_axis=0, concat_axis=0, tiled=True)  6.3 us
  transfers between devices with their start and end apart: 19, of which 10 were waited for; matrix products, arithmetic and copies ran while one was open for 0% of the time, Pallas kernels for 5%

profile of v9, /device:TPU:16, one launch (start us, length us, event | category | flops | bytes accessed | tf_op | source)
XLA Modules:
  0.0 81.9 jit_solution(16553695864337972778)
XLA Ops:
  0.0 4.5 %pack_readings.1 = (f32[16,72,128]{2,1,0:T(8,128)}, bf16[16,32,128]{2,1,0:T(8,128)(2,1)}, bf16[4,32,128]{2,1,0:T(8,128)(2,1)}, bf16[4,32,128]{2,1,0:T(8,128)(2,1)}, f32[32,1024]{1,0:T(8,128)}) custom-call(f32[32,2048]{1,0:T(8,128)} %z_in.1, f32[16,128]{1,0:T(8,128)} %bitcast.22, s32[16,256]{1,0:T(8,128)} %bitcast.21, f32[32,2048]{1,0:T(8,128)} %x_ref.1, ...), custom_call_target="tpu_custom_call" | custom-call | tf_op jit(solution)/shard_map/pack_readings/pallas_call | solution.py:21
  4.5 0.0 copy-start.5
  4.5 6.3 %all-to-all-start = ((f32[16,72,128]{2,1,0:T(8,128)}), f32[16,72,128]{2,1,0:T(8,128)S(1)}, u32[]{:S(2)}, u32[]{:S(2)}) async-start(f32[16,72,128]{2,1,0:T(8,128)} %get-tuple-element.39), calls=%async_computation | async-start | bytes 1179648 | tf_op jit(solution)/shard_map/all_to_all | solution.py:427
  10.8 1.5 %collective-permute-start.4 = (bf16[16,32,128]{2,1,0:T(8,128)(2,1)}, bf16[16,32,128]{2,1,0:T(8,128)(2,1)S(1)}, u32[]{:S(2)}, u32[]{:S(2)}) collective-permute-start(bf16[16,32,128]{2,1,0:T(8,128)(2,1)} %get-tuple-element.45.own_refs_0_), channel_id=1, source_target_pairs={{0,1},{1,0},{2,3},{3,2},{4,5},{5,4},{6,7},{7,6},{8,9},{9,8},{10,11... | collective-permute-start | bytes 393224 | tf_op jit(solution)/shard_map/ppermute | solution.py:346
  12.3 2.8 %collective-permute-start = (bf16[4,32,128]{2,1,0:T(8,128)(2,1)}, bf16[4,32,128]{2,1,0:T(8,128)(2,1)S(1)}, u32[]{:S(2)}, u32[]{:S(2)}) collective-permute-start(bf16[4,32,128]{2,1,0:T(8,128)(2,1)} %get-tuple-element.40), channel_id=1, source_target_pairs={{2,4},{6,8},{10,12},{14,16},{18,20},{22,24},{26,28},{4,2},{8,6},{1... | collective-permute-start | bytes 98312 | tf_op jit(solution)/shard_map/ppermute | solution.py:337
  15.2 0.7 collective-permute-start.1
  15.9 10.5 %collective-permute-done.first_refs_0_ = bf16[4,32,128]{2,1,0:T(8,128)(2,1)S(1)} collective-permute-done((bf16[4,32,128]{2,1,0:T(8,128)(2,1)}, bf16[4,32,128]{2,1,0:T(8,128)(2,1)S(1)}, u32[]{:S(2)}, u32[]{:S(2)}) %collective-permute-start) | collective-permute-done | bytes 32800 | tf_op jit(solution)/shard_map/ppermute | solution.py:337
  26.4 0.0 collective-permute-done.1.second_refs_0_
  26.4 1.5 %collective-permute-start.2 = (bf16[4,32,128]{2,1,0:T(8,128)(2,1)S(1)}, bf16[4,32,128]{2,1,0:T(8,128)(2,1)S(1)}, u32[]{:S(2)}, u32[]{:S(2)}) collective-permute-start(bf16[4,32,128]{2,1,0:T(8,128)(2,1)S(1)} %collective-permute-done.first_refs_0_), channel_id=1, source_target_pairs={{0,1},{1,0},{2,3},{3,2},{4,5},{5,4},{6,7},{7,6},{8,9},{9,8},{10,11... | collective-permute-start | bytes 98312 | tf_op jit(solution)/shard_map/ppermute | solution.py:346
  27.9 0.5 collective-permute-start.3
  28.4 1.5 %collective-permute-start.5 = (f32[32,1024]{1,0:T(8,128)}, f32[32,1024]{1,0:T(8,128)S(1)}, u32[]{:S(2)}, u32[]{:S(2)}) collective-permute-start(f32[32,1024]{1,0:T(8,128)} %get-tuple-element.46), channel_id=1, source_target_pairs={{0,1},{1,0},{2,3},{3,2},{4,5},{5,4},{6,7},{7,6},{8,9},{9,8},{10,11... | collective-permute-start | bytes 393224 | tf_op jit(solution)/shard_map/ppermute | solution.py:346
  29.9 0.7 copy-done.6
  30.6 0.4 invert_order.1
  31.1 0.0 collective-permute-done.2.first_refs_1_
  31.1 1.0 %collective-permute-done.3.second_refs_1_ = bf16[4,32,128]{2,1,0:T(8,128)(2,1)S(1)} collective-permute-done((bf16[4,32,128]{2,1,0:T(8,128)(2,1)S(1)}, bf16[4,32,128]{2,1,0:T(8,128)(2,1)S(1)}, u32[]{:S(2)}, u32[]{:S(2)}) %collective-permute-start.3) | collective-permute-done | bytes 32800 | tf_op jit(solution)/shard_map/ppermute | solution.py:346
  32.1 0.0 collective-permute-done.4.own_refs_1_
  32.2 1.4 %predict.1.guess_ref = f32[64,2048]{1,0:T(8,128)S(1)} custom-call(bf16[4,32,128]{2,1,0:T(8,128)(2,1)S(1)} %collective-permute-done.first_refs_0_, bf16[4,32,128]{2,1,0:T(8,128)(2,1)S(1)} %collective-permute-done.2.first_refs_1_, bf16[4,32,128]{2,1,0:T(8,128)(2,1)S(1)} %collective-permute-done.1.second_refs_0_, ...), custom_call_target="tpu_custom_call" | custom-call | flops 1000000000 | tf_op jit(solution)/shard_map/predict/pallas_call | solution.py:21
  33.6 1.5 %collective-permute-done.5.x_others_refs_0_ = f32[32,1024]{1,0:T(8,128)S(1)} collective-permute-done((f32[32,1024]{1,0:T(8,128)}, f32[32,1024]{1,0:T(8,128)S(1)}, u32[]{:S(2)}, u32[]{:S(2)}) %collective-permute-start.5) | collective-permute-done | bytes 131104 | tf_op jit(solution)/shard_map/ppermute | solution.py:346
  35.1 1.2 %unpack_readings.3 = (f32[32,1024]{1,0:T(8,128)S(1)}, f32[1,1024]{1,0:T(1,128)S(1)}) custom-call(s32[16,128]{1,0:T(8,128)S(1)} %get-tuple-element.48.group_ref, s32[16,128]{1,0:T(8,128)S(1)} %get-tuple-element.49.lane_ref, f32[16,72,128]{2,1,0:T(8,128)S(1)} %all-to-all-done.message_ref), custom_call_target="tpu_custom_call" | custom-call | flops 2000000000 | tf_op jit(solution)/shard_map/unpack_readings/pallas_call | solution.py:21
  36.3 0.0 copy-start
  36.3 0.0 copy-start.2
  36.3 0.0 copy-start.3
  36.3 1.2 %unpack_readings.2 = (f32[32,1024]{1,0:T(8,128)S(1)}, f32[1,1024]{1,0:T(1,128)S(1)}) custom-call(s32[16,128]{1,0:T(8,128)S(1)} %get-tuple-element.48.group_ref, s32[16,128]{1,0:T(8,128)S(1)} %get-tuple-element.49.lane_ref, f32[16,72,128]{2,1,0:T(8,128)S(1)} %all-to-all-done.message_ref), custom_call_target="tpu_custom_call" | custom-call | flops 2000000000 | tf_op jit(solution)/shard_map/unpack_readings/pallas_call | solution.py:21
  37.5 1.5 %collective-permute-start.7 = (f32[32,1024]{1,0:T(8,128)S(1)}, f32[32,1024]{1,0:T(8,128)S(1)}, u32[]{:S(2)}, u32[]{:S(2)}) collective-permute-start(f32[32,1024]{1,0:T(8,128)S(1)} %get-tuple-element.52.z_refs_1_), channel_id=1, source_target_pairs={{0,1},{1,0},{2,3},{3,2},{4,5},{5,4},{6,7},{7,6},{8,9},{9,8},{10,11... | collective-permute-start | bytes 393224 | tf_op jit(solution)/shard_map/ppermute | solution.py:346
  39.1 0.5 collective-permute-start.6
  39.6 2.9 %collective-permute-done.7 = f32[32,1024]{1,0:T(8,128)S(1)} collective-permute-done((f32[32,1024]{1,0:T(8,128)S(1)}, f32[32,1024]{1,0:T(8,128)S(1)}, u32[]{:S(2)}, u32[]{:S(2)}) %collective-permute-start.7) | collective-permute-done | bytes 131104 | tf_op jit(solution)/shard_map/ppermute | solution.py:346
  42.6 1.5 %collective-permute-done.6 = f32[32,1024]{1,0:T(8,128)S(1)} collective-permute-done((f32[32,1024]{1,0:T(8,128)S(1)}, f32[32,1024]{1,0:T(8,128)S(1)}, u32[]{:S(2)}, u32[]{:S(2)}) %collective-permute-start.6) | collective-permute-done | bytes 131104 | tf_op jit(solution)/shard_map/ppermute | solution.py:346
  44.0 1.5 %pull.1 = (f32[16,64,128]{2,1,0:T(8,128)S(1)}, bf16[4,64,128]{2,1,0:T(8,128)(2,1)S(1)}, bf16[4,64,128]{2,1,0:T(8,128)(2,1)S(1)}) custom-call(f32[64,2048]{1,0:T(8,128)S(1)} %predict.1.guess_ref, f32[32,1024]{1,0:T(8,128)S(1)} %get-tuple-element.51.z_refs_0_, f32[32,1024]{1,0:T(8,128)S(1)} %get-tuple-element.52.z_refs_1_, f32[1,32,1024]{2,1,0:T(8,128)S(1)} %bitcast.11, ...), custom_call_target="tpu_custom_call" | custom-call | tf_op jit(solution)/shard_map/pull/pallas_call | solution.py:21
  45.5 1.9 %collective-permute-start.8 = (bf16[4,64,128]{2,1,0:T(8,128)(2,1)S(1)}, bf16[4,64,128]{2,1,0:T(8,128)(2,1)S(1)}, u32[]{:S(2)}, u32[]{:S(2)}) collective-permute-start(bf16[4,64,128]{2,1,0:T(8,128)(2,1)S(1)} %get-tuple-element.56), channel_id=1, source_target_pairs={{2,4},{6,8},{10,12},{14,16},{18,20},{22,24},{26,28},{4,2},{8,6},{1... | collective-permute-start | bytes 196616 | tf_op jit(solution)/shard_map/ppermute | solution.py:337
  47.4 0.1 collective-permute-start.9
  47.5 4.5 %collective-permute-done.8.back_first_ref = bf16[4,64,128]{2,1,0:T(8,128)(2,1)S(1)} collective-permute-done((bf16[4,64,128]{2,1,0:T(8,128)(2,1)S(1)}, bf16[4,64,128]{2,1,0:T(8,128)(2,1)S(1)}, u32[]{:S(2)}, u32[]{:S(2)}) %collective-permute-start.8) | collective-permute-done | bytes 65568 | tf_op jit(solution)/shard_map/ppermute | solution.py:337
  52.0 2.1 %first_update.1 = (f32[8,32,128]{2,1,0:T(8,128)S(1)}, f32[8,32,128]{2,1,0:T(8,128)S(1)}, bf16[8,64,128]{2,1,0:T(8,128)(2,1)S(1)}, bf16[4,64,128]{2,1,0:T(8,128)(2,1)S(1)}) custom-call(f32[16,64,128]{2,1,0:T(8,128)S(1)} %get-tuple-element.55.grad_ref, bf16[4,64,128]{2,1,0:T(8,128)(2,1)S(1)} %collective-permute-done.8.back_first_ref, ...), custom_call_target="tpu_custom_call" | custom-call | tf_op jit(solution)/shard_map/first_update/pallas_call | solution.py:21
  54.1 1.5 %collective-permute-start.12 = (bf16[8,64,128]{2,1,0:T(8,128)(2,1)S(1)}, bf16[8,64,128]{2,1,0:T(8,128)(2,1)S(1)}, u32[]{:S(2)}, u32[]{:S(2)}) collective-permute-start(bf16[8,64,128]{2,1,0:T(8,128)(2,1)S(1)} %get-tuple-element.60.mine_ref), channel_id=1, source_target_pairs={{0,1},{1,0},{2,3},{3,2},{4,5},{5,4},{6,7},{7,6},{8,9},{9,8},{10,11... | collective-permute-start | bytes 393224 | tf_op jit(solution)/shard_map/ppermute | solution.py:346
  55.6 1.9 %collective-permute-start.10 = (bf16[4,64,128]{2,1,0:T(8,128)(2,1)S(1)}, bf16[4,64,128]{2,1,0:T(8,128)(2,1)S(1)}, u32[]{:S(2)}, u32[]{:S(2)}) collective-permute-start(bf16[4,64,128]{2,1,0:T(8,128)(2,1)S(1)} %get-tuple-element.59), channel_id=1, source_target_pairs={{2,4},{6,8},{10,12},{14,16},{18,20},{22,24},{26,28},{4,2},{8,6},{1... | collective-permute-start | bytes 196616 | tf_op jit(solution)/shard_map/ppermute | solution.py:337
  57.5 4.6 %collective-permute-done.10.first_refs_0_ = bf16[4,64,128]{2,1,0:T(8,128)(2,1)S(1)} collective-permute-done((bf16[4,64,128]{2,1,0:T(8,128)(2,1)S(1)}, bf16[4,64,128]{2,1,0:T(8,128)(2,1)S(1)}, u32[]{:S(2)}, u32[]{:S(2)}) %collective-permute-start.10) | collective-permute-done | bytes 65568 | tf_op jit(solution)/shard_map/ppermute | solution.py:337
  62.0 0.6 collective-permute-start.11
  62.7 0.6 join_states.1
  63.3 0.1 collective-permute-start.13
  63.4 2.9 %collective-permute-done.11.first_refs_1_ = bf16[4,64,128]{2,1,0:T(8,128)(2,1)S(1)} collective-permute-done((bf16[4,64,128]{2,1,0:T(8,128)(2,1)S(1)}, bf16[4,64,128]{2,1,0:T(8,128)(2,1)S(1)}, u32[]{:S(2)}, u32[]{:S(2)}) %collective-permute-start.11) | collective-permute-done | bytes 65568 | tf_op jit(solution)/shard_map/ppermute | solution.py:346
  66.3 2.0 %predict_pull.1 = (f32[16,64,128]{2,1,0:T(8,128)S(1)}, bf16[4,64,128]{2,1,0:T(8,128)(2,1)S(1)}, bf16[4,64,128]{2,1,0:T(8,128)(2,1)S(1)}) custom-call(bf16[4,64,128]{2,1,0:T(8,128)(2,1)S(1)} %collective-permute-done.10.first_refs_0_, bf16[4,64,128]{2,1,0:T(8,128)(2,1)S(1)} %collective-permute-done.11.first_refs_1_, ...), custom_call_target="tpu_custom_call" | custom-call | tf_op jit(solution)/shard_map/predict_pull/pallas_call | solution.py:21
  68.3 1.9 %collective-permute-start.14 = (bf16[4,64,128]{2,1,0:T(8,128)(2,1)S(1)}, bf16[4,64,128]{2,1,0:T(8,128)(2,1)S(1)}, u32[]{:S(2)}, u32[]{:S(2)}) collective-permute-start(bf16[4,64,128]{2,1,0:T(8,128)(2,1)S(1)} %get-tuple-element.67), channel_id=1, source_target_pairs={{2,4},{6,8},{10,12},{14,16},{18,20},{22,24},{26,28},{4,2},{8,6},{1... | collective-permute-start | bytes 196616 | tf_op jit(solution)/shard_map/ppermute | solution.py:337
  70.2 0.1 collective-permute-start.15
  70.3 0.7 collective-permute-start.16
  71.0 3.8 %collective-permute-done.14.back_first_ref = bf16[4,64,128]{2,1,0:T(8,128)(2,1)S(1)} collective-permute-done((bf16[4,64,128]{2,1,0:T(8,128)(2,1)S(1)}, bf16[4,64,128]{2,1,0:T(8,128)(2,1)S(1)}, u32[]{:S(2)}, u32[]{:S(2)}) %collective-permute-start.14) | collective-permute-done | bytes 65568 | tf_op jit(solution)/shard_map/ppermute | solution.py:337
  74.8 2.0 %last_update.1 = (f32[32,1024]{1,0:T(8,128)S(1)}, bf16[32,1024]{1,0:T(8,128)(2,1)S(1)}) custom-call(f32[16,64,128]{2,1,0:T(8,128)S(1)} %get-tuple-element.63.grad_ref, bf16[4,64,128]{2,1,0:T(8,128)(2,1)S(1)} %collective-permute-done.14.back_first_ref, bf16[4,64,128]{2,1,0:T(8,128)(2,1)S(1)} %collective-permute-done.15.back_second_ref, s32[2,4]{1,0:T(2,128)S(1)} %bitcast.16, ...), custom_call_target="tpu_custom_call" | custom-call | tf_op jit(solution)/shard_map/last_update/pallas_call | solution.py:21
  76.8 0.7 collective-permute-start.17
  77.5 3.6 %collective-permute-done.17.updates_refs_0_ = bf16[32,1024]{1,0:T(8,128)(2,1)S(1)} collective-permute-done((bf16[32,1024]{1,0:T(8,128)(2,1)S(1)}, bf16[32,1024]{1,0:T(8,128)(2,1)S(1)}, u32[]{:S(2)}, u32[]{:S(2)}) %collective-permute-start.17) | collective-permute-done | bytes 65568 | tf_op jit(solution)/shard_map/ppermute | solution.py:346
  81.2 0.7 finish.1
  (15 shorter events, 0.0 us)
Async XLA Ops:
  0.0 32.1 %copy-start.1 = (bf16[16,4,128,128]{3,2,1,0:T(8,128)(2,1)S(1)}, bf16[16,4,128,128]{3,2,1,0:T(8,128)(2,1)}, u32[]{:S(2)}) copy-start(bf16[16,4,128,128]{3,2,1,0:T(8,128)(2,1)} %tiles_ref.5) | copy-start | bytes 6291460
  0.0 32.1 %copy-start.4 = (s32[1,16,4]{1,2,0:T(4,128)S(1)}, s32[1,16,4]{1,2,0:T(4,128)}, u32[]{:S(2)}) copy-start(s32[1,16,4]{1,2,0:T(4,128)} %param.13) | copy-start | bytes 772
  4.5 27.7 %copy-start.5 = (bf16[16,32,128]{2,1,0:T(8,128)(2,1)S(1)}, bf16[16,32,128]{2,1,0:T(8,128)(2,1)}, u32[]{:S(2)}) copy-start(bf16[16,32,128]{2,1,0:T(8,128)(2,1)} %get-tuple-element.45.own_refs_0_) | copy-start | bytes 393220
  4.5 30.6 %all-to-all-start = ((f32[16,72,128]{2,1,0:T(8,128)}), f32[16,72,128]{2,1,0:T(8,128)S(1)}, u32[]{:S(2)}, u32[]{:S(2)}) async-start(f32[16,72,128]{2,1,0:T(8,128)} %get-tuple-element.39), calls=%async_computation | async-start | bytes 1179648 | tf_op jit(solution)/shard_map/all_to_all | solution.py:427
  10.8 21.3 %collective-permute-start.4 = (bf16[16,32,128]{2,1,0:T(8,128)(2,1)}, bf16[16,32,128]{2,1,0:T(8,128)(2,1)S(1)}, u32[]{:S(2)}, u32[]{:S(2)}) collective-permute-start(bf16[16,32,128]{2,1,0:T(8,128)(2,1)} %get-tuple-element.45.own_refs_0_), channel_id=1, source_target_pairs={{0,1},{1,0},{2,3},{3,2},{4,5},{5,4},{6,7},{7,6},{8,9},{9,8},{10,11... | collective-permute-start | bytes 393224 | tf_op jit(solution)/shard_map/ppermute | solution.py:346
  12.3 14.1 %collective-permute-start = (bf16[4,32,128]{2,1,0:T(8,128)(2,1)}, bf16[4,32,128]{2,1,0:T(8,128)(2,1)S(1)}, u32[]{:S(2)}, u32[]{:S(2)}) collective-permute-start(bf16[4,32,128]{2,1,0:T(8,128)(2,1)} %get-tuple-element.40), channel_id=1, source_target_pairs={{2,4},{6,8},{10,12},{14,16},{18,20},{22,24},{26,28},{4,2},{8,6},{1... | collective-permute-start | bytes 98312 | tf_op jit(solution)/shard_map/ppermute | solution.py:337
  15.2 11.2 %collective-permute-start.1 = (bf16[4,32,128]{2,1,0:T(8,128)(2,1)}, bf16[4,32,128]{2,1,0:T(8,128)(2,1)S(1)}, u32[]{:S(2)}, u32[]{:S(2)}) collective-permute-start(bf16[4,32,128]{2,1,0:T(8,128)(2,1)} %get-tuple-element.41), channel_id=1, source_target_pairs={{0,2},{4,6},{8,10},{12,14},{16,18},{20,22},{24,26},{28,30},{2,0},{... | collective-permute-start | bytes 98312 | tf_op jit(solution)/shard_map/ppermute | solution.py:337
  26.4 4.7 %collective-permute-start.2 = (bf16[4,32,128]{2,1,0:T(8,128)(2,1)S(1)}, bf16[4,32,128]{2,1,0:T(8,128)(2,1)S(1)}, u32[]{:S(2)}, u32[]{:S(2)}) collective-permute-start(bf16[4,32,128]{2,1,0:T(8,128)(2,1)S(1)} %collective-permute-done.first_refs_0_), channel_id=1, source_target_pairs={{0,1},{1,0},{2,3},{3,2},{4,5},{5,4},{6,7},{7,6},{8,9},{9,8},{10,11... | collective-permute-start | bytes 98312 | tf_op jit(solution)/shard_map/ppermute | solution.py:346
  27.9 4.2 %collective-permute-start.3 = (bf16[4,32,128]{2,1,0:T(8,128)(2,1)S(1)}, bf16[4,32,128]{2,1,0:T(8,128)(2,1)S(1)}, u32[]{:S(2)}, u32[]{:S(2)}) collective-permute-start(bf16[4,32,128]{2,1,0:T(8,128)(2,1)S(1)} %collective-permute-done.1.second_refs_0_), channel_id=1, source_target_pairs={{0,1},{1,0},{2,3},{3,2},{4,5},{5,4},{6,7},{7,6},{8,9},{9,8},{10,11... | collective-permute-start | bytes 98312 | tf_op jit(solution)/shard_map/ppermute | solution.py:346
  28.4 6.6 %collective-permute-start.5 = (f32[32,1024]{1,0:T(8,128)}, f32[32,1024]{1,0:T(8,128)S(1)}, u32[]{:S(2)}, u32[]{:S(2)}) collective-permute-start(f32[32,1024]{1,0:T(8,128)} %get-tuple-element.46), channel_id=1, source_target_pairs={{0,1},{1,0},{2,3},{3,2},{4,5},{5,4},{6,7},{7,6},{8,9},{9,8},{10,11... | collective-permute-start | bytes 393224 | tf_op jit(solution)/shard_map/ppermute | solution.py:346
  29.9 0.7 copy-start.6
  36.3 15.7 %copy-start = (bf16[1024,2048]{1,0:T(8,128)(2,1)S(1)}, bf16[1024,2048]{1,0:T(8,128)(2,1)}, u32[]{:S(2)}) copy-start(bf16[1024,2048]{1,0:T(8,128)(2,1)} %gain_ref.3) | copy-start | bytes 12582916
  36.3 15.7 %copy-start.2 = (f32[32,2048]{1,0:T(8,128)S(1)}, f32[32,2048]{1,0:T(8,128)}, u32[]{:S(2)}) copy-start(f32[32,2048]{1,0:T(8,128)} %x_ref.1) | copy-start | bytes 786436
  36.3 15.7 %copy-start.3 = (s32[1,2,4]{2,1,0:T(2,128)S(1)}, s32[1,2,4]{2,1,0:T(2,128)}, u32[]{:S(2)}) copy-start(s32[1,2,4]{2,1,0:T(2,128)} %param.14) | copy-start | bytes 100
  37.5 5.0 %collective-permute-start.7 = (f32[32,1024]{1,0:T(8,128)S(1)}, f32[32,1024]{1,0:T(8,128)S(1)}, u32[]{:S(2)}, u32[]{:S(2)}) collective-permute-start(f32[32,1024]{1,0:T(8,128)S(1)} %get-tuple-element.52.z_refs_1_), channel_id=1, source_target_pairs={{0,1},{1,0},{2,3},{3,2},{4,5},{5,4},{6,7},{7,6},{8,9},{9,8},{10,11... | collective-permute-start | bytes 393224 | tf_op jit(solution)/shard_map/ppermute | solution.py:346
  39.1 5.0 %collective-permute-start.6 = (f32[32,1024]{1,0:T(8,128)S(1)}, f32[32,1024]{1,0:T(8,128)S(1)}, u32[]{:S(2)}, u32[]{:S(2)}) collective-permute-start(f32[32,1024]{1,0:T(8,128)S(1)} %get-tuple-element.51.z_refs_0_), channel_id=1, source_target_pairs={{0,1},{1,0},{2,3},{3,2},{4,5},{5,4},{6,7},{7,6},{8,9},{9,8},{10,11... | collective-permute-start | bytes 393224 | tf_op jit(solution)/shard_map/ppermute | solution.py:346
  45.5 6.5 %collective-permute-start.8 = (bf16[4,64,128]{2,1,0:T(8,128)(2,1)S(1)}, bf16[4,64,128]{2,1,0:T(8,128)(2,1)S(1)}, u32[]{:S(2)}, u32[]{:S(2)}) collective-permute-start(bf16[4,64,128]{2,1,0:T(8,128)(2,1)S(1)} %get-tuple-element.56), channel_id=1, source_target_pairs={{2,4},{6,8},{10,12},{14,16},{18,20},{22,24},{26,28},{4,2},{8,6},{1... | collective-permute-start | bytes 196616 | tf_op jit(solution)/shard_map/ppermute | solution.py:337
  47.4 4.6 %collective-permute-start.9 = (bf16[4,64,128]{2,1,0:T(8,128)(2,1)S(1)}, bf16[4,64,128]{2,1,0:T(8,128)(2,1)S(1)}, u32[]{:S(2)}, u32[]{:S(2)}) collective-permute-start(bf16[4,64,128]{2,1,0:T(8,128)(2,1)S(1)} %get-tuple-element.57), channel_id=1, source_target_pairs={{0,2},{4,6},{8,10},{12,14},{16,18},{20,22},{24,26},{28,30},{2,0},{... | collective-permute-start | bytes 196616 | tf_op jit(solution)/shard_map/ppermute | solution.py:337
  54.1 8.6 %collective-permute-start.12 = (bf16[8,64,128]{2,1,0:T(8,128)(2,1)S(1)}, bf16[8,64,128]{2,1,0:T(8,128)(2,1)S(1)}, u32[]{:S(2)}, u32[]{:S(2)}) collective-permute-start(bf16[8,64,128]{2,1,0:T(8,128)(2,1)S(1)} %get-tuple-element.60.mine_ref), channel_id=1, source_target_pairs={{0,1},{1,0},{2,3},{3,2},{4,5},{5,4},{6,7},{7,6},{8,9},{9,8},{10,11... | collective-permute-start | bytes 393224 | tf_op jit(solution)/shard_map/ppermute | solution.py:346
  55.6 6.5 %collective-permute-start.10 = (bf16[4,64,128]{2,1,0:T(8,128)(2,1)S(1)}, bf16[4,64,128]{2,1,0:T(8,128)(2,1)S(1)}, u32[]{:S(2)}, u32[]{:S(2)}) collective-permute-start(bf16[4,64,128]{2,1,0:T(8,128)(2,1)S(1)} %get-tuple-element.59), channel_id=1, source_target_pairs={{2,4},{6,8},{10,12},{14,16},{18,20},{22,24},{26,28},{4,2},{8,6},{1... | collective-permute-start | bytes 196616 | tf_op jit(solution)/shard_map/ppermute | solution.py:337
  62.0 4.3 %collective-permute-start.11 = (bf16[4,64,128]{2,1,0:T(8,128)(2,1)S(1)}, bf16[4,64,128]{2,1,0:T(8,128)(2,1)S(1)}, u32[]{:S(2)}, u32[]{:S(2)}) collective-permute-start(bf16[4,64,128]{2,1,0:T(8,128)(2,1)S(1)} %collective-permute-done.10.first_refs_0_), channel_id=1, source_target_pairs={{0,1},{1,0},{2,3},{3,2},{4,5},{5,4},{6,7},{7,6},{8,9},{9,8},{10,11... | collective-permute-start | bytes 196616 | tf_op jit(solution)/shard_map/ppermute | solution.py:346
  63.3 3.0 %collective-permute-start.13 = (bf16[4,64,128]{2,1,0:T(8,128)(2,1)S(1)}, bf16[4,64,128]{2,1,0:T(8,128)(2,1)S(1)}, u32[]{:S(2)}, u32[]{:S(2)}) collective-permute-start(bf16[4,64,128]{2,1,0:T(8,128)(2,1)S(1)} %get-tuple-element.62), channel_id=1, source_target_pairs={{0,2},{4,6},{8,10},{12,14},{16,18},{20,22},{24,26},{28,30},{2,0},{... | collective-permute-start | bytes 196616 | tf_op jit(solution)/shard_map/ppermute | solution.py:337
  68.3 6.5 %collective-permute-start.14 = (bf16[4,64,128]{2,1,0:T(8,128)(2,1)S(1)}, bf16[4,64,128]{2,1,0:T(8,128)(2,1)S(1)}, u32[]{:S(2)}, u32[]{:S(2)}) collective-permute-start(bf16[4,64,128]{2,1,0:T(8,128)(2,1)S(1)} %get-tuple-element.67), channel_id=1, source_target_pairs={{2,4},{6,8},{10,12},{14,16},{18,20},{22,24},{26,28},{4,2},{8,6},{1... | collective-permute-start | bytes 196616 | tf_op jit(solution)/shard_map/ppermute | solution.py:337
  70.2 4.6 %collective-permute-start.15 = (bf16[4,64,128]{2,1,0:T(8,128)(2,1)S(1)}, bf16[4,64,128]{2,1,0:T(8,128)(2,1)S(1)}, u32[]{:S(2)}, u32[]{:S(2)}) collective-permute-start(bf16[4,64,128]{2,1,0:T(8,128)(2,1)S(1)} %get-tuple-element.68), channel_id=1, source_target_pairs={{0,2},{4,6},{8,10},{12,14},{16,18},{20,22},{24,26},{28,30},{2,0},{... | collective-permute-start | bytes 196616 | tf_op jit(solution)/shard_map/ppermute | solution.py:337
  70.3 10.9 %collective-permute-start.16 = (f32[8,32,128]{2,1,0:T(8,128)S(1)}, f32[8,32,128]{2,1,0:T(8,128)S(1)}, u32[]{:S(2)}, u32[]{:S(2)}) collective-permute-start(f32[8,32,128]{2,1,0:T(8,128)S(1)} %get-tuple-element.71), channel_id=1, source_target_pairs={{0,1},{1,0},{2,3},{3,2},{4,5},{5,4},{6,7},{7,6},{8,9},{9,8},{10,11... | collective-permute-start | bytes 393224 | tf_op jit(solution)/shard_map/ppermute | solution.py:346
  76.8 4.3 %collective-permute-start.17 = (bf16[32,1024]{1,0:T(8,128)(2,1)S(1)}, bf16[32,1024]{1,0:T(8,128)(2,1)S(1)}, u32[]{:S(2)}, u32[]{:S(2)}) collective-permute-start(bf16[32,1024]{1,0:T(8,128)(2,1)S(1)} %get-tuple-element.72), channel_id=1, source_target_pairs={{0,1},{1,0},{2,3},{3,2},{4,5},{5,4},{6,7},{7,6},{8,9},{9,8},{10,11... | collective-permute-start | bytes 196616 | tf_op jit(solution)/shard_map/ppermute | solution.py:346

commit v10 on v9

--- a/solution.py
+++ b/solution.py
@@ -41,13 +41,11 @@
 
 
 def pack_kernel(
-    z_in, v_in, hub_in, x_in, ties_in, out, rounded_out, first_out, second_out, sent_outs,
-    z_ref, v_ref, hub_ref, x_ref, ties_ref, out_ref, rounded_ref, first_ref, second_ref,
+    z_in, v_in, hub_in, x_in, out, rounded_out, sent_outs,
+    z_ref, v_ref, hub_ref, x_ref, out_ref, rounded_ref,
     sems, out_sems, sent_sems,
 ):
-    pairs = (
-        (x_in, x_ref), (ties_in, ties_ref), (hub_in, hub_ref), (z_in, z_ref), (v_in, v_ref)
-    )
+    pairs = ((x_in, x_ref), (hub_in, hub_ref), (z_in, z_ref), (v_in, v_ref))
     copies = [
         pltpu.make_async_copy(source, target, sems.at[i])
         for i, (source, target) in enumerate(pairs)
@@ -58,9 +56,7 @@
         copy.wait()
     for b in range(rounded_ref.shape[0]):
         rounded_ref[b] = x_ref[:, b * BLK : (b + 1) * BLK].astype(BF16)
-    pick(rounded_ref, ties_ref, 1 - parity(), first_ref)
-    pick(rounded_ref, ties_ref, parity(), second_ref)
-    ready = [(first_ref, first_out), (second_ref, second_out), (rounded_ref, rounded_out)]
+    ready = [(rounded_ref, rounded_out)]
     members = len(sent_outs) + 1
     part = x_ref.shape[1] // members
     for i, sent_out in enumerate(sent_outs, 1):
@@ -197,16 +193,23 @@
     return lax.dot_general(chosen, weights, NT, preferred_element_type=F32)
 
 
+def pick_kernel(own_refs, ties_ref, first_ref, second_ref):
+    snaps = own_refs[0].shape[1]
+    for i, own_ref in enumerate(own_refs):
+        rows = slice(i * snaps, (i + 1) * snaps)
+        pick(own_ref, ties_ref, 1 - parity(), first_ref.at[:, rows])
+        pick(own_ref, ties_ref, parity(), second_ref.at[:, rows])
+
+
 def predict_kernel(
-    first_refs, second_refs, own_refs, tiles_ref, place_ref, out_ref, slots_ref
+    first_ref, second_ref, own_refs, tiles_ref, place_ref, out_ref, slots_ref
 ):
     own, snaps = own_refs[0].shape[:2]
-    ties = first_refs[0].shape[0]
-    for i in range(len(own_refs)):
-        rows = slice(i * snaps, (i + 1) * snaps)
-        slots_ref[:own, rows] = own_refs[i][...]
-        slots_ref[pl.ds(own + ties * (1 - parity()), ties), rows] = first_refs[i][...]
-        slots_ref[pl.ds(own + ties * parity(), ties), rows] = second_refs[i][...]
+    ties = first_ref.shape[0]
+    for i, own_ref in enumerate(own_refs):
+        slots_ref[:own, i * snaps : (i + 1) * snaps] = own_ref[...]
+    slots_ref[pl.ds(own + ties * (1 - parity()), ties)] = first_ref[...]
+    slots_ref[pl.ds(own + ties * parity(), ties)] = second_ref[...]
     predict(tiles_ref, place_ref, out_ref, slots_ref)
 
 
@@ -384,39 +387,32 @@
     holder = holder_line_order[0].reshape(chunks, width)
     depth = (width // BLK) * snaps + 8
 
-    few = shape((ties, snaps, BLK), BF16)
-    message, rounded, first, second, x_sent = call(
+    message, rounded, x_sent = call(
         pack_kernel,
         (
             shape((chunks, depth, BLK), F32),
             shape((own, snaps, BLK), BF16),
-            few,
-            few,
             [shape((snaps, held * BLK), F32)] * (members - 1),
         ),
-        [HBM] * 5,
+        [HBM] * 4,
         (
             phasor_readings,
             reading_error_spread.reshape(lines // BLK, BLK),
             hub,
             starting_voltages,
-            ties_table,
         ),
         scratch=[
             pltpu.VMEM((snaps, lines), F32),
             pltpu.VMEM((lines // BLK, BLK), F32),
             pltpu.VMEM((chunks, width), jnp.int32),
             pltpu.VMEM((snaps, states), F32),
-            pltpu.SMEM(ties_table.shape, jnp.int32),
             pltpu.VMEM((chunks, depth, BLK), F32),
             pltpu.VMEM((own, snaps, BLK), BF16),
-            pltpu.VMEM((ties, snaps, BLK), BF16),
-            pltpu.VMEM((ties, snaps, BLK), BF16),
-            pltpu.SemaphoreType.DMA((5,)),
+            pltpu.SemaphoreType.DMA((4,)),
             pltpu.SemaphoreType.DMA((chunks,)),
-            pltpu.SemaphoreType.DMA((members + 2,)),
+            pltpu.SemaphoreType.DMA((members,)),
         ],
-        out_spec=(HBM, HBM, HBM, HBM, [HBM] * (members - 1)),
+        out_spec=(HBM, HBM, [HBM] * (members - 1)),
         mib=60,
         name="pack_readings",
     )
@@ -439,16 +435,21 @@
     )
     boundary = shape((ties, everything, BLK), BF16)
     owns = [rounded] + [from_snap(rounded, i) for i in range(1, members)]
+    first, second = call(
+        pick_kernel,
+        (boundary, boundary),
+        [[VMEM] * members, SMEM],
+        (owns, ties_table),
+        name="pick_boundary",
+    )
+    first, second, x_sent = lax.optimization_barrier((first, second, x_sent))
     first, second = with_neighbours(first, second)
-    first, second, x_sent = lax.optimization_barrier((first, second, x_sent))
-    firsts = [first] + [from_snap(first, i) for i in range(1, members)]
-    seconds = [second] + [from_snap(second, i) for i in range(1, members)]
     x_others = [from_snap(block, i) for i, block in enumerate(x_sent, 1)]
     guess = call(
         predict_kernel,
         shape((everything, lines), F32),
-        [[VMEM] * members, [VMEM] * members, [VMEM] * members, VMEM, SMEM],
-        (firsts, seconds, owns, derivative_pieces, place),
+        [VMEM, VMEM, [VMEM] * members, VMEM, SMEM],
+        (first, second, owns, derivative_pieces, place),
         scratch=[pltpu.VMEM((slots, everything, BLK), BF16)],
         flops=10**9,
         name="predict",

time: 82.3 us -> 77 us (0.936)
  waiting for transfers between devices: 36.9 us -> 25.6 us
  local copies, waits for them, and re-layouts: 0.75 us -> 3.91 us
  starting transfers between devices: 26.4 us -> 28.6 us
    ppermute x8, waiting for transfers between devices: 23.3 us -> 10.3 us  [swap_pair(): return lax.ppermute(block, 'area', pairs + [(b, a) for a, b in pairs])]
    ppermute x8, starting transfers between devices: 9.5 us -> 13.5 us  [swap_pair(): return lax.ppermute(block, 'area', pairs + [(b, a) for a, b in pairs])]
    unnamed x14 -> x20, local copies, waits for them, and re-layouts: 0.75 us -> 3.91 us
    ppermute x10 -> x8, waiting for transfers between devices: 13.5 us -> 15.3 us  [from_snap(): lax.ppermute(block, 'snap', [(i, (i + distance) % members) for i in range...]
    ppermute x10 -> x8, starting transfers between devices: 10.6 us -> 8.98 us  [from_snap(): lax.ppermute(block, 'snap', [(i, (i + distance) % members) for i in range...]
    pallas_call x11 -> x12, Pallas kernels: 17.7 us -> 18.1 us  [call(): pl.pallas_call(kernel, out_shape=outs, in_specs=ins, out_specs=jax.tree.m...]
  transfers between devices with their start and end apart: 19 -> 17, of which waited for: 10 -> 9; matrix products, arithmetic and copies ran while one was open for 0% -> 0% of each run, Pallas kernels for 5% -> 7%
where the time goes in v10:
time: 77 us; the launch traced here: 76.4 us
  starting transfers between devices  28.6 us (37%)
  waiting for transfers between devices  25.6 us (33%)
  Pallas kernels  18.1 us (24%)
  local copies, waits for them, and re-layouts  3.91 us (5%)
    pallas_call x12, Pallas kernels, call(): pl.pallas_call(kernel, out_shape=outs, in_specs=ins, out_specs=jax.tree.m...  18.1 us
    ppermute x8, waiting for transfers between devices, from_snap(): lax.ppermute(block, 'snap', [(i, (i + distance) % members) for i in range...  15.3 us
    ppermute x8, starting transfers between devices, swap_pair(): return lax.ppermute(block, 'area', pairs + [(b, a) for a, b in pairs])  13.5 us
    ppermute x8, waiting for transfers between devices, swap_pair(): return lax.ppermute(block, 'area', pairs + [(b, a) for a, b in pairs])  10.3 us
    ppermute x8, starting transfers between devices, from_snap(): lax.ppermute(block, 'snap', [(i, (i + distance) % members) for i in range...  8.98 us
    all_to_all x1, starting transfers between devices, on_device(): lax.all_to_all(message, 'area', split_axis=0, concat_axis=0, tiled=True)  6.17 us
    unnamed x20, local copies, waits for them, and re-layouts  3.91 us
  transfers between devices with their start and end apart: 17, of which 9 were waited for; matrix products, arithmetic and copies ran while one was open for 0% of the time, Pallas kernels for 7%

profile of v10, /device:TPU:16, one launch (start us, length us, event | category | flops | bytes accessed | tf_op | source)
XLA Modules:
  0.0 76.4 jit_solution(12462976335172086552)
XLA Ops:
  0.0 4.4 %pack_readings.1 = (f32[16,72,128]{2,1,0:T(8,128)}, bf16[16,32,128]{2,1,0:T(8,128)(2,1)}, f32[32,1024]{1,0:T(8,128)}) custom-call(f32[32,2048]{1,0:T(8,128)} %z_in.1, f32[16,128]{1,0:T(8,128)} %bitcast.22, s32[16,256]{1,0:T(8,128)} %bitcast.21, f32[32,2048]{1,0:T(8,128)} %x_ref.1), custom_call_target="tpu_custom_call" | custom-call | tf_op jit(solution)/shard_map/pack_readings/pallas_call | solution.py:21
  4.4 6.2 %all-to-all-start = ((f32[16,72,128]{2,1,0:T(8,128)}), f32[16,72,128]{2,1,0:T(8,128)S(1)}, u32[]{:S(2)}, u32[]{:S(2)}) async-start(f32[16,72,128]{2,1,0:T(8,128)} %get-tuple-element.39), calls=%async_computation | async-start | bytes 1179648 | tf_op jit(solution)/shard_map/all_to_all | solution.py:423
  10.6 1.5 %collective-permute-start = (bf16[16,32,128]{2,1,0:T(8,128)(2,1)}, bf16[16,32,128]{2,1,0:T(8,128)(2,1)S(1)}, u32[]{:S(2)}, u32[]{:S(2)}) collective-permute-start(bf16[16,32,128]{2,1,0:T(8,128)(2,1)} %get-tuple-element.40.own_refs_0_), channel_id=1, source_target_pairs={{0,1},{1,0},{2,3},{3,2},{4,5},{5,4},{6,7},{7,6},{8,9},{9,8},{10,11... | collective-permute-start | bytes 393224 | tf_op jit(solution)/shard_map/ppermute | solution.py:349
  12.1 4.2 %collective-permute-done.own_refs_1_ = bf16[16,32,128]{2,1,0:T(8,128)(2,1)S(1)} collective-permute-done((bf16[16,32,128]{2,1,0:T(8,128)(2,1)}, bf16[16,32,128]{2,1,0:T(8,128)(2,1)S(1)}, u32[]{:S(2)}, u32[]{:S(2)}) %collective-permute-start) | collective-permute-done | bytes 131104 | tf_op jit(solution)/shard_map/ppermute | solution.py:349
  16.4 0.9 %copy-done.3 = bf16[16,32,128]{2,1,0:T(8,128)(2,1)S(1)} copy-done((bf16[16,32,128]{2,1,0:T(8,128)(2,1)S(1)}, bf16[16,32,128]{2,1,0:T(8,128)(2,1)}, u32[]{:S(2)}) %copy-start.3) | copy-done | bytes 131096
  17.3 0.7 copy-done.5
  17.9 0.6 pick_boundary.1
  18.6 2.3 %collective-permute-start.1 = (bf16[4,64,128]{2,1,0:T(8,128)(2,1)S(1)}, bf16[4,64,128]{2,1,0:T(8,128)(2,1)S(1)}, u32[]{:S(2)}, u32[]{:S(2)}) collective-permute-start(bf16[4,64,128]{2,1,0:T(8,128)(2,1)S(1)} %get-tuple-element.44), channel_id=1, source_target_pairs={{2,4},{6,8},{10,12},{14,16},{18,20},{22,24},{26,28},{4,2},{8,6},{1... | collective-permute-start | bytes 196616 | tf_op jit(solution)/shard_map/ppermute | solution.py:340
  20.9 1.3 %collective-permute-start.2 = (bf16[4,64,128]{2,1,0:T(8,128)(2,1)S(1)}, bf16[4,64,128]{2,1,0:T(8,128)(2,1)S(1)}, u32[]{:S(2)}, u32[]{:S(2)}) collective-permute-start(bf16[4,64,128]{2,1,0:T(8,128)(2,1)S(1)} %get-tuple-element.45), channel_id=1, source_target_pairs={{0,2},{4,6},{8,10},{12,14},{16,18},{20,22},{24,26},{28,30},{2,0},{... | collective-permute-start | bytes 196616 | tf_op jit(solution)/shard_map/ppermute | solution.py:340
  22.1 1.5 %collective-permute-start.3 = (f32[32,1024]{1,0:T(8,128)}, f32[32,1024]{1,0:T(8,128)S(1)}, u32[]{:S(2)}, u32[]{:S(2)}) collective-permute-start(f32[32,1024]{1,0:T(8,128)} %get-tuple-element.46), channel_id=1, source_target_pairs={{0,1},{1,0},{2,3},{3,2},{4,5},{5,4},{6,7},{7,6},{8,9},{9,8},{10,11... | collective-permute-start | bytes 393224 | tf_op jit(solution)/shard_map/ppermute | solution.py:349
  23.7 0.7 copy-done.9
  24.4 0.4 invert_order.1
  24.8 1.8 %collective-permute-done.1.first_ref = bf16[4,64,128]{2,1,0:T(8,128)(2,1)S(1)} collective-permute-done((bf16[4,64,128]{2,1,0:T(8,128)(2,1)S(1)}, bf16[4,64,128]{2,1,0:T(8,128)(2,1)S(1)}, u32[]{:S(2)}, u32[]{:S(2)}) %collective-permute-start.1) | collective-permute-done | bytes 65568 | tf_op jit(solution)/shard_map/ppermute | solution.py:340
  26.6 0.9 %copy-done.4 = bf16[16,32,128]{2,1,0:T(8,128)(2,1)S(1)} copy-done((bf16[16,32,128]{2,1,0:T(8,128)(2,1)S(1)}, bf16[16,32,128]{2,1,0:T(8,128)(2,1)}, u32[]{:S(2)}) %copy-start.4) | copy-done | bytes 131096
  27.5 0.7 copy-done.7
  28.2 1.4 %predict.1.guess_ref = f32[64,2048]{1,0:T(8,128)S(1)} custom-call(bf16[4,64,128]{2,1,0:T(8,128)(2,1)S(1)} %collective-permute-done.1.first_ref, bf16[4,64,128]{2,1,0:T(8,128)(2,1)S(1)} %collective-permute-done.2.second_ref, bf16[16,32,128]{2,1,0:T(8,128)(2,1)S(1)} %copy-done.4, bf16[16,32,128]{2,1,0:T(8,128)(2,1)S(1)} %collective-permute-done.own_refs_1_, ...), custom_call_target="tpu_custom_call" | custom-call | flops 1000000000 | tf_op jit(solution)/shard_map/predict/pallas_call | solution.py:21
  29.6 0.0 collective-permute-done.3.x_others_refs_0_
  29.6 1.2 %unpack_readings.3 = (f32[32,1024]{1,0:T(8,128)S(1)}, f32[1,1024]{1,0:T(1,128)S(1)}) custom-call(s32[16,128]{1,0:T(8,128)S(1)} %get-tuple-element.48.group_ref, s32[16,128]{1,0:T(8,128)S(1)} %get-tuple-element.49.lane_ref, f32[16,72,128]{2,1,0:T(8,128)S(1)} %all-to-all-done.message_ref), custom_call_target="tpu_custom_call" | custom-call | flops 2000000000 | tf_op jit(solution)/shard_map/unpack_readings/pallas_call | solution.py:21
  30.8 0.0 copy-start.8
  30.8 0.0 copy-start
  30.8 0.0 copy-start.2
  30.9 0.0 copy-start.6
  30.9 1.2 %unpack_readings.2 = (f32[32,1024]{1,0:T(8,128)S(1)}, f32[1,1024]{1,0:T(1,128)S(1)}) custom-call(s32[16,128]{1,0:T(8,128)S(1)} %get-tuple-element.48.group_ref, s32[16,128]{1,0:T(8,128)S(1)} %get-tuple-element.49.lane_ref, f32[16,72,128]{2,1,0:T(8,128)S(1)} %all-to-all-done.message_ref), custom_call_target="tpu_custom_call" | custom-call | flops 2000000000 | tf_op jit(solution)/shard_map/unpack_readings/pallas_call | solution.py:21
  32.1 1.6 %collective-permute-start.5 = (f32[32,1024]{1,0:T(8,128)S(1)}, f32[32,1024]{1,0:T(8,128)S(1)}, u32[]{:S(2)}, u32[]{:S(2)}) collective-permute-start(f32[32,1024]{1,0:T(8,128)S(1)} %get-tuple-element.52.z_refs_1_), channel_id=1, source_target_pairs={{0,1},{1,0},{2,3},{3,2},{4,5},{5,4},{6,7},{7,6},{8,9},{9,8},{10,11... | collective-permute-start | bytes 393224 | tf_op jit(solution)/shard_map/ppermute | solution.py:349
  33.7 0.5 collective-permute-start.4
  34.2 2.9 %collective-permute-done.5 = f32[32,1024]{1,0:T(8,128)S(1)} collective-permute-done((f32[32,1024]{1,0:T(8,128)S(1)}, f32[32,1024]{1,0:T(8,128)S(1)}, u32[]{:S(2)}, u32[]{:S(2)}) %collective-permute-start.5) | collective-permute-done | bytes 131104 | tf_op jit(solution)/shard_map/ppermute | solution.py:349
  37.1 1.5 %collective-permute-done.4 = f32[32,1024]{1,0:T(8,128)S(1)} collective-permute-done((f32[32,1024]{1,0:T(8,128)S(1)}, f32[32,1024]{1,0:T(8,128)S(1)}, u32[]{:S(2)}, u32[]{:S(2)}) %collective-permute-start.4) | collective-permute-done | bytes 131104 | tf_op jit(solution)/shard_map/ppermute | solution.py:349
  38.6 1.4 %pull.1 = (f32[16,64,128]{2,1,0:T(8,128)S(1)}, bf16[4,64,128]{2,1,0:T(8,128)(2,1)S(1)}, bf16[4,64,128]{2,1,0:T(8,128)(2,1)S(1)}) custom-call(f32[64,2048]{1,0:T(8,128)S(1)} %predict.1.guess_ref, f32[32,1024]{1,0:T(8,128)S(1)} %get-tuple-element.51.z_refs_0_, f32[32,1024]{1,0:T(8,128)S(1)} %get-tuple-element.52.z_refs_1_, f32[1,32,1024]{2,1,0:T(8,128)S(1)} %bitcast.11, ...), custom_call_target="tpu_custom_call" | custom-call | tf_op jit(solution)/shard_map/pull/pallas_call | solution.py:21
  40.1 3.8 %collective-permute-start.6 = (bf16[4,64,128]{2,1,0:T(8,128)(2,1)S(1)}, bf16[4,64,128]{2,1,0:T(8,128)(2,1)S(1)}, u32[]{:S(2)}, u32[]{:S(2)}) collective-permute-start(bf16[4,64,128]{2,1,0:T(8,128)(2,1)S(1)} %get-tuple-element.56), channel_id=1, source_target_pairs={{2,4},{6,8},{10,12},{14,16},{18,20},{22,24},{26,28},{4,2},{8,6},{1... | collective-permute-start | bytes 196616 | tf_op jit(solution)/shard_map/ppermute | solution.py:340
  43.8 0.1 collective-permute-start.7
  43.9 2.6 %collective-permute-done.6.back_first_ref = bf16[4,64,128]{2,1,0:T(8,128)(2,1)S(1)} collective-permute-done((bf16[4,64,128]{2,1,0:T(8,128)(2,1)S(1)}, bf16[4,64,128]{2,1,0:T(8,128)(2,1)S(1)}, u32[]{:S(2)}, u32[]{:S(2)}) %collective-permute-start.6) | collective-permute-done | bytes 65568 | tf_op jit(solution)/shard_map/ppermute | solution.py:340
  46.6 2.1 %first_update.1 = (f32[8,32,128]{2,1,0:T(8,128)S(1)}, f32[8,32,128]{2,1,0:T(8,128)S(1)}, bf16[8,64,128]{2,1,0:T(8,128)(2,1)S(1)}, bf16[4,64,128]{2,1,0:T(8,128)(2,1)S(1)}) custom-call(f32[16,64,128]{2,1,0:T(8,128)S(1)} %get-tuple-element.55.grad_ref, bf16[4,64,128]{2,1,0:T(8,128)(2,1)S(1)} %collective-permute-done.6.back_first_ref, ...), custom_call_target="tpu_custom_call" | custom-call | tf_op jit(solution)/shard_map/first_update/pallas_call | solution.py:21
  48.7 1.5 %collective-permute-start.10 = (bf16[8,64,128]{2,1,0:T(8,128)(2,1)S(1)}, bf16[8,64,128]{2,1,0:T(8,128)(2,1)S(1)}, u32[]{:S(2)}, u32[]{:S(2)}) collective-permute-start(bf16[8,64,128]{2,1,0:T(8,128)(2,1)S(1)} %get-tuple-element.60.mine_ref), channel_id=1, source_target_pairs={{0,1},{1,0},{2,3},{3,2},{4,5},{5,4},{6,7},{7,6},{8,9},{9,8},{10,11... | collective-permute-start | bytes 393224 | tf_op jit(solution)/shard_map/ppermute | solution.py:349
  50.1 3.5 %collective-permute-start.8 = (bf16[4,64,128]{2,1,0:T(8,128)(2,1)S(1)}, bf16[4,64,128]{2,1,0:T(8,128)(2,1)S(1)}, u32[]{:S(2)}, u32[]{:S(2)}) collective-permute-start(bf16[4,64,128]{2,1,0:T(8,128)(2,1)S(1)} %get-tuple-element.59), channel_id=1, source_target_pairs={{2,4},{6,8},{10,12},{14,16},{18,20},{22,24},{26,28},{4,2},{8,6},{1... | collective-permute-start | bytes 196616 | tf_op jit(solution)/shard_map/ppermute | solution.py:340
  53.7 2.9 %collective-permute-done.8.first_refs_0_ = bf16[4,64,128]{2,1,0:T(8,128)(2,1)S(1)} collective-permute-done((bf16[4,64,128]{2,1,0:T(8,128)(2,1)S(1)}, bf16[4,64,128]{2,1,0:T(8,128)(2,1)S(1)}, u32[]{:S(2)}, u32[]{:S(2)}) %collective-permute-start.8) | collective-permute-done | bytes 65568 | tf_op jit(solution)/shard_map/ppermute | solution.py:340
  56.6 0.6 collective-permute-start.9
  57.2 0.6 join_states.1
  57.8 0.1 collective-permute-start.11
  57.9 2.9 %collective-permute-done.9.first_refs_1_ = bf16[4,64,128]{2,1,0:T(8,128)(2,1)S(1)} collective-permute-done((bf16[4,64,128]{2,1,0:T(8,128)(2,1)S(1)}, bf16[4,64,128]{2,1,0:T(8,128)(2,1)S(1)}, u32[]{:S(2)}, u32[]{:S(2)}) %collective-permute-start.9) | collective-permute-done | bytes 65568 | tf_op jit(solution)/shard_map/ppermute | solution.py:349
  60.9 2.0 %predict_pull.1 = (f32[16,64,128]{2,1,0:T(8,128)S(1)}, bf16[4,64,128]{2,1,0:T(8,128)(2,1)S(1)}, bf16[4,64,128]{2,1,0:T(8,128)(2,1)S(1)}) custom-call(bf16[4,64,128]{2,1,0:T(8,128)(2,1)S(1)} %collective-permute-done.8.first_refs_0_, bf16[4,64,128]{2,1,0:T(8,128)(2,1)S(1)} %collective-permute-done.9.first_refs_1_, ...), custom_call_target="tpu_custom_call" | custom-call | tf_op jit(solution)/shard_map/predict_pull/pallas_call | solution.py:21
  62.8 2.4 %collective-permute-start.12 = (bf16[4,64,128]{2,1,0:T(8,128)(2,1)S(1)}, bf16[4,64,128]{2,1,0:T(8,128)(2,1)S(1)}, u32[]{:S(2)}, u32[]{:S(2)}) collective-permute-start(bf16[4,64,128]{2,1,0:T(8,128)(2,1)S(1)} %get-tuple-element.67), channel_id=1, source_target_pairs={{2,4},{6,8},{10,12},{14,16},{18,20},{22,24},{26,28},{4,2},{8,6},{1... | collective-permute-start | bytes 196616 | tf_op jit(solution)/shard_map/ppermute | solution.py:340
  65.2 0.1 collective-permute-start.13
  65.3 1.1 %collective-permute-start.14 = (f32[8,32,128]{2,1,0:T(8,128)S(1)}, f32[8,32,128]{2,1,0:T(8,128)S(1)}, u32[]{:S(2)}, u32[]{:S(2)}) collective-permute-start(f32[8,32,128]{2,1,0:T(8,128)S(1)} %get-tuple-element.71), channel_id=1, source_target_pairs={{0,1},{1,0},{2,3},{3,2},{4,5},{5,4},{6,7},{7,6},{8,9},{9,8},{10,11... | collective-permute-start | bytes 393224 | tf_op jit(solution)/shard_map/ppermute | solution.py:349
  66.4 2.9 %collective-permute-done.12.back_first_ref = bf16[4,64,128]{2,1,0:T(8,128)(2,1)S(1)} collective-permute-done((bf16[4,64,128]{2,1,0:T(8,128)(2,1)S(1)}, bf16[4,64,128]{2,1,0:T(8,128)(2,1)S(1)}, u32[]{:S(2)}, u32[]{:S(2)}) %collective-permute-start.12) | collective-permute-done | bytes 65568 | tf_op jit(solution)/shard_map/ppermute | solution.py:340
  69.3 2.0 %last_update.1 = (f32[32,1024]{1,0:T(8,128)S(1)}, bf16[32,1024]{1,0:T(8,128)(2,1)S(1)}) custom-call(f32[16,64,128]{2,1,0:T(8,128)S(1)} %get-tuple-element.63.grad_ref, bf16[4,64,128]{2,1,0:T(8,128)(2,1)S(1)} %collective-permute-done.12.back_first_ref, bf16[4,64,128]{2,1,0:T(8,128)(2,1)S(1)} %collective-permute-done.13.back_second_ref, s32[2,4]{1,0:T(2,128)S(1)} %bitcast.16, ...), custom_call_target="tpu_custom_call" | custom-call | tf_op jit(solution)/shard_map/last_update/pallas_call | solution.py:21
  71.4 0.7 collective-permute-start.15
  72.1 3.6 %collective-permute-done.15.updates_refs_0_ = bf16[32,1024]{1,0:T(8,128)(2,1)S(1)} collective-permute-done((bf16[32,1024]{1,0:T(8,128)(2,1)S(1)}, bf16[32,1024]{1,0:T(8,128)(2,1)S(1)}, u32[]{:S(2)}, u32[]{:S(2)}) %collective-permute-start.15) | collective-permute-done | bytes 65568 | tf_op jit(solution)/shard_map/ppermute | solution.py:349
  75.7 0.7 finish.1
  (18 shorter events, 0.0 us)
Async XLA Ops:
  0.0 26.6 %copy-start.1 = (bf16[16,4,128,128]{3,2,1,0:T(8,128)(2,1)S(1)}, bf16[16,4,128,128]{3,2,1,0:T(8,128)(2,1)}, u32[]{:S(2)}) copy-start(bf16[16,4,128,128]{3,2,1,0:T(8,128)(2,1)} %tiles_ref.5) | copy-start | bytes 6291460
  4.4 25.2 %all-to-all-start = ((f32[16,72,128]{2,1,0:T(8,128)}), f32[16,72,128]{2,1,0:T(8,128)S(1)}, u32[]{:S(2)}, u32[]{:S(2)}) async-start(f32[16,72,128]{2,1,0:T(8,128)} %get-tuple-element.39), calls=%async_computation | async-start | bytes 1179648 | tf_op jit(solution)/shard_map/all_to_all | solution.py:423
  10.6 5.8 %collective-permute-start = (bf16[16,32,128]{2,1,0:T(8,128)(2,1)}, bf16[16,32,128]{2,1,0:T(8,128)(2,1)S(1)}, u32[]{:S(2)}, u32[]{:S(2)}) collective-permute-start(bf16[16,32,128]{2,1,0:T(8,128)(2,1)} %get-tuple-element.40.own_refs_0_), channel_id=1, source_target_pairs={{0,1},{1,0},{2,3},{3,2},{4,5},{5,4},{6,7},{7,6},{8,9},{9,8},{10,11... | collective-permute-start | bytes 393224 | tf_op jit(solution)/shard_map/ppermute | solution.py:349
  16.4 0.9 %copy-start.3 = (bf16[16,32,128]{2,1,0:T(8,128)(2,1)S(1)}, bf16[16,32,128]{2,1,0:T(8,128)(2,1)}, u32[]{:S(2)}) copy-start(bf16[16,32,128]{2,1,0:T(8,128)(2,1)} %get-tuple-element.40.own_refs_0_) | copy-start | bytes 393220
  17.3 0.7 copy-start.5
  18.6 8.0 %collective-permute-start.1 = (bf16[4,64,128]{2,1,0:T(8,128)(2,1)S(1)}, bf16[4,64,128]{2,1,0:T(8,128)(2,1)S(1)}, u32[]{:S(2)}, u32[]{:S(2)}) collective-permute-start(bf16[4,64,128]{2,1,0:T(8,128)(2,1)S(1)} %get-tuple-element.44), channel_id=1, source_target_pairs={{2,4},{6,8},{10,12},{14,16},{18,20},{22,24},{26,28},{4,2},{8,6},{1... | collective-permute-start | bytes 196616 | tf_op jit(solution)/shard_map/ppermute | solution.py:340
  20.9 5.7 %collective-permute-start.2 = (bf16[4,64,128]{2,1,0:T(8,128)(2,1)S(1)}, bf16[4,64,128]{2,1,0:T(8,128)(2,1)S(1)}, u32[]{:S(2)}, u32[]{:S(2)}) collective-permute-start(bf16[4,64,128]{2,1,0:T(8,128)(2,1)S(1)} %get-tuple-element.45), channel_id=1, source_target_pairs={{0,2},{4,6},{8,10},{12,14},{16,18},{20,22},{24,26},{28,30},{2,0},{... | collective-permute-start | bytes 196616 | tf_op jit(solution)/shard_map/ppermute | solution.py:340
  22.1 7.5 %collective-permute-start.3 = (f32[32,1024]{1,0:T(8,128)}, f32[32,1024]{1,0:T(8,128)S(1)}, u32[]{:S(2)}, u32[]{:S(2)}) collective-permute-start(f32[32,1024]{1,0:T(8,128)} %get-tuple-element.46), channel_id=1, source_target_pairs={{0,1},{1,0},{2,3},{3,2},{4,5},{5,4},{6,7},{7,6},{8,9},{9,8},{10,11... | collective-permute-start | bytes 393224 | tf_op jit(solution)/shard_map/ppermute | solution.py:349
  23.7 0.7 copy-start.9
  26.6 0.9 %copy-start.4 = (bf16[16,32,128]{2,1,0:T(8,128)(2,1)S(1)}, bf16[16,32,128]{2,1,0:T(8,128)(2,1)}, u32[]{:S(2)}) copy-start(bf16[16,32,128]{2,1,0:T(8,128)(2,1)} %get-tuple-element.40.own_refs_0_) | copy-start | bytes 393220
  27.5 0.7 copy-start.7
  30.8 7.8 %copy-start.8 = (s32[1,16,4]{1,2,0:T(4,128)S(1)}, s32[1,16,4]{1,2,0:T(4,128)}, u32[]{:S(2)}) copy-start(s32[1,16,4]{1,2,0:T(4,128)} %param.13) | copy-start | bytes 772
  30.8 15.7 %copy-start = (bf16[1024,2048]{1,0:T(8,128)(2,1)S(1)}, bf16[1024,2048]{1,0:T(8,128)(2,1)}, u32[]{:S(2)}) copy-start(bf16[1024,2048]{1,0:T(8,128)(2,1)} %gain_ref.3) | copy-start | bytes 12582916
  30.8 15.7 %copy-start.2 = (f32[32,2048]{1,0:T(8,128)S(1)}, f32[32,2048]{1,0:T(8,128)}, u32[]{:S(2)}) copy-start(f32[32,2048]{1,0:T(8,128)} %x_ref.1) | copy-start | bytes 786436
  30.9 15.7 %copy-start.6 = (s32[1,2,4]{2,1,0:T(2,128)S(1)}, s32[1,2,4]{2,1,0:T(2,128)}, u32[]{:S(2)}) copy-start(s32[1,2,4]{2,1,0:T(2,128)} %param.14) | copy-start | bytes 100
  32.1 5.0 %collective-permute-start.5 = (f32[32,1024]{1,0:T(8,128)S(1)}, f32[32,1024]{1,0:T(8,128)S(1)}, u32[]{:S(2)}, u32[]{:S(2)}) collective-permute-start(f32[32,1024]{1,0:T(8,128)S(1)} %get-tuple-element.52.z_refs_1_), channel_id=1, source_target_pairs={{0,1},{1,0},{2,3},{3,2},{4,5},{5,4},{6,7},{7,6},{8,9},{9,8},{10,11... | collective-permute-start | bytes 393224 | tf_op jit(solution)/shard_map/ppermute | solution.py:349
  33.7 5.0 %collective-permute-start.4 = (f32[32,1024]{1,0:T(8,128)S(1)}, f32[32,1024]{1,0:T(8,128)S(1)}, u32[]{:S(2)}, u32[]{:S(2)}) collective-permute-start(f32[32,1024]{1,0:T(8,128)S(1)} %get-tuple-element.51.z_refs_0_), channel_id=1, source_target_pairs={{0,1},{1,0},{2,3},{3,2},{4,5},{5,4},{6,7},{7,6},{8,9},{9,8},{10,11... | collective-permute-start | bytes 393224 | tf_op jit(solution)/shard_map/ppermute | solution.py:349
  40.1 6.5 %collective-permute-start.6 = (bf16[4,64,128]{2,1,0:T(8,128)(2,1)S(1)}, bf16[4,64,128]{2,1,0:T(8,128)(2,1)S(1)}, u32[]{:S(2)}, u32[]{:S(2)}) collective-permute-start(bf16[4,64,128]{2,1,0:T(8,128)(2,1)S(1)} %get-tuple-element.56), channel_id=1, source_target_pairs={{2,4},{6,8},{10,12},{14,16},{18,20},{22,24},{26,28},{4,2},{8,6},{1... | collective-permute-start | bytes 196616 | tf_op jit(solution)/shard_map/ppermute | solution.py:340
  43.8 2.7 %collective-permute-start.7 = (bf16[4,64,128]{2,1,0:T(8,128)(2,1)S(1)}, bf16[4,64,128]{2,1,0:T(8,128)(2,1)S(1)}, u32[]{:S(2)}, u32[]{:S(2)}) collective-permute-start(bf16[4,64,128]{2,1,0:T(8,128)(2,1)S(1)} %get-tuple-element.57), channel_id=1, source_target_pairs={{0,2},{4,6},{8,10},{12,14},{16,18},{20,22},{24,26},{28,30},{2,0},{... | collective-permute-start | bytes 196616 | tf_op jit(solution)/shard_map/ppermute | solution.py:340
  48.7 8.6 %collective-permute-start.10 = (bf16[8,64,128]{2,1,0:T(8,128)(2,1)S(1)}, bf16[8,64,128]{2,1,0:T(8,128)(2,1)S(1)}, u32[]{:S(2)}, u32[]{:S(2)}) collective-permute-start(bf16[8,64,128]{2,1,0:T(8,128)(2,1)S(1)} %get-tuple-element.60.mine_ref), channel_id=1, source_target_pairs={{0,1},{1,0},{2,3},{3,2},{4,5},{5,4},{6,7},{7,6},{8,9},{9,8},{10,11... | collective-permute-start | bytes 393224 | tf_op jit(solution)/shard_map/ppermute | solution.py:349
  50.1 6.5 %collective-permute-start.8 = (bf16[4,64,128]{2,1,0:T(8,128)(2,1)S(1)}, bf16[4,64,128]{2,1,0:T(8,128)(2,1)S(1)}, u32[]{:S(2)}, u32[]{:S(2)}) collective-permute-start(bf16[4,64,128]{2,1,0:T(8,128)(2,1)S(1)} %get-tuple-element.59), channel_id=1, source_target_pairs={{2,4},{6,8},{10,12},{14,16},{18,20},{22,24},{26,28},{4,2},{8,6},{1... | collective-permute-start | bytes 196616 | tf_op jit(solution)/shard_map/ppermute | solution.py:340
  56.6 4.3 %collective-permute-start.9 = (bf16[4,64,128]{2,1,0:T(8,128)(2,1)S(1)}, bf16[4,64,128]{2,1,0:T(8,128)(2,1)S(1)}, u32[]{:S(2)}, u32[]{:S(2)}) collective-permute-start(bf16[4,64,128]{2,1,0:T(8,128)(2,1)S(1)} %collective-permute-done.8.first_refs_0_), channel_id=1, source_target_pairs={{0,1},{1,0},{2,3},{3,2},{4,5},{5,4},{6,7},{7,6},{8,9},{9,8},{10,11... | collective-permute-start | bytes 196616 | tf_op jit(solution)/shard_map/ppermute | solution.py:349
  57.8 3.0 %collective-permute-start.11 = (bf16[4,64,128]{2,1,0:T(8,128)(2,1)S(1)}, bf16[4,64,128]{2,1,0:T(8,128)(2,1)S(1)}, u32[]{:S(2)}, u32[]{:S(2)}) collective-permute-start(bf16[4,64,128]{2,1,0:T(8,128)(2,1)S(1)} %get-tuple-element.62), channel_id=1, source_target_pairs={{0,2},{4,6},{8,10},{12,14},{16,18},{20,22},{24,26},{28,30},{2,0},{... | collective-permute-start | bytes 196616 | tf_op jit(solution)/shard_map/ppermute | solution.py:340
  62.8 6.5 %collective-permute-start.12 = (bf16[4,64,128]{2,1,0:T(8,128)(2,1)S(1)}, bf16[4,64,128]{2,1,0:T(8,128)(2,1)S(1)}, u32[]{:S(2)}, u32[]{:S(2)}) collective-permute-start(bf16[4,64,128]{2,1,0:T(8,128)(2,1)S(1)} %get-tuple-element.67), channel_id=1, source_target_pairs={{2,4},{6,8},{10,12},{14,16},{18,20},{22,24},{26,28},{4,2},{8,6},{1... | collective-permute-start | bytes 196616 | tf_op jit(solution)/shard_map/ppermute | solution.py:340
  65.2 4.1 %collective-permute-start.13 = (bf16[4,64,128]{2,1,0:T(8,128)(2,1)S(1)}, bf16[4,64,128]{2,1,0:T(8,128)(2,1)S(1)}, u32[]{:S(2)}, u32[]{:S(2)}) collective-permute-start(bf16[4,64,128]{2,1,0:T(8,128)(2,1)S(1)} %get-tuple-element.68), channel_id=1, source_target_pairs={{0,2},{4,6},{8,10},{12,14},{16,18},{20,22},{24,26},{28,30},{2,0},{... | collective-permute-start | bytes 196616 | tf_op jit(solution)/shard_map/ppermute | solution.py:340
  65.3 10.4 %collective-permute-start.14 = (f32[8,32,128]{2,1,0:T(8,128)S(1)}, f32[8,32,128]{2,1,0:T(8,128)S(1)}, u32[]{:S(2)}, u32[]{:S(2)}) collective-permute-start(f32[8,32,128]{2,1,0:T(8,128)S(1)} %get-tuple-element.71), channel_id=1, source_target_pairs={{0,1},{1,0},{2,3},{3,2},{4,5},{5,4},{6,7},{7,6},{8,9},{9,8},{10,11... | collective-permute-start | bytes 393224 | tf_op jit(solution)/shard_map/ppermute | solution.py:349
  71.4 4.3 %collective-permute-start.15 = (bf16[32,1024]{1,0:T(8,128)(2,1)S(1)}, bf16[32,1024]{1,0:T(8,128)(2,1)S(1)}, u32[]{:S(2)}, u32[]{:S(2)}) collective-permute-start(bf16[32,1024]{1,0:T(8,128)(2,1)S(1)} %get-tuple-element.72), channel_id=1, source_target_pairs={{0,1},{1,0},{2,3},{3,2},{4,5},{5,4},{6,7},{7,6},{8,9},{9,8},{10,11... | collective-permute-start | bytes 196616 | tf_op jit(solution)/shard_map/ppermute | solution.py:349

commit v11 on v10

--- a/solution.py
+++ b/solution.py
@@ -97,7 +97,9 @@
         copy.wait()
 
 
-def inverse_kernel(own_ref, group_ref, lane_ref):
+def inverse_kernel(own_ref, handed_refs, group_ref, lane_ref, kept_refs):
+    for handed_ref, kept_ref in zip(handed_refs, kept_refs):
+        kept_ref[...] = handed_ref[...]
     chunks, width = own_ref.shape
     blocks = group_ref.shape[0]
     groups = width // BLK
@@ -425,16 +427,19 @@
         message = message.reshape(chunks, each, depth, cap).transpose(0, 2, 1, 3)
         message = message.reshape(chunks, depth, BLK)
 
-    group, lane = call(
+    rounded_others = [from_snap(rounded, i) for i in range(1, members)]
+    handed = [rounded, ties_table, place]
+    table = shape((lines // BLK, BLK), jnp.int32)
+    group, lane, (rounded, ties_table, place) = call(
         inverse_kernel,
-        (shape((lines // BLK, BLK), jnp.int32),) * 2,
-        [VMEM],
-        (holder,),
+        (table, table, [shape(a.shape, a.dtype) for a in handed]),
+        [VMEM, [VMEM] * 3],
+        (holder, handed),
         flops=10**9,
         name="invert_order",
     )
     boundary = shape((ties, everything, BLK), BF16)
-    owns = [rounded] + [from_snap(rounded, i) for i in range(1, members)]
+    owns = [rounded] + rounded_others
     first, second = call(
         pick_kernel,
         (boundary, boundary),

time: 77 us -> 75.6 us (0.982)
  local copies, waits for them, and re-layouts: 3.91 us -> 3.03 us
    ppermute x8, waiting for transfers between devices: 15.3 us -> 11.8 us  [from_snap(): lax.ppermute(block, 'snap', [(i, (i + distance) % members) for i in range...]
    ppermute x8, waiting for transfers between devices: 10.3 us -> 13.5 us  [swap_pair(): return lax.ppermute(block, 'area', pairs + [(b, a) for a, b in pairs])]
    unnamed x20 -> x14, local copies, waits for them, and re-layouts: 3.91 us -> 3.03 us
where the time goes in v11:
time: 75.6 us; the launch traced here: 74.9 us
  starting transfers between devices  28.1 us (37%)
  waiting for transfers between devices  25.4 us (34%)
  Pallas kernels  18.2 us (24%)
  local copies, waits for them, and re-layouts  3.03 us (4%)
    pallas_call x12, Pallas kernels, call(): pl.pallas_call(kernel, out_shape=outs, in_specs=ins, out_specs=jax.tree.m...  18.2 us
    ppermute x8, waiting for transfers between devices, swap_pair(): return lax.ppermute(block, 'area', pairs + [(b, a) for a, b in pairs])  13.5 us
    ppermute x8, starting transfers between devices, swap_pair(): return lax.ppermute(block, 'area', pairs + [(b, a) for a, b in pairs])  13.4 us
    ppermute x8, waiting for transfers between devices, from_snap(): lax.ppermute(block, 'snap', [(i, (i + distance) % members) for i in range...  11.8 us
    ppermute x8, starting transfers between devices, from_snap(): lax.ppermute(block, 'snap', [(i, (i + distance) % members) for i in range...  8.54 us
    all_to_all x1, starting transfers between devices, on_device(): lax.all_to_all(message, 'area', split_axis=0, concat_axis=0, tiled=True)  6.17 us
    unnamed x14, local copies, waits for them, and re-layouts  3.03 us
  transfers between devices with their start and end apart: 17, of which 9 were waited for; matrix products, arithmetic and copies ran while one was open for 0% of the time, Pallas kernels for 7%

profile of v11, /device:TPU:16, one launch (start us, length us, event | category | flops | bytes accessed | tf_op | source)
XLA Modules:
  0.0 74.9 jit_solution(1998652470058093192)
XLA Ops:
  0.0 4.4 %pack_readings.1 = (f32[16,72,128]{2,1,0:T(8,128)}, bf16[16,32,128]{2,1,0:T(8,128)(2,1)}, f32[32,1024]{1,0:T(8,128)}) custom-call(f32[32,2048]{1,0:T(8,128)} %z_in.1, f32[16,128]{1,0:T(8,128)} %bitcast.17, s32[16,256]{1,0:T(8,128)} %bitcast.16, f32[32,2048]{1,0:T(8,128)} %x_ref.1), custom_call_target="tpu_custom_call" | custom-call | tf_op jit(solution)/shard_map/pack_readings/pallas_call | solution.py:21
  4.4 6.2 %all-to-all-start = ((f32[16,72,128]{2,1,0:T(8,128)}), f32[16,72,128]{2,1,0:T(8,128)S(1)}, u32[]{:S(2)}, u32[]{:S(2)}) async-start(f32[16,72,128]{2,1,0:T(8,128)} %get-tuple-element.42), calls=%async_computation | async-start | bytes 1179648 | tf_op jit(solution)/shard_map/all_to_all | solution.py:425
  10.6 1.5 %collective-permute-start = (bf16[16,32,128]{2,1,0:T(8,128)(2,1)}, bf16[16,32,128]{2,1,0:T(8,128)(2,1)S(1)}, u32[]{:S(2)}, u32[]{:S(2)}) collective-permute-start(bf16[16,32,128]{2,1,0:T(8,128)(2,1)} %get-tuple-element.43.handed_refs_0_), channel_id=1, source_target_pairs={{0,1},{1,0},{2,3},{3,2},{4,5},{5,4},{6,7},{7,6},{8,9},{9,8},{10,11... | collective-permute-start | bytes 393224 | tf_op jit(solution)/shard_map/ppermute | solution.py:351
  12.1 0.9 %copy-done.3 = bf16[16,32,128]{2,1,0:T(8,128)(2,1)S(1)} copy-done((bf16[16,32,128]{2,1,0:T(8,128)(2,1)S(1)}, bf16[16,32,128]{2,1,0:T(8,128)(2,1)}, u32[]{:S(2)}) %copy-start.3) | copy-done | bytes 131096
  13.1 0.7 copy-done.4
  13.8 0.7 copy-done.5
  14.5 0.7 copy-done.6
  15.1 0.4 invert_order.1
  15.6 0.8 %collective-permute-done.own_refs_1_ = bf16[16,32,128]{2,1,0:T(8,128)(2,1)S(1)} collective-permute-done((bf16[16,32,128]{2,1,0:T(8,128)(2,1)}, bf16[16,32,128]{2,1,0:T(8,128)(2,1)S(1)}, u32[]{:S(2)}, u32[]{:S(2)}) %collective-permute-start) | collective-permute-done | bytes 131104 | tf_op jit(solution)/shard_map/ppermute | solution.py:351
  16.4 0.6 pick_boundary.1
  17.0 2.3 %collective-permute-start.1 = (bf16[4,64,128]{2,1,0:T(8,128)(2,1)S(1)}, bf16[4,64,128]{2,1,0:T(8,128)(2,1)S(1)}, u32[]{:S(2)}, u32[]{:S(2)}) collective-permute-start(bf16[4,64,128]{2,1,0:T(8,128)(2,1)S(1)} %get-tuple-element.49), channel_id=1, source_target_pairs={{2,4},{6,8},{10,12},{14,16},{18,20},{22,24},{26,28},{4,2},{8,6},{1... | collective-permute-start | bytes 196616 | tf_op jit(solution)/shard_map/ppermute | solution.py:342
  19.3 1.3 %collective-permute-start.2 = (bf16[4,64,128]{2,1,0:T(8,128)(2,1)S(1)}, bf16[4,64,128]{2,1,0:T(8,128)(2,1)S(1)}, u32[]{:S(2)}, u32[]{:S(2)}) collective-permute-start(bf16[4,64,128]{2,1,0:T(8,128)(2,1)S(1)} %get-tuple-element.50), channel_id=1, source_target_pairs={{0,2},{4,6},{8,10},{12,14},{16,18},{20,22},{24,26},{28,30},{2,0},{... | collective-permute-start | bytes 196616 | tf_op jit(solution)/shard_map/ppermute | solution.py:342
  20.6 1.5 %collective-permute-start.3 = (f32[32,1024]{1,0:T(8,128)}, f32[32,1024]{1,0:T(8,128)S(1)}, u32[]{:S(2)}, u32[]{:S(2)}) collective-permute-start(f32[32,1024]{1,0:T(8,128)} %get-tuple-element.52), channel_id=1, source_target_pairs={{0,1},{1,0},{2,3},{3,2},{4,5},{5,4},{6,7},{7,6},{8,9},{9,8},{10,11... | collective-permute-start | bytes 393224 | tf_op jit(solution)/shard_map/ppermute | solution.py:351
  22.1 4.5 %collective-permute-done.1.first_ref = bf16[4,64,128]{2,1,0:T(8,128)(2,1)S(1)} collective-permute-done((bf16[4,64,128]{2,1,0:T(8,128)(2,1)S(1)}, bf16[4,64,128]{2,1,0:T(8,128)(2,1)S(1)}, u32[]{:S(2)}, u32[]{:S(2)}) %collective-permute-start.1) | collective-permute-done | bytes 65568 | tf_op jit(solution)/shard_map/ppermute | solution.py:342
  26.6 0.0 collective-permute-done.2.second_ref
  26.6 1.4 %predict.1.guess_ref = f32[64,2048]{1,0:T(8,128)S(1)} custom-call(bf16[4,64,128]{2,1,0:T(8,128)(2,1)S(1)} %collective-permute-done.1.first_ref, bf16[4,64,128]{2,1,0:T(8,128)(2,1)S(1)} %collective-permute-done.2.second_ref, bf16[16,32,128]{2,1,0:T(8,128)(2,1)S(1)} %get-tuple-element.44.own_refs_0_, ...), custom_call_target="tpu_custom_call" | custom-call | flops 1000000000 | tf_op jit(solution)/shard_map/predict/pallas_call | solution.py:21
  28.0 0.0 collective-permute-done.3.x_others_refs_0_
  28.0 1.2 %unpack_readings.3 = (f32[32,1024]{1,0:T(8,128)S(1)}, f32[1,1024]{1,0:T(1,128)S(1)}) custom-call(s32[16,128]{1,0:T(8,128)S(1)} %get-tuple-element.54.group_ref, s32[16,128]{1,0:T(8,128)S(1)} %get-tuple-element.55.lane_ref, f32[16,72,128]{2,1,0:T(8,128)S(1)} %all-to-all-done.message_ref), custom_call_target="tpu_custom_call" | custom-call | flops 2000000000 | tf_op jit(solution)/shard_map/unpack_readings/pallas_call | solution.py:21
  29.2 0.0 copy-start
  29.3 0.0 copy-start.2
  29.3 1.2 %unpack_readings.2 = (f32[32,1024]{1,0:T(8,128)S(1)}, f32[1,1024]{1,0:T(1,128)S(1)}) custom-call(s32[16,128]{1,0:T(8,128)S(1)} %get-tuple-element.54.group_ref, s32[16,128]{1,0:T(8,128)S(1)} %get-tuple-element.55.lane_ref, f32[16,72,128]{2,1,0:T(8,128)S(1)} %all-to-all-done.message_ref), custom_call_target="tpu_custom_call" | custom-call | flops 2000000000 | tf_op jit(solution)/shard_map/unpack_readings/pallas_call | solution.py:21
  30.5 1.6 %collective-permute-start.5 = (f32[32,1024]{1,0:T(8,128)S(1)}, f32[32,1024]{1,0:T(8,128)S(1)}, u32[]{:S(2)}, u32[]{:S(2)}) collective-permute-start(f32[32,1024]{1,0:T(8,128)S(1)} %get-tuple-element.58.z_refs_1_), channel_id=1, source_target_pairs={{0,1},{1,0},{2,3},{3,2},{4,5},{5,4},{6,7},{7,6},{8,9},{9,8},{10,11... | collective-permute-start | bytes 393224 | tf_op jit(solution)/shard_map/ppermute | solution.py:351
  32.1 0.5 collective-permute-start.4
  32.6 2.9 %collective-permute-done.5 = f32[32,1024]{1,0:T(8,128)S(1)} collective-permute-done((f32[32,1024]{1,0:T(8,128)S(1)}, f32[32,1024]{1,0:T(8,128)S(1)}, u32[]{:S(2)}, u32[]{:S(2)}) %collective-permute-start.5) | collective-permute-done | bytes 131104 | tf_op jit(solution)/shard_map/ppermute | solution.py:351
  35.5 1.5 %collective-permute-done.4 = f32[32,1024]{1,0:T(8,128)S(1)} collective-permute-done((f32[32,1024]{1,0:T(8,128)S(1)}, f32[32,1024]{1,0:T(8,128)S(1)}, u32[]{:S(2)}, u32[]{:S(2)}) %collective-permute-start.4) | collective-permute-done | bytes 131104 | tf_op jit(solution)/shard_map/ppermute | solution.py:351
  37.1 1.4 %pull.1 = (f32[16,64,128]{2,1,0:T(8,128)S(1)}, bf16[4,64,128]{2,1,0:T(8,128)(2,1)S(1)}, bf16[4,64,128]{2,1,0:T(8,128)(2,1)S(1)}) custom-call(f32[64,2048]{1,0:T(8,128)S(1)} %predict.1.guess_ref, f32[32,1024]{1,0:T(8,128)S(1)} %get-tuple-element.57.z_refs_0_, f32[32,1024]{1,0:T(8,128)S(1)} %get-tuple-element.58.z_refs_1_, f32[1,32,1024]{2,1,0:T(8,128)S(1)} %bitcast.11, ...), custom_call_target="tpu_custom_call" | custom-call | tf_op jit(solution)/shard_map/pull/pallas_call | solution.py:21
  38.5 3.7 %collective-permute-start.6 = (bf16[4,64,128]{2,1,0:T(8,128)(2,1)S(1)}, bf16[4,64,128]{2,1,0:T(8,128)(2,1)S(1)}, u32[]{:S(2)}, u32[]{:S(2)}) collective-permute-start(bf16[4,64,128]{2,1,0:T(8,128)(2,1)S(1)} %get-tuple-element.62), channel_id=1, source_target_pairs={{2,4},{6,8},{10,12},{14,16},{18,20},{22,24},{26,28},{4,2},{8,6},{1... | collective-permute-start | bytes 196616 | tf_op jit(solution)/shard_map/ppermute | solution.py:342
  42.2 0.1 collective-permute-start.7
  42.3 2.7 %collective-permute-done.6.back_first_ref = bf16[4,64,128]{2,1,0:T(8,128)(2,1)S(1)} collective-permute-done((bf16[4,64,128]{2,1,0:T(8,128)(2,1)S(1)}, bf16[4,64,128]{2,1,0:T(8,128)(2,1)S(1)}, u32[]{:S(2)}, u32[]{:S(2)}) %collective-permute-start.6) | collective-permute-done | bytes 65568 | tf_op jit(solution)/shard_map/ppermute | solution.py:342
  45.0 2.1 %first_update.1 = (f32[8,32,128]{2,1,0:T(8,128)S(1)}, f32[8,32,128]{2,1,0:T(8,128)S(1)}, bf16[8,64,128]{2,1,0:T(8,128)(2,1)S(1)}, bf16[4,64,128]{2,1,0:T(8,128)(2,1)S(1)}) custom-call(f32[16,64,128]{2,1,0:T(8,128)S(1)} %get-tuple-element.61.grad_ref, bf16[4,64,128]{2,1,0:T(8,128)(2,1)S(1)} %collective-permute-done.6.back_first_ref, ...), custom_call_target="tpu_custom_call" | custom-call | tf_op jit(solution)/shard_map/first_update/pallas_call | solution.py:21
  47.1 1.5 %collective-permute-start.10 = (bf16[8,64,128]{2,1,0:T(8,128)(2,1)S(1)}, bf16[8,64,128]{2,1,0:T(8,128)(2,1)S(1)}, u32[]{:S(2)}, u32[]{:S(2)}) collective-permute-start(bf16[8,64,128]{2,1,0:T(8,128)(2,1)S(1)} %get-tuple-element.66.mine_ref), channel_id=1, source_target_pairs={{0,1},{1,0},{2,3},{3,2},{4,5},{5,4},{6,7},{7,6},{8,9},{9,8},{10,11... | collective-permute-start | bytes 393224 | tf_op jit(solution)/shard_map/ppermute | solution.py:351
  48.6 3.5 %collective-permute-start.8 = (bf16[4,64,128]{2,1,0:T(8,128)(2,1)S(1)}, bf16[4,64,128]{2,1,0:T(8,128)(2,1)S(1)}, u32[]{:S(2)}, u32[]{:S(2)}) collective-permute-start(bf16[4,64,128]{2,1,0:T(8,128)(2,1)S(1)} %get-tuple-element.65), channel_id=1, source_target_pairs={{2,4},{6,8},{10,12},{14,16},{18,20},{22,24},{26,28},{4,2},{8,6},{1... | collective-permute-start | bytes 196616 | tf_op jit(solution)/shard_map/ppermute | solution.py:342
  52.1 2.9 %collective-permute-done.8.first_refs_0_ = bf16[4,64,128]{2,1,0:T(8,128)(2,1)S(1)} collective-permute-done((bf16[4,64,128]{2,1,0:T(8,128)(2,1)S(1)}, bf16[4,64,128]{2,1,0:T(8,128)(2,1)S(1)}, u32[]{:S(2)}, u32[]{:S(2)}) %collective-permute-start.8) | collective-permute-done | bytes 65568 | tf_op jit(solution)/shard_map/ppermute | solution.py:342
  55.0 0.6 collective-permute-start.9
  55.6 0.0 collective-permute-done.10.others_refs_0_
  55.7 0.6 join_states.1
  56.3 0.1 collective-permute-start.11
  56.3 3.0 %collective-permute-done.9.first_refs_1_ = bf16[4,64,128]{2,1,0:T(8,128)(2,1)S(1)} collective-permute-done((bf16[4,64,128]{2,1,0:T(8,128)(2,1)S(1)}, bf16[4,64,128]{2,1,0:T(8,128)(2,1)S(1)}, u32[]{:S(2)}, u32[]{:S(2)}) %collective-permute-start.9) | collective-permute-done | bytes 65568 | tf_op jit(solution)/shard_map/ppermute | solution.py:351
  59.3 2.0 %predict_pull.1 = (f32[16,64,128]{2,1,0:T(8,128)S(1)}, bf16[4,64,128]{2,1,0:T(8,128)(2,1)S(1)}, bf16[4,64,128]{2,1,0:T(8,128)(2,1)S(1)}) custom-call(bf16[4,64,128]{2,1,0:T(8,128)(2,1)S(1)} %collective-permute-done.8.first_refs_0_, bf16[4,64,128]{2,1,0:T(8,128)(2,1)S(1)} %collective-permute-done.9.first_refs_1_, ...), custom_call_target="tpu_custom_call" | custom-call | tf_op jit(solution)/shard_map/predict_pull/pallas_call | solution.py:21
  61.3 2.4 %collective-permute-start.12 = (bf16[4,64,128]{2,1,0:T(8,128)(2,1)S(1)}, bf16[4,64,128]{2,1,0:T(8,128)(2,1)S(1)}, u32[]{:S(2)}, u32[]{:S(2)}) collective-permute-start(bf16[4,64,128]{2,1,0:T(8,128)(2,1)S(1)} %get-tuple-element.73), channel_id=1, source_target_pairs={{2,4},{6,8},{10,12},{14,16},{18,20},{22,24},{26,28},{4,2},{8,6},{1... | collective-permute-start | bytes 196616 | tf_op jit(solution)/shard_map/ppermute | solution.py:342
  63.7 0.1 collective-permute-start.13
  63.8 0.6 collective-permute-start.14
  64.4 3.4 %collective-permute-done.12.back_first_ref = bf16[4,64,128]{2,1,0:T(8,128)(2,1)S(1)} collective-permute-done((bf16[4,64,128]{2,1,0:T(8,128)(2,1)S(1)}, bf16[4,64,128]{2,1,0:T(8,128)(2,1)S(1)}, u32[]{:S(2)}, u32[]{:S(2)}) %collective-permute-start.12) | collective-permute-done | bytes 65568 | tf_op jit(solution)/shard_map/ppermute | solution.py:342
  67.8 0.0 collective-permute-done.13.back_second_ref
  67.8 2.0 %last_update.1 = (f32[32,1024]{1,0:T(8,128)S(1)}, bf16[32,1024]{1,0:T(8,128)(2,1)S(1)}) custom-call(f32[16,64,128]{2,1,0:T(8,128)S(1)} %get-tuple-element.69.grad_ref, bf16[4,64,128]{2,1,0:T(8,128)(2,1)S(1)} %collective-permute-done.12.back_first_ref, bf16[4,64,128]{2,1,0:T(8,128)(2,1)S(1)} %collective-permute-done.13.back_second_ref, ...), custom_call_target="tpu_custom_call" | custom-call | tf_op jit(solution)/shard_map/last_update/pallas_call | solution.py:21
  69.8 0.7 collective-permute-start.15
  70.5 3.7 %collective-permute-done.15.updates_refs_0_ = bf16[32,1024]{1,0:T(8,128)(2,1)S(1)} collective-permute-done((bf16[32,1024]{1,0:T(8,128)(2,1)S(1)}, bf16[32,1024]{1,0:T(8,128)(2,1)S(1)}, u32[]{:S(2)}, u32[]{:S(2)}) %collective-permute-start.15) | collective-permute-done | bytes 65568 | tf_op jit(solution)/shard_map/ppermute | solution.py:351
  74.2 0.7 finish.1
  (12 shorter events, 0.0 us)
Async XLA Ops:
  0.0 26.6 %copy-start.1 = (bf16[16,4,128,128]{3,2,1,0:T(8,128)(2,1)S(1)}, bf16[16,4,128,128]{3,2,1,0:T(8,128)(2,1)}, u32[]{:S(2)}) copy-start(bf16[16,4,128,128]{3,2,1,0:T(8,128)(2,1)} %tiles_ref.5) | copy-start | bytes 6291460
  4.4 23.6 %all-to-all-start = ((f32[16,72,128]{2,1,0:T(8,128)}), f32[16,72,128]{2,1,0:T(8,128)S(1)}, u32[]{:S(2)}, u32[]{:S(2)}) async-start(f32[16,72,128]{2,1,0:T(8,128)} %get-tuple-element.42), calls=%async_computation | async-start | bytes 1179648 | tf_op jit(solution)/shard_map/all_to_all | solution.py:425
  10.6 5.8 %collective-permute-start = (bf16[16,32,128]{2,1,0:T(8,128)(2,1)}, bf16[16,32,128]{2,1,0:T(8,128)(2,1)S(1)}, u32[]{:S(2)}, u32[]{:S(2)}) collective-permute-start(bf16[16,32,128]{2,1,0:T(8,128)(2,1)} %get-tuple-element.43.handed_refs_0_), channel_id=1, source_target_pairs={{0,1},{1,0},{2,3},{3,2},{4,5},{5,4},{6,7},{7,6},{8,9},{9,8},{10,11... | collective-permute-start | bytes 393224 | tf_op jit(solution)/shard_map/ppermute | solution.py:351
  12.1 0.9 %copy-start.3 = (bf16[16,32,128]{2,1,0:T(8,128)(2,1)S(1)}, bf16[16,32,128]{2,1,0:T(8,128)(2,1)}, u32[]{:S(2)}) copy-start(bf16[16,32,128]{2,1,0:T(8,128)(2,1)} %get-tuple-element.43.handed_refs_0_) | copy-start | bytes 393220
  13.1 0.7 copy-start.4
  13.8 0.7 copy-start.5
  14.5 0.7 copy-start.6
  17.0 9.6 %collective-permute-start.1 = (bf16[4,64,128]{2,1,0:T(8,128)(2,1)S(1)}, bf16[4,64,128]{2,1,0:T(8,128)(2,1)S(1)}, u32[]{:S(2)}, u32[]{:S(2)}) collective-permute-start(bf16[4,64,128]{2,1,0:T(8,128)(2,1)S(1)} %get-tuple-element.49), channel_id=1, source_target_pairs={{2,4},{6,8},{10,12},{14,16},{18,20},{22,24},{26,28},{4,2},{8,6},{1... | collective-permute-start | bytes 196616 | tf_op jit(solution)/shard_map/ppermute | solution.py:342
  19.3 7.3 %collective-permute-start.2 = (bf16[4,64,128]{2,1,0:T(8,128)(2,1)S(1)}, bf16[4,64,128]{2,1,0:T(8,128)(2,1)S(1)}, u32[]{:S(2)}, u32[]{:S(2)}) collective-permute-start(bf16[4,64,128]{2,1,0:T(8,128)(2,1)S(1)} %get-tuple-element.50), channel_id=1, source_target_pairs={{0,2},{4,6},{8,10},{12,14},{16,18},{20,22},{24,26},{28,30},{2,0},{... | collective-permute-start | bytes 196616 | tf_op jit(solution)/shard_map/ppermute | solution.py:342
  20.6 7.5 %collective-permute-start.3 = (f32[32,1024]{1,0:T(8,128)}, f32[32,1024]{1,0:T(8,128)S(1)}, u32[]{:S(2)}, u32[]{:S(2)}) collective-permute-start(f32[32,1024]{1,0:T(8,128)} %get-tuple-element.52), channel_id=1, source_target_pairs={{0,1},{1,0},{2,3},{3,2},{4,5},{5,4},{6,7},{7,6},{8,9},{9,8},{10,11... | collective-permute-start | bytes 393224 | tf_op jit(solution)/shard_map/ppermute | solution.py:351
  29.2 15.8 %copy-start = (bf16[1024,2048]{1,0:T(8,128)(2,1)S(1)}, bf16[1024,2048]{1,0:T(8,128)(2,1)}, u32[]{:S(2)}) copy-start(bf16[1024,2048]{1,0:T(8,128)(2,1)} %gain_ref.3) | copy-start | bytes 12582916
  29.3 15.7 %copy-start.2 = (f32[32,2048]{1,0:T(8,128)S(1)}, f32[32,2048]{1,0:T(8,128)}, u32[]{:S(2)}) copy-start(f32[32,2048]{1,0:T(8,128)} %x_ref.1) | copy-start | bytes 786436
  30.5 5.0 %collective-permute-start.5 = (f32[32,1024]{1,0:T(8,128)S(1)}, f32[32,1024]{1,0:T(8,128)S(1)}, u32[]{:S(2)}, u32[]{:S(2)}) collective-permute-start(f32[32,1024]{1,0:T(8,128)S(1)} %get-tuple-element.58.z_refs_1_), channel_id=1, source_target_pairs={{0,1},{1,0},{2,3},{3,2},{4,5},{5,4},{6,7},{7,6},{8,9},{9,8},{10,11... | collective-permute-start | bytes 393224 | tf_op jit(solution)/shard_map/ppermute | solution.py:351
  32.1 5.0 %collective-permute-start.4 = (f32[32,1024]{1,0:T(8,128)S(1)}, f32[32,1024]{1,0:T(8,128)S(1)}, u32[]{:S(2)}, u32[]{:S(2)}) collective-permute-start(f32[32,1024]{1,0:T(8,128)S(1)} %get-tuple-element.57.z_refs_0_), channel_id=1, source_target_pairs={{0,1},{1,0},{2,3},{3,2},{4,5},{5,4},{6,7},{7,6},{8,9},{9,8},{10,11... | collective-permute-start | bytes 393224 | tf_op jit(solution)/shard_map/ppermute | solution.py:351
  38.5 6.5 %collective-permute-start.6 = (bf16[4,64,128]{2,1,0:T(8,128)(2,1)S(1)}, bf16[4,64,128]{2,1,0:T(8,128)(2,1)S(1)}, u32[]{:S(2)}, u32[]{:S(2)}) collective-permute-start(bf16[4,64,128]{2,1,0:T(8,128)(2,1)S(1)} %get-tuple-element.62), channel_id=1, source_target_pairs={{2,4},{6,8},{10,12},{14,16},{18,20},{22,24},{26,28},{4,2},{8,6},{1... | collective-permute-start | bytes 196616 | tf_op jit(solution)/shard_map/ppermute | solution.py:342
  42.2 2.8 %collective-permute-start.7 = (bf16[4,64,128]{2,1,0:T(8,128)(2,1)S(1)}, bf16[4,64,128]{2,1,0:T(8,128)(2,1)S(1)}, u32[]{:S(2)}, u32[]{:S(2)}) collective-permute-start(bf16[4,64,128]{2,1,0:T(8,128)(2,1)S(1)} %get-tuple-element.63), channel_id=1, source_target_pairs={{0,2},{4,6},{8,10},{12,14},{16,18},{20,22},{24,26},{28,30},{2,0},{... | collective-permute-start | bytes 196616 | tf_op jit(solution)/shard_map/ppermute | solution.py:342
  47.1 8.6 %collective-permute-start.10 = (bf16[8,64,128]{2,1,0:T(8,128)(2,1)S(1)}, bf16[8,64,128]{2,1,0:T(8,128)(2,1)S(1)}, u32[]{:S(2)}, u32[]{:S(2)}) collective-permute-start(bf16[8,64,128]{2,1,0:T(8,128)(2,1)S(1)} %get-tuple-element.66.mine_ref), channel_id=1, source_target_pairs={{0,1},{1,0},{2,3},{3,2},{4,5},{5,4},{6,7},{7,6},{8,9},{9,8},{10,11... | collective-permute-start | bytes 393224 | tf_op jit(solution)/shard_map/ppermute | solution.py:351
  48.6 6.5 %collective-permute-start.8 = (bf16[4,64,128]{2,1,0:T(8,128)(2,1)S(1)}, bf16[4,64,128]{2,1,0:T(8,128)(2,1)S(1)}, u32[]{:S(2)}, u32[]{:S(2)}) collective-permute-start(bf16[4,64,128]{2,1,0:T(8,128)(2,1)S(1)} %get-tuple-element.65), channel_id=1, source_target_pairs={{2,4},{6,8},{10,12},{14,16},{18,20},{22,24},{26,28},{4,2},{8,6},{1... | collective-permute-start | bytes 196616 | tf_op jit(solution)/shard_map/ppermute | solution.py:342
  55.0 4.3 %collective-permute-start.9 = (bf16[4,64,128]{2,1,0:T(8,128)(2,1)S(1)}, bf16[4,64,128]{2,1,0:T(8,128)(2,1)S(1)}, u32[]{:S(2)}, u32[]{:S(2)}) collective-permute-start(bf16[4,64,128]{2,1,0:T(8,128)(2,1)S(1)} %collective-permute-done.8.first_refs_0_), channel_id=1, source_target_pairs={{0,1},{1,0},{2,3},{3,2},{4,5},{5,4},{6,7},{7,6},{8,9},{9,8},{10,11... | collective-permute-start | bytes 196616 | tf_op jit(solution)/shard_map/ppermute | solution.py:351
  56.3 3.0 %collective-permute-start.11 = (bf16[4,64,128]{2,1,0:T(8,128)(2,1)S(1)}, bf16[4,64,128]{2,1,0:T(8,128)(2,1)S(1)}, u32[]{:S(2)}, u32[]{:S(2)}) collective-permute-start(bf16[4,64,128]{2,1,0:T(8,128)(2,1)S(1)} %get-tuple-element.68), channel_id=1, source_target_pairs={{0,2},{4,6},{8,10},{12,14},{16,18},{20,22},{24,26},{28,30},{2,0},{... | collective-permute-start | bytes 196616 | tf_op jit(solution)/shard_map/ppermute | solution.py:342
  61.3 6.5 %collective-permute-start.12 = (bf16[4,64,128]{2,1,0:T(8,128)(2,1)S(1)}, bf16[4,64,128]{2,1,0:T(8,128)(2,1)S(1)}, u32[]{:S(2)}, u32[]{:S(2)}) collective-permute-start(bf16[4,64,128]{2,1,0:T(8,128)(2,1)S(1)} %get-tuple-element.73), channel_id=1, source_target_pairs={{2,4},{6,8},{10,12},{14,16},{18,20},{22,24},{26,28},{4,2},{8,6},{1... | collective-permute-start | bytes 196616 | tf_op jit(solution)/shard_map/ppermute | solution.py:342
  63.7 4.1 %collective-permute-start.13 = (bf16[4,64,128]{2,1,0:T(8,128)(2,1)S(1)}, bf16[4,64,128]{2,1,0:T(8,128)(2,1)S(1)}, u32[]{:S(2)}, u32[]{:S(2)}) collective-permute-start(bf16[4,64,128]{2,1,0:T(8,128)(2,1)S(1)} %get-tuple-element.74), channel_id=1, source_target_pairs={{0,2},{4,6},{8,10},{12,14},{16,18},{20,22},{24,26},{28,30},{2,0},{... | collective-permute-start | bytes 196616 | tf_op jit(solution)/shard_map/ppermute | solution.py:342
  63.8 10.4 %collective-permute-start.14 = (f32[8,32,128]{2,1,0:T(8,128)S(1)}, f32[8,32,128]{2,1,0:T(8,128)S(1)}, u32[]{:S(2)}, u32[]{:S(2)}) collective-permute-start(f32[8,32,128]{2,1,0:T(8,128)S(1)} %get-tuple-element.77), channel_id=1, source_target_pairs={{0,1},{1,0},{2,3},{3,2},{4,5},{5,4},{6,7},{7,6},{8,9},{9,8},{10,11... | collective-permute-start | bytes 393224 | tf_op jit(solution)/shard_map/ppermute | solution.py:351
  69.8 4.3 %collective-permute-start.15 = (bf16[32,1024]{1,0:T(8,128)(2,1)S(1)}, bf16[32,1024]{1,0:T(8,128)(2,1)S(1)}, u32[]{:S(2)}, u32[]{:S(2)}) collective-permute-start(bf16[32,1024]{1,0:T(8,128)(2,1)S(1)} %get-tuple-element.78), channel_id=1, source_target_pairs={{0,1},{1,0},{2,3},{3,2},{4,5},{5,4},{6,7},{7,6},{8,9},{9,8},{10,11... | collective-permute-start | bytes 196616 | tf_op jit(solution)/shard_map/ppermute | solution.py:351

commit v12 on v11

--- a/solution.py
+++ b/solution.py
@@ -272,36 +272,63 @@
     )
 
 
-def full_gradient(grad_ref, back_first_ref, back_second_ref, ties_ref, work_ref):
-    work_ref[...] = grad_ref[...]
-    for side, back_ref in ((1 - parity(), back_first_ref), (parity(), back_second_ref)):
-        for t in range(back_ref.shape[0]):
-            b = ties_ref[side, t]
-
-            @pl.when(b >= 0)
-            def _(b=b, t=t, back_ref=back_ref):
-                work_ref[b] += back_ref[t].astype(F32)
-
-    return jnp.concatenate([work_ref[b].astype(BF16) for b in range(work_ref.shape[0])], axis=1)
-
-
-def updates(gradient, gain_ref):
+def partial_update_kernel(grad_ref, ties_ref, gain_ref, part_ref):
+    sides, ties = ties_ref.shape
+    blocks = []
+    for b in range(grad_ref.shape[0]):
+        listed = ties_ref[0, 0] == b
+        for side in range(sides):
+            for t in range(ties):
+                listed = listed | (ties_ref[side, t] == b)
+        block = grad_ref[b]
+        blocks.append(jnp.where(listed, jnp.zeros_like(block), block).astype(BF16))
+    gradient = jnp.concatenate(blocks, axis=1)
     step = min(2 * BLK, gain_ref.shape[0])
     for at in range(0, gain_ref.shape[0], step):
         rows = gain_ref[at : at + step, :]
-        update = lax.dot_general(gradient, rows, NT, preferred_element_type=F32)
+        part_ref[:, at : at + step] = lax.dot_general(
+            gradient, rows, NT, preferred_element_type=F32
+        )
+
+
+def updates(part_ref, grad_ref, back_first_ref, back_second_ref, ties_ref, gain_ref, work_ref):
+    ties = back_first_ref.shape[0]
+    lists = [[ties_ref[side, t] for t in range(ties)] for side in (1 - parity(), parity())]
+    for t, b in enumerate(lists[0]):
+        block = grad_ref[jnp.maximum(b, 0)] + back_first_ref[t].astype(F32)
+        work_ref[t] = jnp.where(b >= 0, block, jnp.zeros_like(block))
+    for t, b in enumerate(lists[1]):
+        at = ties + t
+        for u, other in enumerate(lists[0]):
+            at = jnp.where((b >= 0) & (other == b), u, at)
+        block = grad_ref[jnp.maximum(b, 0)]
+        alone = (b >= 0) & (at == ties + t)
+        work_ref[ties + t] = jnp.where(alone, block, jnp.zeros_like(block))
+        back = back_second_ref[t].astype(F32)
+        work_ref[at] += jnp.where(b >= 0, back, jnp.zeros_like(back))
+    listed = lists[0] + lists[1]
+    gradient = jnp.concatenate([work_ref[n].astype(BF16) for n in range(len(listed))], axis=1)
+    step = min(2 * BLK, gain_ref.shape[0])
+    for at in range(0, gain_ref.shape[0], step):
+        rows = [
+            gain_ref[at : at + step, pl.ds(pl.multiple_of(jnp.maximum(b, 0) * BLK, BLK), BLK)]
+            for b in listed
+        ]
+        update = part_ref[:, at : at + step] + lax.dot_general(
+            gradient, jnp.concatenate(rows, axis=1), NT, preferred_element_type=F32
+        )
         for i in range(step // BLK):
             yield at // BLK + i, update[:, i * BLK : (i + 1) * BLK]
 
 
 def first_update_kernel(
-    grad_ref, back_first_ref, back_second_ref, ties_ref, gain_ref, x_ref, x_others_refs,
+    part_ref, grad_ref, back_first_ref, back_second_ref, ties_ref, gain_ref, x_ref, x_others_refs,
     kept_ref, given_refs, message_ref, first_ref, work_ref,
 ):
-    gradient = full_gradient(grad_ref, back_first_ref, back_second_ref, ties_ref, work_ref)
     held, snaps = kept_ref.shape[:2]
     me = lax.axis_index("snap")
-    for i, update in updates(gradient, gain_ref):
+    operands = part_ref, grad_ref, back_first_ref, back_second_ref, ties_ref, gain_ref, work_ref
+    for i, update in updates(*operands):
         columns = pl.ds(pl.multiple_of((me * held + i) * BLK, BLK), BLK)
         parts = [x_ref[:, columns]] + [o[:, i * BLK : (i + 1) * BLK] for o in x_others_refs]
         state = jnp.concatenate(parts, axis=0) + update
@@ -313,11 +340,11 @@
 
 
 def last_update_kernel(
-    grad_ref, back_first_ref, back_second_ref, ties_ref, gain_ref, kept_ref, mine_ref, sent_refs, work_ref
+    part_ref, grad_ref, back_first_ref, back_second_ref, ties_ref, gain_ref, kept_ref, mine_ref, sent_refs, work_ref
 ):
-    gradient = full_gradient(grad_ref, back_first_ref, back_second_ref, ties_ref, work_ref)
     snaps = mine_ref.shape[0]
-    for i, update in updates(gradient, gain_ref):
+    operands = part_ref, grad_ref, back_first_ref, back_second_ref, ties_ref, gain_ref, work_ref
+    for i, update in updates(*operands):
         columns = slice(i * BLK, (i + 1) * BLK)
         mine_ref[:, columns] = kept_ref[i] + update[:snaps]
         for j, sent_ref in enumerate(sent_refs, 1):
@@ -459,7 +486,7 @@
         flops=10**9,
         name="predict",
     )
-    message, guess, x_others = lax.optimization_barrier((message, guess, x_others))
+    message, guess = lax.optimization_barrier((message, guess))
     halves = []
     for part in range(2):
         halves.append(
@@ -473,6 +500,7 @@
                 name="unpack_readings",
             )
         )
+    halves, x_others = lax.optimization_barrier((halves, x_others))
     readings = [half[0] for half in halves]
     variance = [half[1] for half in halves]
     reading_others = [from_all(half) for half in readings]
@@ -482,7 +510,18 @@
         boundary,
     )
     total = pltpu.VMEM((slots, everything, BLK), F32)
-    work = pltpu.VMEM((own, everything, BLK), F32)
+    work = pltpu.VMEM((2 * ties, everything, BLK), F32)
+
+    def partial_update(grad):
+        return call(
+            partial_update_kernel,
+            shape((everything, held * BLK), F32),
+            [VMEM, SMEM, VMEM],
+            (grad, ties_table, reciprocal_normal_operator),
+            flops=10**9,
+            name="partial_update",
+        )
+
     grad, first, second = call(
         pull_kernel,
         grads,
@@ -500,9 +539,9 @@
             shape((held, everything, BLK), BF16),
             boundary,
         ),
-        [VMEM, VMEM, VMEM, SMEM, VMEM, VMEM, [VMEM] * (members - 1)],
+        [VMEM, VMEM, VMEM, VMEM, SMEM, VMEM, VMEM, [VMEM] * (members - 1)],
         (
-            grad, *arrived, ties_table, reciprocal_normal_operator,
+            partial_update(grad), grad, *arrived, ties_table, reciprocal_normal_operator,
             starting_voltages, x_others,
         ),
         scratch=[work],
@@ -541,8 +580,8 @@
             shape((snaps, held * BLK), F32),
             [shape((snaps, held * BLK), BF16)] * (members - 1),
         ),
-        [VMEM, VMEM, VMEM, SMEM, VMEM, VMEM],
-        (grad, first, second, ties_table, reciprocal_normal_operator, kept),
+        [VMEM, VMEM, VMEM, VMEM, SMEM, VMEM, VMEM],
+        (partial_update(grad), grad, first, second, ties_table, reciprocal_normal_operator, kept),
         scratch=[work],
         name="last_update",
     )

time: 75.6 us -> 74.1 us (0.980)
  Pallas kernels: 18.2 us -> 20.7 us
  waiting for transfers between devices: 25.4 us -> 23.4 us
  starting transfers between devices: 28.1 us -> 26.2 us
    pallas_call x12 -> x14, Pallas kernels: 18.2 us -> 20.7 us  [call(): pl.pallas_call(kernel, out_shape=outs, in_specs=ins, out_specs=jax.tree.m...]
    ppermute x8, starting transfers between devices: 13.4 us -> 11.4 us  [swap_pair(): return lax.ppermute(block, 'area', pairs + [(b, a) for a, b in pairs])]
    ppermute x8, waiting for transfers between devices: 13.5 us -> 11.6 us  [swap_pair(): return lax.ppermute(block, 'area', pairs + [(b, a) for a, b in pairs])]
  transfers between devices with their start and end apart: 17 -> 17, of which waited for: 9 -> 9; matrix products, arithmetic and copies ran while one was open for 0% -> 0% of each run, Pallas kernels for 7% -> 15%
where the time goes in v12:
time: 74.1 us; the launch traced here: 73.5 us
  starting transfers between devices  26.2 us (35%)
  waiting for transfers between devices  23.4 us (32%)
  Pallas kernels  20.7 us (28%)
  local copies, waits for them, and re-layouts  3.03 us (4%)
    pallas_call x14, Pallas kernels, call(): pl.pallas_call(kernel, out_shape=outs, in_specs=ins, out_specs=jax.tree.m...  20.7 us
    ppermute x8, waiting for transfers between devices, from_snap(): lax.ppermute(block, 'snap', [(i, (i + distance) % members) for i in range...  11.8 us
    ppermute x8, waiting for transfers between devices, swap_pair(): return lax.ppermute(block, 'area', pairs + [(b, a) for a, b in pairs])  11.6 us
    ppermute x8, starting transfers between devices, swap_pair(): return lax.ppermute(block, 'area', pairs + [(b, a) for a, b in pairs])  11.4 us
    ppermute x8, starting transfers between devices, from_snap(): lax.ppermute(block, 'snap', [(i, (i + distance) % members) for i in range...  8.6 us
    all_to_all x1, starting transfers between devices, on_device(): lax.all_to_all(message, 'area', split_axis=0, concat_axis=0, tiled=True)  6.17 us
    unnamed x14, local copies, waits for them, and re-layouts  3.03 us
  transfers between devices with their start and end apart: 17, of which 9 were waited for; matrix products, arithmetic and copies ran while one was open for 0% of the time, Pallas kernels for 15%

profile of v12, /device:TPU:16, one launch (start us, length us, event | category | flops | bytes accessed | tf_op | source)
XLA Modules:
  0.0 73.5 jit_solution(10643684781618587055)
XLA Ops:
  0.0 4.4 %pack_readings.1 = (f32[16,72,128]{2,1,0:T(8,128)}, bf16[16,32,128]{2,1,0:T(8,128)(2,1)}, f32[32,1024]{1,0:T(8,128)}) custom-call(f32[32,2048]{1,0:T(8,128)} %z_in.1, f32[16,128]{1,0:T(8,128)} %bitcast.17, s32[16,256]{1,0:T(8,128)} %bitcast.16, f32[32,2048]{1,0:T(8,128)} %x_ref.1), custom_call_target="tpu_custom_call" | custom-call | tf_op jit(solution)/shard_map/pack_readings/pallas_call | solution.py:21
  4.4 6.2 %all-to-all-start = ((f32[16,72,128]{2,1,0:T(8,128)}), f32[16,72,128]{2,1,0:T(8,128)S(1)}, u32[]{:S(2)}, u32[]{:S(2)}) async-start(f32[16,72,128]{2,1,0:T(8,128)} %get-tuple-element.46), calls=%async_computation | async-start | bytes 1179648 | tf_op jit(solution)/shard_map/all_to_all | solution.py:452
  10.6 1.5 %collective-permute-start = (bf16[16,32,128]{2,1,0:T(8,128)(2,1)}, bf16[16,32,128]{2,1,0:T(8,128)(2,1)S(1)}, u32[]{:S(2)}, u32[]{:S(2)}) collective-permute-start(bf16[16,32,128]{2,1,0:T(8,128)(2,1)} %get-tuple-element.47.handed_refs_0_), channel_id=1, source_target_pairs={{0,1},{1,0},{2,3},{3,2},{4,5},{5,4},{6,7},{7,6},{8,9},{9,8},{10,11... | collective-permute-start | bytes 393224 | tf_op jit(solution)/shard_map/ppermute | solution.py:378
  12.1 0.9 %copy-done.3 = bf16[16,32,128]{2,1,0:T(8,128)(2,1)S(1)} copy-done((bf16[16,32,128]{2,1,0:T(8,128)(2,1)S(1)}, bf16[16,32,128]{2,1,0:T(8,128)(2,1)}, u32[]{:S(2)}) %copy-start.3) | copy-done | bytes 131096
  13.1 0.7 copy-done.4
  13.8 0.7 copy-done.5
  14.5 0.7 copy-done.6
  15.1 0.4 invert_order.1
  15.6 0.8 %collective-permute-done.own_refs_1_ = bf16[16,32,128]{2,1,0:T(8,128)(2,1)S(1)} collective-permute-done((bf16[16,32,128]{2,1,0:T(8,128)(2,1)}, bf16[16,32,128]{2,1,0:T(8,128)(2,1)S(1)}, u32[]{:S(2)}, u32[]{:S(2)}) %collective-permute-start) | collective-permute-done | bytes 131104 | tf_op jit(solution)/shard_map/ppermute | solution.py:378
  16.4 0.6 pick_boundary.1
  17.0 2.3 %collective-permute-start.1 = (bf16[4,64,128]{2,1,0:T(8,128)(2,1)S(1)}, bf16[4,64,128]{2,1,0:T(8,128)(2,1)S(1)}, u32[]{:S(2)}, u32[]{:S(2)}) collective-permute-start(bf16[4,64,128]{2,1,0:T(8,128)(2,1)S(1)} %get-tuple-element.53), channel_id=1, source_target_pairs={{2,4},{6,8},{10,12},{14,16},{18,20},{22,24},{26,28},{4,2},{8,6},{1... | collective-permute-start | bytes 196616 | tf_op jit(solution)/shard_map/ppermute | solution.py:369
  19.3 1.3 %collective-permute-start.2 = (bf16[4,64,128]{2,1,0:T(8,128)(2,1)S(1)}, bf16[4,64,128]{2,1,0:T(8,128)(2,1)S(1)}, u32[]{:S(2)}, u32[]{:S(2)}) collective-permute-start(bf16[4,64,128]{2,1,0:T(8,128)(2,1)S(1)} %get-tuple-element.54), channel_id=1, source_target_pairs={{0,2},{4,6},{8,10},{12,14},{16,18},{20,22},{24,26},{28,30},{2,0},{... | collective-permute-start | bytes 196616 | tf_op jit(solution)/shard_map/ppermute | solution.py:369
  20.6 1.5 %collective-permute-start.3 = (f32[32,1024]{1,0:T(8,128)}, f32[32,1024]{1,0:T(8,128)S(1)}, u32[]{:S(2)}, u32[]{:S(2)}) collective-permute-start(f32[32,1024]{1,0:T(8,128)} %get-tuple-element.64), channel_id=1, source_target_pairs={{0,1},{1,0},{2,3},{3,2},{4,5},{5,4},{6,7},{7,6},{8,9},{9,8},{10,11... | collective-permute-start | bytes 393224 | tf_op jit(solution)/shard_map/ppermute | solution.py:378
  22.1 4.5 %collective-permute-done.1.first_ref = bf16[4,64,128]{2,1,0:T(8,128)(2,1)S(1)} collective-permute-done((bf16[4,64,128]{2,1,0:T(8,128)(2,1)S(1)}, bf16[4,64,128]{2,1,0:T(8,128)(2,1)S(1)}, u32[]{:S(2)}, u32[]{:S(2)}) %collective-permute-start.1) | collective-permute-done | bytes 65568 | tf_op jit(solution)/shard_map/ppermute | solution.py:369
  26.6 1.4 %predict.1.guess_ref = f32[64,2048]{1,0:T(8,128)S(1)} custom-call(bf16[4,64,128]{2,1,0:T(8,128)(2,1)S(1)} %collective-permute-done.1.first_ref, bf16[4,64,128]{2,1,0:T(8,128)(2,1)S(1)} %collective-permute-done.2.second_ref, bf16[16,32,128]{2,1,0:T(8,128)(2,1)S(1)} %get-tuple-element.48.own_refs_0_, ...), custom_call_target="tpu_custom_call" | custom-call | flops 1000000000 | tf_op jit(solution)/shard_map/predict/pallas_call | solution.py:21
  28.0 1.2 %unpack_readings.3 = (f32[32,1024]{1,0:T(8,128)S(1)}, f32[1,1024]{1,0:T(1,128)S(1)}) custom-call(s32[16,128]{1,0:T(8,128)S(1)} %get-tuple-element.57.group_ref, s32[16,128]{1,0:T(8,128)S(1)} %get-tuple-element.58.lane_ref, f32[16,72,128]{2,1,0:T(8,128)S(1)} %all-to-all-done.message_ref), custom_call_target="tpu_custom_call" | custom-call | flops 2000000000 | tf_op jit(solution)/shard_map/unpack_readings/pallas_call | solution.py:21
  29.2 0.0 copy-start
  29.2 1.2 %unpack_readings.2 = (f32[32,1024]{1,0:T(8,128)S(1)}, f32[1,1024]{1,0:T(1,128)S(1)}) custom-call(s32[16,128]{1,0:T(8,128)S(1)} %get-tuple-element.57.group_ref, s32[16,128]{1,0:T(8,128)S(1)} %get-tuple-element.58.lane_ref, f32[16,72,128]{2,1,0:T(8,128)S(1)} %all-to-all-done.message_ref), custom_call_target="tpu_custom_call" | custom-call | flops 2000000000 | tf_op jit(solution)/shard_map/unpack_readings/pallas_call | solution.py:21
  30.4 0.0 copy-start.2
  30.5 0.0 collective-permute-done.3.x_others_refs_0_
  30.5 1.6 %collective-permute-start.4 = (f32[32,1024]{1,0:T(8,128)S(1)}, f32[32,1024]{1,0:T(8,128)S(1)}, u32[]{:S(2)}, u32[]{:S(2)}) collective-permute-start(f32[32,1024]{1,0:T(8,128)S(1)} %get-tuple-element.65.z_refs_0_), channel_id=1, source_target_pairs={{0,1},{1,0},{2,3},{3,2},{4,5},{5,4},{6,7},{7,6},{8,9},{9,8},{10,11... | collective-permute-start | bytes 393224 | tf_op jit(solution)/shard_map/ppermute | solution.py:378
  32.0 0.5 collective-permute-start.5
  32.6 2.9 %collective-permute-done.4 = f32[32,1024]{1,0:T(8,128)S(1)} collective-permute-done((f32[32,1024]{1,0:T(8,128)S(1)}, f32[32,1024]{1,0:T(8,128)S(1)}, u32[]{:S(2)}, u32[]{:S(2)}) %collective-permute-start.4) | collective-permute-done | bytes 131104 | tf_op jit(solution)/shard_map/ppermute | solution.py:378
  35.5 1.5 %collective-permute-done.5 = f32[32,1024]{1,0:T(8,128)S(1)} collective-permute-done((f32[32,1024]{1,0:T(8,128)S(1)}, f32[32,1024]{1,0:T(8,128)S(1)}, u32[]{:S(2)}, u32[]{:S(2)}) %collective-permute-start.5) | collective-permute-done | bytes 131104 | tf_op jit(solution)/shard_map/ppermute | solution.py:378
  37.0 1.4 %pull.1 = (f32[16,64,128]{2,1,0:T(8,128)S(1)}, bf16[4,64,128]{2,1,0:T(8,128)(2,1)S(1)}, bf16[4,64,128]{2,1,0:T(8,128)(2,1)S(1)}) custom-call(f32[64,2048]{1,0:T(8,128)S(1)} %predict.1.guess_ref, f32[32,1024]{1,0:T(8,128)S(1)} %get-tuple-element.65.z_refs_0_, f32[32,1024]{1,0:T(8,128)S(1)} %get-tuple-element.66.z_refs_1_, f32[1,32,1024]{2,1,0:T(8,128)S(1)} %bitcast.9, ...), custom_call_target="tpu_custom_call" | custom-call | tf_op jit(solution)/shard_map/pull/pallas_call | solution.py:21
  38.5 3.0 %collective-permute-start.6 = (bf16[4,64,128]{2,1,0:T(8,128)(2,1)S(1)}, bf16[4,64,128]{2,1,0:T(8,128)(2,1)S(1)}, u32[]{:S(2)}, u32[]{:S(2)}) collective-permute-start(bf16[4,64,128]{2,1,0:T(8,128)(2,1)S(1)} %get-tuple-element.70), channel_id=1, source_target_pairs={{2,4},{6,8},{10,12},{14,16},{18,20},{22,24},{26,28},{4,2},{8,6},{1... | collective-permute-start | bytes 196616 | tf_op jit(solution)/shard_map/ppermute | solution.py:369
  41.5 0.1 collective-permute-start.7
  41.5 1.9 %partial_update.2.part_ref = f32[64,1024]{1,0:T(8,128)S(1)} custom-call(f32[16,64,128]{2,1,0:T(8,128)S(1)} %get-tuple-element.69.grad_ref, s32[2,4]{1,0:T(2,128)S(1)} %get-tuple-element.49.ties_ref, bf16[1024,2048]{1,0:T(8,128)(2,1)S(1)} %copy-done), custom_call_target="tpu_custom_call" | custom-call | flops 1000000000 | tf_op jit(solution)/shard_map/partial_update/pallas_call | solution.py:21
  43.5 1.5 %collective-permute-done.6.back_first_ref = bf16[4,64,128]{2,1,0:T(8,128)(2,1)S(1)} collective-permute-done((bf16[4,64,128]{2,1,0:T(8,128)(2,1)S(1)}, bf16[4,64,128]{2,1,0:T(8,128)(2,1)S(1)}, u32[]{:S(2)}, u32[]{:S(2)}) %collective-permute-start.6) | collective-permute-done | bytes 65568 | tf_op jit(solution)/shard_map/ppermute | solution.py:369
  45.0 0.0 collective-permute-done.7.back_second_ref
  45.0 1.4 %first_update.1 = (f32[8,32,128]{2,1,0:T(8,128)S(1)}, f32[8,32,128]{2,1,0:T(8,128)S(1)}, bf16[8,64,128]{2,1,0:T(8,128)(2,1)S(1)}, bf16[4,64,128]{2,1,0:T(8,128)(2,1)S(1)}) custom-call(f32[64,1024]{1,0:T(8,128)S(1)} %partial_update.2.part_ref, f32[16,64,128]{2,1,0:T(8,128)S(1)} %get-tuple-element.69.grad_ref, ...), custom_call_target="tpu_custom_call" | custom-call | tf_op jit(solution)/shard_map/first_update/pallas_call | solution.py:21
  46.4 1.5 %collective-permute-start.10 = (bf16[8,64,128]{2,1,0:T(8,128)(2,1)S(1)}, bf16[8,64,128]{2,1,0:T(8,128)(2,1)S(1)}, u32[]{:S(2)}, u32[]{:S(2)}) collective-permute-start(bf16[8,64,128]{2,1,0:T(8,128)(2,1)S(1)} %get-tuple-element.74.mine_ref), channel_id=1, source_target_pairs={{0,1},{1,0},{2,3},{3,2},{4,5},{5,4},{6,7},{7,6},{8,9},{9,8},{10,11... | collective-permute-start | bytes 393224 | tf_op jit(solution)/shard_map/ppermute | solution.py:378
  47.8 2.8 %collective-permute-start.8 = (bf16[4,64,128]{2,1,0:T(8,128)(2,1)S(1)}, bf16[4,64,128]{2,1,0:T(8,128)(2,1)S(1)}, u32[]{:S(2)}, u32[]{:S(2)}) collective-permute-start(bf16[4,64,128]{2,1,0:T(8,128)(2,1)S(1)} %get-tuple-element.73), channel_id=1, source_target_pairs={{2,4},{6,8},{10,12},{14,16},{18,20},{22,24},{26,28},{4,2},{8,6},{1... | collective-permute-start | bytes 196616 | tf_op jit(solution)/shard_map/ppermute | solution.py:369
  50.6 3.7 %collective-permute-done.8.first_refs_0_ = bf16[4,64,128]{2,1,0:T(8,128)(2,1)S(1)} collective-permute-done((bf16[4,64,128]{2,1,0:T(8,128)(2,1)S(1)}, bf16[4,64,128]{2,1,0:T(8,128)(2,1)S(1)}, u32[]{:S(2)}, u32[]{:S(2)}) %collective-permute-start.8) | collective-permute-done | bytes 65568 | tf_op jit(solution)/shard_map/ppermute | solution.py:369
  54.3 0.6 collective-permute-start.9
  55.0 0.6 join_states.1
  55.6 0.1 collective-permute-start.11
  55.6 2.9 %collective-permute-done.9.first_refs_1_ = bf16[4,64,128]{2,1,0:T(8,128)(2,1)S(1)} collective-permute-done((bf16[4,64,128]{2,1,0:T(8,128)(2,1)S(1)}, bf16[4,64,128]{2,1,0:T(8,128)(2,1)S(1)}, u32[]{:S(2)}, u32[]{:S(2)}) %collective-permute-start.9) | collective-permute-done | bytes 65568 | tf_op jit(solution)/shard_map/ppermute | solution.py:378
  58.6 2.0 %predict_pull.1 = (f32[16,64,128]{2,1,0:T(8,128)S(1)}, bf16[4,64,128]{2,1,0:T(8,128)(2,1)S(1)}, bf16[4,64,128]{2,1,0:T(8,128)(2,1)S(1)}) custom-call(bf16[4,64,128]{2,1,0:T(8,128)(2,1)S(1)} %collective-permute-done.8.first_refs_0_, bf16[4,64,128]{2,1,0:T(8,128)(2,1)S(1)} %collective-permute-done.9.first_refs_1_, ...), custom_call_target="tpu_custom_call" | custom-call | tf_op jit(solution)/shard_map/predict_pull/pallas_call | solution.py:21
  60.6 1.9 %collective-permute-start.12 = (bf16[4,64,128]{2,1,0:T(8,128)(2,1)S(1)}, bf16[4,64,128]{2,1,0:T(8,128)(2,1)S(1)}, u32[]{:S(2)}, u32[]{:S(2)}) collective-permute-start(bf16[4,64,128]{2,1,0:T(8,128)(2,1)S(1)} %get-tuple-element.81), channel_id=1, source_target_pairs={{2,4},{6,8},{10,12},{14,16},{18,20},{22,24},{26,28},{4,2},{8,6},{1... | collective-permute-start | bytes 196616 | tf_op jit(solution)/shard_map/ppermute | solution.py:369
  62.5 0.1 collective-permute-start.13
  62.6 0.7 collective-permute-start.14
  63.3 1.9 %partial_update.3.part_ref = f32[64,1024]{1,0:T(8,128)S(1)} custom-call(f32[16,64,128]{2,1,0:T(8,128)S(1)} %get-tuple-element.77.grad_ref, s32[2,4]{1,0:T(2,128)S(1)} %get-tuple-element.49.ties_ref, bf16[1024,2048]{1,0:T(8,128)(2,1)S(1)} %copy-done), custom_call_target="tpu_custom_call" | custom-call | flops 1000000000 | tf_op jit(solution)/shard_map/partial_update/pallas_call | solution.py:21
  65.2 1.8 %collective-permute-done.12.back_first_ref = bf16[4,64,128]{2,1,0:T(8,128)(2,1)S(1)} collective-permute-done((bf16[4,64,128]{2,1,0:T(8,128)(2,1)S(1)}, bf16[4,64,128]{2,1,0:T(8,128)(2,1)S(1)}, u32[]{:S(2)}, u32[]{:S(2)}) %collective-permute-start.12) | collective-permute-done | bytes 65568 | tf_op jit(solution)/shard_map/ppermute | solution.py:369
  67.1 1.4 %last_update.1 = (f32[32,1024]{1,0:T(8,128)S(1)}, bf16[32,1024]{1,0:T(8,128)(2,1)S(1)}) custom-call(f32[64,1024]{1,0:T(8,128)S(1)} %partial_update.3.part_ref, f32[16,64,128]{2,1,0:T(8,128)S(1)} %get-tuple-element.77.grad_ref, bf16[4,64,128]{2,1,0:T(8,128)(2,1)S(1)} %collective-permute-done.12.back_first_ref, ...), custom_call_target="tpu_custom_call" | custom-call | tf_op jit(solution)/shard_map/last_update/pallas_call | solution.py:21
  68.5 0.7 collective-permute-start.15
  69.1 3.6 %collective-permute-done.15.updates_refs_0_ = bf16[32,1024]{1,0:T(8,128)(2,1)S(1)} collective-permute-done((bf16[32,1024]{1,0:T(8,128)(2,1)S(1)}, bf16[32,1024]{1,0:T(8,128)(2,1)S(1)}, u32[]{:S(2)}, u32[]{:S(2)}) %collective-permute-start.15) | collective-permute-done | bytes 65568 | tf_op jit(solution)/shard_map/ppermute | solution.py:378
  72.8 0.7 %finish.1 = f32[32,2048]{1,0:T(8,128)} custom-call(f32[32,1024]{1,0:T(8,128)S(1)} %get-tuple-element.84.mine_ref, f32[8,32,128]{2,1,0:T(8,128)S(1)} %collective-permute-done.14.states_refs_0_, bf16[32,1024]{1,0:T(8,128)(2,1)S(1)} %collective-permute-done.15.updates_refs_0_), custom_call_target="tpu_custom_call" | custom-call | tf_op jit(solution)/shard_map/finish/pallas_call | solution.py:21
  (14 shorter events, 0.0 us)
Async XLA Ops:
  0.0 26.6 %copy-start.1 = (bf16[16,4,128,128]{3,2,1,0:T(8,128)(2,1)S(1)}, bf16[16,4,128,128]{3,2,1,0:T(8,128)(2,1)}, u32[]{:S(2)}) copy-start(bf16[16,4,128,128]{3,2,1,0:T(8,128)(2,1)} %tiles_ref.5) | copy-start | bytes 6291460
  4.4 23.6 %all-to-all-start = ((f32[16,72,128]{2,1,0:T(8,128)}), f32[16,72,128]{2,1,0:T(8,128)S(1)}, u32[]{:S(2)}, u32[]{:S(2)}) async-start(f32[16,72,128]{2,1,0:T(8,128)} %get-tuple-element.46), calls=%async_computation | async-start | bytes 1179648 | tf_op jit(solution)/shard_map/all_to_all | solution.py:452
  10.6 5.8 %collective-permute-start = (bf16[16,32,128]{2,1,0:T(8,128)(2,1)}, bf16[16,32,128]{2,1,0:T(8,128)(2,1)S(1)}, u32[]{:S(2)}, u32[]{:S(2)}) collective-permute-start(bf16[16,32,128]{2,1,0:T(8,128)(2,1)} %get-tuple-element.47.handed_refs_0_), channel_id=1, source_target_pairs={{0,1},{1,0},{2,3},{3,2},{4,5},{5,4},{6,7},{7,6},{8,9},{9,8},{10,11... | collective-permute-start | bytes 393224 | tf_op jit(solution)/shard_map/ppermute | solution.py:378
  12.1 0.9 %copy-start.3 = (bf16[16,32,128]{2,1,0:T(8,128)(2,1)S(1)}, bf16[16,32,128]{2,1,0:T(8,128)(2,1)}, u32[]{:S(2)}) copy-start(bf16[16,32,128]{2,1,0:T(8,128)(2,1)} %get-tuple-element.47.handed_refs_0_) | copy-start | bytes 393220
  13.1 0.7 copy-start.4
  13.8 0.7 copy-start.5
  14.5 0.7 copy-start.6
  17.0 9.6 %collective-permute-start.1 = (bf16[4,64,128]{2,1,0:T(8,128)(2,1)S(1)}, bf16[4,64,128]{2,1,0:T(8,128)(2,1)S(1)}, u32[]{:S(2)}, u32[]{:S(2)}) collective-permute-start(bf16[4,64,128]{2,1,0:T(8,128)(2,1)S(1)} %get-tuple-element.53), channel_id=1, source_target_pairs={{2,4},{6,8},{10,12},{14,16},{18,20},{22,24},{26,28},{4,2},{8,6},{1... | collective-permute-start | bytes 196616 | tf_op jit(solution)/shard_map/ppermute | solution.py:369
  19.3 7.3 %collective-permute-start.2 = (bf16[4,64,128]{2,1,0:T(8,128)(2,1)S(1)}, bf16[4,64,128]{2,1,0:T(8,128)(2,1)S(1)}, u32[]{:S(2)}, u32[]{:S(2)}) collective-permute-start(bf16[4,64,128]{2,1,0:T(8,128)(2,1)S(1)} %get-tuple-element.54), channel_id=1, source_target_pairs={{0,2},{4,6},{8,10},{12,14},{16,18},{20,22},{24,26},{28,30},{2,0},{... | collective-permute-start | bytes 196616 | tf_op jit(solution)/shard_map/ppermute | solution.py:369
  20.6 9.9 %collective-permute-start.3 = (f32[32,1024]{1,0:T(8,128)}, f32[32,1024]{1,0:T(8,128)S(1)}, u32[]{:S(2)}, u32[]{:S(2)}) collective-permute-start(f32[32,1024]{1,0:T(8,128)} %get-tuple-element.64), channel_id=1, source_target_pairs={{0,1},{1,0},{2,3},{3,2},{4,5},{5,4},{6,7},{7,6},{8,9},{9,8},{10,11... | collective-permute-start | bytes 393224 | tf_op jit(solution)/shard_map/ppermute | solution.py:378
  29.2 12.3 %copy-start = (bf16[1024,2048]{1,0:T(8,128)(2,1)S(1)}, bf16[1024,2048]{1,0:T(8,128)(2,1)}, u32[]{:S(2)}) copy-start(bf16[1024,2048]{1,0:T(8,128)(2,1)} %gain_ref.7) | copy-start | bytes 12582916
  30.4 14.5 %copy-start.2 = (f32[32,2048]{1,0:T(8,128)S(1)}, f32[32,2048]{1,0:T(8,128)}, u32[]{:S(2)}) copy-start(f32[32,2048]{1,0:T(8,128)} %x_ref.1) | copy-start | bytes 786436
  30.5 5.0 %collective-permute-start.4 = (f32[32,1024]{1,0:T(8,128)S(1)}, f32[32,1024]{1,0:T(8,128)S(1)}, u32[]{:S(2)}, u32[]{:S(2)}) collective-permute-start(f32[32,1024]{1,0:T(8,128)S(1)} %get-tuple-element.65.z_refs_0_), channel_id=1, source_target_pairs={{0,1},{1,0},{2,3},{3,2},{4,5},{5,4},{6,7},{7,6},{8,9},{9,8},{10,11... | collective-permute-start | bytes 393224 | tf_op jit(solution)/shard_map/ppermute | solution.py:378
  32.0 5.0 %collective-permute-start.5 = (f32[32,1024]{1,0:T(8,128)S(1)}, f32[32,1024]{1,0:T(8,128)S(1)}, u32[]{:S(2)}, u32[]{:S(2)}) collective-permute-start(f32[32,1024]{1,0:T(8,128)S(1)} %get-tuple-element.66.z_refs_1_), channel_id=1, source_target_pairs={{0,1},{1,0},{2,3},{3,2},{4,5},{5,4},{6,7},{7,6},{8,9},{9,8},{10,11... | collective-permute-start | bytes 393224 | tf_op jit(solution)/shard_map/ppermute | solution.py:378
  38.5 6.5 %collective-permute-start.6 = (bf16[4,64,128]{2,1,0:T(8,128)(2,1)S(1)}, bf16[4,64,128]{2,1,0:T(8,128)(2,1)S(1)}, u32[]{:S(2)}, u32[]{:S(2)}) collective-permute-start(bf16[4,64,128]{2,1,0:T(8,128)(2,1)S(1)} %get-tuple-element.70), channel_id=1, source_target_pairs={{2,4},{6,8},{10,12},{14,16},{18,20},{22,24},{26,28},{4,2},{8,6},{1... | collective-permute-start | bytes 196616 | tf_op jit(solution)/shard_map/ppermute | solution.py:369
  41.5 3.5 %collective-permute-start.7 = (bf16[4,64,128]{2,1,0:T(8,128)(2,1)S(1)}, bf16[4,64,128]{2,1,0:T(8,128)(2,1)S(1)}, u32[]{:S(2)}, u32[]{:S(2)}) collective-permute-start(bf16[4,64,128]{2,1,0:T(8,128)(2,1)S(1)} %get-tuple-element.71), channel_id=1, source_target_pairs={{0,2},{4,6},{8,10},{12,14},{16,18},{20,22},{24,26},{28,30},{2,0},{... | collective-permute-start | bytes 196616 | tf_op jit(solution)/shard_map/ppermute | solution.py:369
  46.4 8.6 %collective-permute-start.10 = (bf16[8,64,128]{2,1,0:T(8,128)(2,1)S(1)}, bf16[8,64,128]{2,1,0:T(8,128)(2,1)S(1)}, u32[]{:S(2)}, u32[]{:S(2)}) collective-permute-start(bf16[8,64,128]{2,1,0:T(8,128)(2,1)S(1)} %get-tuple-element.74.mine_ref), channel_id=1, source_target_pairs={{0,1},{1,0},{2,3},{3,2},{4,5},{5,4},{6,7},{7,6},{8,9},{9,8},{10,11... | collective-permute-start | bytes 393224 | tf_op jit(solution)/shard_map/ppermute | solution.py:378
  47.8 6.5 %collective-permute-start.8 = (bf16[4,64,128]{2,1,0:T(8,128)(2,1)S(1)}, bf16[4,64,128]{2,1,0:T(8,128)(2,1)S(1)}, u32[]{:S(2)}, u32[]{:S(2)}) collective-permute-start(bf16[4,64,128]{2,1,0:T(8,128)(2,1)S(1)} %get-tuple-element.73), channel_id=1, source_target_pairs={{2,4},{6,8},{10,12},{14,16},{18,20},{22,24},{26,28},{4,2},{8,6},{1... | collective-permute-start | bytes 196616 | tf_op jit(solution)/shard_map/ppermute | solution.py:369
  54.3 4.3 %collective-permute-start.9 = (bf16[4,64,128]{2,1,0:T(8,128)(2,1)S(1)}, bf16[4,64,128]{2,1,0:T(8,128)(2,1)S(1)}, u32[]{:S(2)}, u32[]{:S(2)}) collective-permute-start(bf16[4,64,128]{2,1,0:T(8,128)(2,1)S(1)} %collective-permute-done.8.first_refs_0_), channel_id=1, source_target_pairs={{0,1},{1,0},{2,3},{3,2},{4,5},{5,4},{6,7},{7,6},{8,9},{9,8},{10,11... | collective-permute-start | bytes 196616 | tf_op jit(solution)/shard_map/ppermute | solution.py:378
  55.6 3.0 %collective-permute-start.11 = (bf16[4,64,128]{2,1,0:T(8,128)(2,1)S(1)}, bf16[4,64,128]{2,1,0:T(8,128)(2,1)S(1)}, u32[]{:S(2)}, u32[]{:S(2)}) collective-permute-start(bf16[4,64,128]{2,1,0:T(8,128)(2,1)S(1)} %get-tuple-element.76), channel_id=1, source_target_pairs={{0,2},{4,6},{8,10},{12,14},{16,18},{20,22},{24,26},{28,30},{2,0},{... | collective-permute-start | bytes 196616 | tf_op jit(solution)/shard_map/ppermute | solution.py:369
  60.6 6.5 %collective-permute-start.12 = (bf16[4,64,128]{2,1,0:T(8,128)(2,1)S(1)}, bf16[4,64,128]{2,1,0:T(8,128)(2,1)S(1)}, u32[]{:S(2)}, u32[]{:S(2)}) collective-permute-start(bf16[4,64,128]{2,1,0:T(8,128)(2,1)S(1)} %get-tuple-element.81), channel_id=1, source_target_pairs={{2,4},{6,8},{10,12},{14,16},{18,20},{22,24},{26,28},{4,2},{8,6},{1... | collective-permute-start | bytes 196616 | tf_op jit(solution)/shard_map/ppermute | solution.py:369
  62.5 4.6 %collective-permute-start.13 = (bf16[4,64,128]{2,1,0:T(8,128)(2,1)S(1)}, bf16[4,64,128]{2,1,0:T(8,128)(2,1)S(1)}, u32[]{:S(2)}, u32[]{:S(2)}) collective-permute-start(bf16[4,64,128]{2,1,0:T(8,128)(2,1)S(1)} %get-tuple-element.82), channel_id=1, source_target_pairs={{0,2},{4,6},{8,10},{12,14},{16,18},{20,22},{24,26},{28,30},{2,0},{... | collective-permute-start | bytes 196616 | tf_op jit(solution)/shard_map/ppermute | solution.py:369
  62.6 6.6 %collective-permute-start.14 = (f32[8,32,128]{2,1,0:T(8,128)S(1)}, f32[8,32,128]{2,1,0:T(8,128)S(1)}, u32[]{:S(2)}, u32[]{:S(2)}) collective-permute-start(f32[8,32,128]{2,1,0:T(8,128)S(1)} %get-tuple-element.85), channel_id=1, source_target_pairs={{0,1},{1,0},{2,3},{3,2},{4,5},{5,4},{6,7},{7,6},{8,9},{9,8},{10,11... | collective-permute-start | bytes 393224 | tf_op jit(solution)/shard_map/ppermute | solution.py:378
  68.5 4.3 %collective-permute-start.15 = (bf16[32,1024]{1,0:T(8,128)(2,1)S(1)}, bf16[32,1024]{1,0:T(8,128)(2,1)S(1)}, u32[]{:S(2)}, u32[]{:S(2)}) collective-permute-start(bf16[32,1024]{1,0:T(8,128)(2,1)S(1)} %get-tuple-element.86), channel_id=1, source_target_pairs={{0,1},{1,0},{2,3},{3,2},{4,5},{5,4},{6,7},{7,6},{8,9},{9,8},{10,11... | collective-permute-start | bytes 196616 | tf_op jit(solution)/shard_map/ppermute | solution.py:378

commit v13 on v12

--- a/solution.py
+++ b/solution.py
@@ -557,7 +557,9 @@
         (mine, others, ties_table),
         name="join_states",
     )
+    given, second = lax.optimization_barrier((given, second))
     second = swap_pair(second, 0)
+    states_in = [from_snap(block, -i) for i, block in enumerate(given, 1)]
     grad, first, second = call(
         predict_pull_kernel,
         grads,
@@ -571,9 +573,8 @@
         ],
         name="predict_pull",
     )
-    given, first, second = lax.optimization_barrier((given, first, second))
+    grad, states_in = lax.optimization_barrier((grad, states_in))
     first, second = with_neighbours(first, second)
-    states_in = [from_snap(block, -i) for i, block in enumerate(given, 1)]
     mine, sent = call(
         last_update_kernel,
         (

time: 74.1 us -> 75 us (1.012); the launches traced: 73.5 us -> 73.5 us
  starting transfers between devices: 26.2 us -> 28.2 us
  waiting for transfers between devices: 23.4 us -> 21.4 us
    ppermute x8, waiting for transfers between devices: 11.6 us -> 8.12 us  [swap_pair(): return lax.ppermute(block, 'area', pairs + [(b, a) for a, b in pairs])]
    ppermute x8, waiting for transfers between devices: 11.8 us -> 13.3 us  [from_snap(): lax.ppermute(block, 'snap', [(i, (i + distance) % members) for i in range...]
    ppermute x8, starting transfers between devices: 11.4 us -> 12.6 us  [swap_pair(): return lax.ppermute(block, 'area', pairs + [(b, a) for a, b in pairs])]
    ppermute x8, starting transfers between devices: 8.6 us -> 9.37 us  [from_snap(): lax.ppermute(block, 'snap', [(i, (i + distance) % members) for i in range...]
  transfers between devices with their start and end apart: 17 -> 17, of which waited for: 9 -> 10; matrix products, arithmetic and copies ran while one was open for 0% -> 0% of each run, Pallas kernels for 15% -> 15%
where the time goes in v13:
time: 75 us; the launch traced here: 73.5 us
  starting transfers between devices  28.2 us (38%)
  waiting for transfers between devices  21.4 us (29%)
  Pallas kernels  20.7 us (28%)
  local copies, waits for them, and re-layouts  3.03 us (4%)
    pallas_call x14, Pallas kernels, call(): pl.pallas_call(kernel, out_shape=outs, in_specs=ins, out_specs=jax.tree.m...  20.7 us
    ppermute x8, waiting for transfers between devices, from_snap(): lax.ppermute(block, 'snap', [(i, (i + distance) % members) for i in range...  13.3 us
    ppermute x8, starting transfers between devices, swap_pair(): return lax.ppermute(block, 'area', pairs + [(b, a) for a, b in pairs])  12.6 us
    ppermute x8, starting transfers between devices, from_snap(): lax.ppermute(block, 'snap', [(i, (i + distance) % members) for i in range...  9.37 us
    ppermute x8, waiting for transfers between devices, swap_pair(): return lax.ppermute(block, 'area', pairs + [(b, a) for a, b in pairs])  8.12 us
    all_to_all x1, starting transfers between devices, on_device(): lax.all_to_all(message, 'area', split_axis=0, concat_axis=0, tiled=True)  6.17 us
    unnamed x14, local copies, waits for them, and re-layouts  3.03 us
  transfers between devices with their start and end apart: 17, of which 10 were waited for; matrix products, arithmetic and copies ran while one was open for 0% of the time, Pallas kernels for 15%

profile of v13, /device:TPU:16, one launch (start us, length us, event | category | flops | bytes accessed | tf_op | source)
XLA Modules:
  0.0 73.5 jit_solution(8632532931782297963)
XLA Ops:
  0.0 4.4 %pack_readings.1 = (f32[16,72,128]{2,1,0:T(8,128)}, bf16[16,32,128]{2,1,0:T(8,128)(2,1)}, f32[32,1024]{1,0:T(8,128)}) custom-call(f32[32,2048]{1,0:T(8,128)} %z_in.1, f32[16,128]{1,0:T(8,128)} %bitcast.17, s32[16,256]{1,0:T(8,128)} %bitcast.16, f32[32,2048]{1,0:T(8,128)} %x_ref.1), custom_call_target="tpu_custom_call" | custom-call | tf_op jit(solution)/shard_map/pack_readings/pallas_call | solution.py:21
  4.4 6.2 %all-to-all-start = ((f32[16,72,128]{2,1,0:T(8,128)}), f32[16,72,128]{2,1,0:T(8,128)S(1)}, u32[]{:S(2)}, u32[]{:S(2)}) async-start(f32[16,72,128]{2,1,0:T(8,128)} %get-tuple-element.47), calls=%async_computation | async-start | bytes 1179648 | tf_op jit(solution)/shard_map/all_to_all | solution.py:452
  10.6 1.5 %collective-permute-start = (bf16[16,32,128]{2,1,0:T(8,128)(2,1)}, bf16[16,32,128]{2,1,0:T(8,128)(2,1)S(1)}, u32[]{:S(2)}, u32[]{:S(2)}) collective-permute-start(bf16[16,32,128]{2,1,0:T(8,128)(2,1)} %get-tuple-element.48.handed_refs_0_), channel_id=1, source_target_pairs={{0,1},{1,0},{2,3},{3,2},{4,5},{5,4},{6,7},{7,6},{8,9},{9,8},{10,11... | collective-permute-start | bytes 393224 | tf_op jit(solution)/shard_map/ppermute | solution.py:378
  12.1 0.9 %copy-done.3 = bf16[16,32,128]{2,1,0:T(8,128)(2,1)S(1)} copy-done((bf16[16,32,128]{2,1,0:T(8,128)(2,1)S(1)}, bf16[16,32,128]{2,1,0:T(8,128)(2,1)}, u32[]{:S(2)}) %copy-start.3) | copy-done | bytes 131096
  13.1 0.7 copy-done.4
  13.8 0.7 copy-done.5
  14.5 0.7 copy-done.6
  15.1 0.4 invert_order.1
  15.6 0.8 %collective-permute-done.own_refs_1_ = bf16[16,32,128]{2,1,0:T(8,128)(2,1)S(1)} collective-permute-done((bf16[16,32,128]{2,1,0:T(8,128)(2,1)}, bf16[16,32,128]{2,1,0:T(8,128)(2,1)S(1)}, u32[]{:S(2)}, u32[]{:S(2)}) %collective-permute-start) | collective-permute-done | bytes 131104 | tf_op jit(solution)/shard_map/ppermute | solution.py:378
  16.4 0.6 pick_boundary.1
  17.0 2.3 %collective-permute-start.1 = (bf16[4,64,128]{2,1,0:T(8,128)(2,1)S(1)}, bf16[4,64,128]{2,1,0:T(8,128)(2,1)S(1)}, u32[]{:S(2)}, u32[]{:S(2)}) collective-permute-start(bf16[4,64,128]{2,1,0:T(8,128)(2,1)S(1)} %get-tuple-element.54), channel_id=1, source_target_pairs={{2,4},{6,8},{10,12},{14,16},{18,20},{22,24},{26,28},{4,2},{8,6},{1... | collective-permute-start | bytes 196616 | tf_op jit(solution)/shard_map/ppermute | solution.py:369
  19.3 1.3 %collective-permute-start.2 = (bf16[4,64,128]{2,1,0:T(8,128)(2,1)S(1)}, bf16[4,64,128]{2,1,0:T(8,128)(2,1)S(1)}, u32[]{:S(2)}, u32[]{:S(2)}) collective-permute-start(bf16[4,64,128]{2,1,0:T(8,128)(2,1)S(1)} %get-tuple-element.55), channel_id=1, source_target_pairs={{0,2},{4,6},{8,10},{12,14},{16,18},{20,22},{24,26},{28,30},{2,0},{... | collective-permute-start | bytes 196616 | tf_op jit(solution)/shard_map/ppermute | solution.py:369
  20.6 1.5 %collective-permute-start.3 = (f32[32,1024]{1,0:T(8,128)}, f32[32,1024]{1,0:T(8,128)S(1)}, u32[]{:S(2)}, u32[]{:S(2)}) collective-permute-start(f32[32,1024]{1,0:T(8,128)} %get-tuple-element.65), channel_id=1, source_target_pairs={{0,1},{1,0},{2,3},{3,2},{4,5},{5,4},{6,7},{7,6},{8,9},{9,8},{10,11... | collective-permute-start | bytes 393224 | tf_op jit(solution)/shard_map/ppermute | solution.py:378
  22.1 4.5 %collective-permute-done.1.first_ref = bf16[4,64,128]{2,1,0:T(8,128)(2,1)S(1)} collective-permute-done((bf16[4,64,128]{2,1,0:T(8,128)(2,1)S(1)}, bf16[4,64,128]{2,1,0:T(8,128)(2,1)S(1)}, u32[]{:S(2)}, u32[]{:S(2)}) %collective-permute-start.1) | collective-permute-done | bytes 65568 | tf_op jit(solution)/shard_map/ppermute | solution.py:369
  26.6 0.0 collective-permute-done.2.second_ref
  26.6 1.4 %predict.1.guess_ref = f32[64,2048]{1,0:T(8,128)S(1)} custom-call(bf16[4,64,128]{2,1,0:T(8,128)(2,1)S(1)} %collective-permute-done.1.first_ref, bf16[4,64,128]{2,1,0:T(8,128)(2,1)S(1)} %collective-permute-done.2.second_ref, bf16[16,32,128]{2,1,0:T(8,128)(2,1)S(1)} %get-tuple-element.49.own_refs_0_, ...), custom_call_target="tpu_custom_call" | custom-call | flops 1000000000 | tf_op jit(solution)/shard_map/predict/pallas_call | solution.py:21
  28.0 0.0 all-to-all-done.message_ref
  28.0 1.2 %unpack_readings.3 = (f32[32,1024]{1,0:T(8,128)S(1)}, f32[1,1024]{1,0:T(1,128)S(1)}) custom-call(s32[16,128]{1,0:T(8,128)S(1)} %get-tuple-element.58.group_ref, s32[16,128]{1,0:T(8,128)S(1)} %get-tuple-element.59.lane_ref, f32[16,72,128]{2,1,0:T(8,128)S(1)} %all-to-all-done.message_ref), custom_call_target="tpu_custom_call" | custom-call | flops 2000000000 | tf_op jit(solution)/shard_map/unpack_readings/pallas_call | solution.py:21
  29.2 0.0 copy-start
  29.2 1.2 %unpack_readings.2 = (f32[32,1024]{1,0:T(8,128)S(1)}, f32[1,1024]{1,0:T(1,128)S(1)}) custom-call(s32[16,128]{1,0:T(8,128)S(1)} %get-tuple-element.58.group_ref, s32[16,128]{1,0:T(8,128)S(1)} %get-tuple-element.59.lane_ref, f32[16,72,128]{2,1,0:T(8,128)S(1)} %all-to-all-done.message_ref), custom_call_target="tpu_custom_call" | custom-call | flops 2000000000 | tf_op jit(solution)/shard_map/unpack_readings/pallas_call | solution.py:21
  30.4 0.0 copy-start.2
  30.5 1.6 %collective-permute-start.4 = (f32[32,1024]{1,0:T(8,128)S(1)}, f32[32,1024]{1,0:T(8,128)S(1)}, u32[]{:S(2)}, u32[]{:S(2)}) collective-permute-start(f32[32,1024]{1,0:T(8,128)S(1)} %get-tuple-element.66.z_refs_0_), channel_id=1, source_target_pairs={{0,1},{1,0},{2,3},{3,2},{4,5},{5,4},{6,7},{7,6},{8,9},{9,8},{10,11... | collective-permute-start | bytes 393224 | tf_op jit(solution)/shard_map/ppermute | solution.py:378
  32.0 0.5 collective-permute-start.5
  32.6 2.9 %collective-permute-done.4 = f32[32,1024]{1,0:T(8,128)S(1)} collective-permute-done((f32[32,1024]{1,0:T(8,128)S(1)}, f32[32,1024]{1,0:T(8,128)S(1)}, u32[]{:S(2)}, u32[]{:S(2)}) %collective-permute-start.4) | collective-permute-done | bytes 131104 | tf_op jit(solution)/shard_map/ppermute | solution.py:378
  35.5 1.5 %collective-permute-done.5 = f32[32,1024]{1,0:T(8,128)S(1)} collective-permute-done((f32[32,1024]{1,0:T(8,128)S(1)}, f32[32,1024]{1,0:T(8,128)S(1)}, u32[]{:S(2)}, u32[]{:S(2)}) %collective-permute-start.5) | collective-permute-done | bytes 131104 | tf_op jit(solution)/shard_map/ppermute | solution.py:378
  37.0 1.4 %pull.1 = (f32[16,64,128]{2,1,0:T(8,128)S(1)}, bf16[4,64,128]{2,1,0:T(8,128)(2,1)S(1)}, bf16[4,64,128]{2,1,0:T(8,128)(2,1)S(1)}) custom-call(f32[64,2048]{1,0:T(8,128)S(1)} %predict.1.guess_ref, f32[32,1024]{1,0:T(8,128)S(1)} %get-tuple-element.66.z_refs_0_, f32[32,1024]{1,0:T(8,128)S(1)} %get-tuple-element.67.z_refs_1_, f32[1,32,1024]{2,1,0:T(8,128)S(1)} %bitcast.9, ...), custom_call_target="tpu_custom_call" | custom-call | tf_op jit(solution)/shard_map/pull/pallas_call | solution.py:21
  38.5 3.0 %collective-permute-start.6 = (bf16[4,64,128]{2,1,0:T(8,128)(2,1)S(1)}, bf16[4,64,128]{2,1,0:T(8,128)(2,1)S(1)}, u32[]{:S(2)}, u32[]{:S(2)}) collective-permute-start(bf16[4,64,128]{2,1,0:T(8,128)(2,1)S(1)} %get-tuple-element.71), channel_id=1, source_target_pairs={{2,4},{6,8},{10,12},{14,16},{18,20},{22,24},{26,28},{4,2},{8,6},{1... | collective-permute-start | bytes 196616 | tf_op jit(solution)/shard_map/ppermute | solution.py:369
  41.5 0.1 collective-permute-start.7
  41.6 1.9 %partial_update.2.part_ref = f32[64,1024]{1,0:T(8,128)S(1)} custom-call(f32[16,64,128]{2,1,0:T(8,128)S(1)} %get-tuple-element.70.grad_ref, s32[2,4]{1,0:T(2,128)S(1)} %get-tuple-element.50.ties_ref, bf16[1024,2048]{1,0:T(8,128)(2,1)S(1)} %copy-done), custom_call_target="tpu_custom_call" | custom-call | flops 1000000000 | tf_op jit(solution)/shard_map/partial_update/pallas_call | solution.py:21
  43.5 1.5 %collective-permute-done.6.back_first_ref = bf16[4,64,128]{2,1,0:T(8,128)(2,1)S(1)} collective-permute-done((bf16[4,64,128]{2,1,0:T(8,128)(2,1)S(1)}, bf16[4,64,128]{2,1,0:T(8,128)(2,1)S(1)}, u32[]{:S(2)}, u32[]{:S(2)}) %collective-permute-start.6) | collective-permute-done | bytes 65568 | tf_op jit(solution)/shard_map/ppermute | solution.py:369
  45.0 1.4 %first_update.1 = (f32[8,32,128]{2,1,0:T(8,128)S(1)}, f32[8,32,128]{2,1,0:T(8,128)S(1)}, bf16[8,64,128]{2,1,0:T(8,128)(2,1)S(1)}, bf16[4,64,128]{2,1,0:T(8,128)(2,1)S(1)}) custom-call(f32[64,1024]{1,0:T(8,128)S(1)} %partial_update.2.part_ref, f32[16,64,128]{2,1,0:T(8,128)S(1)} %get-tuple-element.70.grad_ref, ...), custom_call_target="tpu_custom_call" | custom-call | tf_op jit(solution)/shard_map/first_update/pallas_call | solution.py:21
  46.4 1.5 %collective-permute-start.10 = (bf16[8,64,128]{2,1,0:T(8,128)(2,1)S(1)}, bf16[8,64,128]{2,1,0:T(8,128)(2,1)S(1)}, u32[]{:S(2)}, u32[]{:S(2)}) collective-permute-start(bf16[8,64,128]{2,1,0:T(8,128)(2,1)S(1)} %get-tuple-element.75.mine_ref), channel_id=1, source_target_pairs={{0,1},{1,0},{2,3},{3,2},{4,5},{5,4},{6,7},{7,6},{8,9},{9,8},{10,11... | collective-permute-start | bytes 393224 | tf_op jit(solution)/shard_map/ppermute | solution.py:378
  47.8 2.8 %collective-permute-start.8 = (bf16[4,64,128]{2,1,0:T(8,128)(2,1)S(1)}, bf16[4,64,128]{2,1,0:T(8,128)(2,1)S(1)}, u32[]{:S(2)}, u32[]{:S(2)}) collective-permute-start(bf16[4,64,128]{2,1,0:T(8,128)(2,1)S(1)} %get-tuple-element.74), channel_id=1, source_target_pairs={{2,4},{6,8},{10,12},{14,16},{18,20},{22,24},{26,28},{4,2},{8,6},{1... | collective-permute-start | bytes 196616 | tf_op jit(solution)/shard_map/ppermute | solution.py:369
  50.6 0.8 %collective-permute-done.10.others_refs_0_ = bf16[8,64,128]{2,1,0:T(8,128)(2,1)S(1)} collective-permute-done((bf16[8,64,128]{2,1,0:T(8,128)(2,1)S(1)}, bf16[8,64,128]{2,1,0:T(8,128)(2,1)S(1)}, u32[]{:S(2)}, u32[]{:S(2)}) %collective-permute-start.10) | collective-permute-done | bytes 131104 | tf_op jit(solution)/shard_map/ppermute | solution.py:378
  51.4 0.6 join_states.1
  52.0 1.5 %collective-permute-start.12 = (f32[8,32,128]{2,1,0:T(8,128)S(1)}, f32[8,32,128]{2,1,0:T(8,128)S(1)}, u32[]{:S(2)}, u32[]{:S(2)}) collective-permute-start(f32[8,32,128]{2,1,0:T(8,128)S(1)} %get-tuple-element.81), channel_id=1, source_target_pairs={{0,1},{1,0},{2,3},{3,2},{4,5},{5,4},{6,7},{7,6},{8,9},{9,8},{10,11... | collective-permute-start | bytes 393224 | tf_op jit(solution)/shard_map/ppermute | solution.py:378
  53.5 0.8 %collective-permute-done.8.first_refs_0_ = bf16[4,64,128]{2,1,0:T(8,128)(2,1)S(1)} collective-permute-done((bf16[4,64,128]{2,1,0:T(8,128)(2,1)S(1)}, bf16[4,64,128]{2,1,0:T(8,128)(2,1)S(1)}, u32[]{:S(2)}, u32[]{:S(2)}) %collective-permute-start.8) | collective-permute-done | bytes 65568 | tf_op jit(solution)/shard_map/ppermute | solution.py:369
  54.3 0.6 collective-permute-start.9
  54.9 3.6 %collective-permute-done.9.first_refs_1_ = bf16[4,64,128]{2,1,0:T(8,128)(2,1)S(1)} collective-permute-done((bf16[4,64,128]{2,1,0:T(8,128)(2,1)S(1)}, bf16[4,64,128]{2,1,0:T(8,128)(2,1)S(1)}, u32[]{:S(2)}, u32[]{:S(2)}) %collective-permute-start.9) | collective-permute-done | bytes 65568 | tf_op jit(solution)/shard_map/ppermute | solution.py:378
  58.6 2.0 %predict_pull.1 = (f32[16,64,128]{2,1,0:T(8,128)S(1)}, bf16[4,64,128]{2,1,0:T(8,128)(2,1)S(1)}, bf16[4,64,128]{2,1,0:T(8,128)(2,1)S(1)}) custom-call(bf16[4,64,128]{2,1,0:T(8,128)(2,1)S(1)} %collective-permute-done.8.first_refs_0_, bf16[4,64,128]{2,1,0:T(8,128)(2,1)S(1)} %collective-permute-done.9.first_refs_1_, ...), custom_call_target="tpu_custom_call" | custom-call | tf_op jit(solution)/shard_map/predict_pull/pallas_call | solution.py:21
  60.6 3.1 %collective-permute-start.13 = (bf16[4,64,128]{2,1,0:T(8,128)(2,1)S(1)}, bf16[4,64,128]{2,1,0:T(8,128)(2,1)S(1)}, u32[]{:S(2)}, u32[]{:S(2)}) collective-permute-start(bf16[4,64,128]{2,1,0:T(8,128)(2,1)S(1)} %get-tuple-element.83), channel_id=1, source_target_pairs={{2,4},{6,8},{10,12},{14,16},{18,20},{22,24},{26,28},{4,2},{8,6},{1... | collective-permute-start | bytes 196616 | tf_op jit(solution)/shard_map/ppermute | solution.py:369
  63.7 0.1 collective-permute-start.14
  63.8 1.9 %partial_update.3.part_ref = f32[64,1024]{1,0:T(8,128)S(1)} custom-call(f32[16,64,128]{2,1,0:T(8,128)S(1)} %get-tuple-element.82.grad_ref, s32[2,4]{1,0:T(2,128)S(1)} %get-tuple-element.50.ties_ref, bf16[1024,2048]{1,0:T(8,128)(2,1)S(1)} %copy-done), custom_call_target="tpu_custom_call" | custom-call | flops 1000000000 | tf_op jit(solution)/shard_map/partial_update/pallas_call | solution.py:21
  65.7 1.3 %collective-permute-done.13.back_first_ref = bf16[4,64,128]{2,1,0:T(8,128)(2,1)S(1)} collective-permute-done((bf16[4,64,128]{2,1,0:T(8,128)(2,1)S(1)}, bf16[4,64,128]{2,1,0:T(8,128)(2,1)S(1)}, u32[]{:S(2)}, u32[]{:S(2)}) %collective-permute-start.13) | collective-permute-done | bytes 65568 | tf_op jit(solution)/shard_map/ppermute | solution.py:369
  67.1 1.4 %last_update.1 = (f32[32,1024]{1,0:T(8,128)S(1)}, bf16[32,1024]{1,0:T(8,128)(2,1)S(1)}) custom-call(f32[64,1024]{1,0:T(8,128)S(1)} %partial_update.3.part_ref, f32[16,64,128]{2,1,0:T(8,128)S(1)} %get-tuple-element.82.grad_ref, bf16[4,64,128]{2,1,0:T(8,128)(2,1)S(1)} %collective-permute-done.13.back_first_ref, ...), custom_call_target="tpu_custom_call" | custom-call | tf_op jit(solution)/shard_map/last_update/pallas_call | solution.py:21
  68.4 0.7 collective-permute-start.15
  69.1 3.6 %collective-permute-done.15.updates_refs_0_ = bf16[32,1024]{1,0:T(8,128)(2,1)S(1)} collective-permute-done((bf16[32,1024]{1,0:T(8,128)(2,1)S(1)}, bf16[32,1024]{1,0:T(8,128)(2,1)S(1)}, u32[]{:S(2)}, u32[]{:S(2)}) %collective-permute-start.15) | collective-permute-done | bytes 65568 | tf_op jit(solution)/shard_map/ppermute | solution.py:378
  72.8 0.7 %finish.1 = f32[32,2048]{1,0:T(8,128)} custom-call(f32[32,1024]{1,0:T(8,128)S(1)} %get-tuple-element.86.mine_ref, f32[8,32,128]{2,1,0:T(8,128)S(1)} %collective-permute-done.12.states_refs_0_, bf16[32,1024]{1,0:T(8,128)(2,1)S(1)} %collective-permute-done.15.updates_refs_0_), custom_call_target="tpu_custom_call" | custom-call | tf_op jit(solution)/shard_map/finish/pallas_call | solution.py:21
  (14 shorter events, 0.0 us)
Async XLA Ops:
  0.0 26.6 %copy-start.1 = (bf16[16,4,128,128]{3,2,1,0:T(8,128)(2,1)S(1)}, bf16[16,4,128,128]{3,2,1,0:T(8,128)(2,1)}, u32[]{:S(2)}) copy-start(bf16[16,4,128,128]{3,2,1,0:T(8,128)(2,1)} %tiles_ref.5) | copy-start | bytes 6291460
  4.4 23.6 %all-to-all-start = ((f32[16,72,128]{2,1,0:T(8,128)}), f32[16,72,128]{2,1,0:T(8,128)S(1)}, u32[]{:S(2)}, u32[]{:S(2)}) async-start(f32[16,72,128]{2,1,0:T(8,128)} %get-tuple-element.47), calls=%async_computation | async-start | bytes 1179648 | tf_op jit(solution)/shard_map/all_to_all | solution.py:452
  10.6 5.8 %collective-permute-start = (bf16[16,32,128]{2,1,0:T(8,128)(2,1)}, bf16[16,32,128]{2,1,0:T(8,128)(2,1)S(1)}, u32[]{:S(2)}, u32[]{:S(2)}) collective-permute-start(bf16[16,32,128]{2,1,0:T(8,128)(2,1)} %get-tuple-element.48.handed_refs_0_), channel_id=1, source_target_pairs={{0,1},{1,0},{2,3},{3,2},{4,5},{5,4},{6,7},{7,6},{8,9},{9,8},{10,11... | collective-permute-start | bytes 393224 | tf_op jit(solution)/shard_map/ppermute | solution.py:378
  12.1 0.9 %copy-start.3 = (bf16[16,32,128]{2,1,0:T(8,128)(2,1)S(1)}, bf16[16,32,128]{2,1,0:T(8,128)(2,1)}, u32[]{:S(2)}) copy-start(bf16[16,32,128]{2,1,0:T(8,128)(2,1)} %get-tuple-element.48.handed_refs_0_) | copy-start | bytes 393220
  13.1 0.7 copy-start.4
  13.8 0.7 copy-start.5
  14.5 0.7 copy-start.6
  17.0 9.6 %collective-permute-start.1 = (bf16[4,64,128]{2,1,0:T(8,128)(2,1)S(1)}, bf16[4,64,128]{2,1,0:T(8,128)(2,1)S(1)}, u32[]{:S(2)}, u32[]{:S(2)}) collective-permute-start(bf16[4,64,128]{2,1,0:T(8,128)(2,1)S(1)} %get-tuple-element.54), channel_id=1, source_target_pairs={{2,4},{6,8},{10,12},{14,16},{18,20},{22,24},{26,28},{4,2},{8,6},{1... | collective-permute-start | bytes 196616 | tf_op jit(solution)/shard_map/ppermute | solution.py:369
  19.3 7.3 %collective-permute-start.2 = (bf16[4,64,128]{2,1,0:T(8,128)(2,1)S(1)}, bf16[4,64,128]{2,1,0:T(8,128)(2,1)S(1)}, u32[]{:S(2)}, u32[]{:S(2)}) collective-permute-start(bf16[4,64,128]{2,1,0:T(8,128)(2,1)S(1)} %get-tuple-element.55), channel_id=1, source_target_pairs={{0,2},{4,6},{8,10},{12,14},{16,18},{20,22},{24,26},{28,30},{2,0},{... | collective-permute-start | bytes 196616 | tf_op jit(solution)/shard_map/ppermute | solution.py:369
  20.6 9.9 %collective-permute-start.3 = (f32[32,1024]{1,0:T(8,128)}, f32[32,1024]{1,0:T(8,128)S(1)}, u32[]{:S(2)}, u32[]{:S(2)}) collective-permute-start(f32[32,1024]{1,0:T(8,128)} %get-tuple-element.65), channel_id=1, source_target_pairs={{0,1},{1,0},{2,3},{3,2},{4,5},{5,4},{6,7},{7,6},{8,9},{9,8},{10,11... | collective-permute-start | bytes 393224 | tf_op jit(solution)/shard_map/ppermute | solution.py:378
  29.2 12.3 %copy-start = (bf16[1024,2048]{1,0:T(8,128)(2,1)S(1)}, bf16[1024,2048]{1,0:T(8,128)(2,1)}, u32[]{:S(2)}) copy-start(bf16[1024,2048]{1,0:T(8,128)(2,1)} %gain_ref.7) | copy-start | bytes 12582916
  30.4 14.5 %copy-start.2 = (f32[32,2048]{1,0:T(8,128)S(1)}, f32[32,2048]{1,0:T(8,128)}, u32[]{:S(2)}) copy-start(f32[32,2048]{1,0:T(8,128)} %x_ref.1) | copy-start | bytes 786436
  30.5 5.0 %collective-permute-start.4 = (f32[32,1024]{1,0:T(8,128)S(1)}, f32[32,1024]{1,0:T(8,128)S(1)}, u32[]{:S(2)}, u32[]{:S(2)}) collective-permute-start(f32[32,1024]{1,0:T(8,128)S(1)} %get-tuple-element.66.z_refs_0_), channel_id=1, source_target_pairs={{0,1},{1,0},{2,3},{3,2},{4,5},{5,4},{6,7},{7,6},{8,9},{9,8},{10,11... | collective-permute-start | bytes 393224 | tf_op jit(solution)/shard_map/ppermute | solution.py:378
  32.0 5.0 %collective-permute-start.5 = (f32[32,1024]{1,0:T(8,128)S(1)}, f32[32,1024]{1,0:T(8,128)S(1)}, u32[]{:S(2)}, u32[]{:S(2)}) collective-permute-start(f32[32,1024]{1,0:T(8,128)S(1)} %get-tuple-element.67.z_refs_1_), channel_id=1, source_target_pairs={{0,1},{1,0},{2,3},{3,2},{4,5},{5,4},{6,7},{7,6},{8,9},{9,8},{10,11... | collective-permute-start | bytes 393224 | tf_op jit(solution)/shard_map/ppermute | solution.py:378
  38.5 6.5 %collective-permute-start.6 = (bf16[4,64,128]{2,1,0:T(8,128)(2,1)S(1)}, bf16[4,64,128]{2,1,0:T(8,128)(2,1)S(1)}, u32[]{:S(2)}, u32[]{:S(2)}) collective-permute-start(bf16[4,64,128]{2,1,0:T(8,128)(2,1)S(1)} %get-tuple-element.71), channel_id=1, source_target_pairs={{2,4},{6,8},{10,12},{14,16},{18,20},{22,24},{26,28},{4,2},{8,6},{1... | collective-permute-start | bytes 196616 | tf_op jit(solution)/shard_map/ppermute | solution.py:369
  41.5 3.5 %collective-permute-start.7 = (bf16[4,64,128]{2,1,0:T(8,128)(2,1)S(1)}, bf16[4,64,128]{2,1,0:T(8,128)(2,1)S(1)}, u32[]{:S(2)}, u32[]{:S(2)}) collective-permute-start(bf16[4,64,128]{2,1,0:T(8,128)(2,1)S(1)} %get-tuple-element.72), channel_id=1, source_target_pairs={{0,2},{4,6},{8,10},{12,14},{16,18},{20,22},{24,26},{28,30},{2,0},{... | collective-permute-start | bytes 196616 | tf_op jit(solution)/shard_map/ppermute | solution.py:369
  46.4 5.0 %collective-permute-start.10 = (bf16[8,64,128]{2,1,0:T(8,128)(2,1)S(1)}, bf16[8,64,128]{2,1,0:T(8,128)(2,1)S(1)}, u32[]{:S(2)}, u32[]{:S(2)}) collective-permute-start(bf16[8,64,128]{2,1,0:T(8,128)(2,1)S(1)} %get-tuple-element.75.mine_ref), channel_id=1, source_target_pairs={{0,1},{1,0},{2,3},{3,2},{4,5},{5,4},{6,7},{7,6},{8,9},{9,8},{10,11... | collective-permute-start | bytes 393224 | tf_op jit(solution)/shard_map/ppermute | solution.py:378
  47.8 6.5 %collective-permute-start.8 = (bf16[4,64,128]{2,1,0:T(8,128)(2,1)S(1)}, bf16[4,64,128]{2,1,0:T(8,128)(2,1)S(1)}, u32[]{:S(2)}, u32[]{:S(2)}) collective-permute-start(bf16[4,64,128]{2,1,0:T(8,128)(2,1)S(1)} %get-tuple-element.74), channel_id=1, source_target_pairs={{2,4},{6,8},{10,12},{14,16},{18,20},{22,24},{26,28},{4,2},{8,6},{1... | collective-permute-start | bytes 196616 | tf_op jit(solution)/shard_map/ppermute | solution.py:369
  52.0 11.8 %collective-permute-start.12 = (f32[8,32,128]{2,1,0:T(8,128)S(1)}, f32[8,32,128]{2,1,0:T(8,128)S(1)}, u32[]{:S(2)}, u32[]{:S(2)}) collective-permute-start(f32[8,32,128]{2,1,0:T(8,128)S(1)} %get-tuple-element.81), channel_id=1, source_target_pairs={{0,1},{1,0},{2,3},{3,2},{4,5},{5,4},{6,7},{7,6},{8,9},{9,8},{10,11... | collective-permute-start | bytes 393224 | tf_op jit(solution)/shard_map/ppermute | solution.py:378
  54.3 4.3 %collective-permute-start.9 = (bf16[4,64,128]{2,1,0:T(8,128)(2,1)S(1)}, bf16[4,64,128]{2,1,0:T(8,128)(2,1)S(1)}, u32[]{:S(2)}, u32[]{:S(2)}) collective-permute-start(bf16[4,64,128]{2,1,0:T(8,128)(2,1)S(1)} %collective-permute-done.8.first_refs_0_), channel_id=1, source_target_pairs={{0,1},{1,0},{2,3},{3,2},{4,5},{5,4},{6,7},{7,6},{8,9},{9,8},{10,11... | collective-permute-start | bytes 196616 | tf_op jit(solution)/shard_map/ppermute | solution.py:378
  54.9 3.6 %collective-permute-start.11 = (bf16[4,64,128]{2,1,0:T(8,128)(2,1)S(1)}, bf16[4,64,128]{2,1,0:T(8,128)(2,1)S(1)}, u32[]{:S(2)}, u32[]{:S(2)}) collective-permute-start(bf16[4,64,128]{2,1,0:T(8,128)(2,1)S(1)} %get-tuple-element.79), channel_id=1, source_target_pairs={{0,2},{4,6},{8,10},{12,14},{16,18},{20,22},{24,26},{28,30},{2,0},{... | collective-permute-start | bytes 196616 | tf_op jit(solution)/shard_map/ppermute | solution.py:369
  60.6 6.5 %collective-permute-start.13 = (bf16[4,64,128]{2,1,0:T(8,128)(2,1)S(1)}, bf16[4,64,128]{2,1,0:T(8,128)(2,1)S(1)}, u32[]{:S(2)}, u32[]{:S(2)}) collective-permute-start(bf16[4,64,128]{2,1,0:T(8,128)(2,1)S(1)} %get-tuple-element.83), channel_id=1, source_target_pairs={{2,4},{6,8},{10,12},{14,16},{18,20},{22,24},{26,28},{4,2},{8,6},{1... | collective-permute-start | bytes 196616 | tf_op jit(solution)/shard_map/ppermute | solution.py:369
  63.7 3.3 %collective-permute-start.14 = (bf16[4,64,128]{2,1,0:T(8,128)(2,1)S(1)}, bf16[4,64,128]{2,1,0:T(8,128)(2,1)S(1)}, u32[]{:S(2)}, u32[]{:S(2)}) collective-permute-start(bf16[4,64,128]{2,1,0:T(8,128)(2,1)S(1)} %get-tuple-element.84), channel_id=1, source_target_pairs={{0,2},{4,6},{8,10},{12,14},{16,18},{20,22},{24,26},{28,30},{2,0},{... | collective-permute-start | bytes 196616 | tf_op jit(solution)/shard_map/ppermute | solution.py:369
  68.4 4.3 %collective-permute-start.15 = (bf16[32,1024]{1,0:T(8,128)(2,1)S(1)}, bf16[32,1024]{1,0:T(8,128)(2,1)S(1)}, u32[]{:S(2)}, u32[]{:S(2)}) collective-permute-start(bf16[32,1024]{1,0:T(8,128)(2,1)S(1)} %get-tuple-element.88), channel_id=1, source_target_pairs={{0,1},{1,0},{2,3},{3,2},{4,5},{5,4},{6,7},{7,6},{8,9},{9,8},{10,11... | collective-permute-start | bytes 196616 | tf_op jit(solution)/shard_map/ppermute | solution.py:378

commit v14 on v12

--- a/solution.py
+++ b/solution.py
@@ -334,34 +334,34 @@
         state = jnp.concatenate(parts, axis=0) + update
         kept_ref[i] = state[:snaps]
         for j, given_ref in enumerate(given_refs, 1):
-            given_ref[i] = state[j * snaps : (j + 1) * snaps]
+            given_ref[i] = update[j * snaps : (j + 1) * snaps]
         message_ref[i] = state.astype(BF16)
     pick(message_ref, ties_ref, 1 - parity(), first_ref, me * held)
 
 
 def last_update_kernel(
-    part_ref, grad_ref, back_first_ref, back_second_ref, ties_ref, gain_ref, kept_ref, mine_ref, sent_refs, work_ref
+    part_ref, grad_ref, back_first_ref, back_second_ref, ties_ref, gain_ref, kept_ref, given_refs,
+    mine_ref, sent_refs, work_ref,
 ):
     snaps = mine_ref.shape[0]
     operands = part_ref, grad_ref, back_first_ref, back_second_ref, ties_ref, gain_ref, work_ref
     for i, update in updates(*operands):
         columns = slice(i * BLK, (i + 1) * BLK)
         mine_ref[:, columns] = kept_ref[i] + update[:snaps]
-        for j, sent_ref in enumerate(sent_refs, 1):
-            sent_ref[:, columns] = update[j * snaps : (j + 1) * snaps].astype(BF16)
-
-
-def finish_kernel(mine_ref, states_refs, updates_refs, out_ref):
+        for j, (given_ref, sent_ref) in enumerate(zip(given_refs, sent_refs), 1):
+            total = given_ref[i] + update[j * snaps : (j + 1) * snaps]
+            sent_ref[:, columns] = total.astype(BF16)
+
+
+def finish_kernel(mine_ref, x_ref, updates_refs, out_ref):
     width = mine_ref.shape[1]
-    members = len(states_refs) + 1
+    members = len(updates_refs) + 1
     me = lax.axis_index("snap")
     out_ref[:, pl.ds(pl.multiple_of(me * width, BLK), width)] = mine_ref[...]
-    for i, (state_ref, update_ref) in enumerate(zip(states_refs, updates_refs), 1):
+    for i, update_ref in enumerate(updates_refs, 1):
         at = lax.rem(me + i, members) * width
-        for b in range(width // BLK):
-            update = update_ref[:, b * BLK : (b + 1) * BLK].astype(F32)
-            columns = pl.ds(pl.multiple_of(at + b * BLK, BLK), BLK)
-            out_ref[:, columns] = state_ref[b] + update
+        columns = pl.ds(pl.multiple_of(at, BLK), width)
+        out_ref[:, columns] = x_ref[:, columns] + update_ref[...].astype(F32)
 
 
 def swap_pair(block, start):
@@ -571,25 +571,23 @@
         ],
         name="predict_pull",
     )
-    given, first, second = lax.optimization_barrier((given, first, second))
     first, second = with_neighbours(first, second)
-    states_in = [from_snap(block, -i) for i, block in enumerate(given, 1)]
     mine, sent = call(
         last_update_kernel,
         (
             shape((snaps, held * BLK), F32),
             [shape((snaps, held * BLK), BF16)] * (members - 1),
         ),
-        [VMEM, VMEM, VMEM, VMEM, SMEM, VMEM, VMEM],
-        (partial_update(grad), grad, first, second, ties_table, reciprocal_normal_operator, kept),
+        [VMEM, VMEM, VMEM, VMEM, SMEM, VMEM, VMEM, [VMEM] * (members - 1)],
+        (partial_update(grad), grad, first, second, ties_table, reciprocal_normal_operator, kept, given),
         scratch=[work],
         name="last_update",
     )
     return call(
         finish_kernel,
         shape((snaps, states), F32),
-        [VMEM, [VMEM] * (members - 1), [VMEM] * (members - 1)],
-        (mine, states_in, [from_snap(block, -i) for i, block in enumerate(sent, 1)]),
+        [VMEM, VMEM, [VMEM] * (members - 1)],
+        (mine, starting_voltages, [from_snap(block, -i) for i, block in enumerate(sent, 1)]),
         name="finish",
     )
 

time: 74.1 us -> 74.1 us (level)
    ppermute x8 -> x7, starting transfers between devices: 8.6 us -> 7.9 us  [from_snap(): lax.ppermute(block, 'snap', [(i, (i + distance) % members) for i in range...]
    ppermute x8 -> x7, waiting for transfers between devices: 11.8 us -> 11.8 us  [from_snap(): lax.ppermute(block, 'snap', [(i, (i + distance) % members) for i in range...]
  transfers between devices with their start and end apart: 17 -> 16, of which waited for: 9 -> 9; matrix products, arithmetic and copies ran while one was open for 0% -> 0% of each run, Pallas kernels for 15% -> 13%
where the time goes in v14:
time: 74.1 us; the launch traced here: 73.5 us
  starting transfers between devices  25.5 us (34%)
  waiting for transfers between devices  24.1 us (33%)
  Pallas kernels  20.7 us (28%)
  local copies, waits for them, and re-layouts  3.03 us (4%)
    pallas_call x14, Pallas kernels, call(): pl.pallas_call(kernel, out_shape=outs, in_specs=ins, out_specs=jax.tree.m...  20.7 us
    ppermute x8, waiting for transfers between devices, swap_pair(): return lax.ppermute(block, 'area', pairs + [(b, a) for a, b in pairs])  12.2 us
    ppermute x7, waiting for transfers between devices, from_snap(): lax.ppermute(block, 'snap', [(i, (i + distance) % members) for i in range...  11.8 us
    ppermute x8, starting transfers between devices, swap_pair(): return lax.ppermute(block, 'area', pairs + [(b, a) for a, b in pairs])  11.4 us
    ppermute x7, starting transfers between devices, from_snap(): lax.ppermute(block, 'snap', [(i, (i + distance) % members) for i in range...  7.9 us
    all_to_all x1, starting transfers between devices, on_device(): lax.all_to_all(message, 'area', split_axis=0, concat_axis=0, tiled=True)  6.17 us
    unnamed x14, local copies, waits for them, and re-layouts  3.03 us
  transfers between devices with their start and end apart: 16, of which 9 were waited for; matrix products, arithmetic and copies ran while one was open for 0% of the time, Pallas kernels for 13%

profile of v14, /device:TPU:16, one launch (start us, length us, event | category | flops | bytes accessed | tf_op | source)
XLA Modules:
  0.0 73.5 jit_solution(1148910897057036119)
XLA Ops:
  0.0 4.4 %pack_readings.1 = (f32[16,72,128]{2,1,0:T(8,128)}, bf16[16,32,128]{2,1,0:T(8,128)(2,1)}, f32[32,1024]{1,0:T(8,128)}) custom-call(f32[32,2048]{1,0:T(8,128)} %z_in.1, f32[16,128]{1,0:T(8,128)} %bitcast.17, s32[16,256]{1,0:T(8,128)} %bitcast.16, f32[32,2048]{1,0:T(8,128)} %x_ref.3), custom_call_target="tpu_custom_call" | custom-call | tf_op jit(solution)/shard_map/pack_readings/pallas_call | solution.py:21
  4.4 6.2 %all-to-all-start = ((f32[16,72,128]{2,1,0:T(8,128)}), f32[16,72,128]{2,1,0:T(8,128)S(1)}, u32[]{:S(2)}, u32[]{:S(2)}) async-start(f32[16,72,128]{2,1,0:T(8,128)} %get-tuple-element.43), calls=%async_computation | async-start | bytes 1179648 | tf_op jit(solution)/shard_map/all_to_all | solution.py:452
  10.6 1.5 %collective-permute-start = (bf16[16,32,128]{2,1,0:T(8,128)(2,1)}, bf16[16,32,128]{2,1,0:T(8,128)(2,1)S(1)}, u32[]{:S(2)}, u32[]{:S(2)}) collective-permute-start(bf16[16,32,128]{2,1,0:T(8,128)(2,1)} %get-tuple-element.44.handed_refs_0_), channel_id=1, source_target_pairs={{0,1},{1,0},{2,3},{3,2},{4,5},{5,4},{6,7},{7,6},{8,9},{9,8},{10,11... | collective-permute-start | bytes 393224 | tf_op jit(solution)/shard_map/ppermute | solution.py:378
  12.1 0.9 %copy-done.3 = bf16[16,32,128]{2,1,0:T(8,128)(2,1)S(1)} copy-done((bf16[16,32,128]{2,1,0:T(8,128)(2,1)S(1)}, bf16[16,32,128]{2,1,0:T(8,128)(2,1)}, u32[]{:S(2)}) %copy-start.3) | copy-done | bytes 131096
  13.1 0.7 copy-done.4
  13.8 0.7 copy-done.5
  14.5 0.7 copy-done.6
  15.1 0.4 invert_order.1
  15.6 0.8 %collective-permute-done.own_refs_1_ = bf16[16,32,128]{2,1,0:T(8,128)(2,1)S(1)} collective-permute-done((bf16[16,32,128]{2,1,0:T(8,128)(2,1)}, bf16[16,32,128]{2,1,0:T(8,128)(2,1)S(1)}, u32[]{:S(2)}, u32[]{:S(2)}) %collective-permute-start) | collective-permute-done | bytes 131104 | tf_op jit(solution)/shard_map/ppermute | solution.py:378
  16.4 0.6 pick_boundary.1
  17.0 2.3 %collective-permute-start.1 = (bf16[4,64,128]{2,1,0:T(8,128)(2,1)S(1)}, bf16[4,64,128]{2,1,0:T(8,128)(2,1)S(1)}, u32[]{:S(2)}, u32[]{:S(2)}) collective-permute-start(bf16[4,64,128]{2,1,0:T(8,128)(2,1)S(1)} %get-tuple-element.50), channel_id=1, source_target_pairs={{2,4},{6,8},{10,12},{14,16},{18,20},{22,24},{26,28},{4,2},{8,6},{1... | collective-permute-start | bytes 196616 | tf_op jit(solution)/shard_map/ppermute | solution.py:369
  19.3 1.3 %collective-permute-start.2 = (bf16[4,64,128]{2,1,0:T(8,128)(2,1)S(1)}, bf16[4,64,128]{2,1,0:T(8,128)(2,1)S(1)}, u32[]{:S(2)}, u32[]{:S(2)}) collective-permute-start(bf16[4,64,128]{2,1,0:T(8,128)(2,1)S(1)} %get-tuple-element.51), channel_id=1, source_target_pairs={{0,2},{4,6},{8,10},{12,14},{16,18},{20,22},{24,26},{28,30},{2,0},{... | collective-permute-start | bytes 196616 | tf_op jit(solution)/shard_map/ppermute | solution.py:369
  20.6 1.5 %collective-permute-start.3 = (f32[32,1024]{1,0:T(8,128)}, f32[32,1024]{1,0:T(8,128)S(1)}, u32[]{:S(2)}, u32[]{:S(2)}) collective-permute-start(f32[32,1024]{1,0:T(8,128)} %get-tuple-element.61), channel_id=1, source_target_pairs={{0,1},{1,0},{2,3},{3,2},{4,5},{5,4},{6,7},{7,6},{8,9},{9,8},{10,11... | collective-permute-start | bytes 393224 | tf_op jit(solution)/shard_map/ppermute | solution.py:378
  22.1 4.5 %collective-permute-done.1.first_ref = bf16[4,64,128]{2,1,0:T(8,128)(2,1)S(1)} collective-permute-done((bf16[4,64,128]{2,1,0:T(8,128)(2,1)S(1)}, bf16[4,64,128]{2,1,0:T(8,128)(2,1)S(1)}, u32[]{:S(2)}, u32[]{:S(2)}) %collective-permute-start.1) | collective-permute-done | bytes 65568 | tf_op jit(solution)/shard_map/ppermute | solution.py:369
  26.6 0.0 collective-permute-done.2.second_ref
  26.6 1.4 %predict.1.guess_ref = f32[64,2048]{1,0:T(8,128)S(1)} custom-call(bf16[4,64,128]{2,1,0:T(8,128)(2,1)S(1)} %collective-permute-done.1.first_ref, bf16[4,64,128]{2,1,0:T(8,128)(2,1)S(1)} %collective-permute-done.2.second_ref, bf16[16,32,128]{2,1,0:T(8,128)(2,1)S(1)} %get-tuple-element.45.own_refs_0_, ...), custom_call_target="tpu_custom_call" | custom-call | flops 1000000000 | tf_op jit(solution)/shard_map/predict/pallas_call | solution.py:21
  28.0 0.0 all-to-all-done.message_ref
  28.0 1.2 %unpack_readings.3 = (f32[32,1024]{1,0:T(8,128)S(1)}, f32[1,1024]{1,0:T(1,128)S(1)}) custom-call(s32[16,128]{1,0:T(8,128)S(1)} %get-tuple-element.54.group_ref, s32[16,128]{1,0:T(8,128)S(1)} %get-tuple-element.55.lane_ref, f32[16,72,128]{2,1,0:T(8,128)S(1)} %all-to-all-done.message_ref), custom_call_target="tpu_custom_call" | custom-call | flops 2000000000 | tf_op jit(solution)/shard_map/unpack_readings/pallas_call | solution.py:21
  29.2 0.0 copy-start
  29.2 1.2 %unpack_readings.2 = (f32[32,1024]{1,0:T(8,128)S(1)}, f32[1,1024]{1,0:T(1,128)S(1)}) custom-call(s32[16,128]{1,0:T(8,128)S(1)} %get-tuple-element.54.group_ref, s32[16,128]{1,0:T(8,128)S(1)} %get-tuple-element.55.lane_ref, f32[16,72,128]{2,1,0:T(8,128)S(1)} %all-to-all-done.message_ref), custom_call_target="tpu_custom_call" | custom-call | flops 2000000000 | tf_op jit(solution)/shard_map/unpack_readings/pallas_call | solution.py:21
  30.4 0.0 copy-start.2
  30.5 1.6 %collective-permute-start.4 = (f32[32,1024]{1,0:T(8,128)S(1)}, f32[32,1024]{1,0:T(8,128)S(1)}, u32[]{:S(2)}, u32[]{:S(2)}) collective-permute-start(f32[32,1024]{1,0:T(8,128)S(1)} %get-tuple-element.62.z_refs_0_), channel_id=1, source_target_pairs={{0,1},{1,0},{2,3},{3,2},{4,5},{5,4},{6,7},{7,6},{8,9},{9,8},{10,11... | collective-permute-start | bytes 393224 | tf_op jit(solution)/shard_map/ppermute | solution.py:378
  32.0 0.5 collective-permute-start.5
  32.6 2.9 %collective-permute-done.4 = f32[32,1024]{1,0:T(8,128)S(1)} collective-permute-done((f32[32,1024]{1,0:T(8,128)S(1)}, f32[32,1024]{1,0:T(8,128)S(1)}, u32[]{:S(2)}, u32[]{:S(2)}) %collective-permute-start.4) | collective-permute-done | bytes 131104 | tf_op jit(solution)/shard_map/ppermute | solution.py:378
  35.5 1.5 %collective-permute-done.5 = f32[32,1024]{1,0:T(8,128)S(1)} collective-permute-done((f32[32,1024]{1,0:T(8,128)S(1)}, f32[32,1024]{1,0:T(8,128)S(1)}, u32[]{:S(2)}, u32[]{:S(2)}) %collective-permute-start.5) | collective-permute-done | bytes 131104 | tf_op jit(solution)/shard_map/ppermute | solution.py:378
  37.0 1.4 %pull.1 = (f32[16,64,128]{2,1,0:T(8,128)S(1)}, bf16[4,64,128]{2,1,0:T(8,128)(2,1)S(1)}, bf16[4,64,128]{2,1,0:T(8,128)(2,1)S(1)}) custom-call(f32[64,2048]{1,0:T(8,128)S(1)} %predict.1.guess_ref, f32[32,1024]{1,0:T(8,128)S(1)} %get-tuple-element.62.z_refs_0_, f32[32,1024]{1,0:T(8,128)S(1)} %get-tuple-element.63.z_refs_1_, f32[1,32,1024]{2,1,0:T(8,128)S(1)} %bitcast.9, ...), custom_call_target="tpu_custom_call" | custom-call | tf_op jit(solution)/shard_map/pull/pallas_call | solution.py:21
  38.5 3.0 %collective-permute-start.6 = (bf16[4,64,128]{2,1,0:T(8,128)(2,1)S(1)}, bf16[4,64,128]{2,1,0:T(8,128)(2,1)S(1)}, u32[]{:S(2)}, u32[]{:S(2)}) collective-permute-start(bf16[4,64,128]{2,1,0:T(8,128)(2,1)S(1)} %get-tuple-element.67), channel_id=1, source_target_pairs={{2,4},{6,8},{10,12},{14,16},{18,20},{22,24},{26,28},{4,2},{8,6},{1... | collective-permute-start | bytes 196616 | tf_op jit(solution)/shard_map/ppermute | solution.py:369
  41.5 0.1 collective-permute-start.7
  41.6 1.9 %partial_update.2.part_ref = f32[64,1024]{1,0:T(8,128)S(1)} custom-call(f32[16,64,128]{2,1,0:T(8,128)S(1)} %get-tuple-element.66.grad_ref, s32[2,4]{1,0:T(2,128)S(1)} %get-tuple-element.46.ties_ref, bf16[1024,2048]{1,0:T(8,128)(2,1)S(1)} %copy-done), custom_call_target="tpu_custom_call" | custom-call | flops 1000000000 | tf_op jit(solution)/shard_map/partial_update/pallas_call | solution.py:21
  43.5 1.5 %collective-permute-done.6.back_first_ref = bf16[4,64,128]{2,1,0:T(8,128)(2,1)S(1)} collective-permute-done((bf16[4,64,128]{2,1,0:T(8,128)(2,1)S(1)}, bf16[4,64,128]{2,1,0:T(8,128)(2,1)S(1)}, u32[]{:S(2)}, u32[]{:S(2)}) %collective-permute-start.6) | collective-permute-done | bytes 65568 | tf_op jit(solution)/shard_map/ppermute | solution.py:369
  44.9 0.0 collective-permute-done.7.back_second_ref
  45.0 1.4 %first_update.1 = (f32[8,32,128]{2,1,0:T(8,128)S(1)}, f32[8,32,128]{2,1,0:T(8,128)S(1)}, bf16[8,64,128]{2,1,0:T(8,128)(2,1)S(1)}, bf16[4,64,128]{2,1,0:T(8,128)(2,1)S(1)}) custom-call(f32[64,1024]{1,0:T(8,128)S(1)} %partial_update.2.part_ref, f32[16,64,128]{2,1,0:T(8,128)S(1)} %get-tuple-element.66.grad_ref, ...), custom_call_target="tpu_custom_call" | custom-call | tf_op jit(solution)/shard_map/first_update/pallas_call | solution.py:21
  46.4 1.5 %collective-permute-start.10 = (bf16[8,64,128]{2,1,0:T(8,128)(2,1)S(1)}, bf16[8,64,128]{2,1,0:T(8,128)(2,1)S(1)}, u32[]{:S(2)}, u32[]{:S(2)}) collective-permute-start(bf16[8,64,128]{2,1,0:T(8,128)(2,1)S(1)} %get-tuple-element.71.mine_ref), channel_id=1, source_target_pairs={{0,1},{1,0},{2,3},{3,2},{4,5},{5,4},{6,7},{7,6},{8,9},{9,8},{10,11... | collective-permute-start | bytes 393224 | tf_op jit(solution)/shard_map/ppermute | solution.py:378
  47.9 2.8 %collective-permute-start.8 = (bf16[4,64,128]{2,1,0:T(8,128)(2,1)S(1)}, bf16[4,64,128]{2,1,0:T(8,128)(2,1)S(1)}, u32[]{:S(2)}, u32[]{:S(2)}) collective-permute-start(bf16[4,64,128]{2,1,0:T(8,128)(2,1)S(1)} %get-tuple-element.70), channel_id=1, source_target_pairs={{2,4},{6,8},{10,12},{14,16},{18,20},{22,24},{26,28},{4,2},{8,6},{1... | collective-permute-start | bytes 196616 | tf_op jit(solution)/shard_map/ppermute | solution.py:369
  50.6 3.7 %collective-permute-done.8.first_refs_0_ = bf16[4,64,128]{2,1,0:T(8,128)(2,1)S(1)} collective-permute-done((bf16[4,64,128]{2,1,0:T(8,128)(2,1)S(1)}, bf16[4,64,128]{2,1,0:T(8,128)(2,1)S(1)}, u32[]{:S(2)}, u32[]{:S(2)}) %collective-permute-start.8) | collective-permute-done | bytes 65568 | tf_op jit(solution)/shard_map/ppermute | solution.py:369
  54.3 0.6 collective-permute-start.9
  54.9 0.6 join_states.1
  55.6 0.1 collective-permute-start.11
  55.6 3.0 %collective-permute-done.9.first_refs_1_ = bf16[4,64,128]{2,1,0:T(8,128)(2,1)S(1)} collective-permute-done((bf16[4,64,128]{2,1,0:T(8,128)(2,1)S(1)}, bf16[4,64,128]{2,1,0:T(8,128)(2,1)S(1)}, u32[]{:S(2)}, u32[]{:S(2)}) %collective-permute-start.9) | collective-permute-done | bytes 65568 | tf_op jit(solution)/shard_map/ppermute | solution.py:378
  58.6 2.0 %predict_pull.1 = (f32[16,64,128]{2,1,0:T(8,128)S(1)}, bf16[4,64,128]{2,1,0:T(8,128)(2,1)S(1)}, bf16[4,64,128]{2,1,0:T(8,128)(2,1)S(1)}) custom-call(bf16[4,64,128]{2,1,0:T(8,128)(2,1)S(1)} %collective-permute-done.8.first_refs_0_, bf16[4,64,128]{2,1,0:T(8,128)(2,1)S(1)} %collective-permute-done.9.first_refs_1_, ...), custom_call_target="tpu_custom_call" | custom-call | tf_op jit(solution)/shard_map/predict_pull/pallas_call | solution.py:21
  60.6 1.9 %collective-permute-start.12 = (bf16[4,64,128]{2,1,0:T(8,128)(2,1)S(1)}, bf16[4,64,128]{2,1,0:T(8,128)(2,1)S(1)}, u32[]{:S(2)}, u32[]{:S(2)}) collective-permute-start(bf16[4,64,128]{2,1,0:T(8,128)(2,1)S(1)} %get-tuple-element.75), channel_id=1, source_target_pairs={{2,4},{6,8},{10,12},{14,16},{18,20},{22,24},{26,28},{4,2},{8,6},{1... | collective-permute-start | bytes 196616 | tf_op jit(solution)/shard_map/ppermute | solution.py:369
  62.5 0.1 collective-permute-start.13
  62.6 1.9 %partial_update.3.part_ref = f32[64,1024]{1,0:T(8,128)S(1)} custom-call(f32[16,64,128]{2,1,0:T(8,128)S(1)} %get-tuple-element.74.grad_ref, s32[2,4]{1,0:T(2,128)S(1)} %get-tuple-element.46.ties_ref, bf16[1024,2048]{1,0:T(8,128)(2,1)S(1)} %copy-done), custom_call_target="tpu_custom_call" | custom-call | flops 1000000000 | tf_op jit(solution)/shard_map/partial_update/pallas_call | solution.py:21
  64.5 2.5 %collective-permute-done.12.back_first_ref = bf16[4,64,128]{2,1,0:T(8,128)(2,1)S(1)} collective-permute-done((bf16[4,64,128]{2,1,0:T(8,128)(2,1)S(1)}, bf16[4,64,128]{2,1,0:T(8,128)(2,1)S(1)}, u32[]{:S(2)}, u32[]{:S(2)}) %collective-permute-start.12) | collective-permute-done | bytes 65568 | tf_op jit(solution)/shard_map/ppermute | solution.py:369
  67.1 1.4 %last_update.1 = (f32[32,1024]{1,0:T(8,128)S(1)}, bf16[32,1024]{1,0:T(8,128)(2,1)S(1)}) custom-call(f32[64,1024]{1,0:T(8,128)S(1)} %partial_update.3.part_ref, f32[16,64,128]{2,1,0:T(8,128)S(1)} %get-tuple-element.74.grad_ref, bf16[4,64,128]{2,1,0:T(8,128)(2,1)S(1)} %collective-permute-done.12.back_first_ref, ...), custom_call_target="tpu_custom_call" | custom-call | tf_op jit(solution)/shard_map/last_update/pallas_call | solution.py:21
  68.4 0.7 collective-permute-start.14
  69.1 3.6 %collective-permute-done.14.updates_refs_0_ = bf16[32,1024]{1,0:T(8,128)(2,1)S(1)} collective-permute-done((bf16[32,1024]{1,0:T(8,128)(2,1)S(1)}, bf16[32,1024]{1,0:T(8,128)(2,1)S(1)}, u32[]{:S(2)}, u32[]{:S(2)}) %collective-permute-start.14) | collective-permute-done | bytes 65568 | tf_op jit(solution)/shard_map/ppermute | solution.py:378
  72.8 0.7 finish.1
  (12 shorter events, 0.0 us)
Async XLA Ops:
  0.0 26.6 %copy-start.1 = (bf16[16,4,128,128]{3,2,1,0:T(8,128)(2,1)S(1)}, bf16[16,4,128,128]{3,2,1,0:T(8,128)(2,1)}, u32[]{:S(2)}) copy-start(bf16[16,4,128,128]{3,2,1,0:T(8,128)(2,1)} %tiles_ref.5) | copy-start | bytes 6291460
  4.4 23.6 %all-to-all-start = ((f32[16,72,128]{2,1,0:T(8,128)}), f32[16,72,128]{2,1,0:T(8,128)S(1)}, u32[]{:S(2)}, u32[]{:S(2)}) async-start(f32[16,72,128]{2,1,0:T(8,128)} %get-tuple-element.43), calls=%async_computation | async-start | bytes 1179648 | tf_op jit(solution)/shard_map/all_to_all | solution.py:452
  10.6 5.8 %collective-permute-start = (bf16[16,32,128]{2,1,0:T(8,128)(2,1)}, bf16[16,32,128]{2,1,0:T(8,128)(2,1)S(1)}, u32[]{:S(2)}, u32[]{:S(2)}) collective-permute-start(bf16[16,32,128]{2,1,0:T(8,128)(2,1)} %get-tuple-element.44.handed_refs_0_), channel_id=1, source_target_pairs={{0,1},{1,0},{2,3},{3,2},{4,5},{5,4},{6,7},{7,6},{8,9},{9,8},{10,11... | collective-permute-start | bytes 393224 | tf_op jit(solution)/shard_map/ppermute | solution.py:378
  12.1 0.9 %copy-start.3 = (bf16[16,32,128]{2,1,0:T(8,128)(2,1)S(1)}, bf16[16,32,128]{2,1,0:T(8,128)(2,1)}, u32[]{:S(2)}) copy-start(bf16[16,32,128]{2,1,0:T(8,128)(2,1)} %get-tuple-element.44.handed_refs_0_) | copy-start | bytes 393220
  13.1 0.7 copy-start.4
  13.8 0.7 copy-start.5
  14.5 0.7 copy-start.6
  17.0 9.6 %collective-permute-start.1 = (bf16[4,64,128]{2,1,0:T(8,128)(2,1)S(1)}, bf16[4,64,128]{2,1,0:T(8,128)(2,1)S(1)}, u32[]{:S(2)}, u32[]{:S(2)}) collective-permute-start(bf16[4,64,128]{2,1,0:T(8,128)(2,1)S(1)} %get-tuple-element.50), channel_id=1, source_target_pairs={{2,4},{6,8},{10,12},{14,16},{18,20},{22,24},{26,28},{4,2},{8,6},{1... | collective-permute-start | bytes 196616 | tf_op jit(solution)/shard_map/ppermute | solution.py:369
  19.3 7.3 %collective-permute-start.2 = (bf16[4,64,128]{2,1,0:T(8,128)(2,1)S(1)}, bf16[4,64,128]{2,1,0:T(8,128)(2,1)S(1)}, u32[]{:S(2)}, u32[]{:S(2)}) collective-permute-start(bf16[4,64,128]{2,1,0:T(8,128)(2,1)S(1)} %get-tuple-element.51), channel_id=1, source_target_pairs={{0,2},{4,6},{8,10},{12,14},{16,18},{20,22},{24,26},{28,30},{2,0},{... | collective-permute-start | bytes 196616 | tf_op jit(solution)/shard_map/ppermute | solution.py:369
  20.6 9.9 %collective-permute-start.3 = (f32[32,1024]{1,0:T(8,128)}, f32[32,1024]{1,0:T(8,128)S(1)}, u32[]{:S(2)}, u32[]{:S(2)}) collective-permute-start(f32[32,1024]{1,0:T(8,128)} %get-tuple-element.61), channel_id=1, source_target_pairs={{0,1},{1,0},{2,3},{3,2},{4,5},{5,4},{6,7},{7,6},{8,9},{9,8},{10,11... | collective-permute-start | bytes 393224 | tf_op jit(solution)/shard_map/ppermute | solution.py:378
  29.2 12.3 %copy-start = (bf16[1024,2048]{1,0:T(8,128)(2,1)S(1)}, bf16[1024,2048]{1,0:T(8,128)(2,1)}, u32[]{:S(2)}) copy-start(bf16[1024,2048]{1,0:T(8,128)(2,1)} %gain_ref.7) | copy-start | bytes 12582916
  30.4 14.5 %copy-start.2 = (f32[32,2048]{1,0:T(8,128)S(1)}, f32[32,2048]{1,0:T(8,128)}, u32[]{:S(2)}) copy-start(f32[32,2048]{1,0:T(8,128)} %x_ref.3) | copy-start | bytes 786436
  30.5 5.0 %collective-permute-start.4 = (f32[32,1024]{1,0:T(8,128)S(1)}, f32[32,1024]{1,0:T(8,128)S(1)}, u32[]{:S(2)}, u32[]{:S(2)}) collective-permute-start(f32[32,1024]{1,0:T(8,128)S(1)} %get-tuple-element.62.z_refs_0_), channel_id=1, source_target_pairs={{0,1},{1,0},{2,3},{3,2},{4,5},{5,4},{6,7},{7,6},{8,9},{9,8},{10,11... | collective-permute-start | bytes 393224 | tf_op jit(solution)/shard_map/ppermute | solution.py:378
  32.0 5.0 %collective-permute-start.5 = (f32[32,1024]{1,0:T(8,128)S(1)}, f32[32,1024]{1,0:T(8,128)S(1)}, u32[]{:S(2)}, u32[]{:S(2)}) collective-permute-start(f32[32,1024]{1,0:T(8,128)S(1)} %get-tuple-element.63.z_refs_1_), channel_id=1, source_target_pairs={{0,1},{1,0},{2,3},{3,2},{4,5},{5,4},{6,7},{7,6},{8,9},{9,8},{10,11... | collective-permute-start | bytes 393224 | tf_op jit(solution)/shard_map/ppermute | solution.py:378
  38.5 6.5 %collective-permute-start.6 = (bf16[4,64,128]{2,1,0:T(8,128)(2,1)S(1)}, bf16[4,64,128]{2,1,0:T(8,128)(2,1)S(1)}, u32[]{:S(2)}, u32[]{:S(2)}) collective-permute-start(bf16[4,64,128]{2,1,0:T(8,128)(2,1)S(1)} %get-tuple-element.67), channel_id=1, source_target_pairs={{2,4},{6,8},{10,12},{14,16},{18,20},{22,24},{26,28},{4,2},{8,6},{1... | collective-permute-start | bytes 196616 | tf_op jit(solution)/shard_map/ppermute | solution.py:369
  41.5 3.5 %collective-permute-start.7 = (bf16[4,64,128]{2,1,0:T(8,128)(2,1)S(1)}, bf16[4,64,128]{2,1,0:T(8,128)(2,1)S(1)}, u32[]{:S(2)}, u32[]{:S(2)}) collective-permute-start(bf16[4,64,128]{2,1,0:T(8,128)(2,1)S(1)} %get-tuple-element.68), channel_id=1, source_target_pairs={{0,2},{4,6},{8,10},{12,14},{16,18},{20,22},{24,26},{28,30},{2,0},{... | collective-permute-start | bytes 196616 | tf_op jit(solution)/shard_map/ppermute | solution.py:369
  46.4 8.6 %collective-permute-start.10 = (bf16[8,64,128]{2,1,0:T(8,128)(2,1)S(1)}, bf16[8,64,128]{2,1,0:T(8,128)(2,1)S(1)}, u32[]{:S(2)}, u32[]{:S(2)}) collective-permute-start(bf16[8,64,128]{2,1,0:T(8,128)(2,1)S(1)} %get-tuple-element.71.mine_ref), channel_id=1, source_target_pairs={{0,1},{1,0},{2,3},{3,2},{4,5},{5,4},{6,7},{7,6},{8,9},{9,8},{10,11... | collective-permute-start | bytes 393224 | tf_op jit(solution)/shard_map/ppermute | solution.py:378
  47.9 6.5 %collective-permute-start.8 = (bf16[4,64,128]{2,1,0:T(8,128)(2,1)S(1)}, bf16[4,64,128]{2,1,0:T(8,128)(2,1)S(1)}, u32[]{:S(2)}, u32[]{:S(2)}) collective-permute-start(bf16[4,64,128]{2,1,0:T(8,128)(2,1)S(1)} %get-tuple-element.70), channel_id=1, source_target_pairs={{2,4},{6,8},{10,12},{14,16},{18,20},{22,24},{26,28},{4,2},{8,6},{1... | collective-permute-start | bytes 196616 | tf_op jit(solution)/shard_map/ppermute | solution.py:369
  54.3 4.3 %collective-permute-start.9 = (bf16[4,64,128]{2,1,0:T(8,128)(2,1)S(1)}, bf16[4,64,128]{2,1,0:T(8,128)(2,1)S(1)}, u32[]{:S(2)}, u32[]{:S(2)}) collective-permute-start(bf16[4,64,128]{2,1,0:T(8,128)(2,1)S(1)} %collective-permute-done.8.first_refs_0_), channel_id=1, source_target_pairs={{0,1},{1,0},{2,3},{3,2},{4,5},{5,4},{6,7},{7,6},{8,9},{9,8},{10,11... | collective-permute-start | bytes 196616 | tf_op jit(solution)/shard_map/ppermute | solution.py:378
  55.6 3.0 %collective-permute-start.11 = (bf16[4,64,128]{2,1,0:T(8,128)(2,1)S(1)}, bf16[4,64,128]{2,1,0:T(8,128)(2,1)S(1)}, u32[]{:S(2)}, u32[]{:S(2)}) collective-permute-start(bf16[4,64,128]{2,1,0:T(8,128)(2,1)S(1)} %get-tuple-element.73), channel_id=1, source_target_pairs={{0,2},{4,6},{8,10},{12,14},{16,18},{20,22},{24,26},{28,30},{2,0},{... | collective-permute-start | bytes 196616 | tf_op jit(solution)/shard_map/ppermute | solution.py:369
  60.6 6.5 %collective-permute-start.12 = (bf16[4,64,128]{2,1,0:T(8,128)(2,1)S(1)}, bf16[4,64,128]{2,1,0:T(8,128)(2,1)S(1)}, u32[]{:S(2)}, u32[]{:S(2)}) collective-permute-start(bf16[4,64,128]{2,1,0:T(8,128)(2,1)S(1)} %get-tuple-element.75), channel_id=1, source_target_pairs={{2,4},{6,8},{10,12},{14,16},{18,20},{22,24},{26,28},{4,2},{8,6},{1... | collective-permute-start | bytes 196616 | tf_op jit(solution)/shard_map/ppermute | solution.py:369
  62.5 4.6 %collective-permute-start.13 = (bf16[4,64,128]{2,1,0:T(8,128)(2,1)S(1)}, bf16[4,64,128]{2,1,0:T(8,128)(2,1)S(1)}, u32[]{:S(2)}, u32[]{:S(2)}) collective-permute-start(bf16[4,64,128]{2,1,0:T(8,128)(2,1)S(1)} %get-tuple-element.76), channel_id=1, source_target_pairs={{0,2},{4,6},{8,10},{12,14},{16,18},{20,22},{24,26},{28,30},{2,0},{... | collective-permute-start | bytes 196616 | tf_op jit(solution)/shard_map/ppermute | solution.py:369
  68.4 4.3 %collective-permute-start.14 = (bf16[32,1024]{1,0:T(8,128)(2,1)S(1)}, bf16[32,1024]{1,0:T(8,128)(2,1)S(1)}, u32[]{:S(2)}, u32[]{:S(2)}) collective-permute-start(bf16[32,1024]{1,0:T(8,128)(2,1)S(1)} %get-tuple-element.80), channel_id=1, source_target_pairs={{0,1},{1,0},{2,3},{3,2},{4,5},{5,4},{6,7},{7,6},{8,9},{9,8},{10,11... | collective-permute-start | bytes 196616 | tf_op jit(solution)/shard_map/ppermute | solution.py:378

commit v15 on v12

--- a/solution.py
+++ b/solution.py
@@ -221,9 +221,12 @@
 
 
 def weigh(j, guess, z_refs, others_refs, v_refs):
-    each = z_refs[0].shape[1] // BLK
-    z_ref, others_ref, v_ref = z_refs[j // each], others_refs[j // each], v_refs[j // each]
-    columns = slice(j % each * BLK, (j % each + 1) * BLK)
+    part = 0
+    while j >= z_refs[part].shape[1] // BLK:
+        j -= z_refs[part].shape[1] // BLK
+        part += 1
+    z_ref, others_ref, v_ref = z_refs[part], others_refs[part], v_refs[part]
+    columns = slice(j * BLK, (j + 1) * BLK)
     readings = [z_ref[:, columns]] + [o[:, columns] for o in split(others_ref)]
     resid = jnp.concatenate(readings, axis=0) - guess
     spread = jnp.sum(resid * resid, axis=0, keepdims=True) / resid.shape[0]
@@ -487,23 +490,29 @@
         name="predict",
     )
     message, guess = lax.optimization_barrier((message, guess))
-    halves = []
-    for part in range(2):
-        halves.append(
-            call(
-                functools.partial(unpack_kernel, part * (lines // BLK // 2)),
-                (shape((snaps, lines // 2), F32), shape((1, lines // 2), F32)),
-                [VMEM, VMEM, VMEM],
-                (group, lane, message),
-                scratch=[pltpu.VMEM((chunks * (width // BLK), BLK), F32)],
-                flops=2 * 10**9,
-                name="unpack_readings",
-            )
+    blocks = lines // BLK
+    cuts = (0, blocks // 4, blocks * 11 // 16, blocks)
+    readings, variance, reading_others = [], [], []
+    for part, (start, stop) in enumerate(zip(cuts, cuts[1:])):
+        if part == 2:
+            message, reading_others[0] = lax.optimization_barrier((message, reading_others[0]))
+        some = call(
+            functools.partial(unpack_kernel, start),
+            (
+                shape((snaps, (stop - start) * BLK), F32),
+                shape((1, (stop - start) * BLK), F32),
+            ),
+            [VMEM, VMEM, VMEM],
+            (group, lane, message),
+            scratch=[pltpu.VMEM((chunks * (width // BLK), BLK), F32)],
+            flops=2 * 10**9,
+            name="unpack_readings",
         )
-    halves, x_others = lax.optimization_barrier((halves, x_others))
-    readings = [half[0] for half in halves]
-    variance = [half[1] for half in halves]
-    reading_others = [from_all(half) for half in readings]
+        if part == 1:
+            some, x_others = lax.optimization_barrier((some, x_others))
+        readings.append(some[0])
+        variance.append(some[1])
+        reading_others.append(from_all(some[0]))
     grads = (
         shape((own, everything, BLK), F32),
         boundary,
@@ -525,7 +534,7 @@
     grad, first, second = call(
         pull_kernel,
         grads,
-        [VMEM, [VMEM] * 2, [VMEM] * 2, [VMEM] * 2, VMEM, SMEM],
+        [VMEM, [VMEM] * 3, [VMEM] * 3, [VMEM] * 3, VMEM, SMEM],
         (guess, readings, reading_others, variance, derivative_pieces, place),
         scratch=[total, pltpu.VMEM((everything, lines), BF16)],
         name="pull",
@@ -561,7 +570,7 @@
     grad, first, second = call(
         predict_pull_kernel,
         grads,
-        [[VMEM] * members, VMEM, VMEM, [VMEM] * 2, [VMEM] * 2, [VMEM] * 2, VMEM, SMEM],
+        [[VMEM] * members, VMEM, VMEM, [VMEM] * 3, [VMEM] * 3, [VMEM] * 3, VMEM, SMEM],
         (firsts, aug, second, readings, reading_others, variance, derivative_pieces, place),
         scratch=[
             pltpu.VMEM((slots, everything, BLK), BF16),

time: 74.1 us -> 75.7 us (1.022)
  waiting for transfers between devices: 23.4 us -> 25.6 us
    ppermute x8, waiting for transfers between devices: 11.6 us -> 13.6 us  [swap_pair(): return lax.ppermute(block, 'area', pairs + [(b, a) for a, b in pairs])]
    ppermute x8, starting transfers between devices: 11.4 us -> 9.52 us  [swap_pair(): return lax.ppermute(block, 'area', pairs + [(b, a) for a, b in pairs])]
    ppermute x8 -> x9, starting transfers between devices: 8.6 us -> 10 us  [from_snap(): lax.ppermute(block, 'snap', [(i, (i + distance) % members) for i in range...]
    ppermute x8 -> x9, waiting for transfers between devices: 11.8 us -> 12 us  [from_snap(): lax.ppermute(block, 'snap', [(i, (i + distance) % members) for i in range...]
    pallas_call x14 -> x15, Pallas kernels: 20.7 us -> 20.9 us  [call(): pl.pallas_call(kernel, out_shape=outs, in_specs=ins, out_specs=jax.tree.m...]
  transfers between devices with their start and end apart: 17 -> 18, of which waited for: 9 -> 10; matrix products, arithmetic and copies ran while one was open for 0% -> 0% of each run, Pallas kernels for 15% -> 14%
where the time goes in v15:
time: 75.7 us; the launch traced here: 75.3 us
  starting transfers between devices  25.7 us (34%)
  waiting for transfers between devices  25.6 us (34%)
  Pallas kernels  20.9 us (28%)
  local copies, waits for them, and re-layouts  3.03 us (4%)
    pallas_call x15, Pallas kernels, call(): pl.pallas_call(kernel, out_shape=outs, in_specs=ins, out_specs=jax.tree.m...  20.9 us
    ppermute x8, waiting for transfers between devices, swap_pair(): return lax.ppermute(block, 'area', pairs + [(b, a) for a, b in pairs])  13.6 us
    ppermute x9, waiting for transfers between devices, from_snap(): lax.ppermute(block, 'snap', [(i, (i + distance) % members) for i in range...  12 us
    ppermute x9, starting transfers between devices, from_snap(): lax.ppermute(block, 'snap', [(i, (i + distance) % members) for i in range...  10 us
    ppermute x8, starting transfers between devices, swap_pair(): return lax.ppermute(block, 'area', pairs + [(b, a) for a, b in pairs])  9.52 us
    all_to_all x1, starting transfers between devices, on_device(): lax.all_to_all(message, 'area', split_axis=0, concat_axis=0, tiled=True)  6.17 us
    unnamed x14, local copies, waits for them, and re-layouts  3.03 us
  transfers between devices with their start and end apart: 18, of which 10 were waited for; matrix products, arithmetic and copies ran while one was open for 0% of the time, Pallas kernels for 14%

profile of v15, /device:TPU:16, one launch (start us, length us, event | category | flops | bytes accessed | tf_op | source)
XLA Modules:
  0.0 75.3 jit_solution(17849688449337469543)
XLA Ops:
  0.0 4.4 %pack_readings.1 = (f32[16,72,128]{2,1,0:T(8,128)}, bf16[16,32,128]{2,1,0:T(8,128)(2,1)}, f32[32,1024]{1,0:T(8,128)}) custom-call(f32[32,2048]{1,0:T(8,128)} %z_in.1, f32[16,128]{1,0:T(8,128)} %bitcast.20, s32[16,256]{1,0:T(8,128)} %bitcast.19, f32[32,2048]{1,0:T(8,128)} %x_ref.1), custom_call_target="tpu_custom_call" | custom-call | tf_op jit(solution)/shard_map/pack_readings/pallas_call | solution.py:21
  4.4 6.2 %all-to-all-start = ((f32[16,72,128]{2,1,0:T(8,128)}), f32[16,72,128]{2,1,0:T(8,128)S(1)}, u32[]{:S(2)}, u32[]{:S(2)}) async-start(f32[16,72,128]{2,1,0:T(8,128)} %get-tuple-element.48), calls=%async_computation | async-start | bytes 1179648 | tf_op jit(solution)/shard_map/all_to_all | solution.py:455
  10.6 1.5 %collective-permute-start = (bf16[16,32,128]{2,1,0:T(8,128)(2,1)}, bf16[16,32,128]{2,1,0:T(8,128)(2,1)S(1)}, u32[]{:S(2)}, u32[]{:S(2)}) collective-permute-start(bf16[16,32,128]{2,1,0:T(8,128)(2,1)} %get-tuple-element.49.handed_refs_0_), channel_id=1, source_target_pairs={{0,1},{1,0},{2,3},{3,2},{4,5},{5,4},{6,7},{7,6},{8,9},{9,8},{10,11... | collective-permute-start | bytes 393224 | tf_op jit(solution)/shard_map/ppermute | solution.py:381
  12.1 0.9 %copy-done.3 = bf16[16,32,128]{2,1,0:T(8,128)(2,1)S(1)} copy-done((bf16[16,32,128]{2,1,0:T(8,128)(2,1)S(1)}, bf16[16,32,128]{2,1,0:T(8,128)(2,1)}, u32[]{:S(2)}) %copy-start.3) | copy-done | bytes 131096
  13.1 0.7 copy-done.4
  13.8 0.7 copy-done.5
  14.5 0.7 copy-done.6
  15.1 0.5 invert_order.1
  15.6 0.8 %collective-permute-done.own_refs_1_ = bf16[16,32,128]{2,1,0:T(8,128)(2,1)S(1)} collective-permute-done((bf16[16,32,128]{2,1,0:T(8,128)(2,1)}, bf16[16,32,128]{2,1,0:T(8,128)(2,1)S(1)}, u32[]{:S(2)}, u32[]{:S(2)}) %collective-permute-start) | collective-permute-done | bytes 131104 | tf_op jit(solution)/shard_map/ppermute | solution.py:381
  16.4 0.6 pick_boundary.1
  17.0 2.3 %collective-permute-start.1 = (bf16[4,64,128]{2,1,0:T(8,128)(2,1)S(1)}, bf16[4,64,128]{2,1,0:T(8,128)(2,1)S(1)}, u32[]{:S(2)}, u32[]{:S(2)}) collective-permute-start(bf16[4,64,128]{2,1,0:T(8,128)(2,1)S(1)} %get-tuple-element.55), channel_id=1, source_target_pairs={{2,4},{6,8},{10,12},{14,16},{18,20},{22,24},{26,28},{4,2},{8,6},{1... | collective-permute-start | bytes 196616 | tf_op jit(solution)/shard_map/ppermute | solution.py:372
  19.3 1.3 %collective-permute-start.2 = (bf16[4,64,128]{2,1,0:T(8,128)(2,1)S(1)}, bf16[4,64,128]{2,1,0:T(8,128)(2,1)S(1)}, u32[]{:S(2)}, u32[]{:S(2)}) collective-permute-start(bf16[4,64,128]{2,1,0:T(8,128)(2,1)S(1)} %get-tuple-element.56), channel_id=1, source_target_pairs={{0,2},{4,6},{8,10},{12,14},{16,18},{20,22},{24,26},{28,30},{2,0},{... | collective-permute-start | bytes 196616 | tf_op jit(solution)/shard_map/ppermute | solution.py:372
  20.6 1.5 %collective-permute-start.3 = (f32[32,1024]{1,0:T(8,128)}, f32[32,1024]{1,0:T(8,128)S(1)}, u32[]{:S(2)}, u32[]{:S(2)}) collective-permute-start(f32[32,1024]{1,0:T(8,128)} %get-tuple-element.65), channel_id=1, source_target_pairs={{0,1},{1,0},{2,3},{3,2},{4,5},{5,4},{6,7},{7,6},{8,9},{9,8},{10,11... | collective-permute-start | bytes 393224 | tf_op jit(solution)/shard_map/ppermute | solution.py:381
  22.1 4.5 %collective-permute-done.1.first_ref = bf16[4,64,128]{2,1,0:T(8,128)(2,1)S(1)} collective-permute-done((bf16[4,64,128]{2,1,0:T(8,128)(2,1)S(1)}, bf16[4,64,128]{2,1,0:T(8,128)(2,1)S(1)}, u32[]{:S(2)}, u32[]{:S(2)}) %collective-permute-start.1) | collective-permute-done | bytes 65568 | tf_op jit(solution)/shard_map/ppermute | solution.py:372
  26.6 1.4 %predict.1.guess_ref = f32[64,2048]{1,0:T(8,128)S(1)} custom-call(bf16[4,64,128]{2,1,0:T(8,128)(2,1)S(1)} %collective-permute-done.1.first_ref, bf16[4,64,128]{2,1,0:T(8,128)(2,1)S(1)} %collective-permute-done.2.second_ref, bf16[16,32,128]{2,1,0:T(8,128)(2,1)S(1)} %get-tuple-element.50.own_refs_0_, ...), custom_call_target="tpu_custom_call" | custom-call | flops 1000000000 | tf_op jit(solution)/shard_map/predict/pallas_call | solution.py:21
  28.0 0.6 unpack_readings.3
  28.7 1.6 %collective-permute-start.4 = (f32[32,512]{1,0:T(8,128)S(1)}, f32[32,512]{1,0:T(8,128)S(1)}, u32[]{:S(2)}, u32[]{:S(2)}) collective-permute-start(f32[32,512]{1,0:T(8,128)S(1)} %get-tuple-element.62.z_refs_0_), channel_id=1, source_target_pairs={{0,1},{1,0},{2,3},{3,2},{4,5},{5,4},{6,7},{7,6},{8,9},{9,8},{10,11... | collective-permute-start | bytes 196616 | tf_op jit(solution)/shard_map/ppermute | solution.py:381
  30.3 1.1 %unpack_readings.4 = (f32[32,896]{1,0:T(8,128)S(1)}, f32[1,896]{1,0:T(1,128)S(1)}) custom-call(s32[16,128]{1,0:T(8,128)S(1)} %get-tuple-element.59.group_ref, s32[16,128]{1,0:T(8,128)S(1)} %get-tuple-element.60.lane_ref, f32[16,72,128]{2,1,0:T(8,128)S(1)} %all-to-all-done.message_ref), custom_call_target="tpu_custom_call" | custom-call | flops 2000000000 | tf_op jit(solution)/shard_map/unpack_readings/pallas_call | solution.py:21
  31.3 0.6 collective-permute-start.5
  31.9 1.5 %collective-permute-done.4 = f32[32,512]{1,0:T(8,128)S(1)} collective-permute-done((f32[32,512]{1,0:T(8,128)S(1)}, f32[32,512]{1,0:T(8,128)S(1)}, u32[]{:S(2)}, u32[]{:S(2)}) %collective-permute-start.4) | collective-permute-done | bytes 65568 | tf_op jit(solution)/shard_map/ppermute | solution.py:381
  33.4 0.8 %unpack_readings.5 = (f32[32,640]{1,0:T(8,128)S(1)}, f32[1,640]{1,0:T(1,128)S(1)}) custom-call(s32[16,128]{1,0:T(8,128)S(1)} %get-tuple-element.59.group_ref, s32[16,128]{1,0:T(8,128)S(1)} %get-tuple-element.60.lane_ref, f32[16,72,128]{2,1,0:T(8,128)S(1)} %all-to-all-done.message_ref), custom_call_target="tpu_custom_call" | custom-call | flops 2000000000 | tf_op jit(solution)/shard_map/unpack_readings/pallas_call | solution.py:21
  34.2 0.0 copy-start.2
  34.2 1.6 %collective-permute-start.6 = (f32[32,640]{1,0:T(8,128)S(1)}, f32[32,640]{1,0:T(8,128)S(1)}, u32[]{:S(2)}, u32[]{:S(2)}) collective-permute-start(f32[32,640]{1,0:T(8,128)S(1)} %get-tuple-element.68.z_refs_2_), channel_id=1, source_target_pairs={{0,1},{1,0},{2,3},{3,2},{4,5},{5,4},{6,7},{7,6},{8,9},{9,8},{10,11... | collective-permute-start | bytes 245768 | tf_op jit(solution)/shard_map/ppermute | solution.py:381
  35.8 0.4 collective-permute-done.5
  36.2 2.5 %collective-permute-done.6 = f32[32,640]{1,0:T(8,128)S(1)} collective-permute-done((f32[32,640]{1,0:T(8,128)S(1)}, f32[32,640]{1,0:T(8,128)S(1)}, u32[]{:S(2)}, u32[]{:S(2)}) %collective-permute-start.6) | collective-permute-done | bytes 81952 | tf_op jit(solution)/shard_map/ppermute | solution.py:381
  38.7 1.4 %pull.1 = (f32[16,64,128]{2,1,0:T(8,128)S(1)}, bf16[4,64,128]{2,1,0:T(8,128)(2,1)S(1)}, bf16[4,64,128]{2,1,0:T(8,128)(2,1)S(1)}) custom-call(f32[64,2048]{1,0:T(8,128)S(1)} %predict.1.guess_ref, f32[32,512]{1,0:T(8,128)S(1)} %get-tuple-element.62.z_refs_0_, f32[32,896]{1,0:T(8,128)S(1)} %get-tuple-element.66.z_refs_1_, ...), custom_call_target="tpu_custom_call" | custom-call | tf_op jit(solution)/shard_map/pull/pallas_call | solution.py:21
  40.2 1.9 %collective-permute-start.7 = (bf16[4,64,128]{2,1,0:T(8,128)(2,1)S(1)}, bf16[4,64,128]{2,1,0:T(8,128)(2,1)S(1)}, u32[]{:S(2)}, u32[]{:S(2)}) collective-permute-start(bf16[4,64,128]{2,1,0:T(8,128)(2,1)S(1)} %get-tuple-element.74), channel_id=1, source_target_pairs={{2,4},{6,8},{10,12},{14,16},{18,20},{22,24},{26,28},{4,2},{8,6},{1... | collective-permute-start | bytes 196616 | tf_op jit(solution)/shard_map/ppermute | solution.py:372
  42.1 0.1 collective-permute-start.8
  42.2 1.9 %partial_update.2.part_ref = f32[64,1024]{1,0:T(8,128)S(1)} custom-call(f32[16,64,128]{2,1,0:T(8,128)S(1)} %get-tuple-element.73.grad_ref, s32[2,4]{1,0:T(2,128)S(1)} %get-tuple-element.51.ties_ref, bf16[1024,2048]{1,0:T(8,128)(2,1)S(1)} %copy-done), custom_call_target="tpu_custom_call" | custom-call | flops 1000000000 | tf_op jit(solution)/shard_map/partial_update/pallas_call | solution.py:21
  44.1 2.5 %collective-permute-done.7.back_first_ref = bf16[4,64,128]{2,1,0:T(8,128)(2,1)S(1)} collective-permute-done((bf16[4,64,128]{2,1,0:T(8,128)(2,1)S(1)}, bf16[4,64,128]{2,1,0:T(8,128)(2,1)S(1)}, u32[]{:S(2)}, u32[]{:S(2)}) %collective-permute-start.7) | collective-permute-done | bytes 65568 | tf_op jit(solution)/shard_map/ppermute | solution.py:372
  46.7 1.4 %first_update.1 = (f32[8,32,128]{2,1,0:T(8,128)S(1)}, f32[8,32,128]{2,1,0:T(8,128)S(1)}, bf16[8,64,128]{2,1,0:T(8,128)(2,1)S(1)}, bf16[4,64,128]{2,1,0:T(8,128)(2,1)S(1)}) custom-call(f32[64,1024]{1,0:T(8,128)S(1)} %partial_update.2.part_ref, f32[16,64,128]{2,1,0:T(8,128)S(1)} %get-tuple-element.73.grad_ref, ...), custom_call_target="tpu_custom_call" | custom-call | tf_op jit(solution)/shard_map/first_update/pallas_call | solution.py:21
  48.1 1.6 %collective-permute-start.11 = (bf16[8,64,128]{2,1,0:T(8,128)(2,1)S(1)}, bf16[8,64,128]{2,1,0:T(8,128)(2,1)S(1)}, u32[]{:S(2)}, u32[]{:S(2)}) collective-permute-start(bf16[8,64,128]{2,1,0:T(8,128)(2,1)S(1)} %get-tuple-element.78.mine_ref), channel_id=1, source_target_pairs={{0,1},{1,0},{2,3},{3,2},{4,5},{5,4},{6,7},{7,6},{8,9},{9,8},{10,11... | collective-permute-start | bytes 393224 | tf_op jit(solution)/shard_map/ppermute | solution.py:381
  49.7 1.9 %collective-permute-start.9 = (bf16[4,64,128]{2,1,0:T(8,128)(2,1)S(1)}, bf16[4,64,128]{2,1,0:T(8,128)(2,1)S(1)}, u32[]{:S(2)}, u32[]{:S(2)}) collective-permute-start(bf16[4,64,128]{2,1,0:T(8,128)(2,1)S(1)} %get-tuple-element.77), channel_id=1, source_target_pairs={{2,4},{6,8},{10,12},{14,16},{18,20},{22,24},{26,28},{4,2},{8,6},{1... | collective-permute-start | bytes 196616 | tf_op jit(solution)/shard_map/ppermute | solution.py:372
  51.6 4.6 %collective-permute-done.9.first_refs_0_ = bf16[4,64,128]{2,1,0:T(8,128)(2,1)S(1)} collective-permute-done((bf16[4,64,128]{2,1,0:T(8,128)(2,1)S(1)}, bf16[4,64,128]{2,1,0:T(8,128)(2,1)S(1)}, u32[]{:S(2)}, u32[]{:S(2)}) %collective-permute-start.9) | collective-permute-done | bytes 65568 | tf_op jit(solution)/shard_map/ppermute | solution.py:372
  56.1 0.5 collective-permute-start.10
  56.7 0.6 join_states.1
  57.3 0.1 collective-permute-start.12
  57.3 3.1 %collective-permute-done.10.first_refs_1_ = bf16[4,64,128]{2,1,0:T(8,128)(2,1)S(1)} collective-permute-done((bf16[4,64,128]{2,1,0:T(8,128)(2,1)S(1)}, bf16[4,64,128]{2,1,0:T(8,128)(2,1)S(1)}, u32[]{:S(2)}, u32[]{:S(2)}) %collective-permute-start.10) | collective-permute-done | bytes 65568 | tf_op jit(solution)/shard_map/ppermute | solution.py:381
  60.4 2.0 %predict_pull.1 = (f32[16,64,128]{2,1,0:T(8,128)S(1)}, bf16[4,64,128]{2,1,0:T(8,128)(2,1)S(1)}, bf16[4,64,128]{2,1,0:T(8,128)(2,1)S(1)}) custom-call(bf16[4,64,128]{2,1,0:T(8,128)(2,1)S(1)} %collective-permute-done.9.first_refs_0_, bf16[4,64,128]{2,1,0:T(8,128)(2,1)S(1)} %collective-permute-done.10.first_refs_1_, ...), custom_call_target="tpu_custom_call" | custom-call | tf_op jit(solution)/shard_map/predict_pull/pallas_call | solution.py:21
  62.4 1.9 %collective-permute-start.13 = (bf16[4,64,128]{2,1,0:T(8,128)(2,1)S(1)}, bf16[4,64,128]{2,1,0:T(8,128)(2,1)S(1)}, u32[]{:S(2)}, u32[]{:S(2)}) collective-permute-start(bf16[4,64,128]{2,1,0:T(8,128)(2,1)S(1)} %get-tuple-element.85), channel_id=1, source_target_pairs={{2,4},{6,8},{10,12},{14,16},{18,20},{22,24},{26,28},{4,2},{8,6},{1... | collective-permute-start | bytes 196616 | tf_op jit(solution)/shard_map/ppermute | solution.py:372
  64.3 0.1 collective-permute-start.14
  64.4 0.6 collective-permute-start.15
  65.0 1.9 %partial_update.3.part_ref = f32[64,1024]{1,0:T(8,128)S(1)} custom-call(f32[16,64,128]{2,1,0:T(8,128)S(1)} %get-tuple-element.81.grad_ref, s32[2,4]{1,0:T(2,128)S(1)} %get-tuple-element.51.ties_ref, bf16[1024,2048]{1,0:T(8,128)(2,1)S(1)} %copy-done), custom_call_target="tpu_custom_call" | custom-call | flops 1000000000 | tf_op jit(solution)/shard_map/partial_update/pallas_call | solution.py:21
  66.9 2.0 %collective-permute-done.13.back_first_ref = bf16[4,64,128]{2,1,0:T(8,128)(2,1)S(1)} collective-permute-done((bf16[4,64,128]{2,1,0:T(8,128)(2,1)S(1)}, bf16[4,64,128]{2,1,0:T(8,128)(2,1)S(1)}, u32[]{:S(2)}, u32[]{:S(2)}) %collective-permute-start.13) | collective-permute-done | bytes 65568 | tf_op jit(solution)/shard_map/ppermute | solution.py:372
  68.9 1.4 %last_update.1 = (f32[32,1024]{1,0:T(8,128)S(1)}, bf16[32,1024]{1,0:T(8,128)(2,1)S(1)}) custom-call(f32[64,1024]{1,0:T(8,128)S(1)} %partial_update.3.part_ref, f32[16,64,128]{2,1,0:T(8,128)S(1)} %get-tuple-element.81.grad_ref, bf16[4,64,128]{2,1,0:T(8,128)(2,1)S(1)} %collective-permute-done.13.back_first_ref, ...), custom_call_target="tpu_custom_call" | custom-call | tf_op jit(solution)/shard_map/last_update/pallas_call | solution.py:21
  70.3 0.6 collective-permute-start.16
  70.9 3.7 %collective-permute-done.16.updates_refs_0_ = bf16[32,1024]{1,0:T(8,128)(2,1)S(1)} collective-permute-done((bf16[32,1024]{1,0:T(8,128)(2,1)S(1)}, bf16[32,1024]{1,0:T(8,128)(2,1)S(1)}, u32[]{:S(2)}, u32[]{:S(2)}) %collective-permute-start.16) | collective-permute-done | bytes 65568 | tf_op jit(solution)/shard_map/ppermute | solution.py:381
  74.6 0.7 finish.1
  (17 shorter events, 0.0 us)
Async XLA Ops:
  0.0 26.6 %copy-start.1 = (bf16[16,4,128,128]{3,2,1,0:T(8,128)(2,1)S(1)}, bf16[16,4,128,128]{3,2,1,0:T(8,128)(2,1)}, u32[]{:S(2)}) copy-start(bf16[16,4,128,128]{3,2,1,0:T(8,128)(2,1)} %tiles_ref.5) | copy-start | bytes 6291460
  4.4 23.6 %all-to-all-start = ((f32[16,72,128]{2,1,0:T(8,128)}), f32[16,72,128]{2,1,0:T(8,128)S(1)}, u32[]{:S(2)}, u32[]{:S(2)}) async-start(f32[16,72,128]{2,1,0:T(8,128)} %get-tuple-element.48), calls=%async_computation | async-start | bytes 1179648 | tf_op jit(solution)/shard_map/all_to_all | solution.py:455
  10.6 5.8 %collective-permute-start = (bf16[16,32,128]{2,1,0:T(8,128)(2,1)}, bf16[16,32,128]{2,1,0:T(8,128)(2,1)S(1)}, u32[]{:S(2)}, u32[]{:S(2)}) collective-permute-start(bf16[16,32,128]{2,1,0:T(8,128)(2,1)} %get-tuple-element.49.handed_refs_0_), channel_id=1, source_target_pairs={{0,1},{1,0},{2,3},{3,2},{4,5},{5,4},{6,7},{7,6},{8,9},{9,8},{10,11... | collective-permute-start | bytes 393224 | tf_op jit(solution)/shard_map/ppermute | solution.py:381
  12.1 0.9 %copy-start.3 = (bf16[16,32,128]{2,1,0:T(8,128)(2,1)S(1)}, bf16[16,32,128]{2,1,0:T(8,128)(2,1)}, u32[]{:S(2)}) copy-start(bf16[16,32,128]{2,1,0:T(8,128)(2,1)} %get-tuple-element.49.handed_refs_0_) | copy-start | bytes 393220
  13.1 0.7 copy-start.4
  13.8 0.7 copy-start.5
  14.5 0.7 copy-start.6
  17.0 9.6 %collective-permute-start.1 = (bf16[4,64,128]{2,1,0:T(8,128)(2,1)S(1)}, bf16[4,64,128]{2,1,0:T(8,128)(2,1)S(1)}, u32[]{:S(2)}, u32[]{:S(2)}) collective-permute-start(bf16[4,64,128]{2,1,0:T(8,128)(2,1)S(1)} %get-tuple-element.55), channel_id=1, source_target_pairs={{2,4},{6,8},{10,12},{14,16},{18,20},{22,24},{26,28},{4,2},{8,6},{1... | collective-permute-start | bytes 196616 | tf_op jit(solution)/shard_map/ppermute | solution.py:372
  19.3 7.3 %collective-permute-start.2 = (bf16[4,64,128]{2,1,0:T(8,128)(2,1)S(1)}, bf16[4,64,128]{2,1,0:T(8,128)(2,1)S(1)}, u32[]{:S(2)}, u32[]{:S(2)}) collective-permute-start(bf16[4,64,128]{2,1,0:T(8,128)(2,1)S(1)} %get-tuple-element.56), channel_id=1, source_target_pairs={{0,2},{4,6},{8,10},{12,14},{16,18},{20,22},{24,26},{28,30},{2,0},{... | collective-permute-start | bytes 196616 | tf_op jit(solution)/shard_map/ppermute | solution.py:372
  20.6 10.8 %collective-permute-start.3 = (f32[32,1024]{1,0:T(8,128)}, f32[32,1024]{1,0:T(8,128)S(1)}, u32[]{:S(2)}, u32[]{:S(2)}) collective-permute-start(f32[32,1024]{1,0:T(8,128)} %get-tuple-element.65), channel_id=1, source_target_pairs={{0,1},{1,0},{2,3},{3,2},{4,5},{5,4},{6,7},{7,6},{8,9},{9,8},{10,11... | collective-permute-start | bytes 393224 | tf_op jit(solution)/shard_map/ppermute | solution.py:381
  28.7 4.7 %collective-permute-start.4 = (f32[32,512]{1,0:T(8,128)S(1)}, f32[32,512]{1,0:T(8,128)S(1)}, u32[]{:S(2)}, u32[]{:S(2)}) collective-permute-start(f32[32,512]{1,0:T(8,128)S(1)} %get-tuple-element.62.z_refs_0_), channel_id=1, source_target_pairs={{0,1},{1,0},{2,3},{3,2},{4,5},{5,4},{6,7},{7,6},{8,9},{9,8},{10,11... | collective-permute-start | bytes 196616 | tf_op jit(solution)/shard_map/ppermute | solution.py:381
  31.3 4.9 %collective-permute-start.5 = (f32[32,896]{1,0:T(8,128)S(1)}, f32[32,896]{1,0:T(8,128)S(1)}, u32[]{:S(2)}, u32[]{:S(2)}) collective-permute-start(f32[32,896]{1,0:T(8,128)S(1)} %get-tuple-element.66.z_refs_1_), channel_id=1, source_target_pairs={{0,1},{1,0},{2,3},{3,2},{4,5},{5,4},{6,7},{7,6},{8,9},{9,8},{10,11... | collective-permute-start | bytes 344072 | tf_op jit(solution)/shard_map/ppermute | solution.py:381
  33.4 8.8 %copy-start = (bf16[1024,2048]{1,0:T(8,128)(2,1)S(1)}, bf16[1024,2048]{1,0:T(8,128)(2,1)}, u32[]{:S(2)}) copy-start(bf16[1024,2048]{1,0:T(8,128)(2,1)} %gain_ref.7) | copy-start | bytes 12582916
  34.2 12.5 %copy-start.2 = (f32[32,2048]{1,0:T(8,128)S(1)}, f32[32,2048]{1,0:T(8,128)}, u32[]{:S(2)}) copy-start(f32[32,2048]{1,0:T(8,128)} %x_ref.1) | copy-start | bytes 786436
  34.2 4.5 %collective-permute-start.6 = (f32[32,640]{1,0:T(8,128)S(1)}, f32[32,640]{1,0:T(8,128)S(1)}, u32[]{:S(2)}, u32[]{:S(2)}) collective-permute-start(f32[32,640]{1,0:T(8,128)S(1)} %get-tuple-element.68.z_refs_2_), channel_id=1, source_target_pairs={{0,1},{1,0},{2,3},{3,2},{4,5},{5,4},{6,7},{7,6},{8,9},{9,8},{10,11... | collective-permute-start | bytes 245768 | tf_op jit(solution)/shard_map/ppermute | solution.py:381
  40.2 6.5 %collective-permute-start.7 = (bf16[4,64,128]{2,1,0:T(8,128)(2,1)S(1)}, bf16[4,64,128]{2,1,0:T(8,128)(2,1)S(1)}, u32[]{:S(2)}, u32[]{:S(2)}) collective-permute-start(bf16[4,64,128]{2,1,0:T(8,128)(2,1)S(1)} %get-tuple-element.74), channel_id=1, source_target_pairs={{2,4},{6,8},{10,12},{14,16},{18,20},{22,24},{26,28},{4,2},{8,6},{1... | collective-permute-start | bytes 196616 | tf_op jit(solution)/shard_map/ppermute | solution.py:372
  42.1 4.6 %collective-permute-start.8 = (bf16[4,64,128]{2,1,0:T(8,128)(2,1)S(1)}, bf16[4,64,128]{2,1,0:T(8,128)(2,1)S(1)}, u32[]{:S(2)}, u32[]{:S(2)}) collective-permute-start(bf16[4,64,128]{2,1,0:T(8,128)(2,1)S(1)} %get-tuple-element.75), channel_id=1, source_target_pairs={{0,2},{4,6},{8,10},{12,14},{16,18},{20,22},{24,26},{28,30},{2,0},{... | collective-permute-start | bytes 196616 | tf_op jit(solution)/shard_map/ppermute | solution.py:372
  48.1 8.6 %collective-permute-start.11 = (bf16[8,64,128]{2,1,0:T(8,128)(2,1)S(1)}, bf16[8,64,128]{2,1,0:T(8,128)(2,1)S(1)}, u32[]{:S(2)}, u32[]{:S(2)}) collective-permute-start(bf16[8,64,128]{2,1,0:T(8,128)(2,1)S(1)} %get-tuple-element.78.mine_ref), channel_id=1, source_target_pairs={{0,1},{1,0},{2,3},{3,2},{4,5},{5,4},{6,7},{7,6},{8,9},{9,8},{10,11... | collective-permute-start | bytes 393224 | tf_op jit(solution)/shard_map/ppermute | solution.py:381
  49.7 6.5 %collective-permute-start.9 = (bf16[4,64,128]{2,1,0:T(8,128)(2,1)S(1)}, bf16[4,64,128]{2,1,0:T(8,128)(2,1)S(1)}, u32[]{:S(2)}, u32[]{:S(2)}) collective-permute-start(bf16[4,64,128]{2,1,0:T(8,128)(2,1)S(1)} %get-tuple-element.77), channel_id=1, source_target_pairs={{2,4},{6,8},{10,12},{14,16},{18,20},{22,24},{26,28},{4,2},{8,6},{1... | collective-permute-start | bytes 196616 | tf_op jit(solution)/shard_map/ppermute | solution.py:372
  56.1 4.3 %collective-permute-start.10 = (bf16[4,64,128]{2,1,0:T(8,128)(2,1)S(1)}, bf16[4,64,128]{2,1,0:T(8,128)(2,1)S(1)}, u32[]{:S(2)}, u32[]{:S(2)}) collective-permute-start(bf16[4,64,128]{2,1,0:T(8,128)(2,1)S(1)} %collective-permute-done.9.first_refs_0_), channel_id=1, source_target_pairs={{0,1},{1,0},{2,3},{3,2},{4,5},{5,4},{6,7},{7,6},{8,9},{9,8},{10,11... | collective-permute-start | bytes 196616 | tf_op jit(solution)/shard_map/ppermute | solution.py:381
  57.3 3.1 %collective-permute-start.12 = (bf16[4,64,128]{2,1,0:T(8,128)(2,1)S(1)}, bf16[4,64,128]{2,1,0:T(8,128)(2,1)S(1)}, u32[]{:S(2)}, u32[]{:S(2)}) collective-permute-start(bf16[4,64,128]{2,1,0:T(8,128)(2,1)S(1)} %get-tuple-element.80), channel_id=1, source_target_pairs={{0,2},{4,6},{8,10},{12,14},{16,18},{20,22},{24,26},{28,30},{2,0},{... | collective-permute-start | bytes 196616 | tf_op jit(solution)/shard_map/ppermute | solution.py:372
  62.4 6.5 %collective-permute-start.13 = (bf16[4,64,128]{2,1,0:T(8,128)(2,1)S(1)}, bf16[4,64,128]{2,1,0:T(8,128)(2,1)S(1)}, u32[]{:S(2)}, u32[]{:S(2)}) collective-permute-start(bf16[4,64,128]{2,1,0:T(8,128)(2,1)S(1)} %get-tuple-element.85), channel_id=1, source_target_pairs={{2,4},{6,8},{10,12},{14,16},{18,20},{22,24},{26,28},{4,2},{8,6},{1... | collective-permute-start | bytes 196616 | tf_op jit(solution)/shard_map/ppermute | solution.py:372
  64.3 4.6 %collective-permute-start.14 = (bf16[4,64,128]{2,1,0:T(8,128)(2,1)S(1)}, bf16[4,64,128]{2,1,0:T(8,128)(2,1)S(1)}, u32[]{:S(2)}, u32[]{:S(2)}) collective-permute-start(bf16[4,64,128]{2,1,0:T(8,128)(2,1)S(1)} %get-tuple-element.86), channel_id=1, source_target_pairs={{0,2},{4,6},{8,10},{12,14},{16,18},{20,22},{24,26},{28,30},{2,0},{... | collective-permute-start | bytes 196616 | tf_op jit(solution)/shard_map/ppermute | solution.py:372
  64.4 6.5 %collective-permute-start.15 = (f32[8,32,128]{2,1,0:T(8,128)S(1)}, f32[8,32,128]{2,1,0:T(8,128)S(1)}, u32[]{:S(2)}, u32[]{:S(2)}) collective-permute-start(f32[8,32,128]{2,1,0:T(8,128)S(1)} %get-tuple-element.89), channel_id=1, source_target_pairs={{0,1},{1,0},{2,3},{3,2},{4,5},{5,4},{6,7},{7,6},{8,9},{9,8},{10,11... | collective-permute-start | bytes 393224 | tf_op jit(solution)/shard_map/ppermute | solution.py:381
  70.3 4.3 %collective-permute-start.16 = (bf16[32,1024]{1,0:T(8,128)(2,1)S(1)}, bf16[32,1024]{1,0:T(8,128)(2,1)S(1)}, u32[]{:S(2)}, u32[]{:S(2)}) collective-permute-start(bf16[32,1024]{1,0:T(8,128)(2,1)S(1)} %get-tuple-element.90), channel_id=1, source_target_pairs={{0,1},{1,0},{2,3},{3,2},{4,5},{5,4},{6,7},{7,6},{8,9},{9,8},{10,11... | collective-permute-start | bytes 196616 | tf_op jit(solution)/shard_map/ppermute | solution.py:381

commit v16 on v15

--- a/solution.py
+++ b/solution.py
@@ -491,7 +491,7 @@
     )
     message, guess = lax.optimization_barrier((message, guess))
     blocks = lines // BLK
-    cuts = (0, blocks // 4, blocks * 11 // 16, blocks)
+    cuts = (0, blocks * 3 // 16, blocks * 13 // 16, blocks)
     readings, variance, reading_others = [], [], []
     for part, (start, stop) in enumerate(zip(cuts, cuts[1:])):
         if part == 2:

time: 75.7 us -> 74.9 us (0.989)
  waiting for transfers between devices: 25.6 us -> 24.4 us
    ppermute x9, waiting for transfers between devices: 12 us -> 11.1 us  [from_snap(): lax.ppermute(block, 'snap', [(i, (i + distance) % members) for i in range...]
  transfers between devices with their start and end apart: 18 -> 18, of which waited for: 10 -> 9; matrix products, arithmetic and copies ran while one was open for 0% -> 0% of each run, Pallas kernels for 14% -> 15%
where the time goes in v16:
time: 74.9 us; the launch traced here: 74.5 us
  starting transfers between devices  26 us (35%)
  waiting for transfers between devices  24.4 us (33%)
  Pallas kernels  20.9 us (28%)
  local copies, waits for them, and re-layouts  3.03 us (4%)
    pallas_call x15, Pallas kernels, call(): pl.pallas_call(kernel, out_shape=outs, in_specs=ins, out_specs=jax.tree.m...  20.9 us
    ppermute x8, waiting for transfers between devices, swap_pair(): return lax.ppermute(block, 'area', pairs + [(b, a) for a, b in pairs])  13.2 us
    ppermute x9, waiting for transfers between devices, from_snap(): lax.ppermute(block, 'snap', [(i, (i + distance) % members) for i in range...  11.1 us
    ppermute x9, starting transfers between devices, from_snap(): lax.ppermute(block, 'snap', [(i, (i + distance) % members) for i in range...  10 us
    ppermute x8, starting transfers between devices, swap_pair(): return lax.ppermute(block, 'area', pairs + [(b, a) for a, b in pairs])  9.82 us
    all_to_all x1, starting transfers between devices, on_device(): lax.all_to_all(message, 'area', split_axis=0, concat_axis=0, tiled=True)  6.17 us
    unnamed x14, local copies, waits for them, and re-layouts  3.03 us
  transfers between devices with their start and end apart: 18, of which 9 were waited for; matrix products, arithmetic and copies ran while one was open for 0% of the time, Pallas kernels for 15%

profile of v16, /device:TPU:16, one launch (start us, length us, event | category | flops | bytes accessed | tf_op | source)
XLA Modules:
  0.0 74.5 jit_solution(16988893897503817433)
XLA Ops:
  0.0 4.4 %pack_readings.1 = (f32[16,72,128]{2,1,0:T(8,128)}, bf16[16,32,128]{2,1,0:T(8,128)(2,1)}, f32[32,1024]{1,0:T(8,128)}) custom-call(f32[32,2048]{1,0:T(8,128)} %z_in.1, f32[16,128]{1,0:T(8,128)} %bitcast.20, s32[16,256]{1,0:T(8,128)} %bitcast.19, f32[32,2048]{1,0:T(8,128)} %x_ref.1), custom_call_target="tpu_custom_call" | custom-call | tf_op jit(solution)/shard_map/pack_readings/pallas_call | solution.py:21
  4.4 6.2 %all-to-all-start = ((f32[16,72,128]{2,1,0:T(8,128)}), f32[16,72,128]{2,1,0:T(8,128)S(1)}, u32[]{:S(2)}, u32[]{:S(2)}) async-start(f32[16,72,128]{2,1,0:T(8,128)} %get-tuple-element.48), calls=%async_computation | async-start | bytes 1179648 | tf_op jit(solution)/shard_map/all_to_all | solution.py:455
  10.6 1.5 %collective-permute-start = (bf16[16,32,128]{2,1,0:T(8,128)(2,1)}, bf16[16,32,128]{2,1,0:T(8,128)(2,1)S(1)}, u32[]{:S(2)}, u32[]{:S(2)}) collective-permute-start(bf16[16,32,128]{2,1,0:T(8,128)(2,1)} %get-tuple-element.49.handed_refs_0_), channel_id=1, source_target_pairs={{0,1},{1,0},{2,3},{3,2},{4,5},{5,4},{6,7},{7,6},{8,9},{9,8},{10,11... | collective-permute-start | bytes 393224 | tf_op jit(solution)/shard_map/ppermute | solution.py:381
  12.1 0.9 %copy-done.3 = bf16[16,32,128]{2,1,0:T(8,128)(2,1)S(1)} copy-done((bf16[16,32,128]{2,1,0:T(8,128)(2,1)S(1)}, bf16[16,32,128]{2,1,0:T(8,128)(2,1)}, u32[]{:S(2)}) %copy-start.3) | copy-done | bytes 131096
  13.1 0.7 copy-done.4
  13.8 0.7 copy-done.5
  14.5 0.7 copy-done.6
  15.1 0.5 invert_order.1
  15.6 0.8 %collective-permute-done.own_refs_1_ = bf16[16,32,128]{2,1,0:T(8,128)(2,1)S(1)} collective-permute-done((bf16[16,32,128]{2,1,0:T(8,128)(2,1)}, bf16[16,32,128]{2,1,0:T(8,128)(2,1)S(1)}, u32[]{:S(2)}, u32[]{:S(2)}) %collective-permute-start) | collective-permute-done | bytes 131104 | tf_op jit(solution)/shard_map/ppermute | solution.py:381
  16.4 0.6 pick_boundary.1
  17.0 2.3 %collective-permute-start.1 = (bf16[4,64,128]{2,1,0:T(8,128)(2,1)S(1)}, bf16[4,64,128]{2,1,0:T(8,128)(2,1)S(1)}, u32[]{:S(2)}, u32[]{:S(2)}) collective-permute-start(bf16[4,64,128]{2,1,0:T(8,128)(2,1)S(1)} %get-tuple-element.55), channel_id=1, source_target_pairs={{2,4},{6,8},{10,12},{14,16},{18,20},{22,24},{26,28},{4,2},{8,6},{1... | collective-permute-start | bytes 196616 | tf_op jit(solution)/shard_map/ppermute | solution.py:372
  19.3 1.3 %collective-permute-start.2 = (bf16[4,64,128]{2,1,0:T(8,128)(2,1)S(1)}, bf16[4,64,128]{2,1,0:T(8,128)(2,1)S(1)}, u32[]{:S(2)}, u32[]{:S(2)}) collective-permute-start(bf16[4,64,128]{2,1,0:T(8,128)(2,1)S(1)} %get-tuple-element.56), channel_id=1, source_target_pairs={{0,2},{4,6},{8,10},{12,14},{16,18},{20,22},{24,26},{28,30},{2,0},{... | collective-permute-start | bytes 196616 | tf_op jit(solution)/shard_map/ppermute | solution.py:372
  20.6 1.5 %collective-permute-start.3 = (f32[32,1024]{1,0:T(8,128)}, f32[32,1024]{1,0:T(8,128)S(1)}, u32[]{:S(2)}, u32[]{:S(2)}) collective-permute-start(f32[32,1024]{1,0:T(8,128)} %get-tuple-element.65), channel_id=1, source_target_pairs={{0,1},{1,0},{2,3},{3,2},{4,5},{5,4},{6,7},{7,6},{8,9},{9,8},{10,11... | collective-permute-start | bytes 393224 | tf_op jit(solution)/shard_map/ppermute | solution.py:381
  22.1 4.5 %collective-permute-done.1.first_ref = bf16[4,64,128]{2,1,0:T(8,128)(2,1)S(1)} collective-permute-done((bf16[4,64,128]{2,1,0:T(8,128)(2,1)S(1)}, bf16[4,64,128]{2,1,0:T(8,128)(2,1)S(1)}, u32[]{:S(2)}, u32[]{:S(2)}) %collective-permute-start.1) | collective-permute-done | bytes 65568 | tf_op jit(solution)/shard_map/ppermute | solution.py:372
  26.6 1.4 %predict.1.guess_ref = f32[64,2048]{1,0:T(8,128)S(1)} custom-call(bf16[4,64,128]{2,1,0:T(8,128)(2,1)S(1)} %collective-permute-done.1.first_ref, bf16[4,64,128]{2,1,0:T(8,128)(2,1)S(1)} %collective-permute-done.2.second_ref, bf16[16,32,128]{2,1,0:T(8,128)(2,1)S(1)} %get-tuple-element.50.own_refs_0_, ...), custom_call_target="tpu_custom_call" | custom-call | flops 1000000000 | tf_op jit(solution)/shard_map/predict/pallas_call | solution.py:21
  28.0 0.5 unpack_readings.3
  28.5 1.6 %collective-permute-start.4 = (f32[32,384]{1,0:T(8,128)S(1)}, f32[32,384]{1,0:T(8,128)S(1)}, u32[]{:S(2)}, u32[]{:S(2)}) collective-permute-start(f32[32,384]{1,0:T(8,128)S(1)} %get-tuple-element.62.z_refs_0_), channel_id=1, source_target_pairs={{0,1},{1,0},{2,3},{3,2},{4,5},{5,4},{6,7},{7,6},{8,9},{9,8},{10,11... | collective-permute-start | bytes 147464 | tf_op jit(solution)/shard_map/ppermute | solution.py:381
  30.1 1.5 %unpack_readings.4 = (f32[32,1280]{1,0:T(8,128)S(1)}, f32[1,1280]{1,0:T(1,128)S(1)}) custom-call(s32[16,128]{1,0:T(8,128)S(1)} %get-tuple-element.59.group_ref, s32[16,128]{1,0:T(8,128)S(1)} %get-tuple-element.60.lane_ref, f32[16,72,128]{2,1,0:T(8,128)S(1)} %all-to-all-done.message_ref), custom_call_target="tpu_custom_call" | custom-call | flops 2000000000 | tf_op jit(solution)/shard_map/unpack_readings/pallas_call | solution.py:21
  31.6 0.0 collective-permute-done.3.x_others_refs_0_
  31.6 0.6 collective-permute-start.5
  32.2 1.0 %collective-permute-done.4 = f32[32,384]{1,0:T(8,128)S(1)} collective-permute-done((f32[32,384]{1,0:T(8,128)S(1)}, f32[32,384]{1,0:T(8,128)S(1)}, u32[]{:S(2)}, u32[]{:S(2)}) %collective-permute-start.4) | collective-permute-done | bytes 49184 | tf_op jit(solution)/shard_map/ppermute | solution.py:381
  33.2 0.5 unpack_readings.5
  33.7 0.0 copy-start.2
  33.7 1.6 %collective-permute-start.6 = (f32[32,384]{1,0:T(8,128)S(1)}, f32[32,384]{1,0:T(8,128)S(1)}, u32[]{:S(2)}, u32[]{:S(2)}) collective-permute-start(f32[32,384]{1,0:T(8,128)S(1)} %get-tuple-element.68.z_refs_2_), channel_id=1, source_target_pairs={{0,1},{1,0},{2,3},{3,2},{4,5},{5,4},{6,7},{7,6},{8,9},{9,8},{10,11... | collective-permute-start | bytes 147464 | tf_op jit(solution)/shard_map/ppermute | solution.py:381
  35.3 2.6 %collective-permute-done.6 = f32[32,384]{1,0:T(8,128)S(1)} collective-permute-done((f32[32,384]{1,0:T(8,128)S(1)}, f32[32,384]{1,0:T(8,128)S(1)}, u32[]{:S(2)}, u32[]{:S(2)}) %collective-permute-start.6) | collective-permute-done | bytes 49184 | tf_op jit(solution)/shard_map/ppermute | solution.py:381
  37.9 1.5 %pull.1 = (f32[16,64,128]{2,1,0:T(8,128)S(1)}, bf16[4,64,128]{2,1,0:T(8,128)(2,1)S(1)}, bf16[4,64,128]{2,1,0:T(8,128)(2,1)S(1)}) custom-call(f32[64,2048]{1,0:T(8,128)S(1)} %predict.1.guess_ref, f32[32,384]{1,0:T(8,128)S(1)} %get-tuple-element.62.z_refs_0_, f32[32,1280]{1,0:T(8,128)S(1)} %get-tuple-element.66.z_refs_1_, ...), custom_call_target="tpu_custom_call" | custom-call | tf_op jit(solution)/shard_map/pull/pallas_call | solution.py:21
  39.3 2.2 %collective-permute-start.7 = (bf16[4,64,128]{2,1,0:T(8,128)(2,1)S(1)}, bf16[4,64,128]{2,1,0:T(8,128)(2,1)S(1)}, u32[]{:S(2)}, u32[]{:S(2)}) collective-permute-start(bf16[4,64,128]{2,1,0:T(8,128)(2,1)S(1)} %get-tuple-element.74), channel_id=1, source_target_pairs={{2,4},{6,8},{10,12},{14,16},{18,20},{22,24},{26,28},{4,2},{8,6},{1... | collective-permute-start | bytes 196616 | tf_op jit(solution)/shard_map/ppermute | solution.py:372
  41.6 0.1 collective-permute-start.8
  41.7 1.9 %partial_update.2.part_ref = f32[64,1024]{1,0:T(8,128)S(1)} custom-call(f32[16,64,128]{2,1,0:T(8,128)S(1)} %get-tuple-element.73.grad_ref, s32[2,4]{1,0:T(2,128)S(1)} %get-tuple-element.51.ties_ref, bf16[1024,2048]{1,0:T(8,128)(2,1)S(1)} %copy-done), custom_call_target="tpu_custom_call" | custom-call | flops 1000000000 | tf_op jit(solution)/shard_map/partial_update/pallas_call | solution.py:21
  43.6 2.2 %collective-permute-done.7.back_first_ref = bf16[4,64,128]{2,1,0:T(8,128)(2,1)S(1)} collective-permute-done((bf16[4,64,128]{2,1,0:T(8,128)(2,1)S(1)}, bf16[4,64,128]{2,1,0:T(8,128)(2,1)S(1)}, u32[]{:S(2)}, u32[]{:S(2)}) %collective-permute-start.7) | collective-permute-done | bytes 65568 | tf_op jit(solution)/shard_map/ppermute | solution.py:372
  45.8 1.4 %first_update.1 = (f32[8,32,128]{2,1,0:T(8,128)S(1)}, f32[8,32,128]{2,1,0:T(8,128)S(1)}, bf16[8,64,128]{2,1,0:T(8,128)(2,1)S(1)}, bf16[4,64,128]{2,1,0:T(8,128)(2,1)S(1)}) custom-call(f32[64,1024]{1,0:T(8,128)S(1)} %partial_update.2.part_ref, f32[16,64,128]{2,1,0:T(8,128)S(1)} %get-tuple-element.73.grad_ref, ...), custom_call_target="tpu_custom_call" | custom-call | tf_op jit(solution)/shard_map/first_update/pallas_call | solution.py:21
  47.2 1.6 %collective-permute-start.11 = (bf16[8,64,128]{2,1,0:T(8,128)(2,1)S(1)}, bf16[8,64,128]{2,1,0:T(8,128)(2,1)S(1)}, u32[]{:S(2)}, u32[]{:S(2)}) collective-permute-start(bf16[8,64,128]{2,1,0:T(8,128)(2,1)S(1)} %get-tuple-element.78.mine_ref), channel_id=1, source_target_pairs={{0,1},{1,0},{2,3},{3,2},{4,5},{5,4},{6,7},{7,6},{8,9},{9,8},{10,11... | collective-permute-start | bytes 393224 | tf_op jit(solution)/shard_map/ppermute | solution.py:381
  48.8 1.9 %collective-permute-start.9 = (bf16[4,64,128]{2,1,0:T(8,128)(2,1)S(1)}, bf16[4,64,128]{2,1,0:T(8,128)(2,1)S(1)}, u32[]{:S(2)}, u32[]{:S(2)}) collective-permute-start(bf16[4,64,128]{2,1,0:T(8,128)(2,1)S(1)} %get-tuple-element.77), channel_id=1, source_target_pairs={{2,4},{6,8},{10,12},{14,16},{18,20},{22,24},{26,28},{4,2},{8,6},{1... | collective-permute-start | bytes 196616 | tf_op jit(solution)/shard_map/ppermute | solution.py:372
  50.7 4.6 %collective-permute-done.9.first_refs_0_ = bf16[4,64,128]{2,1,0:T(8,128)(2,1)S(1)} collective-permute-done((bf16[4,64,128]{2,1,0:T(8,128)(2,1)S(1)}, bf16[4,64,128]{2,1,0:T(8,128)(2,1)S(1)}, u32[]{:S(2)}, u32[]{:S(2)}) %collective-permute-start.9) | collective-permute-done | bytes 65568 | tf_op jit(solution)/shard_map/ppermute | solution.py:372
  55.3 0.5 collective-permute-start.10
  55.8 0.6 join_states.1
  56.4 0.1 collective-permute-start.12
  56.5 3.0 %collective-permute-done.10.first_refs_1_ = bf16[4,64,128]{2,1,0:T(8,128)(2,1)S(1)} collective-permute-done((bf16[4,64,128]{2,1,0:T(8,128)(2,1)S(1)}, bf16[4,64,128]{2,1,0:T(8,128)(2,1)S(1)}, u32[]{:S(2)}, u32[]{:S(2)}) %collective-permute-start.10) | collective-permute-done | bytes 65568 | tf_op jit(solution)/shard_map/ppermute | solution.py:381
  59.5 2.0 %predict_pull.1 = (f32[16,64,128]{2,1,0:T(8,128)S(1)}, bf16[4,64,128]{2,1,0:T(8,128)(2,1)S(1)}, bf16[4,64,128]{2,1,0:T(8,128)(2,1)S(1)}) custom-call(bf16[4,64,128]{2,1,0:T(8,128)(2,1)S(1)} %collective-permute-done.9.first_refs_0_, bf16[4,64,128]{2,1,0:T(8,128)(2,1)S(1)} %collective-permute-done.10.first_refs_1_, ...), custom_call_target="tpu_custom_call" | custom-call | tf_op jit(solution)/shard_map/predict_pull/pallas_call | solution.py:21
  61.5 1.9 %collective-permute-start.13 = (bf16[4,64,128]{2,1,0:T(8,128)(2,1)S(1)}, bf16[4,64,128]{2,1,0:T(8,128)(2,1)S(1)}, u32[]{:S(2)}, u32[]{:S(2)}) collective-permute-start(bf16[4,64,128]{2,1,0:T(8,128)(2,1)S(1)} %get-tuple-element.85), channel_id=1, source_target_pairs={{2,4},{6,8},{10,12},{14,16},{18,20},{22,24},{26,28},{4,2},{8,6},{1... | collective-permute-start | bytes 196616 | tf_op jit(solution)/shard_map/ppermute | solution.py:372
  63.4 0.1 collective-permute-start.14
  63.5 0.6 collective-permute-start.15
  64.1 1.9 %partial_update.3.part_ref = f32[64,1024]{1,0:T(8,128)S(1)} custom-call(f32[16,64,128]{2,1,0:T(8,128)S(1)} %get-tuple-element.81.grad_ref, s32[2,4]{1,0:T(2,128)S(1)} %get-tuple-element.51.ties_ref, bf16[1024,2048]{1,0:T(8,128)(2,1)S(1)} %copy-done), custom_call_target="tpu_custom_call" | custom-call | flops 1000000000 | tf_op jit(solution)/shard_map/partial_update/pallas_call | solution.py:21
  66.1 1.9 %collective-permute-done.13.back_first_ref = bf16[4,64,128]{2,1,0:T(8,128)(2,1)S(1)} collective-permute-done((bf16[4,64,128]{2,1,0:T(8,128)(2,1)S(1)}, bf16[4,64,128]{2,1,0:T(8,128)(2,1)S(1)}, u32[]{:S(2)}, u32[]{:S(2)}) %collective-permute-start.13) | collective-permute-done | bytes 65568 | tf_op jit(solution)/shard_map/ppermute | solution.py:372
  68.0 1.4 %last_update.1 = (f32[32,1024]{1,0:T(8,128)S(1)}, bf16[32,1024]{1,0:T(8,128)(2,1)S(1)}) custom-call(f32[64,1024]{1,0:T(8,128)S(1)} %partial_update.3.part_ref, f32[16,64,128]{2,1,0:T(8,128)S(1)} %get-tuple-element.81.grad_ref, bf16[4,64,128]{2,1,0:T(8,128)(2,1)S(1)} %collective-permute-done.13.back_first_ref, ...), custom_call_target="tpu_custom_call" | custom-call | tf_op jit(solution)/shard_map/last_update/pallas_call | solution.py:21
  69.4 0.6 collective-permute-start.16
  70.0 3.7 %collective-permute-done.16.updates_refs_0_ = bf16[32,1024]{1,0:T(8,128)(2,1)S(1)} collective-permute-done((bf16[32,1024]{1,0:T(8,128)(2,1)S(1)}, bf16[32,1024]{1,0:T(8,128)(2,1)S(1)}, u32[]{:S(2)}, u32[]{:S(2)}) %collective-permute-start.16) | collective-permute-done | bytes 65568 | tf_op jit(solution)/shard_map/ppermute | solution.py:381
  73.7 0.7 finish.1
  (17 shorter events, 0.0 us)
Async XLA Ops:
  0.0 26.6 %copy-start.1 = (bf16[16,4,128,128]{3,2,1,0:T(8,128)(2,1)S(1)}, bf16[16,4,128,128]{3,2,1,0:T(8,128)(2,1)}, u32[]{:S(2)}) copy-start(bf16[16,4,128,128]{3,2,1,0:T(8,128)(2,1)} %tiles_ref.5) | copy-start | bytes 6291460
  4.4 23.6 %all-to-all-start = ((f32[16,72,128]{2,1,0:T(8,128)}), f32[16,72,128]{2,1,0:T(8,128)S(1)}, u32[]{:S(2)}, u32[]{:S(2)}) async-start(f32[16,72,128]{2,1,0:T(8,128)} %get-tuple-element.48), calls=%async_computation | async-start | bytes 1179648 | tf_op jit(solution)/shard_map/all_to_all | solution.py:455
  10.6 5.8 %collective-permute-start = (bf16[16,32,128]{2,1,0:T(8,128)(2,1)}, bf16[16,32,128]{2,1,0:T(8,128)(2,1)S(1)}, u32[]{:S(2)}, u32[]{:S(2)}) collective-permute-start(bf16[16,32,128]{2,1,0:T(8,128)(2,1)} %get-tuple-element.49.handed_refs_0_), channel_id=1, source_target_pairs={{0,1},{1,0},{2,3},{3,2},{4,5},{5,4},{6,7},{7,6},{8,9},{9,8},{10,11... | collective-permute-start | bytes 393224 | tf_op jit(solution)/shard_map/ppermute | solution.py:381
  12.1 0.9 %copy-start.3 = (bf16[16,32,128]{2,1,0:T(8,128)(2,1)S(1)}, bf16[16,32,128]{2,1,0:T(8,128)(2,1)}, u32[]{:S(2)}) copy-start(bf16[16,32,128]{2,1,0:T(8,128)(2,1)} %get-tuple-element.49.handed_refs_0_) | copy-start | bytes 393220
  13.1 0.7 copy-start.4
  13.8 0.7 copy-start.5
  14.5 0.7 copy-start.6
  17.0 9.6 %collective-permute-start.1 = (bf16[4,64,128]{2,1,0:T(8,128)(2,1)S(1)}, bf16[4,64,128]{2,1,0:T(8,128)(2,1)S(1)}, u32[]{:S(2)}, u32[]{:S(2)}) collective-permute-start(bf16[4,64,128]{2,1,0:T(8,128)(2,1)S(1)} %get-tuple-element.55), channel_id=1, source_target_pairs={{2,4},{6,8},{10,12},{14,16},{18,20},{22,24},{26,28},{4,2},{8,6},{1... | collective-permute-start | bytes 196616 | tf_op jit(solution)/shard_map/ppermute | solution.py:372
  19.3 7.3 %collective-permute-start.2 = (bf16[4,64,128]{2,1,0:T(8,128)(2,1)S(1)}, bf16[4,64,128]{2,1,0:T(8,128)(2,1)S(1)}, u32[]{:S(2)}, u32[]{:S(2)}) collective-permute-start(bf16[4,64,128]{2,1,0:T(8,128)(2,1)S(1)} %get-tuple-element.56), channel_id=1, source_target_pairs={{0,2},{4,6},{8,10},{12,14},{16,18},{20,22},{24,26},{28,30},{2,0},{... | collective-permute-start | bytes 196616 | tf_op jit(solution)/shard_map/ppermute | solution.py:372
  20.6 11.1 %collective-permute-start.3 = (f32[32,1024]{1,0:T(8,128)}, f32[32,1024]{1,0:T(8,128)S(1)}, u32[]{:S(2)}, u32[]{:S(2)}) collective-permute-start(f32[32,1024]{1,0:T(8,128)} %get-tuple-element.65), channel_id=1, source_target_pairs={{0,1},{1,0},{2,3},{3,2},{4,5},{5,4},{6,7},{7,6},{8,9},{9,8},{10,11... | collective-permute-start | bytes 393224 | tf_op jit(solution)/shard_map/ppermute | solution.py:381
  28.5 4.7 %collective-permute-start.4 = (f32[32,384]{1,0:T(8,128)S(1)}, f32[32,384]{1,0:T(8,128)S(1)}, u32[]{:S(2)}, u32[]{:S(2)}) collective-permute-start(f32[32,384]{1,0:T(8,128)S(1)} %get-tuple-element.62.z_refs_0_), channel_id=1, source_target_pairs={{0,1},{1,0},{2,3},{3,2},{4,5},{5,4},{6,7},{7,6},{8,9},{9,8},{10,11... | collective-permute-start | bytes 147464 | tf_op jit(solution)/shard_map/ppermute | solution.py:381
  31.6 6.2 %collective-permute-start.5 = (f32[32,1280]{1,0:T(8,128)S(1)}, f32[32,1280]{1,0:T(8,128)S(1)}, u32[]{:S(2)}, u32[]{:S(2)}) collective-permute-start(f32[32,1280]{1,0:T(8,128)S(1)} %get-tuple-element.66.z_refs_1_), channel_id=1, source_target_pairs={{0,1},{1,0},{2,3},{3,2},{4,5},{5,4},{6,7},{7,6},{8,9},{9,8},{10,11... | collective-permute-start | bytes 491528 | tf_op jit(solution)/shard_map/ppermute | solution.py:381
  33.2 8.5 %copy-start = (bf16[1024,2048]{1,0:T(8,128)(2,1)S(1)}, bf16[1024,2048]{1,0:T(8,128)(2,1)}, u32[]{:S(2)}) copy-start(bf16[1024,2048]{1,0:T(8,128)(2,1)} %gain_ref.7) | copy-start | bytes 12582916
  33.7 12.1 %copy-start.2 = (f32[32,2048]{1,0:T(8,128)S(1)}, f32[32,2048]{1,0:T(8,128)}, u32[]{:S(2)}) copy-start(f32[32,2048]{1,0:T(8,128)} %x_ref.1) | copy-start | bytes 786436
  33.7 4.2 %collective-permute-start.6 = (f32[32,384]{1,0:T(8,128)S(1)}, f32[32,384]{1,0:T(8,128)S(1)}, u32[]{:S(2)}, u32[]{:S(2)}) collective-permute-start(f32[32,384]{1,0:T(8,128)S(1)} %get-tuple-element.68.z_refs_2_), channel_id=1, source_target_pairs={{0,1},{1,0},{2,3},{3,2},{4,5},{5,4},{6,7},{7,6},{8,9},{9,8},{10,11... | collective-permute-start | bytes 147464 | tf_op jit(solution)/shard_map/ppermute | solution.py:381
  39.3 6.5 %collective-permute-start.7 = (bf16[4,64,128]{2,1,0:T(8,128)(2,1)S(1)}, bf16[4,64,128]{2,1,0:T(8,128)(2,1)S(1)}, u32[]{:S(2)}, u32[]{:S(2)}) collective-permute-start(bf16[4,64,128]{2,1,0:T(8,128)(2,1)S(1)} %get-tuple-element.74), channel_id=1, source_target_pairs={{2,4},{6,8},{10,12},{14,16},{18,20},{22,24},{26,28},{4,2},{8,6},{1... | collective-permute-start | bytes 196616 | tf_op jit(solution)/shard_map/ppermute | solution.py:372
  41.6 4.3 %collective-permute-start.8 = (bf16[4,64,128]{2,1,0:T(8,128)(2,1)S(1)}, bf16[4,64,128]{2,1,0:T(8,128)(2,1)S(1)}, u32[]{:S(2)}, u32[]{:S(2)}) collective-permute-start(bf16[4,64,128]{2,1,0:T(8,128)(2,1)S(1)} %get-tuple-element.75), channel_id=1, source_target_pairs={{0,2},{4,6},{8,10},{12,14},{16,18},{20,22},{24,26},{28,30},{2,0},{... | collective-permute-start | bytes 196616 | tf_op jit(solution)/shard_map/ppermute | solution.py:372
  47.2 8.6 %collective-permute-start.11 = (bf16[8,64,128]{2,1,0:T(8,128)(2,1)S(1)}, bf16[8,64,128]{2,1,0:T(8,128)(2,1)S(1)}, u32[]{:S(2)}, u32[]{:S(2)}) collective-permute-start(bf16[8,64,128]{2,1,0:T(8,128)(2,1)S(1)} %get-tuple-element.78.mine_ref), channel_id=1, source_target_pairs={{0,1},{1,0},{2,3},{3,2},{4,5},{5,4},{6,7},{7,6},{8,9},{9,8},{10,11... | collective-permute-start | bytes 393224 | tf_op jit(solution)/shard_map/ppermute | solution.py:381
  48.8 6.5 %collective-permute-start.9 = (bf16[4,64,128]{2,1,0:T(8,128)(2,1)S(1)}, bf16[4,64,128]{2,1,0:T(8,128)(2,1)S(1)}, u32[]{:S(2)}, u32[]{:S(2)}) collective-permute-start(bf16[4,64,128]{2,1,0:T(8,128)(2,1)S(1)} %get-tuple-element.77), channel_id=1, source_target_pairs={{2,4},{6,8},{10,12},{14,16},{18,20},{22,24},{26,28},{4,2},{8,6},{1... | collective-permute-start | bytes 196616 | tf_op jit(solution)/shard_map/ppermute | solution.py:372
  55.3 4.3 %collective-permute-start.10 = (bf16[4,64,128]{2,1,0:T(8,128)(2,1)S(1)}, bf16[4,64,128]{2,1,0:T(8,128)(2,1)S(1)}, u32[]{:S(2)}, u32[]{:S(2)}) collective-permute-start(bf16[4,64,128]{2,1,0:T(8,128)(2,1)S(1)} %collective-permute-done.9.first_refs_0_), channel_id=1, source_target_pairs={{0,1},{1,0},{2,3},{3,2},{4,5},{5,4},{6,7},{7,6},{8,9},{9,8},{10,11... | collective-permute-start | bytes 196616 | tf_op jit(solution)/shard_map/ppermute | solution.py:381
  56.4 3.1 %collective-permute-start.12 = (bf16[4,64,128]{2,1,0:T(8,128)(2,1)S(1)}, bf16[4,64,128]{2,1,0:T(8,128)(2,1)S(1)}, u32[]{:S(2)}, u32[]{:S(2)}) collective-permute-start(bf16[4,64,128]{2,1,0:T(8,128)(2,1)S(1)} %get-tuple-element.80), channel_id=1, source_target_pairs={{0,2},{4,6},{8,10},{12,14},{16,18},{20,22},{24,26},{28,30},{2,0},{... | collective-permute-start | bytes 196616 | tf_op jit(solution)/shard_map/ppermute | solution.py:372
  61.5 6.5 %collective-permute-start.13 = (bf16[4,64,128]{2,1,0:T(8,128)(2,1)S(1)}, bf16[4,64,128]{2,1,0:T(8,128)(2,1)S(1)}, u32[]{:S(2)}, u32[]{:S(2)}) collective-permute-start(bf16[4,64,128]{2,1,0:T(8,128)(2,1)S(1)} %get-tuple-element.85), channel_id=1, source_target_pairs={{2,4},{6,8},{10,12},{14,16},{18,20},{22,24},{26,28},{4,2},{8,6},{1... | collective-permute-start | bytes 196616 | tf_op jit(solution)/shard_map/ppermute | solution.py:372
  63.4 4.6 %collective-permute-start.14 = (bf16[4,64,128]{2,1,0:T(8,128)(2,1)S(1)}, bf16[4,64,128]{2,1,0:T(8,128)(2,1)S(1)}, u32[]{:S(2)}, u32[]{:S(2)}) collective-permute-start(bf16[4,64,128]{2,1,0:T(8,128)(2,1)S(1)} %get-tuple-element.86), channel_id=1, source_target_pairs={{0,2},{4,6},{8,10},{12,14},{16,18},{20,22},{24,26},{28,30},{2,0},{... | collective-permute-start | bytes 196616 | tf_op jit(solution)/shard_map/ppermute | solution.py:372
  63.5 6.5 %collective-permute-start.15 = (f32[8,32,128]{2,1,0:T(8,128)S(1)}, f32[8,32,128]{2,1,0:T(8,128)S(1)}, u32[]{:S(2)}, u32[]{:S(2)}) collective-permute-start(f32[8,32,128]{2,1,0:T(8,128)S(1)} %get-tuple-element.89), channel_id=1, source_target_pairs={{0,1},{1,0},{2,3},{3,2},{4,5},{5,4},{6,7},{7,6},{8,9},{9,8},{10,11... | collective-permute-start | bytes 393224 | tf_op jit(solution)/shard_map/ppermute | solution.py:381
  69.4 4.3 %collective-permute-start.16 = (bf16[32,1024]{1,0:T(8,128)(2,1)S(1)}, bf16[32,1024]{1,0:T(8,128)(2,1)S(1)}, u32[]{:S(2)}, u32[]{:S(2)}) collective-permute-start(bf16[32,1024]{1,0:T(8,128)(2,1)S(1)} %get-tuple-element.90), channel_id=1, source_target_pairs={{0,1},{1,0},{2,3},{3,2},{4,5},{5,4},{6,7},{7,6},{8,9},{9,8},{10,11... | collective-permute-start | bytes 196616 | tf_op jit(solution)/shard_map/ppermute | solution.py:381

commit v17 on v16

--- a/solution.py
+++ b/solution.py
@@ -491,7 +491,7 @@
     )
     message, guess = lax.optimization_barrier((message, guess))
     blocks = lines // BLK
-    cuts = (0, blocks * 3 // 16, blocks * 13 // 16, blocks)
+    cuts = (0, blocks * 11 // 16, blocks)
     readings, variance, reading_others = [], [], []
     for part, (start, stop) in enumerate(zip(cuts, cuts[1:])):
         if part == 2:
@@ -534,7 +534,7 @@
     grad, first, second = call(
         pull_kernel,
         grads,
-        [VMEM, [VMEM] * 3, [VMEM] * 3, [VMEM] * 3, VMEM, SMEM],
+        [VMEM, [VMEM] * 2, [VMEM] * 2, [VMEM] * 2, VMEM, SMEM],
         (guess, readings, reading_others, variance, derivative_pieces, place),
         scratch=[total, pltpu.VMEM((everything, lines), BF16)],
         name="pull",
@@ -570,7 +570,7 @@
     grad, first, second = call(
         predict_pull_kernel,
         grads,
-        [[VMEM] * members, VMEM, VMEM, [VMEM] * 3, [VMEM] * 3, [VMEM] * 3, VMEM, SMEM],
+        [[VMEM] * members, VMEM, VMEM, [VMEM] * 2, [VMEM] * 2, [VMEM] * 2, VMEM, SMEM],
         (firsts, aug, second, readings, reading_others, variance, derivative_pieces, place),
         scratch=[
             pltpu.VMEM((slots, everything, BLK), BF16),

time: 74.9 us -> 73.3 us (0.979)
  waiting for transfers between devices: 24.4 us -> 22.2 us
    ppermute x8, waiting for transfers between devices: 13.2 us -> 11.6 us  [swap_pair(): return lax.ppermute(block, 'area', pairs + [(b, a) for a, b in pairs])]
    ppermute x8, starting transfers between devices: 9.82 us -> 11.1 us  [swap_pair(): return lax.ppermute(block, 'area', pairs + [(b, a) for a, b in pairs])]
    ppermute x9 -> x8, starting transfers between devices: 10 us -> 9.36 us  [from_snap(): lax.ppermute(block, 'snap', [(i, (i + distance) % members) for i in range...]
    ppermute x9 -> x8, waiting for transfers between devices: 11.1 us -> 10.6 us  [from_snap(): lax.ppermute(block, 'snap', [(i, (i + distance) % members) for i in range...]
    pallas_call x15 -> x14, Pallas kernels: 20.9 us -> 20.7 us  [call(): pl.pallas_call(kernel, out_shape=outs, in_specs=ins, out_specs=jax.tree.m...]
  transfers between devices with their start and end apart: 18 -> 17, of which waited for: 9 -> 8; matrix products, arithmetic and copies ran while one was open for 0% -> 0% of each run, Pallas kernels for 15% -> 15%
where the time goes in v17:
time: 73.3 us; the launch traced here: 72.7 us
  starting transfers between devices  26.6 us (36%)
  waiting for transfers between devices  22.2 us (30%)
  Pallas kernels  20.7 us (28%)
  local copies, waits for them, and re-layouts  3.03 us (4%)
    pallas_call x14, Pallas kernels, call(): pl.pallas_call(kernel, out_shape=outs, in_specs=ins, out_specs=jax.tree.m...  20.7 us
    ppermute x8, waiting for transfers between devices, swap_pair(): return lax.ppermute(block, 'area', pairs + [(b, a) for a, b in pairs])  11.6 us
    ppermute x8, starting transfers between devices, swap_pair(): return lax.ppermute(block, 'area', pairs + [(b, a) for a, b in pairs])  11.1 us
    ppermute x8, waiting for transfers between devices, from_snap(): lax.ppermute(block, 'snap', [(i, (i + distance) % members) for i in range...  10.6 us
    ppermute x8, starting transfers between devices, from_snap(): lax.ppermute(block, 'snap', [(i, (i + distance) % members) for i in range...  9.36 us
    all_to_all x1, starting transfers between devices, on_device(): lax.all_to_all(message, 'area', split_axis=0, concat_axis=0, tiled=True)  6.17 us
    unnamed x14, local copies, waits for them, and re-layouts  3.03 us
  transfers between devices with their start and end apart: 17, of which 8 were waited for; matrix products, arithmetic and copies ran while one was open for 0% of the time, Pallas kernels for 15%

profile of v17, /device:TPU:16, one launch (start us, length us, event | category | flops | bytes accessed | tf_op | source)
XLA Modules:
  0.0 72.7 jit_solution(7533961045968619991)
XLA Ops:
  0.0 4.4 %pack_readings.1 = (f32[16,72,128]{2,1,0:T(8,128)}, bf16[16,32,128]{2,1,0:T(8,128)(2,1)}, f32[32,1024]{1,0:T(8,128)}) custom-call(f32[32,2048]{1,0:T(8,128)} %z_in.1, f32[16,128]{1,0:T(8,128)} %bitcast.17, s32[16,256]{1,0:T(8,128)} %bitcast.16, f32[32,2048]{1,0:T(8,128)} %x_ref.1), custom_call_target="tpu_custom_call" | custom-call | tf_op jit(solution)/shard_map/pack_readings/pallas_call | solution.py:21
  4.4 6.2 %all-to-all-start = ((f32[16,72,128]{2,1,0:T(8,128)}), f32[16,72,128]{2,1,0:T(8,128)S(1)}, u32[]{:S(2)}, u32[]{:S(2)}) async-start(f32[16,72,128]{2,1,0:T(8,128)} %get-tuple-element.44), calls=%async_computation | async-start | bytes 1179648 | tf_op jit(solution)/shard_map/all_to_all | solution.py:455
  10.6 1.5 %collective-permute-start = (bf16[16,32,128]{2,1,0:T(8,128)(2,1)}, bf16[16,32,128]{2,1,0:T(8,128)(2,1)S(1)}, u32[]{:S(2)}, u32[]{:S(2)}) collective-permute-start(bf16[16,32,128]{2,1,0:T(8,128)(2,1)} %get-tuple-element.45.handed_refs_0_), channel_id=1, source_target_pairs={{0,1},{1,0},{2,3},{3,2},{4,5},{5,4},{6,7},{7,6},{8,9},{9,8},{10,11... | collective-permute-start | bytes 393224 | tf_op jit(solution)/shard_map/ppermute | solution.py:381
  12.1 0.9 %copy-done.3 = bf16[16,32,128]{2,1,0:T(8,128)(2,1)S(1)} copy-done((bf16[16,32,128]{2,1,0:T(8,128)(2,1)S(1)}, bf16[16,32,128]{2,1,0:T(8,128)(2,1)}, u32[]{:S(2)}) %copy-start.3) | copy-done | bytes 131096
  13.1 0.7 copy-done.4
  13.8 0.7 copy-done.5
  14.5 0.7 copy-done.6
  15.1 0.4 invert_order.1
  15.6 0.8 %collective-permute-done.own_refs_1_ = bf16[16,32,128]{2,1,0:T(8,128)(2,1)S(1)} collective-permute-done((bf16[16,32,128]{2,1,0:T(8,128)(2,1)}, bf16[16,32,128]{2,1,0:T(8,128)(2,1)S(1)}, u32[]{:S(2)}, u32[]{:S(2)}) %collective-permute-start) | collective-permute-done | bytes 131104 | tf_op jit(solution)/shard_map/ppermute | solution.py:381
  16.4 0.6 pick_boundary.1
  17.0 2.3 %collective-permute-start.1 = (bf16[4,64,128]{2,1,0:T(8,128)(2,1)S(1)}, bf16[4,64,128]{2,1,0:T(8,128)(2,1)S(1)}, u32[]{:S(2)}, u32[]{:S(2)}) collective-permute-start(bf16[4,64,128]{2,1,0:T(8,128)(2,1)S(1)} %get-tuple-element.51), channel_id=1, source_target_pairs={{2,4},{6,8},{10,12},{14,16},{18,20},{22,24},{26,28},{4,2},{8,6},{1... | collective-permute-start | bytes 196616 | tf_op jit(solution)/shard_map/ppermute | solution.py:372
  19.3 1.3 %collective-permute-start.2 = (bf16[4,64,128]{2,1,0:T(8,128)(2,1)S(1)}, bf16[4,64,128]{2,1,0:T(8,128)(2,1)S(1)}, u32[]{:S(2)}, u32[]{:S(2)}) collective-permute-start(bf16[4,64,128]{2,1,0:T(8,128)(2,1)S(1)} %get-tuple-element.52), channel_id=1, source_target_pairs={{0,2},{4,6},{8,10},{12,14},{16,18},{20,22},{24,26},{28,30},{2,0},{... | collective-permute-start | bytes 196616 | tf_op jit(solution)/shard_map/ppermute | solution.py:372
  20.6 1.5 %collective-permute-start.3 = (f32[32,1024]{1,0:T(8,128)}, f32[32,1024]{1,0:T(8,128)S(1)}, u32[]{:S(2)}, u32[]{:S(2)}) collective-permute-start(f32[32,1024]{1,0:T(8,128)} %get-tuple-element.61), channel_id=1, source_target_pairs={{0,1},{1,0},{2,3},{3,2},{4,5},{5,4},{6,7},{7,6},{8,9},{9,8},{10,11... | collective-permute-start | bytes 393224 | tf_op jit(solution)/shard_map/ppermute | solution.py:381
  22.1 4.5 %collective-permute-done.1.first_ref = bf16[4,64,128]{2,1,0:T(8,128)(2,1)S(1)} collective-permute-done((bf16[4,64,128]{2,1,0:T(8,128)(2,1)S(1)}, bf16[4,64,128]{2,1,0:T(8,128)(2,1)S(1)}, u32[]{:S(2)}, u32[]{:S(2)}) %collective-permute-start.1) | collective-permute-done | bytes 65568 | tf_op jit(solution)/shard_map/ppermute | solution.py:372
  26.6 0.0 collective-permute-done.2.second_ref
  26.6 1.4 %predict.1.guess_ref = f32[64,2048]{1,0:T(8,128)S(1)} custom-call(bf16[4,64,128]{2,1,0:T(8,128)(2,1)S(1)} %collective-permute-done.1.first_ref, bf16[4,64,128]{2,1,0:T(8,128)(2,1)S(1)} %collective-permute-done.2.second_ref, bf16[16,32,128]{2,1,0:T(8,128)(2,1)S(1)} %get-tuple-element.46.own_refs_0_, ...), custom_call_target="tpu_custom_call" | custom-call | flops 1000000000 | tf_op jit(solution)/shard_map/predict/pallas_call | solution.py:21
  28.0 0.0 all-to-all-done.message_ref
  28.0 1.6 %unpack_readings.2 = (f32[32,1408]{1,0:T(8,128)S(1)}, f32[1,1408]{1,0:T(1,128)S(1)}) custom-call(s32[16,128]{1,0:T(8,128)S(1)} %get-tuple-element.55.group_ref, s32[16,128]{1,0:T(8,128)S(1)} %get-tuple-element.56.lane_ref, f32[16,72,128]{2,1,0:T(8,128)S(1)} %all-to-all-done.message_ref), custom_call_target="tpu_custom_call" | custom-call | flops 2000000000 | tf_op jit(solution)/shard_map/unpack_readings/pallas_call | solution.py:21
  29.6 0.0 copy-start
  29.7 1.6 %collective-permute-start.4 = (f32[32,1408]{1,0:T(8,128)S(1)}, f32[32,1408]{1,0:T(8,128)S(1)}, u32[]{:S(2)}, u32[]{:S(2)}) collective-permute-start(f32[32,1408]{1,0:T(8,128)S(1)} %get-tuple-element.58.z_refs_0_), channel_id=1, source_target_pairs={{0,1},{1,0},{2,3},{3,2},{4,5},{5,4},{6,7},{7,6},{8,9},{9,8},{10,11... | collective-permute-start | bytes 540680 | tf_op jit(solution)/shard_map/ppermute | solution.py:381
  31.2 0.8 %unpack_readings.3 = (f32[32,640]{1,0:T(8,128)S(1)}, f32[1,640]{1,0:T(1,128)S(1)}) custom-call(s32[16,128]{1,0:T(8,128)S(1)} %get-tuple-element.55.group_ref, s32[16,128]{1,0:T(8,128)S(1)} %get-tuple-element.56.lane_ref, f32[16,72,128]{2,1,0:T(8,128)S(1)} %all-to-all-done.message_ref), custom_call_target="tpu_custom_call" | custom-call | flops 2000000000 | tf_op jit(solution)/shard_map/unpack_readings/pallas_call | solution.py:21
  32.0 0.0 copy-start.2
  32.0 0.0 collective-permute-done.3.x_others_refs_0_
  32.0 0.6 collective-permute-start.5
  32.6 3.9 %collective-permute-done.5 = f32[32,640]{1,0:T(8,128)S(1)} collective-permute-done((f32[32,640]{1,0:T(8,128)S(1)}, f32[32,640]{1,0:T(8,128)S(1)}, u32[]{:S(2)}, u32[]{:S(2)}) %collective-permute-start.5) | collective-permute-done | bytes 81952 | tf_op jit(solution)/shard_map/ppermute | solution.py:381
  36.6 1.4 %pull.1 = (f32[16,64,128]{2,1,0:T(8,128)S(1)}, bf16[4,64,128]{2,1,0:T(8,128)(2,1)S(1)}, bf16[4,64,128]{2,1,0:T(8,128)(2,1)S(1)}) custom-call(f32[64,2048]{1,0:T(8,128)S(1)} %predict.1.guess_ref, f32[32,1408]{1,0:T(8,128)S(1)} %get-tuple-element.58.z_refs_0_, f32[32,640]{1,0:T(8,128)S(1)} %get-tuple-element.62.z_refs_1_, f32[1,32,1408]{2,1,0:T(8,128)S(1)} %bitcast.9, ...), custom_call_target="tpu_custom_call" | custom-call | tf_op jit(solution)/shard_map/pull/pallas_call | solution.py:21
  38.0 2.6 %collective-permute-start.6 = (bf16[4,64,128]{2,1,0:T(8,128)(2,1)S(1)}, bf16[4,64,128]{2,1,0:T(8,128)(2,1)S(1)}, u32[]{:S(2)}, u32[]{:S(2)}) collective-permute-start(bf16[4,64,128]{2,1,0:T(8,128)(2,1)S(1)} %get-tuple-element.66), channel_id=1, source_target_pairs={{2,4},{6,8},{10,12},{14,16},{18,20},{22,24},{26,28},{4,2},{8,6},{1... | collective-permute-start | bytes 196616 | tf_op jit(solution)/shard_map/ppermute | solution.py:372
  40.6 0.1 collective-permute-start.7
  40.7 1.9 %partial_update.2.part_ref = f32[64,1024]{1,0:T(8,128)S(1)} custom-call(f32[16,64,128]{2,1,0:T(8,128)S(1)} %get-tuple-element.65.grad_ref, s32[2,4]{1,0:T(2,128)S(1)} %get-tuple-element.47.ties_ref, bf16[1024,2048]{1,0:T(8,128)(2,1)S(1)} %copy-done), custom_call_target="tpu_custom_call" | custom-call | flops 1000000000 | tf_op jit(solution)/shard_map/partial_update/pallas_call | solution.py:21
  42.6 1.8 %collective-permute-done.6.back_first_ref = bf16[4,64,128]{2,1,0:T(8,128)(2,1)S(1)} collective-permute-done((bf16[4,64,128]{2,1,0:T(8,128)(2,1)S(1)}, bf16[4,64,128]{2,1,0:T(8,128)(2,1)S(1)}, u32[]{:S(2)}, u32[]{:S(2)}) %collective-permute-start.6) | collective-permute-done | bytes 65568 | tf_op jit(solution)/shard_map/ppermute | solution.py:372
  44.5 1.4 %first_update.1 = (f32[8,32,128]{2,1,0:T(8,128)S(1)}, f32[8,32,128]{2,1,0:T(8,128)S(1)}, bf16[8,64,128]{2,1,0:T(8,128)(2,1)S(1)}, bf16[4,64,128]{2,1,0:T(8,128)(2,1)S(1)}) custom-call(f32[64,1024]{1,0:T(8,128)S(1)} %partial_update.2.part_ref, f32[16,64,128]{2,1,0:T(8,128)S(1)} %get-tuple-element.65.grad_ref, ...), custom_call_target="tpu_custom_call" | custom-call | tf_op jit(solution)/shard_map/first_update/pallas_call | solution.py:21
  45.9 1.1 %collective-permute-start.10 = (bf16[8,64,128]{2,1,0:T(8,128)(2,1)S(1)}, bf16[8,64,128]{2,1,0:T(8,128)(2,1)S(1)}, u32[]{:S(2)}, u32[]{:S(2)}) collective-permute-start(bf16[8,64,128]{2,1,0:T(8,128)(2,1)S(1)} %get-tuple-element.70.mine_ref), channel_id=1, source_target_pairs={{0,1},{1,0},{2,3},{3,2},{4,5},{5,4},{6,7},{7,6},{8,9},{9,8},{10,11... | collective-permute-start | bytes 393224 | tf_op jit(solution)/shard_map/ppermute | solution.py:381
  47.0 2.8 %collective-permute-start.8 = (bf16[4,64,128]{2,1,0:T(8,128)(2,1)S(1)}, bf16[4,64,128]{2,1,0:T(8,128)(2,1)S(1)}, u32[]{:S(2)}, u32[]{:S(2)}) collective-permute-start(bf16[4,64,128]{2,1,0:T(8,128)(2,1)S(1)} %get-tuple-element.69), channel_id=1, source_target_pairs={{2,4},{6,8},{10,12},{14,16},{18,20},{22,24},{26,28},{4,2},{8,6},{1... | collective-permute-start | bytes 196616 | tf_op jit(solution)/shard_map/ppermute | solution.py:372
  49.8 3.7 %collective-permute-done.8.first_refs_0_ = bf16[4,64,128]{2,1,0:T(8,128)(2,1)S(1)} collective-permute-done((bf16[4,64,128]{2,1,0:T(8,128)(2,1)S(1)}, bf16[4,64,128]{2,1,0:T(8,128)(2,1)S(1)}, u32[]{:S(2)}, u32[]{:S(2)}) %collective-permute-start.8) | collective-permute-done | bytes 65568 | tf_op jit(solution)/shard_map/ppermute | solution.py:372
  53.5 1.0 %collective-permute-start.9 = (bf16[4,64,128]{2,1,0:T(8,128)(2,1)S(1)}, bf16[4,64,128]{2,1,0:T(8,128)(2,1)S(1)}, u32[]{:S(2)}, u32[]{:S(2)}) collective-permute-start(bf16[4,64,128]{2,1,0:T(8,128)(2,1)S(1)} %collective-permute-done.8.first_refs_0_), channel_id=1, source_target_pairs={{0,1},{1,0},{2,3},{3,2},{4,5},{5,4},{6,7},{7,6},{8,9},{9,8},{10,11... | collective-permute-start | bytes 196616 | tf_op jit(solution)/shard_map/ppermute | solution.py:381
  54.5 0.6 join_states.1
  55.1 0.1 collective-permute-start.11
  55.2 2.6 %collective-permute-done.9.first_refs_1_ = bf16[4,64,128]{2,1,0:T(8,128)(2,1)S(1)} collective-permute-done((bf16[4,64,128]{2,1,0:T(8,128)(2,1)S(1)}, bf16[4,64,128]{2,1,0:T(8,128)(2,1)S(1)}, u32[]{:S(2)}, u32[]{:S(2)}) %collective-permute-start.9) | collective-permute-done | bytes 65568 | tf_op jit(solution)/shard_map/ppermute | solution.py:381
  57.8 2.0 %predict_pull.1 = (f32[16,64,128]{2,1,0:T(8,128)S(1)}, bf16[4,64,128]{2,1,0:T(8,128)(2,1)S(1)}, bf16[4,64,128]{2,1,0:T(8,128)(2,1)S(1)}) custom-call(bf16[4,64,128]{2,1,0:T(8,128)(2,1)S(1)} %collective-permute-done.8.first_refs_0_, bf16[4,64,128]{2,1,0:T(8,128)(2,1)S(1)} %collective-permute-done.9.first_refs_1_, ...), custom_call_target="tpu_custom_call" | custom-call | tf_op jit(solution)/shard_map/predict_pull/pallas_call | solution.py:21
  59.7 1.9 %collective-permute-start.12 = (bf16[4,64,128]{2,1,0:T(8,128)(2,1)S(1)}, bf16[4,64,128]{2,1,0:T(8,128)(2,1)S(1)}, u32[]{:S(2)}, u32[]{:S(2)}) collective-permute-start(bf16[4,64,128]{2,1,0:T(8,128)(2,1)S(1)} %get-tuple-element.77), channel_id=1, source_target_pairs={{2,4},{6,8},{10,12},{14,16},{18,20},{22,24},{26,28},{4,2},{8,6},{1... | collective-permute-start | bytes 196616 | tf_op jit(solution)/shard_map/ppermute | solution.py:372
  61.7 0.1 collective-permute-start.13
  61.7 1.0 %collective-permute-start.14 = (f32[8,32,128]{2,1,0:T(8,128)S(1)}, f32[8,32,128]{2,1,0:T(8,128)S(1)}, u32[]{:S(2)}, u32[]{:S(2)}) collective-permute-start(f32[8,32,128]{2,1,0:T(8,128)S(1)} %get-tuple-element.81), channel_id=1, source_target_pairs={{0,1},{1,0},{2,3},{3,2},{4,5},{5,4},{6,7},{7,6},{8,9},{9,8},{10,11... | collective-permute-start | bytes 393224 | tf_op jit(solution)/shard_map/ppermute | solution.py:381
  62.8 1.9 %partial_update.3.part_ref = f32[64,1024]{1,0:T(8,128)S(1)} custom-call(f32[16,64,128]{2,1,0:T(8,128)S(1)} %get-tuple-element.73.grad_ref, s32[2,4]{1,0:T(2,128)S(1)} %get-tuple-element.47.ties_ref, bf16[1024,2048]{1,0:T(8,128)(2,1)S(1)} %copy-done), custom_call_target="tpu_custom_call" | custom-call | flops 1000000000 | tf_op jit(solution)/shard_map/partial_update/pallas_call | solution.py:21
  64.7 1.5 %collective-permute-done.12.back_first_ref = bf16[4,64,128]{2,1,0:T(8,128)(2,1)S(1)} collective-permute-done((bf16[4,64,128]{2,1,0:T(8,128)(2,1)S(1)}, bf16[4,64,128]{2,1,0:T(8,128)(2,1)S(1)}, u32[]{:S(2)}, u32[]{:S(2)}) %collective-permute-start.12) | collective-permute-done | bytes 65568 | tf_op jit(solution)/shard_map/ppermute | solution.py:372
  66.2 1.4 %last_update.1 = (f32[32,1024]{1,0:T(8,128)S(1)}, bf16[32,1024]{1,0:T(8,128)(2,1)S(1)}) custom-call(f32[64,1024]{1,0:T(8,128)S(1)} %partial_update.3.part_ref, f32[16,64,128]{2,1,0:T(8,128)S(1)} %get-tuple-element.73.grad_ref, bf16[4,64,128]{2,1,0:T(8,128)(2,1)S(1)} %collective-permute-done.12.back_first_ref, ...), custom_call_target="tpu_custom_call" | custom-call | tf_op jit(solution)/shard_map/last_update/pallas_call | solution.py:21
  67.6 1.0 %collective-permute-start.15 = (bf16[32,1024]{1,0:T(8,128)(2,1)S(1)}, bf16[32,1024]{1,0:T(8,128)(2,1)S(1)}, u32[]{:S(2)}, u32[]{:S(2)}) collective-permute-start(bf16[32,1024]{1,0:T(8,128)(2,1)S(1)} %get-tuple-element.82), channel_id=1, source_target_pairs={{0,1},{1,0},{2,3},{3,2},{4,5},{5,4},{6,7},{7,6},{8,9},{9,8},{10,11... | collective-permute-start | bytes 196616 | tf_op jit(solution)/shard_map/ppermute | solution.py:381
  68.7 3.3 %collective-permute-done.15.updates_refs_0_ = bf16[32,1024]{1,0:T(8,128)(2,1)S(1)} collective-permute-done((bf16[32,1024]{1,0:T(8,128)(2,1)S(1)}, bf16[32,1024]{1,0:T(8,128)(2,1)S(1)}, u32[]{:S(2)}, u32[]{:S(2)}) %collective-permute-start.15) | collective-permute-done | bytes 65568 | tf_op jit(solution)/shard_map/ppermute | solution.py:381
  71.9 0.7 %finish.1 = f32[32,2048]{1,0:T(8,128)} custom-call(f32[32,1024]{1,0:T(8,128)S(1)} %get-tuple-element.80.mine_ref, f32[8,32,128]{2,1,0:T(8,128)S(1)} %collective-permute-done.14.states_refs_0_, bf16[32,1024]{1,0:T(8,128)(2,1)S(1)} %collective-permute-done.15.updates_refs_0_), custom_call_target="tpu_custom_call" | custom-call | tf_op jit(solution)/shard_map/finish/pallas_call | solution.py:21
  (14 shorter events, 0.0 us)
Async XLA Ops:
  0.0 26.6 %copy-start.1 = (bf16[16,4,128,128]{3,2,1,0:T(8,128)(2,1)S(1)}, bf16[16,4,128,128]{3,2,1,0:T(8,128)(2,1)}, u32[]{:S(2)}) copy-start(bf16[16,4,128,128]{3,2,1,0:T(8,128)(2,1)} %tiles_ref.5) | copy-start | bytes 6291460
  4.4 23.6 %all-to-all-start = ((f32[16,72,128]{2,1,0:T(8,128)}), f32[16,72,128]{2,1,0:T(8,128)S(1)}, u32[]{:S(2)}, u32[]{:S(2)}) async-start(f32[16,72,128]{2,1,0:T(8,128)} %get-tuple-element.44), calls=%async_computation | async-start | bytes 1179648 | tf_op jit(solution)/shard_map/all_to_all | solution.py:455
  10.6 5.8 %collective-permute-start = (bf16[16,32,128]{2,1,0:T(8,128)(2,1)}, bf16[16,32,128]{2,1,0:T(8,128)(2,1)S(1)}, u32[]{:S(2)}, u32[]{:S(2)}) collective-permute-start(bf16[16,32,128]{2,1,0:T(8,128)(2,1)} %get-tuple-element.45.handed_refs_0_), channel_id=1, source_target_pairs={{0,1},{1,0},{2,3},{3,2},{4,5},{5,4},{6,7},{7,6},{8,9},{9,8},{10,11... | collective-permute-start | bytes 393224 | tf_op jit(solution)/shard_map/ppermute | solution.py:381
  12.1 0.9 %copy-start.3 = (bf16[16,32,128]{2,1,0:T(8,128)(2,1)S(1)}, bf16[16,32,128]{2,1,0:T(8,128)(2,1)}, u32[]{:S(2)}) copy-start(bf16[16,32,128]{2,1,0:T(8,128)(2,1)} %get-tuple-element.45.handed_refs_0_) | copy-start | bytes 393220
  13.1 0.7 copy-start.4
  13.8 0.7 copy-start.5
  14.5 0.7 copy-start.6
  17.0 9.6 %collective-permute-start.1 = (bf16[4,64,128]{2,1,0:T(8,128)(2,1)S(1)}, bf16[4,64,128]{2,1,0:T(8,128)(2,1)S(1)}, u32[]{:S(2)}, u32[]{:S(2)}) collective-permute-start(bf16[4,64,128]{2,1,0:T(8,128)(2,1)S(1)} %get-tuple-element.51), channel_id=1, source_target_pairs={{2,4},{6,8},{10,12},{14,16},{18,20},{22,24},{26,28},{4,2},{8,6},{1... | collective-permute-start | bytes 196616 | tf_op jit(solution)/shard_map/ppermute | solution.py:372
  19.3 7.3 %collective-permute-start.2 = (bf16[4,64,128]{2,1,0:T(8,128)(2,1)S(1)}, bf16[4,64,128]{2,1,0:T(8,128)(2,1)S(1)}, u32[]{:S(2)}, u32[]{:S(2)}) collective-permute-start(bf16[4,64,128]{2,1,0:T(8,128)(2,1)S(1)} %get-tuple-element.52), channel_id=1, source_target_pairs={{0,2},{4,6},{8,10},{12,14},{16,18},{20,22},{24,26},{28,30},{2,0},{... | collective-permute-start | bytes 196616 | tf_op jit(solution)/shard_map/ppermute | solution.py:372
  20.6 11.5 %collective-permute-start.3 = (f32[32,1024]{1,0:T(8,128)}, f32[32,1024]{1,0:T(8,128)S(1)}, u32[]{:S(2)}, u32[]{:S(2)}) collective-permute-start(f32[32,1024]{1,0:T(8,128)} %get-tuple-element.61), channel_id=1, source_target_pairs={{0,1},{1,0},{2,3},{3,2},{4,5},{5,4},{6,7},{7,6},{8,9},{9,8},{10,11... | collective-permute-start | bytes 393224 | tf_op jit(solution)/shard_map/ppermute | solution.py:381
  29.6 11.0 %copy-start = (bf16[1024,2048]{1,0:T(8,128)(2,1)S(1)}, bf16[1024,2048]{1,0:T(8,128)(2,1)}, u32[]{:S(2)}) copy-start(bf16[1024,2048]{1,0:T(8,128)(2,1)} %gain_ref.7) | copy-start | bytes 12582916
  29.7 6.9 %collective-permute-start.4 = (f32[32,1408]{1,0:T(8,128)S(1)}, f32[32,1408]{1,0:T(8,128)S(1)}, u32[]{:S(2)}, u32[]{:S(2)}) collective-permute-start(f32[32,1408]{1,0:T(8,128)S(1)} %get-tuple-element.58.z_refs_0_), channel_id=1, source_target_pairs={{0,1},{1,0},{2,3},{3,2},{4,5},{5,4},{6,7},{7,6},{8,9},{9,8},{10,11... | collective-permute-start | bytes 540680 | tf_op jit(solution)/shard_map/ppermute | solution.py:381
  32.0 12.5 %copy-start.2 = (f32[32,2048]{1,0:T(8,128)S(1)}, f32[32,2048]{1,0:T(8,128)}, u32[]{:S(2)}) copy-start(f32[32,2048]{1,0:T(8,128)} %x_ref.1) | copy-start | bytes 786436
  32.0 4.5 %collective-permute-start.5 = (f32[32,640]{1,0:T(8,128)S(1)}, f32[32,640]{1,0:T(8,128)S(1)}, u32[]{:S(2)}, u32[]{:S(2)}) collective-permute-start(f32[32,640]{1,0:T(8,128)S(1)} %get-tuple-element.62.z_refs_1_), channel_id=1, source_target_pairs={{0,1},{1,0},{2,3},{3,2},{4,5},{5,4},{6,7},{7,6},{8,9},{9,8},{10,11... | collective-permute-start | bytes 245768 | tf_op jit(solution)/shard_map/ppermute | solution.py:381
  38.0 6.5 %collective-permute-start.6 = (bf16[4,64,128]{2,1,0:T(8,128)(2,1)S(1)}, bf16[4,64,128]{2,1,0:T(8,128)(2,1)S(1)}, u32[]{:S(2)}, u32[]{:S(2)}) collective-permute-start(bf16[4,64,128]{2,1,0:T(8,128)(2,1)S(1)} %get-tuple-element.66), channel_id=1, source_target_pairs={{2,4},{6,8},{10,12},{14,16},{18,20},{22,24},{26,28},{4,2},{8,6},{1... | collective-permute-start | bytes 196616 | tf_op jit(solution)/shard_map/ppermute | solution.py:372
  40.6 3.9 %collective-permute-start.7 = (bf16[4,64,128]{2,1,0:T(8,128)(2,1)S(1)}, bf16[4,64,128]{2,1,0:T(8,128)(2,1)S(1)}, u32[]{:S(2)}, u32[]{:S(2)}) collective-permute-start(bf16[4,64,128]{2,1,0:T(8,128)(2,1)S(1)} %get-tuple-element.67), channel_id=1, source_target_pairs={{0,2},{4,6},{8,10},{12,14},{16,18},{20,22},{24,26},{28,30},{2,0},{... | collective-permute-start | bytes 196616 | tf_op jit(solution)/shard_map/ppermute | solution.py:372
  45.9 8.6 %collective-permute-start.10 = (bf16[8,64,128]{2,1,0:T(8,128)(2,1)S(1)}, bf16[8,64,128]{2,1,0:T(8,128)(2,1)S(1)}, u32[]{:S(2)}, u32[]{:S(2)}) collective-permute-start(bf16[8,64,128]{2,1,0:T(8,128)(2,1)S(1)} %get-tuple-element.70.mine_ref), channel_id=1, source_target_pairs={{0,1},{1,0},{2,3},{3,2},{4,5},{5,4},{6,7},{7,6},{8,9},{9,8},{10,11... | collective-permute-start | bytes 393224 | tf_op jit(solution)/shard_map/ppermute | solution.py:381
  47.0 6.5 %collective-permute-start.8 = (bf16[4,64,128]{2,1,0:T(8,128)(2,1)S(1)}, bf16[4,64,128]{2,1,0:T(8,128)(2,1)S(1)}, u32[]{:S(2)}, u32[]{:S(2)}) collective-permute-start(bf16[4,64,128]{2,1,0:T(8,128)(2,1)S(1)} %get-tuple-element.69), channel_id=1, source_target_pairs={{2,4},{6,8},{10,12},{14,16},{18,20},{22,24},{26,28},{4,2},{8,6},{1... | collective-permute-start | bytes 196616 | tf_op jit(solution)/shard_map/ppermute | solution.py:372
  53.5 4.3 %collective-permute-start.9 = (bf16[4,64,128]{2,1,0:T(8,128)(2,1)S(1)}, bf16[4,64,128]{2,1,0:T(8,128)(2,1)S(1)}, u32[]{:S(2)}, u32[]{:S(2)}) collective-permute-start(bf16[4,64,128]{2,1,0:T(8,128)(2,1)S(1)} %collective-permute-done.8.first_refs_0_), channel_id=1, source_target_pairs={{0,1},{1,0},{2,3},{3,2},{4,5},{5,4},{6,7},{7,6},{8,9},{9,8},{10,11... | collective-permute-start | bytes 196616 | tf_op jit(solution)/shard_map/ppermute | solution.py:381
  55.1 2.7 %collective-permute-start.11 = (bf16[4,64,128]{2,1,0:T(8,128)(2,1)S(1)}, bf16[4,64,128]{2,1,0:T(8,128)(2,1)S(1)}, u32[]{:S(2)}, u32[]{:S(2)}) collective-permute-start(bf16[4,64,128]{2,1,0:T(8,128)(2,1)S(1)} %get-tuple-element.72), channel_id=1, source_target_pairs={{0,2},{4,6},{8,10},{12,14},{16,18},{20,22},{24,26},{28,30},{2,0},{... | collective-permute-start | bytes 196616 | tf_op jit(solution)/shard_map/ppermute | solution.py:372
  59.7 6.5 %collective-permute-start.12 = (bf16[4,64,128]{2,1,0:T(8,128)(2,1)S(1)}, bf16[4,64,128]{2,1,0:T(8,128)(2,1)S(1)}, u32[]{:S(2)}, u32[]{:S(2)}) collective-permute-start(bf16[4,64,128]{2,1,0:T(8,128)(2,1)S(1)} %get-tuple-element.77), channel_id=1, source_target_pairs={{2,4},{6,8},{10,12},{14,16},{18,20},{22,24},{26,28},{4,2},{8,6},{1... | collective-permute-start | bytes 196616 | tf_op jit(solution)/shard_map/ppermute | solution.py:372
  61.7 4.6 %collective-permute-start.13 = (bf16[4,64,128]{2,1,0:T(8,128)(2,1)S(1)}, bf16[4,64,128]{2,1,0:T(8,128)(2,1)S(1)}, u32[]{:S(2)}, u32[]{:S(2)}) collective-permute-start(bf16[4,64,128]{2,1,0:T(8,128)(2,1)S(1)} %get-tuple-element.78), channel_id=1, source_target_pairs={{0,2},{4,6},{8,10},{12,14},{16,18},{20,22},{24,26},{28,30},{2,0},{... | collective-permute-start | bytes 196616 | tf_op jit(solution)/shard_map/ppermute | solution.py:372
  61.7 6.9 %collective-permute-start.14 = (f32[8,32,128]{2,1,0:T(8,128)S(1)}, f32[8,32,128]{2,1,0:T(8,128)S(1)}, u32[]{:S(2)}, u32[]{:S(2)}) collective-permute-start(f32[8,32,128]{2,1,0:T(8,128)S(1)} %get-tuple-element.81), channel_id=1, source_target_pairs={{0,1},{1,0},{2,3},{3,2},{4,5},{5,4},{6,7},{7,6},{8,9},{9,8},{10,11... | collective-permute-start | bytes 393224 | tf_op jit(solution)/shard_map/ppermute | solution.py:381
  67.6 4.3 %collective-permute-start.15 = (bf16[32,1024]{1,0:T(8,128)(2,1)S(1)}, bf16[32,1024]{1,0:T(8,128)(2,1)S(1)}, u32[]{:S(2)}, u32[]{:S(2)}) collective-permute-start(bf16[32,1024]{1,0:T(8,128)(2,1)S(1)} %get-tuple-element.82), channel_id=1, source_target_pairs={{0,1},{1,0},{2,3},{3,2},{4,5},{5,4},{6,7},{7,6},{8,9},{9,8},{10,11... | collective-permute-start | bytes 196616 | tf_op jit(solution)/shard_map/ppermute | solution.py:381
